TPU v7x, 32 devices: a whole 2x2x4 slice. The times are simulated.
32 devices in a mesh: space: 4 (over y, core), tm: 8 (over z, x).
Axes of the slice: x: 2, y: 2, z: 4, core: 2. Of those that a mesh axis runs over, the one named last changes fastest.
Arguments:
- eigenvectors: bfloat16 [8, 2, 3, 4, 256, 256], P('tm', None, None, 'space'), may hold values from -0.078125 to 0.078125
- momenta: int32 [6, 3], replicated, may hold values from -2 to 2
- displacement: int32 [6], replicated, may hold values from 0 to 3, as said below
- source_times: int32 [4], replicated, may hold values from 0 to 7
- perambulators: bfloat16 [8, 4, 2, 256, 256], P('tm', None, None, 'space'), may hold values from -1 to 1
Outputs:
- correlator: float32 [8, 4, 2, 6, 6], P('tm')
- two_meson: float32 [8, 4, 2, 6, 6], P('tm')
Inputs may be any that keep to these rules, and one draw needn't show every extreme that they name: `displacement`: 0 keeps the site, 1, 2, 3 move one site forward along x, y, z; each of the four values is used by some operator.
All inputs are finite; a program needn't handle non-finite values.
Results may differ from a plain program's by a relative error of at most 0.0078.
Values may be sent and summed in bfloat16 or wider, within the bound.
No kernel may reach another device: no remote copies, remote signals or barrier semaphores. Data moves between devices by JAX's collectives and lax.ppermute only.
A program may use at most 64 MiB of HBM per device.

v0:
```python
import functools
import math

import jax
import jax.numpy as jnp
from jax import lax
from jax.experimental import pallas as pl
from jax.experimental.pallas import tpu as pltpu
from jax.sharding import PartitionSpec as P

LX = 16
LY = 16
PLANE = LX * LY
LANES = 128
F32 = jnp.float32
BF16 = jnp.bfloat16
VMEM_LIMIT = 58 * 1024 * 1024

ANY = pl.BlockSpec(memory_space=pl.ANY)
SMEM = pl.BlockSpec(memory_space=pltpu.SMEM)
VMEM = pl.BlockSpec(memory_space=pltpu.VMEM)


def swap_bit(block, axis, mask):
    count = lax.axis_size(axis)
    return lax.ppermute(block, axis, [(i, i ^ mask) for i in range(count)])


def along_line(block, distance, line):
    route = [
        (2 * z + x, 2 * (z + distance) + x)
        for z in range(line)
        for x in range(2)
        if 0 <= z + distance < line
    ]
    return lax.ppermute(block, "tm", route)


def gather_by_swaps(block):
    count = lax.axis_size("space")
    held = {0: block}
    mask = count // 2
    while mask:
        for key in sorted(held):
            held[key | mask] = swap_bit(held[key], "space", mask)
        mask //= 2
    return [held[key] for key in range(count)]


def params():
    return pltpu.CompilerParams(vmem_limit_bytes=VMEM_LIMIT)


def elemental_kernel(slots, held, stage, last, *refs):
    do_ref, src_ref, off_ref, where_ref, zphase_ref, phase_ref = refs[:6]
    slab_refs = refs[6 : 6 + held]
    rest = refs[6 + held :]
    if stage:
        prior_ref, rest = rest[0], rest[1:]
    if last:
        full_ref, keep_ref, send_ref = rest[:3]
        rest = rest[3:]
    else:
        out_ref, rest = rest[0], rest[1:]
    slabs, turned, acc, sems = rest
    operators, vectors = acc.shape[0], acc.shape[1]
    colours = turned.shape[0]

    copies = []
    for m in range(held):
        copies.append(
            pltpu.make_async_copy(
                slab_refs[m], slabs.at[m, :, pl.ds(0, PLANE), :], sems.at[2 * m]
            )
        )
        copies.append(
            pltpu.make_async_copy(
                slab_refs[m].at[:, pl.ds(0, LX), :],
                slabs.at[m, :, pl.ds(PLANE, LX), :],
                sems.at[2 * m + 1],
            )
        )
    for copy in copies:
        copy.start()
    if stage:
        acc[...] = prior_ref[...]
    else:
        acc[...] = jnp.zeros_like(acc)
    for copy in copies:
        copy.wait()

    row = lax.broadcasted_iota(jnp.int32, (PLANE, PLANE), 0)
    column = lax.broadcasted_iota(jnp.int32, (PLANE, PLANE), 1)
    wanted = jnp.where(row % LX == LX - 1, row - (LX - 1), row + 1)
    step_x = (column == wanted).astype(F32).astype(BF16)

    def one_slab(m, carry):
        for colour in range(colours):
            for part in range(2):
                block = slabs[m, part * colours + colour, pl.ds(0, PLANE), :]
                turned[colour, :, pl.ds(part * PLANE, PLANE)] = block.T
                moved = jnp.dot(step_x, block, preferred_element_type=F32)
                slabs[held, part * colours + colour, pl.ds(0, PLANE), :] = moved.astype(BF16)

        def one_operator(o, inner):
            @pl.when(do_ref[m, o] == stage)
            def _():
                src = src_ref[m, o]
                off = pl.multiple_of(off_ref[o], LX)
                cos_z, sin_z = zphase_ref[0, m, o], zphase_ref[1, m, o]
                cos_p, sin_p = phase_ref[o, 0], phase_ref[o, 1]
                cosine = cos_p * cos_z - sin_p * sin_z
                sine = sin_p * cos_z + cos_p * sin_z
                wide = vectors // LANES
                cosine = jnp.concatenate([cosine] * wide, axis=1)
                sine = jnp.concatenate([sine] * wide, axis=1)
                total = None
                for colour in range(colours):
                    real = slabs[src, colour, pl.ds(off, PLANE), :].astype(F32)
                    imaginary = slabs[src, colours + colour, pl.ds(off, PLANE), :].astype(F32)
                    w_real = (cosine * real + sine * imaginary).astype(BF16)
                    w_imaginary = (cosine * imaginary - sine * real).astype(BF16)
                    right = jnp.concatenate(
                        [
                            jnp.concatenate([w_real, w_imaginary], axis=1),
                            jnp.concatenate([w_imaginary, -w_real], axis=1),
                        ],
                        axis=0,
                    )
                    term = jnp.dot(turned[colour], right, preferred_element_type=F32)
                    total = term if total is None else total + term
                acc[o] += total

            return inner

        return lax.fori_loop(0, operators, one_operator, carry)

    lax.fori_loop(0, held, one_slab, 0)

    if last:
        block_rows = keep_ref.shape[2]
        first = pl.multiple_of(where_ref[0] * block_rows, block_rows)
        half = where_ref[1]
        for o in range(operators):
            full_ref[o] = acc[o].astype(BF16)
        for o in range(operators):
            for part in range(2):
                own = full_ref[o, pl.ds(first, block_rows), pl.ds(part * vectors, vectors)]
                low, high = own[:, :LANES], own[:, LANES:]
                keep_ref[part, o] = jnp.where(half == 0, low, high)
                send_ref[part, o] = jnp.where(half == 0, high, low)
    else:
        out_ref[...] = acc[...]


def elementals(stage, last, tables, slab_list, prior, block_rows):
    parts_colours, plane, vectors = slab_list[0].shape
    colours = parts_colours // 2
    slots = len(slab_list)
    operators = tables[0].shape[1]
    wide = jax.ShapeDtypeStruct((operators, vectors, 2 * vectors), F32)
    if last:
        piece = jax.ShapeDtypeStruct((2, operators, block_rows, LANES), BF16)
        outs = (jax.ShapeDtypeStruct(wide.shape, BF16), piece, piece)
        out_specs = (VMEM, VMEM, VMEM)
    else:
        outs, out_specs = wide, VMEM
    priors = [prior] if stage else []
    return pl.pallas_call(
        functools.partial(elemental_kernel, slots, slots, stage, last),
        out_shape=outs,
        in_specs=[SMEM] * 5 + [VMEM] + [ANY] * slots + [VMEM] * len(priors),
        out_specs=out_specs,
        scratch_shapes=[
            pltpu.VMEM((slots + 1, parts_colours, plane + LX, vectors), BF16),
            pltpu.VMEM((colours, vectors, 2 * plane), BF16),
            pltpu.VMEM(wide.shape, F32),
            pltpu.SemaphoreType.DMA((2 * slots,)),
        ],
        compiler_params=params(),
        cost_estimate=pl.CostEstimate(
            flops=2 * slots * operators * parts_colours * plane * vectors * 2 * vectors // 2,
            bytes_accessed=slots * parts_colours * plane * vectors * 2,
            transcendentals=0,
        ),
        name="elementals_last" if last else "elementals_first",
    )(*tables, *slab_list, *priors)


def both_kernel(blocks, where_ref, order_ref, e_ref, *refs):
    peram_refs = refs[:blocks]
    keep_ref, send_ref, whole, left, turned, middle, sems = refs[blocks:]
    sources, _, vectors, _ = whole.shape
    operators = e_ref.shape[0]
    block_rows = keep_ref.shape[3]
    copies = []
    for m in range(blocks):
        begin = pl.multiple_of(order_ref[m] * block_rows, block_rows)
        copies.append(
            pltpu.make_async_copy(
                peram_refs[m], whole.at[:, :, pl.ds(begin, block_rows), :], sems.at[m]
            )
        )
    for copy in copies:
        copy.start()
    for copy in copies:
        copy.wait()
    first = pl.multiple_of(where_ref[0] * block_rows, block_rows)
    half = where_ref[1]
    for s in range(sources):
        for part in range(2):
            turned[part] = whole[s, part].T
        real = turned[0, pl.ds(first, block_rows), :]
        imaginary = turned[1, pl.ds(first, block_rows), :]
        base = 2 * s * block_rows
        left[pl.ds(base, block_rows), :] = jnp.concatenate([real, -imaginary], axis=1)
        left[pl.ds(base + block_rows, block_rows), :] = jnp.concatenate([imaginary, real], axis=1)
    for a in range(operators):
        product = lax.dot_general(
            left[...], e_ref[a], (((1,), (1,)), ((), ())), preferred_element_type=F32
        )
        high = product.astype(BF16)
        low = (product - high.astype(F32)).astype(BF16)
        for s in range(sources):
            for part in range(2):
                base = (2 * s + part) * block_rows
                rows = pl.ds(a * block_rows, block_rows)
                columns = pl.ds(part * vectors, vectors)
                middle[0, s, rows, columns] = high[base : base + block_rows]
                middle[1, s, rows, columns] = low[base : base + block_rows]
    for s in range(sources):
        real, imaginary = whole[s, 0], whole[s, 1]
        right = jnp.concatenate(
            [
                jnp.concatenate([real, -imaginary], axis=1),
                jnp.concatenate([imaginary, real], axis=1),
            ],
            axis=0,
        )
        image = jnp.dot(middle[0, s], right, preferred_element_type=F32)
        image = image + jnp.dot(middle[1, s], right, preferred_element_type=F32)
        image = image.astype(BF16)
        for a in range(operators):
            for part in range(2):
                rows = image[a * block_rows : (a + 1) * block_rows]
                low = rows[:, part * vectors : part * vectors + LANES]
                high = rows[:, part * vectors + LANES : (part + 1) * vectors]
                keep_ref[s, part, a] = jnp.where(half == 0, low, high)
                send_ref[s, part, a] = jnp.where(half == 0, high, low)


def both_sides(where, order, elements, perams):
    blocks = len(perams)
    sources, _, block_rows, vectors = perams[0].shape
    operators = elements.shape[0]
    piece = jax.ShapeDtypeStruct((sources, 2, operators, block_rows, LANES), BF16)
    return pl.pallas_call(
        functools.partial(both_kernel, blocks),
        out_shape=(piece, piece),
        in_specs=[SMEM, SMEM, VMEM] + [ANY] * blocks,
        out_specs=(VMEM, VMEM),
        scratch_shapes=[
            pltpu.VMEM((sources, 2, vectors, vectors), BF16),
            pltpu.VMEM((sources * 2 * block_rows, 2 * vectors), BF16),
            pltpu.VMEM((2, vectors, vectors), BF16),
            pltpu.VMEM((2, sources, operators * block_rows, 2 * vectors), BF16),
            pltpu.SemaphoreType.DMA((blocks,)),
        ],
        compiler_params=params(),
        cost_estimate=pl.CostEstimate(
            flops=2 * 3 * sources * operators * 4 * block_rows * vectors * vectors,
            bytes_accessed=8 * sources * vectors * vectors,
            transcendentals=0,
        ),
        name="both_sides",
    )(where, order, elements, *perams)


def trace_kernel(offsets, pick_ref, *refs):
    count = len(offsets)
    same, other = refs[:count], refs[count : 2 * count]
    own_ref, pair_ref, out_ref, picked, wide_e, wide_g, sems = refs[2 * count :]
    sources = own_ref.shape[0]
    _, operators, block_rows, lanes = same[0].shape
    rows = 2 * operators
    for s in range(sources):
        for cls, pool in enumerate((same, other)):
            for at, distance in enumerate(offsets):

                @pl.when((pick_ref[0, s] == cls) & (pick_ref[1, s] == distance))
                def _(pool=pool, at=at, s=s):
                    pltpu.make_async_copy(pool[at], picked.at[s], sems.at[s]).start()

    def spread(wide, count_rows):
        pieces = [
            wide[pl.ds(k, count_rows, stride=block_rows), :].astype(BF16)
            for k in range(block_rows)
        ]
        return jnp.concatenate(pieces, axis=1)

    for s in range(sources):
        wide_g[pl.ds(0, rows * block_rows), :] = (
            own_ref[s].astype(F32).reshape(rows * block_rows, lanes)
        )
        wide_g[pl.ds(rows * block_rows, rows * block_rows), :] = (
            pair_ref[s].astype(F32).reshape(rows * block_rows, lanes)
        )
        pltpu.make_async_copy(same[0], picked.at[s], sems.at[s]).wait()
        wide_e[...] = picked[s].astype(F32).reshape(rows * block_rows, lanes)
        out_ref[s] = lax.dot_general(
            spread(wide_g, 2 * rows),
            spread(wide_e, rows),
            (((1,), (1,)), ((), ())),
            preferred_element_type=F32,
        )


def traces(pick, offsets, same, other, own, pair):
    sources, _, operators, block_rows, lanes = own.shape
    rows = 2 * operators
    return pl.pallas_call(
        functools.partial(trace_kernel, offsets),
        out_shape=jax.ShapeDtypeStruct((sources, 2 * rows, rows), F32),
        in_specs=[SMEM] + [ANY] * (2 * len(offsets)) + [VMEM, VMEM],
        out_specs=VMEM,
        scratch_shapes=[
            pltpu.VMEM((sources,) + same[0].shape, BF16),
            pltpu.VMEM((rows * block_rows, lanes), F32),
            pltpu.VMEM((2 * rows * block_rows, lanes), F32),
            pltpu.SemaphoreType.DMA((sources,)),
        ],
        compiler_params=params(),
        cost_estimate=pl.CostEstimate(
            flops=4 * sources * rows * rows * block_rows * lanes,
            bytes_accessed=6 * own.size,
            transcendentals=0,
        ),
        name="traces",
    )(pick, *same, *other, own, pair)


def phase_tables(momenta, z_coords, z_extent):
    plane = jnp.arange(PLANE, dtype=jnp.int32)
    along_x = (momenta[:, 0:1] * (plane % LX)[None] % LX).astype(F32) * (2.0 * math.pi / LX)
    along_y = (momenta[:, 1:2] * (plane // LX)[None] % LY).astype(F32) * (2.0 * math.pi / LY)
    angle = along_x + along_y
    table = jnp.stack([jnp.cos(angle), jnp.sin(angle)], axis=1)
    table = jnp.broadcast_to(table[..., None], table.shape + (LANES,))
    along_z = (momenta[:, 2][None, :] * z_coords[:, None] % z_extent).astype(F32) * (
        2.0 * math.pi / z_extent
    )
    return table, jnp.stack([jnp.cos(along_z), jnp.sin(along_z)])


def body(eigenvectors, momenta, displacement, source_times, perambulators):
    _, parts, colours, _, plane, vectors = eigenvectors.shape
    slabs = lax.axis_size("space")
    line = lax.axis_size("tm") // 2
    block_rows = vectors // slabs
    me = lax.axis_index("space").astype(jnp.int32)
    time = lax.axis_index("tm").astype(jnp.int32)
    where = jnp.stack([me, time % 2])
    order = jnp.arange(slabs, dtype=jnp.int32) ^ me
    above = ((order + 1) % slabs) ^ me
    near = min(2, slabs)

    own = eigenvectors.reshape(parts * colours, plane, vectors)
    slab_list = gather_by_swaps(own)
    near_list = [own] + [swap_bit(own, "space", 1)] * (near - 1)

    moves_z = displacement[None, :] == 3
    slot = jnp.arange(slabs, dtype=jnp.int32)[:, None]

    def tables(held):
        source = jnp.where(
            moves_z, above[:held, None], jnp.where(displacement[None, :] == 1, held, slot[:held])
        )
        late = (slot[:held] >= near) | (moves_z & (above[:held, None] >= near))
        plane_phase, z_phase = phase_tables(momenta, order[:held], slabs)
        return (
            late.astype(jnp.int32),
            source.astype(jnp.int32),
            jnp.where(displacement == 2, LX, 0).astype(jnp.int32),
            where,
            z_phase,
            plane_phase,
        )

    early = elementals(0, False, tables(near), near_list, None, block_rows)
    full, keep, send = elementals(1, True, tables(slabs), slab_list, early, block_rows)
    received = swap_bit(send, "tm", 1)

    offsets = [0]
    same, other = [keep], [received]
    for distance in range(1, line):
        for sign in (1, -1):
            offsets.append(-sign * distance)
            same.append(along_line(keep, sign * distance, line))
    for distance in range(1, line):
        for sign in (1, -1):
            other.append(along_line(received, sign * distance, line))

    peram, _ = lax.optimization_barrier((perambulators[0], slab_list[slabs // 2]))
    perams = gather_by_swaps(peram)
    g_keep, g_send = both_sides(where, order, full, perams)
    g_pair = swap_bit(g_send, "tm", 1)

    pick = jnp.stack([(source_times % 2) ^ (time % 2), source_times // 2 - time // 2])
    raw = traces(pick.astype(jnp.int32), offsets, same, other, g_keep, g_pair)
    operators = momenta.shape[0]
    rows = 2 * operators
    mine = raw[:, :rows] + swap_bit(raw[:, rows:], "tm", 1)
    total = lax.psum(mine, "space")
    n = operators
    real = total[:, :n, :n] - total[:, n:, n:]
    imaginary = total[:, :n, n:] + total[:, n:, :n]
    diag_real = jnp.diagonal(real, axis1=1, axis2=2)
    diag_imaginary = jnp.diagonal(imaginary, axis1=1, axis2=2)
    pair_real = (
        diag_real[:, :, None] * diag_real[:, None, :]
        - diag_imaginary[:, :, None] * diag_imaginary[:, None, :]
    )
    pair_imaginary = (
        diag_real[:, :, None] * diag_imaginary[:, None, :]
        + diag_imaginary[:, :, None] * diag_real[:, None, :]
    )
    correlator = jnp.stack([real, imaginary], axis=1)[None]
    two_meson = jnp.stack([pair_real, pair_imaginary], axis=1)[None]
    return (correlator, two_meson)


def solution(mesh):
    placed = (
        P("tm", None, None, "space", None, None),
        P(),
        P(),
        P(),
        P("tm", None, None, "space", None),
    )
    return jax.shard_map(
        body,
        mesh=mesh,
        in_specs=placed,
        out_specs=(P("tm", None, None, None, None), P("tm", None, None, None, None)),
        check_vma=False,
    )
```

profile of v0, /device:TPU:0, one launch (start us, length us, event | category | flops | bytes accessed | tf_op | source)
XLA Modules:
  0.0 151.9 jit_solution(14267063404269130867)
XLA Ops:
  0.6 0.5 collective-permute-start
  1.1 2.6 %collective-permute-start.1 = (bf16[6,256,256]{2,1,0:T(8,128)(2,1)}, bf16[6,256,256]{2,1,0:T(8,128)(2,1)S(1)}, u32[]{:S(2)}, u32[]{:S(2)}) collective-permute-start(bf16[6,256,256]{2,1,0:T(8,128)(2,1)} %bitcast.37), channel_id=1, source_target_pairs={{0,16},{8,24},{16,0},{24,8},{1,17},{9,25},{17,1},{25,9},{2,18},{10... | collective-permute-start | bytes 2359304 | tf_op jit(solution)/shard_map/ppermute | solution.py:26
  3.8 0.7 broadcast_compare_fusion.1
  4.5 0.8 slice_bitcast_fusion.1
  5.5 0.6 pad_maximum_fusion.1.refs_4_
  6.4 0.6 pad_maximum_fusion.2.refs_4_
  7.0 0.6 or_convert_fusion.refs_0_
  7.6 0.6 select_select_fusion.1.refs_1_
  8.3 0.7 select_select_fusion.refs_1_
  8.9 13.2 %collective-permute-done.1.refs_8_ = bf16[6,256,256]{2,1,0:T(8,128)(2,1)S(1)} collective-permute-done((bf16[6,256,256]{2,1,0:T(8,128)(2,1)}, bf16[6,256,256]{2,1,0:T(8,128)(2,1)S(1)}, u32[]{:S(2)}, u32[]{:S(2)}) %collective-permute-start.1) | collective-permute-done | bytes 786464 | tf_op jit(solution)/shard_map/ppermute | solution.py:26
  22.1 1.3 compare_select_fusion.8.refs_2_
  23.4 0.6 or_convert_fusion.1.refs_0_
  24.0 1.8 %collective-permute-start.17 = (bf16[4,2,64,256]{3,2,1,0:T(8,128)(2,1)}, bf16[4,2,64,256]{3,2,1,0:T(8,128)(2,1)S(1)}, u32[]{:S(2)}, u32[]{:S(2)}) collective-permute-start(bf16[4,2,64,256]{3,2,1,0:T(8,128)(2,1)} %bitcast.40), channel_id=1, source_target_pairs={{0,16},{8,24},{16,0},{24,8},{1,17},{9,25},{17,1},{25,9},{2,18},{10... | collective-permute-start | bytes 786440 | tf_op jit(solution)/shard_map/ppermute | solution.py:26
  25.8 0.6 pad_add_fusion.1.refs_3_.where_ref
  26.6 1.6 %broadcast_in_dim.130.refs_5_ = f32[6,2,256,128]{3,2,1,0:T(8,128)} broadcast(f32[6,2,256]{2,1,0:T(2,128)S(1)} %pad_maximum_fusion), dimensions={0,1,2} | broadcast | bytes 1585152 | tf_op jit(solution)/shard_map/broadcast_in_dim | solution.py:348
  28.2 14.0 %elementals_first.1.refs_10_ = f32[6,256,512]{2,1,0:T(8,128)} custom-call(s32[2,6]{1,0:T(2,128)} %or_convert_fusion.refs_0_, s32[2,6]{1,0:T(2,128)} %select_select_fusion.1.refs_1_, s32[6]{0:T(128)} %compare_select_fusion.8.refs_2_, s32[2]{0:T(128)} %pad_add_fusion.1.refs_3_.where_ref, f32[2,2,6]{2,1,0:T(2,128)} %pad_maximum_fusion.2.refs_4_, ...), custom_call_target="tpu_custom_call" | custom-call | flops 2415919104 | bytes 1572864 | tf_op jit(solution)/shard_map/elementals_first/pallas_call | solution.py:169
  42.6 1.0 copy-done.19
  43.6 20.4 %elementals_last.1 = (bf16[6,256,512]{2,1,0:T(8,128)(2,1)}, bf16[2,6,64,128]{3,2,1,0:T(8,128)(2,1)}, bf16[2,6,64,128]{3,2,1,0:T(8,128)(2,1)}) custom-call(s32[4,6]{1,0:T(4,128)} %or_convert_fusion.1.refs_0_, s32[4,6]{1,0:T(4,128)} %select_select_fusion.refs_1_, s32[6]{0:T(128)} %compare_select_fusion.8.refs_2_, s32[2]{0:T(128)} %pad_add_fusion.1.refs_3_.where_ref, ...), custom_call_target="tpu_custom_call" | custom-call | flops 4831838208 | bytes 3145728 | tf_op jit(solution)/shard_map/elementals_last/pallas_call | solution.py:169
  64.0 3.5 %collective-permute-start.3 = (bf16[2,6,64,128]{3,2,1,0:T(8,128)(2,1)}, bf16[2,6,64,128]{3,2,1,0:T(8,128)(2,1)S(1)}, u32[]{:S(2)}, u32[]{:S(2)}) collective-permute-start(bf16[2,6,64,128]{3,2,1,0:T(8,128)(2,1)} %get-tuple-element.8.refs_0_), channel_id=1, source_target_pairs={{0,2},{1,3},{2,4},{3,5},{4,6},{5,7},{8,10},{9,11},{10,12},{11,13},... | collective-permute-start | bytes 589832 | tf_op jit(solution)/shard_map/ppermute | solution.py:36
  67.6 0.7 copy-done.21
  68.3 6.7 %both_sides.1 = (bf16[4,2,6,64,128]{4,3,2,1,0:T(8,128)(2,1)}, bf16[4,2,6,64,128]{4,3,2,1,0:T(8,128)(2,1)}) custom-call(s32[2]{0:T(128)} %pad_add_fusion.1.refs_3_.where_ref, s32[4]{0:T(128)} %copy-done.15, bf16[6,256,512]{2,1,0:T(8,128)(2,1)} %get-tuple-element.10.e_ref, bf16[4,2,64,256]{3,2,1,0:T(8,128)(2,1)} %bitcast.42, ...), custom_call_target="tpu_custom_call" | custom-call | flops 2415919104 | bytes 2097152 | tf_op jit(solution)/shard_map/both_sides/pallas_call | solution.py:257
  75.0 1.6 %collective-permute-start.19 = (bf16[4,2,6,64,128]{4,3,2,1,0:T(8,128)(2,1)}, bf16[4,2,6,64,128]{4,3,2,1,0:T(8,128)(2,1)S(1)}, u32[]{:S(2)}, u32[]{:S(2)}) collective-permute-start(bf16[4,2,6,64,128]{4,3,2,1,0:T(8,128)(2,1)} %get-tuple-element.13), channel_id=1, source_target_pairs={{0,1},{1,0},{2,3},{3,2},{4,5},{5,4},{6,7},{7,6},{8,9},{9,8},{10,11... | collective-permute-start | bytes 2359304 | tf_op jit(solution)/shard_map/ppermute | solution.py:26
  76.6 1.3 collective-permute-start.4
  77.9 5.6 %collective-permute-start.5 = (bf16[2,6,64,128]{3,2,1,0:T(8,128)(2,1)S(1)}, bf16[2,6,64,128]{3,2,1,0:T(8,128)(2,1)S(1)}, u32[]{:S(2)}, u32[]{:S(2)}) collective-permute-start(bf16[2,6,64,128]{3,2,1,0:T(8,128)(2,1)S(1)} %copy-done.1), channel_id=1, source_target_pairs={{0,4},{1,5},{2,6},{3,7},{8,12},{9,13},{10,14},{11,15},{16,20},{17,... | collective-permute-start | bytes 589832 | tf_op jit(solution)/shard_map/ppermute | solution.py:36
  83.5 0.6 collective-permute-start.9
  84.1 1.3 collective-permute-start.6
  85.4 6.5 %collective-permute-start.7 = (bf16[2,6,64,128]{3,2,1,0:T(8,128)(2,1)S(1)}, bf16[2,6,64,128]{3,2,1,0:T(8,128)(2,1)S(1)}, u32[]{:S(2)}, u32[]{:S(2)}) collective-permute-start(bf16[2,6,64,128]{3,2,1,0:T(8,128)(2,1)S(1)} %copy-done.1), channel_id=1, source_target_pairs={{0,6},{1,7},{8,14},{9,15},{16,22},{17,23},{24,30},{25,31}} | collective-permute-start | bytes 589832 | tf_op jit(solution)/shard_map/ppermute | solution.py:36
  91.9 1.3 collective-permute-start.8
  93.2 5.7 %collective-permute-done.9.refs_7_ = bf16[2,6,64,128]{3,2,1,0:T(8,128)(2,1)S(1)} collective-permute-done((bf16[2,6,64,128]{3,2,1,0:T(8,128)(2,1)S(1)}, bf16[2,6,64,128]{3,2,1,0:T(8,128)(2,1)S(1)}, u32[]{:S(2)}, u32[]{:S(2)}) %collective-permute-start.9) | collective-permute-done | bytes 196640 | tf_op jit(solution)/shard_map/ppermute | solution.py:26
  98.9 3.5 %collective-permute-start.10 = (bf16[2,6,64,128]{3,2,1,0:T(8,128)(2,1)S(1)}, bf16[2,6,64,128]{3,2,1,0:T(8,128)(2,1)S(1)}, u32[]{:S(2)}, u32[]{:S(2)}) collective-permute-start(bf16[2,6,64,128]{3,2,1,0:T(8,128)(2,1)S(1)} %collective-permute-done.9.refs_7_), channel_id=1, source_target_pairs={{0,2},{1,3},{2,4},{3,5},{4,6},{5,7},{8,10},{9,11},{10,12},{11,13},... | collective-permute-start | bytes 589832 | tf_op jit(solution)/shard_map/ppermute | solution.py:36
  102.4 1.3 collective-permute-start.11
  103.7 5.6 %collective-permute-start.12 = (bf16[2,6,64,128]{3,2,1,0:T(8,128)(2,1)S(1)}, bf16[2,6,64,128]{3,2,1,0:T(8,128)(2,1)S(1)}, u32[]{:S(2)}, u32[]{:S(2)}) collective-permute-start(bf16[2,6,64,128]{3,2,1,0:T(8,128)(2,1)S(1)} %collective-permute-done.9.refs_7_), channel_id=1, source_target_pairs={{0,4},{1,5},{2,6},{3,7},{8,12},{9,13},{10,14},{11,15},{16,20},{17,... | collective-permute-start | bytes 589832 | tf_op jit(solution)/shard_map/ppermute | solution.py:36
  109.3 1.3 collective-permute-start.13
  110.7 5.1 %collective-permute-start.14 = (bf16[2,6,64,128]{3,2,1,0:T(8,128)(2,1)S(1)}, bf16[2,6,64,128]{3,2,1,0:T(8,128)(2,1)S(1)}, u32[]{:S(2)}, u32[]{:S(2)}) collective-permute-start(bf16[2,6,64,128]{3,2,1,0:T(8,128)(2,1)S(1)} %collective-permute-done.9.refs_7_), channel_id=1, source_target_pairs={{0,6},{1,7},{8,14},{9,15},{16,22},{17,23},{24,30},{25,31}} | collective-permute-start | bytes 589832 | tf_op jit(solution)/shard_map/ppermute | solution.py:36
  115.8 1.3 collective-permute-start.15
  117.2 0.6 pad_add_fusion.pick_ref
  117.7 7.9 %collective-permute-done.13.refs_11_ = bf16[2,6,64,128]{3,2,1,0:T(8,128)(2,1)S(1)} collective-permute-done((bf16[2,6,64,128]{3,2,1,0:T(8,128)(2,1)S(1)}, bf16[2,6,64,128]{3,2,1,0:T(8,128)(2,1)S(1)}, u32[]{:S(2)}, u32[]{:S(2)}) %collective-permute-start.13) | collective-permute-done | bytes 196640 | tf_op jit(solution)/shard_map/ppermute | solution.py:36
  125.7 0.5 copy-done.12
  126.7 6.3 %traces.1 = f32[4,24,12]{2,1,0:T(8,128)} custom-call(s32[2,4]{1,0:T(2,128)} %pad_add_fusion.pick_ref, bf16[2,6,64,128]{3,2,1,0:T(8,128)(2,1)} %get-tuple-element.8.refs_0_, bf16[2,6,64,128]{3,2,1,0:T(8,128)(2,1)} %copy-done.2, bf16[2,6,64,128]{3,2,1,0:T(8,128)(2,1)} %copy-done.3, bf16[2,6,64,128]{3,2,1,0:T(8,128)(2,1)} %copy-done.4, ...), custom_call_target="tpu_custom_call" | custom-call | flops 18874368 | bytes 2359296 | tf_op jit(solution)/shard_map/traces/pallas_call | solution.py:321
  133.0 0.8 slice.66
  133.7 1.2 collective-permute-start.20
  135.0 2.7 %collective-permute-done.20 = f32[4,12,12]{2,1,0:T(8,128)S(1)} collective-permute-done((f32[4,12,12]{2,1,0:T(8,128)S(1)}, f32[4,12,12]{2,1,0:T(8,128)S(1)}, u32[]{:S(2)}, u32[]{:S(2)}) %collective-permute-start.20) | collective-permute-done | bytes 2336 | tf_op jit(solution)/shard_map/ppermute | solution.py:26
  137.6 0.8 slice_add_fusion
  138.4 10.4 %psum.7 = f32[4,12,12]{2,1,0:T(8,128)S(1)} all-reduce(f32[4,12,12]{2,1,0:T(8,128)S(1)} %slice_add_fusion), channel_id=1, replica_groups=mesh['space'=4,'tm'=8] {'space'}, use_global_device_ids=true, to_apply=%region_0.1 | all-reduce | flops 576 | bytes 4608 | tf_op jit(solution)/shard_map/psum | solution.py:413
  149.1 0.6 copy.13
  149.7 0.6 gather_fusion.1
  150.4 0.6 gather_fusion
  151.2 0.6 maximum_bitcast_fusion.1
  (86 shorter events, 2.4 us)
Async XLA Ops:
  0.6 25.9 %collective-permute-start = (bf16[6,256,256]{2,1,0:T(8,128)(2,1)}, bf16[6,256,256]{2,1,0:T(8,128)(2,1)S(1)}, u32[]{:S(2)}, u32[]{:S(2)}) collective-permute-start(bf16[6,256,256]{2,1,0:T(8,128)(2,1)} %bitcast.36), channel_id=1, source_target_pairs={{0,8},{8,0},{16,24},{24,16},{1,9},{9,1},{17,25},{25,17},{2,10},{10... | collective-permute-start | bytes 2359304 | tf_op jit(solution)/shard_map/ppermute | solution.py:26
  1.1 20.9 %collective-permute-start.1 = (bf16[6,256,256]{2,1,0:T(8,128)(2,1)}, bf16[6,256,256]{2,1,0:T(8,128)(2,1)S(1)}, u32[]{:S(2)}, u32[]{:S(2)}) collective-permute-start(bf16[6,256,256]{2,1,0:T(8,128)(2,1)} %bitcast.37), channel_id=1, source_target_pairs={{0,16},{8,24},{16,0},{24,8},{1,17},{9,25},{17,1},{25,9},{2,18},{10... | collective-permute-start | bytes 2359304 | tf_op jit(solution)/shard_map/ppermute | solution.py:26
  3.8 38.4 %copy-start.15 = (s32[4]{0:T(128)}, s32[4]{0:T(128)S(1)}, u32[]{:S(2)}) copy-start(s32[4]{0:T(128)S(1)} %iota_xor_fusion.order_ref) | copy-start | bytes 52
  22.1 20.1 %copy-start.18 = (bf16[6,256,256]{2,1,0:T(8,128)(2,1)}, bf16[6,256,256]{2,1,0:T(8,128)(2,1)S(1)}, u32[]{:S(2)}) copy-start(bf16[6,256,256]{2,1,0:T(8,128)(2,1)S(1)} %collective-permute-done.1.refs_8_) | copy-start | bytes 2359300
  22.1 20.5 %collective-permute-start.2 = (bf16[6,256,256]{2,1,0:T(8,128)(2,1)S(1)}, bf16[6,256,256]{2,1,0:T(8,128)(2,1)S(1)}, u32[]{:S(2)}, u32[]{:S(2)}) collective-permute-start(bf16[6,256,256]{2,1,0:T(8,128)(2,1)S(1)} %collective-permute-done.1.refs_8_), channel_id=1, source_target_pairs={{0,8},{8,0},{16,24},{24,16},{1,9},{9,1},{17,25},{25,17},{2,10},{10... | collective-permute-start | bytes 2359304 | tf_op jit(solution)/shard_map/ppermute | solution.py:26
  24.0 18.2 %collective-permute-start.17 = (bf16[4,2,64,256]{3,2,1,0:T(8,128)(2,1)}, bf16[4,2,64,256]{3,2,1,0:T(8,128)(2,1)S(1)}, u32[]{:S(2)}, u32[]{:S(2)}) collective-permute-start(bf16[4,2,64,256]{3,2,1,0:T(8,128)(2,1)} %bitcast.40), channel_id=1, source_target_pairs={{0,16},{8,24},{16,0},{24,8},{1,17},{9,25},{17,1},{25,9},{2,18},{10... | collective-permute-start | bytes 786440 | tf_op jit(solution)/shard_map/ppermute | solution.py:26
  26.4 41.2 %collective-permute-start.16 = (bf16[4,2,64,256]{3,2,1,0:T(8,128)(2,1)}, bf16[4,2,64,256]{3,2,1,0:T(8,128)(2,1)S(1)}, u32[]{:S(2)}, u32[]{:S(2)}) collective-permute-start(bf16[4,2,64,256]{3,2,1,0:T(8,128)(2,1)} %bitcast.41), channel_id=1, source_target_pairs={{0,8},{8,0},{16,24},{24,16},{1,9},{9,1},{17,25},{25,17},{2,10},{10... | collective-permute-start | bytes 786440 | tf_op jit(solution)/shard_map/ppermute | solution.py:26
  26.6 1.6 %copy-start.17 = (bf16[6,256,256]{2,1,0:T(8,128)(2,1)}, bf16[6,256,256]{2,1,0:T(8,128)(2,1)S(1)}, u32[]{:S(2)}) copy-start(bf16[6,256,256]{2,1,0:T(8,128)(2,1)S(1)} %collective-permute-done.refs_7_) | copy-start | bytes 2359300
  42.2 21.8 %copy-start.20 = (bf16[4,2,64,256]{3,2,1,0:T(8,128)(2,1)}, bf16[4,2,64,256]{3,2,1,0:T(8,128)(2,1)S(1)}, u32[]{:S(2)}) copy-start(bf16[4,2,64,256]{3,2,1,0:T(8,128)(2,1)S(1)} %collective-permute-done.17.refs_2_) | copy-start | bytes 786436
  42.2 25.3 %collective-permute-start.18 = (bf16[4,2,64,256]{3,2,1,0:T(8,128)(2,1)S(1)}, bf16[4,2,64,256]{3,2,1,0:T(8,128)(2,1)S(1)}, u32[]{:S(2)}, u32[]{:S(2)}) collective-permute-start(bf16[4,2,64,256]{3,2,1,0:T(8,128)(2,1)S(1)} %collective-permute-done.17.refs_2_), channel_id=1, source_target_pairs={{0,8},{8,0},{16,24},{24,16},{1,9},{9,1},{17,25},{25,17},{2,10},{10... | collective-permute-start | bytes 786440 | tf_op jit(solution)/shard_map/ppermute | solution.py:26
  42.6 1.0 copy-start.19
  64.0 20.1 %collective-permute-start.3 = (bf16[2,6,64,128]{3,2,1,0:T(8,128)(2,1)}, bf16[2,6,64,128]{3,2,1,0:T(8,128)(2,1)S(1)}, u32[]{:S(2)}, u32[]{:S(2)}) collective-permute-start(bf16[2,6,64,128]{3,2,1,0:T(8,128)(2,1)} %get-tuple-element.8.refs_0_), channel_id=1, source_target_pairs={{0,2},{1,3},{2,4},{3,5},{4,6},{5,7},{8,10},{9,11},{10,12},{11,13},... | collective-permute-start | bytes 589832 | tf_op jit(solution)/shard_map/ppermute | solution.py:36
  67.5 0.7 copy-start.21
  67.5 0.8 copy-start.22
  68.3 8.3 %copy-start.1 = (bf16[2,6,64,128]{3,2,1,0:T(8,128)(2,1)S(1)}, bf16[2,6,64,128]{3,2,1,0:T(8,128)(2,1)}, u32[]{:S(2)}) copy-start(bf16[2,6,64,128]{3,2,1,0:T(8,128)(2,1)} %get-tuple-element.8.refs_0_) | copy-start | bytes 589828
  68.3 15.2 %copy-start.23 = (bf16[2,6,64,128]{3,2,1,0:T(8,128)(2,1)S(1)}, bf16[2,6,64,128]{3,2,1,0:T(8,128)(2,1)}, u32[]{:S(2)}) copy-start(bf16[2,6,64,128]{3,2,1,0:T(8,128)(2,1)} %get-tuple-element.9) | copy-start | bytes 589828
  68.3 48.8 %copy-start.16 = (s32[4]{0:T(128)S(1)}, s32[4]{0:T(128)}, u32[]{:S(2)}) copy-start(s32[4]{0:T(128)} %param.8) | copy-start | bytes 52
  75.0 50.6 %collective-permute-start.19 = (bf16[4,2,6,64,128]{4,3,2,1,0:T(8,128)(2,1)}, bf16[4,2,6,64,128]{4,3,2,1,0:T(8,128)(2,1)S(1)}, u32[]{:S(2)}, u32[]{:S(2)}) collective-permute-start(bf16[4,2,6,64,128]{4,3,2,1,0:T(8,128)(2,1)} %get-tuple-element.13), channel_id=1, source_target_pairs={{0,1},{1,0},{2,3},{3,2},{4,5},{5,4},{6,7},{7,6},{8,9},{9,8},{10,11... | collective-permute-start | bytes 2359304 | tf_op jit(solution)/shard_map/ppermute | solution.py:26
  76.6 8.8 %collective-permute-start.4 = (bf16[2,6,64,128]{3,2,1,0:T(8,128)(2,1)S(1)}, bf16[2,6,64,128]{3,2,1,0:T(8,128)(2,1)S(1)}, u32[]{:S(2)}, u32[]{:S(2)}) collective-permute-start(bf16[2,6,64,128]{3,2,1,0:T(8,128)(2,1)S(1)} %copy-done.1), channel_id=1, source_target_pairs={{2,0},{3,1},{4,2},{5,3},{6,4},{7,5},{10,8},{11,9},{12,10},{13,11},... | collective-permute-start | bytes 589832 | tf_op jit(solution)/shard_map/ppermute | solution.py:36
  77.9 14.0 %collective-permute-start.5 = (bf16[2,6,64,128]{3,2,1,0:T(8,128)(2,1)S(1)}, bf16[2,6,64,128]{3,2,1,0:T(8,128)(2,1)S(1)}, u32[]{:S(2)}, u32[]{:S(2)}) collective-permute-start(bf16[2,6,64,128]{3,2,1,0:T(8,128)(2,1)S(1)} %copy-done.1), channel_id=1, source_target_pairs={{0,4},{1,5},{2,6},{3,7},{8,12},{9,13},{10,14},{11,15},{16,20},{17,... | collective-permute-start | bytes 589832 | tf_op jit(solution)/shard_map/ppermute | solution.py:36
  83.5 15.4 %collective-permute-start.9 = (bf16[2,6,64,128]{3,2,1,0:T(8,128)(2,1)S(1)}, bf16[2,6,64,128]{3,2,1,0:T(8,128)(2,1)S(1)}, u32[]{:S(2)}, u32[]{:S(2)}) collective-permute-start(bf16[2,6,64,128]{3,2,1,0:T(8,128)(2,1)S(1)} %copy-done.23), channel_id=1, source_target_pairs={{0,1},{1,0},{2,3},{3,2},{4,5},{5,4},{6,7},{7,6},{8,9},{9,8},{10,11... | collective-permute-start | bytes 589832 | tf_op jit(solution)/shard_map/ppermute | solution.py:26
  84.1 41.6 %copy-start.2 = (bf16[2,6,64,128]{3,2,1,0:T(8,128)(2,1)}, bf16[2,6,64,128]{3,2,1,0:T(8,128)(2,1)S(1)}, u32[]{:S(2)}) copy-start(bf16[2,6,64,128]{3,2,1,0:T(8,128)(2,1)S(1)} %collective-permute-done.3.refs_1_) | copy-start | bytes 589828
  84.1 18.3 %collective-permute-start.6 = (bf16[2,6,64,128]{3,2,1,0:T(8,128)(2,1)S(1)}, bf16[2,6,64,128]{3,2,1,0:T(8,128)(2,1)S(1)}, u32[]{:S(2)}, u32[]{:S(2)}) collective-permute-start(bf16[2,6,64,128]{3,2,1,0:T(8,128)(2,1)S(1)} %copy-done.1), channel_id=1, source_target_pairs={{4,0},{5,1},{6,2},{7,3},{12,8},{13,9},{14,10},{15,11},{20,16},{21,... | collective-permute-start | bytes 589832 | tf_op jit(solution)/shard_map/ppermute | solution.py:36
  85.4 40.3 %copy-start.3 = (bf16[2,6,64,128]{3,2,1,0:T(8,128)(2,1)}, bf16[2,6,64,128]{3,2,1,0:T(8,128)(2,1)S(1)}, u32[]{:S(2)}) copy-start(bf16[2,6,64,128]{3,2,1,0:T(8,128)(2,1)S(1)} %collective-permute-done.4.refs_2_) | copy-start | bytes 589828
  85.4 18.3 %collective-permute-start.7 = (bf16[2,6,64,128]{3,2,1,0:T(8,128)(2,1)S(1)}, bf16[2,6,64,128]{3,2,1,0:T(8,128)(2,1)S(1)}, u32[]{:S(2)}, u32[]{:S(2)}) collective-permute-start(bf16[2,6,64,128]{3,2,1,0:T(8,128)(2,1)S(1)} %copy-done.1), channel_id=1, source_target_pairs={{0,6},{1,7},{8,14},{9,15},{16,22},{17,23},{24,30},{25,31}} | collective-permute-start | bytes 589832 | tf_op jit(solution)/shard_map/ppermute | solution.py:36
  91.9 33.8 %copy-start.4 = (bf16[2,6,64,128]{3,2,1,0:T(8,128)(2,1)}, bf16[2,6,64,128]{3,2,1,0:T(8,128)(2,1)S(1)}, u32[]{:S(2)}) copy-start(bf16[2,6,64,128]{3,2,1,0:T(8,128)(2,1)S(1)} %collective-permute-done.5.refs_3_) | copy-start | bytes 589828
  91.9 17.4 %collective-permute-start.8 = (bf16[2,6,64,128]{3,2,1,0:T(8,128)(2,1)S(1)}, bf16[2,6,64,128]{3,2,1,0:T(8,128)(2,1)S(1)}, u32[]{:S(2)}, u32[]{:S(2)}) collective-permute-start(bf16[2,6,64,128]{3,2,1,0:T(8,128)(2,1)S(1)} %copy-done.1), channel_id=1, source_target_pairs={{6,0},{7,1},{14,8},{15,9},{22,16},{23,17},{30,24},{31,25}} | collective-permute-start | bytes 589832 | tf_op jit(solution)/shard_map/ppermute | solution.py:36
  98.9 26.8 %copy-start.5 = (bf16[2,6,64,128]{3,2,1,0:T(8,128)(2,1)}, bf16[2,6,64,128]{3,2,1,0:T(8,128)(2,1)S(1)}, u32[]{:S(2)}) copy-start(bf16[2,6,64,128]{3,2,1,0:T(8,128)(2,1)S(1)} %collective-permute-done.9.refs_7_) | copy-start | bytes 589828
  98.9 11.7 %collective-permute-start.10 = (bf16[2,6,64,128]{3,2,1,0:T(8,128)(2,1)S(1)}, bf16[2,6,64,128]{3,2,1,0:T(8,128)(2,1)S(1)}, u32[]{:S(2)}, u32[]{:S(2)}) collective-permute-start(bf16[2,6,64,128]{3,2,1,0:T(8,128)(2,1)S(1)} %collective-permute-done.9.refs_7_), channel_id=1, source_target_pairs={{0,2},{1,3},{2,4},{3,5},{4,6},{5,7},{8,10},{9,11},{10,12},{11,13},... | collective-permute-start | bytes 589832 | tf_op jit(solution)/shard_map/ppermute | solution.py:36
  102.4 23.3 %copy-start.6 = (bf16[2,6,64,128]{3,2,1,0:T(8,128)(2,1)}, bf16[2,6,64,128]{3,2,1,0:T(8,128)(2,1)S(1)}, u32[]{:S(2)}) copy-start(bf16[2,6,64,128]{3,2,1,0:T(8,128)(2,1)S(1)} %collective-permute-done.6.refs_4_) | copy-start | bytes 589828
  102.4 13.4 %collective-permute-start.11 = (bf16[2,6,64,128]{3,2,1,0:T(8,128)(2,1)S(1)}, bf16[2,6,64,128]{3,2,1,0:T(8,128)(2,1)S(1)}, u32[]{:S(2)}, u32[]{:S(2)}) collective-permute-start(bf16[2,6,64,128]{3,2,1,0:T(8,128)(2,1)S(1)} %collective-permute-done.9.refs_7_), channel_id=1, source_target_pairs={{2,0},{3,1},{4,2},{5,3},{6,4},{7,5},{10,8},{11,9},{12,10},{13,11},... | collective-permute-start | bytes 589832 | tf_op jit(solution)/shard_map/ppermute | solution.py:36
  103.7 21.9 %copy-start.7 = (bf16[2,6,64,128]{3,2,1,0:T(8,128)(2,1)}, bf16[2,6,64,128]{3,2,1,0:T(8,128)(2,1)S(1)}, u32[]{:S(2)}) copy-start(bf16[2,6,64,128]{3,2,1,0:T(8,128)(2,1)S(1)} %collective-permute-done.7.refs_5_) | copy-start | bytes 589828
  103.7 14.0 %collective-permute-start.12 = (bf16[2,6,64,128]{3,2,1,0:T(8,128)(2,1)S(1)}, bf16[2,6,64,128]{3,2,1,0:T(8,128)(2,1)S(1)}, u32[]{:S(2)}, u32[]{:S(2)}) collective-permute-start(bf16[2,6,64,128]{3,2,1,0:T(8,128)(2,1)S(1)} %collective-permute-done.9.refs_7_), channel_id=1, source_target_pairs={{0,4},{1,5},{2,6},{3,7},{8,12},{9,13},{10,14},{11,15},{16,20},{17,... | collective-permute-start | bytes 589832 | tf_op jit(solution)/shard_map/ppermute | solution.py:36
  109.3 16.4 %copy-start.8 = (bf16[2,6,64,128]{3,2,1,0:T(8,128)(2,1)}, bf16[2,6,64,128]{3,2,1,0:T(8,128)(2,1)S(1)}, u32[]{:S(2)}) copy-start(bf16[2,6,64,128]{3,2,1,0:T(8,128)(2,1)S(1)} %collective-permute-done.8.refs_6_) | copy-start | bytes 589828
  109.3 16.2 %collective-permute-start.13 = (bf16[2,6,64,128]{3,2,1,0:T(8,128)(2,1)S(1)}, bf16[2,6,64,128]{3,2,1,0:T(8,128)(2,1)S(1)}, u32[]{:S(2)}, u32[]{:S(2)}) collective-permute-start(bf16[2,6,64,128]{3,2,1,0:T(8,128)(2,1)S(1)} %collective-permute-done.9.refs_7_), channel_id=1, source_target_pairs={{4,0},{5,1},{6,2},{7,3},{12,8},{13,9},{14,10},{15,11},{20,16},{21,... | collective-permute-start | bytes 589832 | tf_op jit(solution)/shard_map/ppermute | solution.py:36
  110.6 15.1 %copy-start.9 = (bf16[2,6,64,128]{3,2,1,0:T(8,128)(2,1)}, bf16[2,6,64,128]{3,2,1,0:T(8,128)(2,1)S(1)}, u32[]{:S(2)}) copy-start(bf16[2,6,64,128]{3,2,1,0:T(8,128)(2,1)S(1)} %collective-permute-done.10.refs_8_) | copy-start | bytes 589828
  110.7 14.9 %collective-permute-start.14 = (bf16[2,6,64,128]{3,2,1,0:T(8,128)(2,1)S(1)}, bf16[2,6,64,128]{3,2,1,0:T(8,128)(2,1)S(1)}, u32[]{:S(2)}, u32[]{:S(2)}) collective-permute-start(bf16[2,6,64,128]{3,2,1,0:T(8,128)(2,1)S(1)} %collective-permute-done.9.refs_7_), channel_id=1, source_target_pairs={{0,6},{1,7},{8,14},{9,15},{16,22},{17,23},{24,30},{25,31}} | collective-permute-start | bytes 589832 | tf_op jit(solution)/shard_map/ppermute | solution.py:36
  115.8 9.9 %copy-start.10 = (bf16[2,6,64,128]{3,2,1,0:T(8,128)(2,1)}, bf16[2,6,64,128]{3,2,1,0:T(8,128)(2,1)S(1)}, u32[]{:S(2)}) copy-start(bf16[2,6,64,128]{3,2,1,0:T(8,128)(2,1)S(1)} %collective-permute-done.11.refs_9_) | copy-start | bytes 589828
  115.8 9.8 %collective-permute-start.15 = (bf16[2,6,64,128]{3,2,1,0:T(8,128)(2,1)S(1)}, bf16[2,6,64,128]{3,2,1,0:T(8,128)(2,1)S(1)}, u32[]{:S(2)}, u32[]{:S(2)}) collective-permute-start(bf16[2,6,64,128]{3,2,1,0:T(8,128)(2,1)S(1)} %collective-permute-done.9.refs_7_), channel_id=1, source_target_pairs={{6,0},{7,1},{14,8},{15,9},{22,16},{23,17},{30,24},{31,25}} | collective-permute-start | bytes 589832 | tf_op jit(solution)/shard_map/ppermute | solution.py:36
  117.7 8.0 %copy-start.11 = (bf16[2,6,64,128]{3,2,1,0:T(8,128)(2,1)}, bf16[2,6,64,128]{3,2,1,0:T(8,128)(2,1)S(1)}, u32[]{:S(2)}) copy-start(bf16[2,6,64,128]{3,2,1,0:T(8,128)(2,1)S(1)} %collective-permute-done.12.refs_10_) | copy-start | bytes 589828
  125.6 0.7 copy-start.12
  125.6 0.8 copy-start.13
  125.6 0.8 copy-start.14
  125.6 1.1 copy-start
  133.7 3.9 %collective-permute-start.20 = (f32[4,12,12]{2,1,0:T(8,128)S(1)}, f32[4,12,12]{2,1,0:T(8,128)S(1)}, u32[]{:S(2)}, u32[]{:S(2)}) collective-permute-start(f32[4,12,12]{2,1,0:T(8,128)S(1)} %slice.66), channel_id=1, source_target_pairs={{0,1},{1,0},{2,3},{3,2},{4,5},{5,4},{6,7},{7,6},{8,9},{9,8},{10,11... | collective-permute-start | bytes 6920 | tf_op jit(solution)/shard_map/ppermute | solution.py:26
where the time goes:
time: 153 us; the launch traced here: 152 us
  Pallas kernels  47.4 us (31%)
  starting transfers between devices  46.3 us (30%)
  waiting for transfers between devices  29.4 us (19%)
  blocking collectives  10.4 us (7%)
  other arithmetic  9.03 us (6%)
  local copies, waits for them, and re-layouts  8.2 us (5%)
    ppermute x12, starting transfers between devices, along_line(): return lax.ppermute(block, 'tm', route)  37.4 us
    pallas_call x2, Pallas kernels, elementals(): pl.pallas_call(functools.partial(elemental_kernel, slots, slots, stage, l...  34.4 us
    ppermute x9, waiting for transfers between devices, swap_bit(): return lax.ppermute(block, axis, [(i, i ^ mask) for i in range(count)])  21.5 us
    psum x1, blocking collectives, body(): total = lax.psum(mine, 'space')  10.4 us
    ppermute x9, starting transfers between devices, swap_bit(): return lax.ppermute(block, axis, [(i, i ^ mask) for i in range(count)])  8.84 us
    ppermute x12, waiting for transfers between devices, along_line(): return lax.ppermute(block, 'tm', route)  7.88 us
    pallas_call x1, Pallas kernels, both_sides(): pl.pallas_call(functools.partial(both_kernel, blocks), out_shape=(piece,...  6.72 us
    pallas_call x1, Pallas kernels, traces(): pl.pallas_call(functools.partial(trace_kernel, offsets), out_shape=jax.Sh...  6.27 us
  transfers between devices with their start and end apart: 21, of which 4 were waited for; matrix products, arithmetic and copies ran while one was open for 6% of the time, Pallas kernels for 27%

commit v1 on v0

v1 whole, which is shorter than its diff:
```python
import functools
import math

import jax
import jax.numpy as jnp
from jax import lax
from jax.experimental import pallas as pl
from jax.experimental.pallas import tpu as pltpu
from jax.sharding import PartitionSpec as P

LX = 16
LY = 16
PLANE = LX * LY
LANES = 128
F32 = jnp.float32
BF16 = jnp.bfloat16
CHUNK = 32
VMEM_LIMIT = 58 * 1024 * 1024

ANY = pl.BlockSpec(memory_space=pl.ANY)
SMEM = pl.BlockSpec(memory_space=pltpu.SMEM)
VMEM = pl.BlockSpec(memory_space=pltpu.VMEM)


def swap_bit(block, axis, mask):
    count = lax.axis_size(axis)
    return lax.ppermute(block, axis, [(i, i ^ mask) for i in range(count)])


def along_line(block, distance, line):
    route = [
        (2 * z + x, 2 * (z + distance) + x)
        for z in range(line)
        for x in range(2)
        if 0 <= z + distance < line
    ]
    return lax.ppermute(block, "tm", route)


def gather_by_swaps(block):
    count = lax.axis_size("space")
    held = {0: block}
    mask = count // 2
    while mask:
        for key in sorted(held):
            held[key | mask] = swap_bit(held[key], "space", mask)
        mask //= 2
    return [held[key] for key in range(count)]


def params():
    return pltpu.CompilerParams(vmem_limit_bytes=VMEM_LIMIT)


def elemental_kernel(held, near, late, last, whole, first_colour, *refs):
    move_ref, zphase_ref, phase_ref = refs[:3]
    slab_refs = refs[3 : 3 + held]
    rest = refs[3 + held :]
    if late:
        prior_ref, rest = rest[0], rest[1:]
    if last:
        full_ref, keep_ref, send_ref = rest[:3]
        rest = rest[3:]
    else:
        out_ref, rest = rest[0], rest[1:]
    slabs, turned, mixed, acc, sems = rest
    operators = acc.shape[0]
    vectors = acc.shape[2]
    colours = turned.shape[0]
    count = lax.axis_size("space")
    me = lax.axis_index("space")

    copies = []
    for m in range(held):
        source = slab_refs[m]
        if m < whole:
            source = source.at[:, pl.ds(first_colour, colours)]
        copies.append(
            pltpu.make_async_copy(source, slabs.at[m, :, :, pl.ds(0, PLANE), :], sems.at[2 * m])
        )
        copies.append(
            pltpu.make_async_copy(
                source.at[:, :, pl.ds(0, LX), :],
                slabs.at[m, :, :, pl.ds(PLANE, LX), :],
                sems.at[2 * m + 1],
            )
        )
    for copy in copies:
        copy.start()
    if late:
        acc[...] = prior_ref[...]
    else:
        acc[...] = jnp.zeros_like(acc)
    for copy in copies:
        copy.wait()

    row = lax.broadcasted_iota(jnp.int32, (PLANE, PLANE), 0)
    column = lax.broadcasted_iota(jnp.int32, (PLANE, PLANE), 1)
    wanted = jnp.where(row % LX == LX - 1, row - (LX - 1), row + 1)
    step_x = (column == wanted).astype(F32).astype(BF16)

    def one_slab(m, carry):
        here = me ^ m
        above = lax.rem(here + 1, count) ^ me
        far = above >= near

        @pl.when((m >= near) | far if late else m >= 0)
        def _():
            for colour in range(colours):
                for part in range(2):
                    block = slabs[m, part, colour, pl.ds(0, PLANE), :]
                    flat = block.T
                    same = flat if part == 0 else -flat
                    turned[colour, pl.ds(0, vectors), pl.ds(part * PLANE, PLANE)] = flat
                    turned[colour, pl.ds(vectors, vectors), pl.ds((1 - part) * PLANE, PLANE)] = same
                    moved = jnp.dot(step_x, block, preferred_element_type=F32)
                    slabs[held, part, colour, pl.ds(0, PLANE), :] = moved.astype(BF16)

            def one_operator(o, inner):
                move = move_ref[o]
                waits = (m >= near) | ((move == 3) & far)

                @pl.when(waits if late else jnp.logical_not(waits))
                def _():
                    src = jnp.where(move == 3, above, jnp.where(move == 1, held, m))
                    off = pl.multiple_of(jnp.where(move == 2, LX, 0), LX)
                    cos_z, sin_z = zphase_ref[0, here, o], zphase_ref[1, here, o]
                    for begin in range(0, PLANE, CHUNK):
                        cos_p = phase_ref[o, 0, pl.ds(begin, CHUNK), :]
                        sin_p = phase_ref[o, 1, pl.ds(begin, CHUNK), :]
                        cosine = cos_p * cos_z - sin_p * sin_z
                        sine = sin_p * cos_z + cos_p * sin_z
                        cosine = jnp.concatenate([cosine] * (vectors // LANES), axis=1)
                        sine = jnp.concatenate([sine] * (vectors // LANES), axis=1)
                        for colour in range(colours):
                            real = slabs[src, 0, colour, pl.ds(off + begin, CHUNK), :].astype(F32)
                            imag = slabs[src, 1, colour, pl.ds(off + begin, CHUNK), :].astype(F32)
                            mixed[colour, pl.ds(begin, CHUNK), :] = (
                                cosine * real + sine * imag
                            ).astype(BF16)
                            mixed[colour, pl.ds(PLANE + begin, CHUNK), :] = (
                                cosine * imag - sine * real
                            ).astype(BF16)
                    total = None
                    for colour in range(colours):
                        term = jnp.dot(turned[colour], mixed[colour], preferred_element_type=F32)
                        total = term if total is None else total + term
                    acc[o] += total

                return inner

            lax.fori_loop(0, operators, one_operator, 0)

        return carry

    lax.fori_loop(0, held, one_slab, 0)

    if last:
        block_rows = keep_ref.shape[2]
        first = pl.multiple_of(me * block_rows, block_rows)
        half = lax.rem(lax.axis_index("tm"), 2)
        for o in range(operators):
            full_ref[o] = acc[o].astype(BF16)
        for o in range(operators):
            for part in range(2):
                own = full_ref[o, pl.ds(part * vectors + first, block_rows), :]
                low, high = own[:, :LANES], own[:, LANES:]
                keep_ref[part, o] = jnp.where(half == 0, low, high)
                send_ref[part, o] = jnp.where(half == 0, high, low)
    else:
        out_ref[...] = acc[...]


def elementals(tables, slab_list, near, prior, last, colours, whole, first_colour, block_rows):
    _, _, plane, vectors = slab_list[0].shape
    held = len(slab_list)
    operators = tables[0].shape[0]
    late = prior is not None
    wide = jax.ShapeDtypeStruct((operators, 2 * vectors, vectors), F32)
    if last:
        piece = jax.ShapeDtypeStruct((2, operators, block_rows, LANES), BF16)
        outs = (jax.ShapeDtypeStruct(wide.shape, BF16), piece, piece)
        out_specs = (VMEM, VMEM, VMEM)
    else:
        outs, out_specs = wide, VMEM
    priors = [prior] if late else []
    return pl.pallas_call(
        functools.partial(elemental_kernel, held, near, late, last, whole, first_colour),
        out_shape=outs,
        in_specs=[SMEM, SMEM, VMEM] + [ANY] * held + [VMEM] * len(priors),
        out_specs=out_specs,
        scratch_shapes=[
            pltpu.VMEM((held + 1, 2, colours, plane + LX, vectors), BF16),
            pltpu.VMEM((colours, 2 * vectors, 2 * plane), BF16),
            pltpu.VMEM((colours, 2 * plane, vectors), BF16),
            pltpu.VMEM(wide.shape, F32),
            pltpu.SemaphoreType.DMA((2 * held,)),
        ],
        compiler_params=params(),
        cost_estimate=pl.CostEstimate(
            flops=8 * held * operators * colours * plane * vectors * vectors,
            bytes_accessed=held * 2 * colours * plane * vectors * 2,
            transcendentals=0,
        ),
        name="elementals_late" if late else "elementals_early",
    )(*tables, *slab_list, *priors)


def both_kernel(blocks, e_ref, *refs):
    peram_refs = refs[:blocks]
    keep_ref, send_ref, whole, left, middle, sems = refs[blocks:]
    sources, _, vectors, _ = whole.shape
    operators = e_ref.shape[0]
    block_rows = keep_ref.shape[3]
    me = lax.axis_index("space")
    half = lax.rem(lax.axis_index("tm"), 2)
    copies = []
    for m in range(blocks):
        begin = pl.multiple_of((me ^ m) * block_rows, block_rows)
        copies.append(
            pltpu.make_async_copy(
                peram_refs[m], whole.at[:, :, pl.ds(begin, block_rows), :], sems.at[m]
            )
        )
    for copy in copies:
        copy.start()
    for copy in copies:
        copy.wait()
    row = lax.broadcasted_iota(jnp.int32, (block_rows, vectors), 0)
    column = lax.broadcasted_iota(jnp.int32, (block_rows, vectors), 1)
    chosen = (column == row + me * block_rows).astype(F32).astype(BF16)
    for s in range(sources):
        for part in range(2):
            flat = lax.dot_general(
                chosen, whole[s, part], (((1,), (1,)), ((), ())), preferred_element_type=F32
            )
            left[pl.ds((part * sources + s) * block_rows, block_rows), :] = flat.astype(BF16)
    group = sources * block_rows
    for a in range(operators):
        product = lax.dot_general(
            left[...], e_ref[a], (((1,), (1,)), ((), ())), preferred_element_type=F32
        )
        real = product[:group, :vectors] - product[group:, vectors:]
        imaginary = product[:group, vectors:] + product[group:, :vectors]
        for part, block in enumerate((real, imaginary)):
            high = block.astype(BF16)
            low = (block - high.astype(F32)).astype(BF16)
            for s in range(sources):
                base = s * block_rows
                rows = pl.ds(a * block_rows, block_rows)
                columns = pl.ds(part * vectors, vectors)
                middle[0, s, rows, columns] = high[base : base + block_rows]
                middle[1, s, rows, columns] = low[base : base + block_rows]
    for s in range(sources):
        real, imaginary = whole[s, 0], whole[s, 1]
        right = jnp.concatenate(
            [
                jnp.concatenate([real, -imaginary], axis=1),
                jnp.concatenate([imaginary, real], axis=1),
            ],
            axis=0,
        )
        image = jnp.dot(middle[0, s], right, preferred_element_type=F32)
        image = image + jnp.dot(middle[1, s], right, preferred_element_type=F32)
        image = image.astype(BF16)
        for a in range(operators):
            for part in range(2):
                rows = image[a * block_rows : (a + 1) * block_rows]
                low = rows[:, part * vectors : part * vectors + LANES]
                high = rows[:, part * vectors + LANES : (part + 1) * vectors]
                keep_ref[s, part, a] = jnp.where(half == 0, low, high)
                send_ref[s, part, a] = jnp.where(half == 0, high, low)


def both_sides(elements, perams):
    blocks = len(perams)
    sources, _, block_rows, vectors = perams[0].shape
    operators = elements.shape[0]
    piece = jax.ShapeDtypeStruct((sources, 2, operators, block_rows, LANES), BF16)
    return pl.pallas_call(
        functools.partial(both_kernel, blocks),
        out_shape=(piece, piece),
        in_specs=[VMEM] + [ANY] * blocks,
        out_specs=(VMEM, VMEM),
        scratch_shapes=[
            pltpu.VMEM((sources, 2, vectors, vectors), BF16),
            pltpu.VMEM((2 * sources * block_rows, vectors), BF16),
            pltpu.VMEM((2, sources, operators * block_rows, 2 * vectors), BF16),
            pltpu.SemaphoreType.DMA((blocks,)),
        ],
        compiler_params=params(),
        cost_estimate=pl.CostEstimate(
            flops=2 * 3 * sources * operators * 4 * block_rows * vectors * vectors,
            bytes_accessed=8 * sources * vectors * vectors,
            transcendentals=0,
        ),
        name="both_sides",
    )(elements, *perams)


def spread(wide, count_rows, block_rows):
    pieces = [
        wide[pl.ds(k, count_rows, stride=block_rows), :].astype(BF16) for k in range(block_rows)
    ]
    return jnp.concatenate(pieces, axis=1)


def lay_kernel(own_ref, pair_ref, out_ref, wide):
    sources, _, operators, block_rows, lanes = own_ref.shape
    rows = 2 * operators
    for s in range(sources):
        for at, ref in enumerate((own_ref, pair_ref)):
            wide[pl.ds(at * rows * block_rows, rows * block_rows), :] = (
                ref[s].astype(F32).reshape(rows * block_rows, lanes)
            )
        out_ref[s] = spread(wide, 2 * rows, block_rows)


def lay_out(own, pair):
    sources, _, operators, block_rows, lanes = own.shape
    rows = 2 * operators
    return pl.pallas_call(
        lay_kernel,
        out_shape=jax.ShapeDtypeStruct((sources, 2 * rows, block_rows * lanes), BF16),
        in_specs=[VMEM, VMEM],
        out_specs=VMEM,
        scratch_shapes=[pltpu.VMEM((2 * rows * block_rows, lanes), F32)],
        compiler_params=params(),
        cost_estimate=pl.CostEstimate(
            flops=own.size, bytes_accessed=8 * own.size, transcendentals=0
        ),
        name="lay_out",
    )(own, pair)


def trace_kernel(offsets, times_ref, *refs):
    count = len(offsets)
    pools = refs[:count]
    laid_ref, mine_ref, pair_ref, picked, wide, sems = refs[count:]
    sources = laid_ref.shape[0]
    _, _, operators, block_rows, lanes = pools[0].shape
    rows = 2 * operators
    time = lax.axis_index("tm")
    for s in range(sources):
        source = times_ref[s]
        away = source // 2 - time // 2
        side = lax.rem(source + time, 2)
        for at, distance in enumerate(offsets):

            @pl.when(away == distance)
            def _(at=at, s=s, side=side):
                pltpu.make_async_copy(pools[at].at[side], picked.at[s], sems.at[s]).start()

    for s in range(sources):
        pltpu.make_async_copy(pools[0].at[0], picked.at[s], sems.at[s]).wait()
        wide[...] = picked[s].astype(F32).reshape(rows * block_rows, lanes)
        product = lax.dot_general(
            laid_ref[s],
            spread(wide, rows, block_rows),
            (((1,), (1,)), ((), ())),
            preferred_element_type=F32,
        )
        mine_ref[s] = product[:rows]
        pair_ref[s] = product[rows:]


def traces(source_times, offsets, pools, laid):
    sources = laid.shape[0]
    _, _, operators, block_rows, lanes = pools[0].shape
    rows = 2 * operators
    result = jax.ShapeDtypeStruct((sources, rows, rows), F32)
    return pl.pallas_call(
        functools.partial(trace_kernel, offsets),
        out_shape=(result, result),
        in_specs=[SMEM] + [ANY] * len(offsets) + [VMEM],
        out_specs=(VMEM, VMEM),
        scratch_shapes=[
            pltpu.VMEM((sources,) + pools[0].shape[1:], BF16),
            pltpu.VMEM((rows * block_rows, lanes), F32),
            pltpu.SemaphoreType.DMA((sources,)),
        ],
        compiler_params=params(),
        cost_estimate=pl.CostEstimate(
            flops=4 * sources * rows * rows * block_rows * lanes,
            bytes_accessed=2 * laid.size,
            transcendentals=0,
        ),
        name="traces",
    )(source_times, *pools, laid)


def finish_kernel(count, *refs):
    parts = refs[:count]
    correlator_ref, pairs_ref = refs[count:]
    sources, rows, _ = parts[0].shape
    n = rows // 2
    eye = lax.broadcasted_iota(jnp.int32, (n, n), 0) == lax.broadcasted_iota(jnp.int32, (n, n), 1)
    for s in range(sources):
        terms = [ref[s] for ref in parts]
        while len(terms) > 1:
            terms = [one + two for one, two in zip(terms[::2], terms[1::2])]
        total = terms[0]
        real = total[:n, :n] - total[n:, n:]
        imaginary = total[:n, n:] + total[n:, :n]
        correlator_ref[0, s, 0] = real
        correlator_ref[0, s, 1] = imaginary
        down_real, down_imaginary, over_real, over_imaginary = (
            jnp.sum(jnp.where(eye, block, 0.0), axis=axis, keepdims=True)
            for axis in (1, 0)
            for block in (real, imaginary)
        )
        pairs_ref[0, s, 0] = down_real * over_real - down_imaginary * over_imaginary
        pairs_ref[0, s, 1] = down_real * over_imaginary + down_imaginary * over_real


def finish(parts):
    sources, rows, _ = parts[0].shape
    result = jax.ShapeDtypeStruct((1, sources, 2, rows // 2, rows // 2), F32)
    return pl.pallas_call(
        functools.partial(finish_kernel, len(parts)),
        out_shape=(result, result),
        in_specs=[VMEM] * len(parts),
        out_specs=(VMEM, VMEM),
        compiler_params=params(),
        name="finish",
    )(*parts)


def phase_tables(momenta, z_coords, z_extent):
    plane = jnp.arange(PLANE, dtype=jnp.int32)
    along_x = (momenta[:, 0:1] * (plane % LX)[None] % LX).astype(F32) * (2.0 * math.pi / LX)
    along_y = (momenta[:, 1:2] * (plane // LX)[None] % LY).astype(F32) * (2.0 * math.pi / LY)
    angle = along_x + along_y
    table = jnp.stack([jnp.cos(angle), jnp.sin(angle)], axis=1)
    table = jnp.broadcast_to(table[..., None], table.shape + (LANES,))
    along_z = (momenta[:, 2][None, :] * z_coords[:, None] % z_extent).astype(F32) * (
        2.0 * math.pi / z_extent
    )
    return table, jnp.stack([jnp.cos(along_z), jnp.sin(along_z)])


def body(eigenvectors, momenta, displacement, source_times, perambulators):
    _, parts, colours, _, plane, vectors = eigenvectors.shape
    slabs = lax.axis_size("space")
    line = lax.axis_size("tm") // 2
    block_rows = vectors // slabs
    near = 2

    own = eigenvectors.reshape(parts, colours, plane, vectors)
    cut = colours - 1
    groups = [(0, cut), (cut, colours - cut)]
    far = [own[:, begin : begin + size] for begin, size in groups]
    held = [{0: block} for block in far]
    beside = swap_bit(own, "space", 1)
    mask = slabs // 2
    while mask >= near:
        for keys in held:
            for key in sorted(keys):
                keys[key | mask] = swap_bit(keys[key], "space", mask)
        mask //= 2

    plane_phase, z_phase = phase_tables(momenta, jnp.arange(slabs, dtype=jnp.int32), slabs)
    tables = (displacement, z_phase, plane_phase)
    total = elementals(tables, [own, beside], near, None, False, colours, near, 0, block_rows)

    for at, (begin, size) in enumerate(groups):
        last = at == len(groups) - 1
        keys = held[at]
        arrived = sorted(key for key in keys if key >= near)
        if at == 0:
            tied = lax.optimization_barrier(tuple(keys[key] for key in arrived) + (total,))
            keys.update(zip(arrived, tied))
            total = tied[-1]
        for key in arrived:
            keys[key | 1] = swap_bit(keys[key], "space", 1)
        slab_list = [own, beside] + [keys[key] for key in range(near, slabs)]
        total = elementals(tables, slab_list, near, total, last, size, near, begin, block_rows)
    full, keep, send = total

    peram, _ = lax.optimization_barrier((perambulators[0], held[-1][slabs // 2]))
    perams = gather_by_swaps(peram)

    received = swap_bit(send, "tm", 1)
    piece = jnp.stack([keep, received])
    offsets, pools = [0], [piece]
    for distance in range(1, line):
        for sign in (1, -1):
            offsets.append(-sign * distance)
            pools.append(along_line(piece, sign * distance, line))

    g_keep, g_send = both_sides(full, perams)
    laid = lay_out(g_keep, swap_bit(g_send, "tm", 1))
    mine, pair = traces(source_times, offsets, pools, laid)

    both = jnp.stack([mine, pair])
    both = both + swap_bit(both, "space", 1)
    mine, pair = both[0], both[1]
    sums = [mine]
    sums += [swap_bit(mine, "space", mask) for mask in range(2, slabs, 2)]
    sums += [swap_bit(pair, "tm", 1)]
    sums += [across(pair, mask) for mask in range(2, slabs, 2)]
    return finish(sums)


def across(block, mask):
    rows, times = lax.axis_size("space"), lax.axis_size("tm")
    route = [
        (i * times + t, (i ^ mask) * times + (t ^ 1)) for i in range(rows) for t in range(times)
    ]
    return lax.ppermute(block, ("space", "tm"), route)


def solution(mesh):
    placed = (
        P("tm", None, None, "space", None, None),
        P(),
        P(),
        P(),
        P("tm", None, None, "space", None),
    )
    return jax.shard_map(
        body,
        mesh=mesh,
        in_specs=placed,
        out_specs=(P("tm", None, None, None, None), P("tm", None, None, None, None)),
        check_vma=False,
    )
```

time: 153 us -> 161 us (1.052)
  waiting for transfers between devices: 29.4 us -> 61.1 us
  starting transfers between devices: 46.3 us -> 25.3 us
  Pallas kernels: 47.4 us -> 59.9 us
  blocking collectives: 10.4 us -> 0 us
  other arithmetic: 9.03 us -> 2.58 us
  local copies, waits for them, and re-layouts: 8.2 us -> 10.1 us
    ppermute x12 -> x6, starting transfers between devices: 37.4 us -> 13.7 us  [along_line(): return lax.ppermute(block, 'tm', route)]
    ppermute x12 -> x6, waiting for transfers between devices: 7.88 us -> 26.8 us  [along_line(): return lax.ppermute(block, 'tm', route)]
    pallas_call x3 -> x6, Pallas kernels: 40.7 us -> 53.1 us  [the longest x3 42.2 us: elementals(): pl.pallas_call(functools.partial(elemental_kernel, held, near, late, last...]
    ppermute x9 -> x13, waiting for transfers between devices: 21.5 us -> 32.2 us  [swap_bit(): return lax.ppermute(block, axis, [(i, i ^ mask) for i in range(count)])]
    psum x1 -> x0, blocking collectives: 10.4 us -> none  [body(): total = lax.psum(mine, 'space')]
    pallas_call x0 -> x2, local copies, waits for them, and re-layouts: none -> 2.75 us  [finish(): pl.pallas_call(functools.partial(finish_kernel, len(parts)), out_shape=(r...]
    select_n x3 -> x0, other arithmetic: 2.53 us -> none  [the longest x1 1.27 us: tables(): jnp.where(displacement == 2, LX, 0).astype(jnp.int32)]
    ppermute x9 -> x13, starting transfers between devices: 8.84 us -> 11.1 us  [swap_bit(): return lax.ppermute(block, axis, [(i, i ^ mask) for i in range(count)])]
  transfers between devices with their start and end apart: 21 -> 20, of which waited for: 4 -> 10; matrix products, arithmetic and copies ran while one was open for 6% -> 3% of each run, Pallas kernels for 27% -> 29%
where the time goes in v1:
time: 161 us; the launch traced here: 160 us
  waiting for transfers between devices  61.1 us (38%)
  Pallas kernels  59.9 us (37%)
  starting transfers between devices  25.3 us (16%)
  local copies, waits for them, and re-layouts  10.1 us (6%)
  other arithmetic  2.58 us (2%)
    pallas_call x3, Pallas kernels, elementals(): pl.pallas_call(functools.partial(elemental_kernel, held, near, late, last...  42.2 us
    ppermute x13, waiting for transfers between devices, swap_bit(): return lax.ppermute(block, axis, [(i, i ^ mask) for i in range(count)])  32.2 us
    ppermute x6, waiting for transfers between devices, along_line(): return lax.ppermute(block, 'tm', route)  26.8 us
    ppermute x6, starting transfers between devices, along_line(): return lax.ppermute(block, 'tm', route)  13.7 us
    ppermute x13, starting transfers between devices, swap_bit(): return lax.ppermute(block, axis, [(i, i ^ mask) for i in range(count)])  11.1 us
    pallas_call x1, Pallas kernels, both_sides(): pl.pallas_call(functools.partial(both_kernel, blocks), out_shape=(piece,...  6.77 us
    pallas_call x1, Pallas kernels, traces(): pl.pallas_call(functools.partial(trace_kernel, offsets), out_shape=(resul...  4.73 us
    pallas_call x1, Pallas kernels, lay_out(): pl.pallas_call(lay_kernel, out_shape=jax.ShapeDtypeStruct((sources, 2 * r...  4.54 us
  transfers between devices with their start and end apart: 20, of which 10 were waited for; matrix products, arithmetic and copies ran while one was open for 3% of the time, Pallas kernels for 29%

profile of v1, /device:TPU:0, one launch (start us, length us, event | category | flops | bytes accessed | tf_op | source)
XLA Modules:
  0.0 160.1 jit_solution(17078465992625637081)
XLA Ops:
  0.6 0.5 collective-permute-start
  1.2 1.1 slice.35
  2.2 2.6 %collective-permute-start.3 = (bf16[2,2,256,256]{3,2,1,0:T(8,128)(2,1)S(1)}, bf16[2,2,256,256]{3,2,1,0:T(8,128)(2,1)S(1)}, u32[]{:S(2)}, u32[]{:S(2)}) collective-permute-start(bf16[2,2,256,256]{3,2,1,0:T(8,128)(2,1)S(1)} %slice.35), channel_id=1, source_target_pairs={{0,16},{8,24},{16,0},{24,8},{1,17},{9,25},{17,1},{25,9},{2,18},{10... | collective-permute-start | bytes 1572872 | tf_op jit(solution)/shard_map/ppermute | solution.py:27
  4.8 1.0 slice.34
  5.9 0.3 fusion.13
  6.3 0.6 pad_maximum_fusion.3.refs_1_
  6.9 1.7 %broadcast_in_dim.2.refs_2_ = f32[6,2,256,128]{3,2,1,0:T(8,128)} broadcast(f32[6,2,256]{2,1,0:T(2,128)S(1)} %pad_maximum_fusion.2), dimensions={0,1,2} | broadcast | bytes 1585152 | tf_op jit(solution)/shard_map/broadcast_in_dim | solution.py:435
  8.6 15.0 %elementals_early.1.refs_7_ = f32[6,512,256]{2,1,0:T(8,128)} custom-call(s32[6]{0:T(128)} %refs_0_.5, f32[2,4,6]{2,1,0:T(4,128)} %pad_maximum_fusion.3.refs_1_, f32[6,2,256,128]{3,2,1,0:T(8,128)} %broadcast_in_dim.2.refs_2_, bf16[2,3,256,256]{3,2,1,0:T(8,128)(2,1)} %bitcast.19, bf16[2,3,256,256]{3,2,1,0:T(8,128)(2,1)} %copy-done.14), custom_call_target="tpu_custom_call" | custom-call | flops 4831838208 | bytes 1572864 | tf_op jit(solution)/shard_map/elementals_early/pallas_call | solution.py:187
  23.6 0.3 collective-permute-start.4
  23.9 1.9 %collective-permute-start.13 = (bf16[4,2,64,256]{3,2,1,0:T(8,128)(2,1)S(1)}, bf16[4,2,64,256]{3,2,1,0:T(8,128)(2,1)S(1)}, u32[]{:S(2)}, u32[]{:S(2)}) collective-permute-start(bf16[4,2,64,256]{3,2,1,0:T(8,128)(2,1)S(1)} %bitcast.29), channel_id=1, source_target_pairs={{0,16},{8,24},{16,0},{24,8},{1,17},{9,25},{17,1},{25,9},{2,18},{10... | collective-permute-start | bytes 786440 | tf_op jit(solution)/shard_map/ppermute | solution.py:27
  25.8 0.2 collective-permute-start.12
  25.9 0.3 collective-permute-start.2
  26.3 6.4 %collective-permute-done.13.refs_2_ = bf16[4,2,64,256]{3,2,1,0:T(8,128)(2,1)S(1)} collective-permute-done((bf16[4,2,64,256]{3,2,1,0:T(8,128)(2,1)S(1)}, bf16[4,2,64,256]{3,2,1,0:T(8,128)(2,1)S(1)}, u32[]{:S(2)}, u32[]{:S(2)}) %collective-permute-start.13) | collective-permute-done | bytes 262176 | tf_op jit(solution)/shard_map/ppermute | solution.py:27
  32.7 0.8 copy-done.16
  33.5 15.8 %elementals_late.2.refs_7_ = f32[6,512,256]{2,1,0:T(8,128)} custom-call(s32[6]{0:T(128)} %refs_0_.5, f32[2,4,6]{2,1,0:T(4,128)} %pad_maximum_fusion.3.refs_1_, f32[6,2,256,128]{3,2,1,0:T(8,128)} %broadcast_in_dim.2.refs_2_, bf16[2,3,256,256]{3,2,1,0:T(8,128)(2,1)} %bitcast.20, bf16[2,3,256,256]{3,2,1,0:T(8,128)(2,1)} %copy-done.14, ...), custom_call_target="tpu_custom_call" | custom-call | flops 6442450944 | bytes 2097152 | tf_op jit(solution)/shard_map/elementals_late/pallas_call | solution.py:187
  49.4 0.7 copy-done.22
  50.0 11.5 %elementals_late.3 = (bf16[6,512,256]{2,1,0:T(8,128)(2,1)}, bf16[2,6,64,128]{3,2,1,0:T(8,128)(2,1)}, bf16[2,6,64,128]{3,2,1,0:T(8,128)(2,1)}) custom-call(s32[6]{0:T(128)} %refs_0_.5, f32[2,4,6]{2,1,0:T(4,128)} %pad_maximum_fusion.3.refs_1_, f32[6,2,256,128]{3,2,1,0:T(8,128)} %broadcast_in_dim.2.refs_2_, bf16[2,3,256,256]{3,2,1,0:T(8,128)(2,1)} %bitcast.21, ...), custom_call_target="tpu_custom_call" | custom-call | flops 3221225472 | bytes 1048576 | tf_op jit(solution)/shard_map/elementals_late/pallas_call | solution.py:187
  61.6 0.7 copy-done.20
  62.3 6.8 %both_sides.1 = (bf16[4,2,6,64,128]{4,3,2,1,0:T(8,128)(2,1)}, bf16[4,2,6,64,128]{4,3,2,1,0:T(8,128)(2,1)}) custom-call(bf16[6,512,256]{2,1,0:T(8,128)(2,1)} %get-tuple-element.16.e_ref, bf16[4,2,64,256]{3,2,1,0:T(8,128)(2,1)} %bitcast.28, bf16[4,2,64,256]{3,2,1,0:T(8,128)(2,1)} %copy-done.20, bf16[4,2,64,256]{3,2,1,0:T(8,128)(2,1)} %copy-done.19, ...), custom_call_target="tpu_custom_call" | custom-call | flops 2415919104 | bytes 2097152 | tf_op jit(solution)/shard_map/both_sides/pallas_call | solution.py:280
  69.1 1.8 %collective-permute-start.15 = (bf16[4,2,6,64,128]{4,3,2,1,0:T(8,128)(2,1)}, bf16[4,2,6,64,128]{4,3,2,1,0:T(8,128)(2,1)S(1)}, u32[]{:S(2)}, u32[]{:S(2)}) collective-permute-start(bf16[4,2,6,64,128]{4,3,2,1,0:T(8,128)(2,1)} %get-tuple-element.19), channel_id=1, source_target_pairs={{0,1},{1,0},{2,3},{3,2},{4,5},{5,4},{6,7},{7,6},{8,9},{9,8},{10,11... | collective-permute-start | bytes 2359304 | tf_op jit(solution)/shard_map/ppermute | solution.py:27
  70.9 0.3 collective-permute-start.5
  71.2 22.3 %collective-permute-done.5 = bf16[2,6,64,128]{3,2,1,0:T(8,128)(2,1)S(1)} collective-permute-done((bf16[2,6,64,128]{3,2,1,0:T(8,128)(2,1)S(1)}, bf16[2,6,64,128]{3,2,1,0:T(8,128)(2,1)S(1)}, u32[]{:S(2)}, u32[]{:S(2)}) %collective-permute-start.5) | collective-permute-done | bytes 196640 | tf_op jit(solution)/shard_map/ppermute | solution.py:27
  93.6 5.7 %collective-permute-start.10 = (bf16[2,2,6,64,128]{4,3,2,1,0:T(8,128)(2,1)S(1)}, bf16[2,2,6,64,128]{4,3,2,1,0:T(8,128)(2,1)S(1)}, u32[]{:S(2)}, u32[]{:S(2)}) collective-permute-start(bf16[2,2,6,64,128]{4,3,2,1,0:T(8,128)(2,1)S(1)} %pad_maximum_fusion.refs_0_), channel_id=1, source_target_pairs={{0,6},{1,7},{8,14},{9,15},{16,22},{17,23},{24,30},{25,31}} | collective-permute-start | bytes 1179656 | tf_op jit(solution)/shard_map/ppermute | solution.py:37
  99.3 1.3 collective-permute-start.11
  100.6 1.3 collective-permute-start.6
  101.9 1.3 collective-permute-start.7
  103.2 5.6 %collective-permute-done.10.refs_5_ = bf16[2,2,6,64,128]{4,3,2,1,0:T(8,128)(2,1)S(1)} collective-permute-done((bf16[2,2,6,64,128]{4,3,2,1,0:T(8,128)(2,1)S(1)}, bf16[2,2,6,64,128]{4,3,2,1,0:T(8,128)(2,1)S(1)}, u32[]{:S(2)}, u32[]{:S(2)}) %collective-permute-start.10) | collective-permute-done | bytes 393248 | tf_op jit(solution)/shard_map/ppermute | solution.py:37
  108.8 2.6 %collective-permute-start.8 = (bf16[2,2,6,64,128]{4,3,2,1,0:T(8,128)(2,1)S(1)}, bf16[2,2,6,64,128]{4,3,2,1,0:T(8,128)(2,1)S(1)}, u32[]{:S(2)}, u32[]{:S(2)}) collective-permute-start(bf16[2,2,6,64,128]{4,3,2,1,0:T(8,128)(2,1)S(1)} %pad_maximum_fusion.refs_0_), channel_id=1, source_target_pairs={{0,4},{1,5},{2,6},{3,7},{8,12},{9,13},{10,14},{11,15},{16,20},{17,... | collective-permute-start | bytes 1179656 | tf_op jit(solution)/shard_map/ppermute | solution.py:37
  111.5 1.5 collective-permute-start.9
  112.9 4.5 %lay_out.1.refs_7_ = bf16[4,24,8192]{2,1,0:T(8,128)(2,1)} custom-call(bf16[4,2,6,64,128]{4,3,2,1,0:T(8,128)(2,1)} %get-tuple-element.18.own_ref, bf16[4,2,6,64,128]{4,3,2,1,0:T(8,128)(2,1)} %copy-done.1), custom_call_target="tpu_custom_call" | custom-call | flops 393216 | bytes 3145728 | tf_op jit(solution)/shard_map/lay_out/pallas_call | solution.py:322
  117.5 4.3 %collective-permute-done.7.refs_2_ = bf16[2,2,6,64,128]{4,3,2,1,0:T(8,128)(2,1)S(1)} collective-permute-done((bf16[2,2,6,64,128]{4,3,2,1,0:T(8,128)(2,1)S(1)}, bf16[2,2,6,64,128]{4,3,2,1,0:T(8,128)(2,1)S(1)}, u32[]{:S(2)}, u32[]{:S(2)}) %collective-permute-start.7) | collective-permute-done | bytes 393248 | tf_op jit(solution)/shard_map/ppermute | solution.py:37
  121.9 2.6 %collective-permute-done.8.refs_3_ = bf16[2,2,6,64,128]{4,3,2,1,0:T(8,128)(2,1)S(1)} collective-permute-done((bf16[2,2,6,64,128]{4,3,2,1,0:T(8,128)(2,1)S(1)}, bf16[2,2,6,64,128]{4,3,2,1,0:T(8,128)(2,1)S(1)}, u32[]{:S(2)}, u32[]{:S(2)}) %collective-permute-start.8) | collective-permute-done | bytes 393248 | tf_op jit(solution)/shard_map/ppermute | solution.py:37
  124.4 14.3 %collective-permute-done.9.refs_4_ = bf16[2,2,6,64,128]{4,3,2,1,0:T(8,128)(2,1)S(1)} collective-permute-done((bf16[2,2,6,64,128]{4,3,2,1,0:T(8,128)(2,1)S(1)}, bf16[2,2,6,64,128]{4,3,2,1,0:T(8,128)(2,1)S(1)}, u32[]{:S(2)}, u32[]{:S(2)}) %collective-permute-start.9) | collective-permute-done | bytes 393248 | tf_op jit(solution)/shard_map/ppermute | solution.py:37
  138.8 0.7 copy-done.7
  139.5 4.7 %traces.1 = (f32[4,12,12]{2,1,0:T(8,128)}, f32[4,12,12]{2,1,0:T(8,128)}) custom-call(s32[4]{0:T(128)} %times_ref.1, bf16[2,2,6,64,128]{4,3,2,1,0:T(8,128)(2,1)} %copy-done, bf16[2,2,6,64,128]{4,3,2,1,0:T(8,128)(2,1)} %copy-done.4, bf16[2,2,6,64,128]{4,3,2,1,0:T(8,128)(2,1)} %copy-done.5, bf16[2,2,6,64,128]{4,3,2,1,0:T(8,128)(2,1)} %copy-done.6, ...), custom_call_target="tpu_custom_call" | custom-call | flops 18874368 | bytes 1572864 | tf_op jit(solution)/shard_map/traces/pallas_call | solution.py:372
  144.3 0.8 pad_maximum_fusion.1
  145.1 1.2 collective-permute-done.16
  146.3 0.8 fusion.14
  147.2 1.6 collective-permute-start.17
  148.7 1.5 collective-permute-start.18
  150.2 0.5 collective-permute-start.19
  150.7 0.4 collective-permute-done.17.refs_1_
  151.1 1.8 %collective-permute-done.18.refs_2_ = f32[4,12,12]{2,1,0:T(8,128)S(1)} collective-permute-done((f32[4,12,12]{2,1,0:T(8,128)S(1)}, f32[4,12,12]{2,1,0:T(8,128)S(1)}, u32[]{:S(2)}, u32[]{:S(2)}) %collective-permute-start.18) | collective-permute-done | bytes 2336 | tf_op jit(solution)/shard_map/ppermute | solution.py:27
  152.9 2.1 %collective-permute-done.19.refs_3_ = f32[4,12,12]{2,1,0:T(8,128)S(1)} collective-permute-done((f32[4,12,12]{2,1,0:T(8,128)S(1)}, f32[4,12,12]{2,1,0:T(8,128)S(1)}, u32[]{:S(2)}, u32[]{:S(2)}) %collective-permute-start.19) | collective-permute-done | bytes 2336 | tf_op jit(solution)/shard_map/ppermute | solution.py:510
  155.1 0.6 copy-done.12
  155.7 1.6 %finish.1 = (f32[1,4,2,6,6]{4,3,2,1,0:T(8,128)}, f32[1,4,2,6,6]{4,3,2,1,0:T(8,128)}) custom-call(f32[4,12,12]{2,1,0:T(8,128)} %copy-done.9, f32[4,12,12]{2,1,0:T(8,128)} %copy-done.10, f32[4,12,12]{2,1,0:T(8,128)} %copy-done.11, f32[4,12,12]{2,1,0:T(8,128)} %copy-done.12), custom_call_target="tpu_custom_call" | custom-call | tf_op jit(solution)/shard_map/finish/pallas_call | solution.py:419
  157.3 1.4 copy.7
  158.7 1.4 copy.8
  (62 shorter events, 0.5 us)
Async XLA Ops:
  0.6 5.3 %copy-start.13 = (s32[6,3]{0,1:T(4,128)S(1)}, s32[6,3]{0,1:T(4,128)}, u32[]{:S(2)}) copy-start(s32[6,3]{0,1:T(4,128)} %param.6) | copy-start | bytes 220
  0.6 6.3 %collective-permute-start = (bf16[2,3,256,256]{3,2,1,0:T(8,128)(2,1)}, bf16[2,3,256,256]{3,2,1,0:T(8,128)(2,1)S(1)}, u32[]{:S(2)}, u32[]{:S(2)}) collective-permute-start(bf16[2,3,256,256]{3,2,1,0:T(8,128)(2,1)} %bitcast.16), channel_id=1, source_target_pairs={{0,8},{8,0},{16,24},{24,16},{1,9},{9,1},{17,25},{25,17},{2,10},{10... | collective-permute-start | bytes 2359304 | tf_op jit(solution)/shard_map/ppermute | solution.py:27
  2.2 21.3 %collective-permute-start.3 = (bf16[2,2,256,256]{3,2,1,0:T(8,128)(2,1)S(1)}, bf16[2,2,256,256]{3,2,1,0:T(8,128)(2,1)S(1)}, u32[]{:S(2)}, u32[]{:S(2)}) collective-permute-start(bf16[2,2,256,256]{3,2,1,0:T(8,128)(2,1)S(1)} %slice.35), channel_id=1, source_target_pairs={{0,16},{8,24},{16,0},{24,8},{1,17},{9,25},{17,1},{25,9},{2,18},{10... | collective-permute-start | bytes 1572872 | tf_op jit(solution)/shard_map/ppermute | solution.py:27
  5.8 18.1 %collective-permute-start.1 = (bf16[2,1,256,256]{3,2,1,0:T(8,128)(2,1)S(1)}, bf16[2,1,256,256]{3,2,1,0:T(8,128)(2,1)S(1)}, u32[]{:S(2)}, u32[]{:S(2)}) collective-permute-start(bf16[2,1,256,256]{3,2,1,0:T(8,128)(2,1)S(1)} %slice.34), channel_id=1, source_target_pairs={{0,16},{8,24},{16,0},{24,8},{1,17},{9,25},{17,1},{25,9},{2,18},{10... | collective-permute-start | bytes 786440 | tf_op jit(solution)/shard_map/ppermute | solution.py:27
  6.9 1.7 %copy-start.14 = (bf16[2,3,256,256]{3,2,1,0:T(8,128)(2,1)}, bf16[2,3,256,256]{3,2,1,0:T(8,128)(2,1)S(1)}, u32[]{:S(2)}) copy-start(bf16[2,3,256,256]{3,2,1,0:T(8,128)(2,1)S(1)} %collective-permute-done.refs_4_) | copy-start | bytes 2359300
  8.6 15.3 %copy-start.17 = (bf16[1,4,2,64,256]{4,3,2,1,0:T(8,128)(2,1)S(1)}, bf16[1,4,2,64,256]{4,3,2,1,0:T(8,128)(2,1)}, u32[]{:S(2)}) copy-start(bf16[1,4,2,64,256]{4,3,2,1,0:T(8,128)(2,1)} %param.9) | copy-start | bytes 786436
  23.6 9.1 %copy-start.15 = (bf16[2,2,256,256]{3,2,1,0:T(8,128)(2,1)}, bf16[2,2,256,256]{3,2,1,0:T(8,128)(2,1)S(1)}, u32[]{:S(2)}) copy-start(bf16[2,2,256,256]{3,2,1,0:T(8,128)(2,1)S(1)} %collective-permute-done.3.refs_5_) | copy-start | bytes 1572868
  23.6 9.1 %collective-permute-start.4 = (bf16[2,2,256,256]{3,2,1,0:T(8,128)(2,1)S(1)}, bf16[2,2,256,256]{3,2,1,0:T(8,128)(2,1)S(1)}, u32[]{:S(2)}, u32[]{:S(2)}) collective-permute-start(bf16[2,2,256,256]{3,2,1,0:T(8,128)(2,1)S(1)} %collective-permute-done.3.refs_5_), channel_id=1, source_target_pairs={{0,8},{8,0},{16,24},{24,16},{1,9},{9,1},{17,25},{25,17},{2,10},{10... | collective-permute-start | bytes 1572872 | tf_op jit(solution)/shard_map/ppermute | solution.py:27
  23.9 25.4 %copy-start.18 = (bf16[2,1,256,256]{3,2,1,0:T(8,128)(2,1)}, bf16[2,1,256,256]{3,2,1,0:T(8,128)(2,1)S(1)}, u32[]{:S(2)}) copy-start(bf16[2,1,256,256]{3,2,1,0:T(8,128)(2,1)S(1)} %collective-permute-done.1.refs_5_) | copy-start | bytes 786436
  23.9 8.8 %collective-permute-start.13 = (bf16[4,2,64,256]{3,2,1,0:T(8,128)(2,1)S(1)}, bf16[4,2,64,256]{3,2,1,0:T(8,128)(2,1)S(1)}, u32[]{:S(2)}, u32[]{:S(2)}) collective-permute-start(bf16[4,2,64,256]{3,2,1,0:T(8,128)(2,1)S(1)} %bitcast.29), channel_id=1, source_target_pairs={{0,16},{8,24},{16,0},{24,8},{1,17},{9,25},{17,1},{25,9},{2,18},{10... | collective-permute-start | bytes 786440 | tf_op jit(solution)/shard_map/ppermute | solution.py:27
  25.8 35.8 %collective-permute-start.12 = (bf16[4,2,64,256]{3,2,1,0:T(8,128)(2,1)S(1)}, bf16[4,2,64,256]{3,2,1,0:T(8,128)(2,1)S(1)}, u32[]{:S(2)}, u32[]{:S(2)}) collective-permute-start(bf16[4,2,64,256]{3,2,1,0:T(8,128)(2,1)S(1)} %bitcast.30), channel_id=1, source_target_pairs={{0,8},{8,0},{16,24},{24,16},{1,9},{9,1},{17,25},{25,17},{2,10},{10... | collective-permute-start | bytes 786440 | tf_op jit(solution)/shard_map/ppermute | solution.py:27
  25.9 23.4 %collective-permute-start.2 = (bf16[2,1,256,256]{3,2,1,0:T(8,128)(2,1)S(1)}, bf16[2,1,256,256]{3,2,1,0:T(8,128)(2,1)S(1)}, u32[]{:S(2)}, u32[]{:S(2)}) collective-permute-start(bf16[2,1,256,256]{3,2,1,0:T(8,128)(2,1)S(1)} %collective-permute-done.1.refs_5_), channel_id=1, source_target_pairs={{0,8},{8,0},{16,24},{24,16},{1,9},{9,1},{17,25},{25,17},{2,10},{10... | collective-permute-start | bytes 786440 | tf_op jit(solution)/shard_map/ppermute | solution.py:27
  32.7 16.6 %copy-start.19 = (bf16[4,2,64,256]{3,2,1,0:T(8,128)(2,1)}, bf16[4,2,64,256]{3,2,1,0:T(8,128)(2,1)S(1)}, u32[]{:S(2)}) copy-start(bf16[4,2,64,256]{3,2,1,0:T(8,128)(2,1)S(1)} %collective-permute-done.13.refs_2_) | copy-start | bytes 786436
  32.7 28.8 %collective-permute-start.14 = (bf16[4,2,64,256]{3,2,1,0:T(8,128)(2,1)S(1)}, bf16[4,2,64,256]{3,2,1,0:T(8,128)(2,1)S(1)}, u32[]{:S(2)}, u32[]{:S(2)}) collective-permute-start(bf16[4,2,64,256]{3,2,1,0:T(8,128)(2,1)S(1)} %collective-permute-done.13.refs_2_), channel_id=1, source_target_pairs={{0,8},{8,0},{16,24},{24,16},{1,9},{9,1},{17,25},{25,17},{2,10},{10... | collective-permute-start | bytes 786440 | tf_op jit(solution)/shard_map/ppermute | solution.py:27
  32.7 0.8 copy-start.16
  49.3 0.7 copy-start.22
  61.5 0.7 copy-start.20
  61.6 0.8 copy-start.21
  62.3 8.5 %copy-start.23 = (bf16[2,6,64,128]{3,2,1,0:T(8,128)(2,1)S(1)}, bf16[2,6,64,128]{3,2,1,0:T(8,128)(2,1)}, u32[]{:S(2)}) copy-start(bf16[2,6,64,128]{3,2,1,0:T(8,128)(2,1)} %get-tuple-element.15) | copy-start | bytes 589828
  62.3 31.2 %copy-start.8 = (bf16[2,6,64,128]{3,2,1,0:T(8,128)(2,1)S(1)}, bf16[2,6,64,128]{3,2,1,0:T(8,128)(2,1)}, u32[]{:S(2)}) copy-start(bf16[2,6,64,128]{3,2,1,0:T(8,128)(2,1)} %get-tuple-element.14) | copy-start | bytes 589828
  69.1 42.3 %collective-permute-start.15 = (bf16[4,2,6,64,128]{4,3,2,1,0:T(8,128)(2,1)}, bf16[4,2,6,64,128]{4,3,2,1,0:T(8,128)(2,1)S(1)}, u32[]{:S(2)}, u32[]{:S(2)}) collective-permute-start(bf16[4,2,6,64,128]{4,3,2,1,0:T(8,128)(2,1)} %get-tuple-element.19), channel_id=1, source_target_pairs={{0,1},{1,0},{2,3},{3,2},{4,5},{5,4},{6,7},{7,6},{8,9},{9,8},{10,11... | collective-permute-start | bytes 2359304 | tf_op jit(solution)/shard_map/ppermute | solution.py:27
  70.9 22.6 %collective-permute-start.5 = (bf16[2,6,64,128]{3,2,1,0:T(8,128)(2,1)S(1)}, bf16[2,6,64,128]{3,2,1,0:T(8,128)(2,1)S(1)}, u32[]{:S(2)}, u32[]{:S(2)}) collective-permute-start(bf16[2,6,64,128]{3,2,1,0:T(8,128)(2,1)S(1)} %copy-done.23), channel_id=1, source_target_pairs={{0,1},{1,0},{2,3},{3,2},{4,5},{5,4},{6,7},{7,6},{8,9},{9,8},{10,11... | collective-permute-start | bytes 589832 | tf_op jit(solution)/shard_map/ppermute | solution.py:27
  93.6 23.9 %copy-start = (bf16[2,2,6,64,128]{4,3,2,1,0:T(8,128)(2,1)}, bf16[2,2,6,64,128]{4,3,2,1,0:T(8,128)(2,1)S(1)}, u32[]{:S(2)}) copy-start(bf16[2,2,6,64,128]{4,3,2,1,0:T(8,128)(2,1)S(1)} %pad_maximum_fusion.refs_0_) | copy-start | bytes 1179652
  93.6 15.2 %collective-permute-start.10 = (bf16[2,2,6,64,128]{4,3,2,1,0:T(8,128)(2,1)S(1)}, bf16[2,2,6,64,128]{4,3,2,1,0:T(8,128)(2,1)S(1)}, u32[]{:S(2)}, u32[]{:S(2)}) collective-permute-start(bf16[2,2,6,64,128]{4,3,2,1,0:T(8,128)(2,1)S(1)} %pad_maximum_fusion.refs_0_), channel_id=1, source_target_pairs={{0,6},{1,7},{8,14},{9,15},{16,22},{17,23},{24,30},{25,31}} | collective-permute-start | bytes 1179656 | tf_op jit(solution)/shard_map/ppermute | solution.py:37
  99.3 18.2 %collective-permute-start.11 = (bf16[2,2,6,64,128]{4,3,2,1,0:T(8,128)(2,1)S(1)}, bf16[2,2,6,64,128]{4,3,2,1,0:T(8,128)(2,1)S(1)}, u32[]{:S(2)}, u32[]{:S(2)}) collective-permute-start(bf16[2,2,6,64,128]{4,3,2,1,0:T(8,128)(2,1)S(1)} %pad_maximum_fusion.refs_0_), channel_id=1, source_target_pairs={{6,0},{7,1},{14,8},{15,9},{22,16},{23,17},{30,24},{31,25}} | collective-permute-start | bytes 1179656 | tf_op jit(solution)/shard_map/ppermute | solution.py:37
  100.6 16.9 %collective-permute-start.6 = (bf16[2,2,6,64,128]{4,3,2,1,0:T(8,128)(2,1)S(1)}, bf16[2,2,6,64,128]{4,3,2,1,0:T(8,128)(2,1)S(1)}, u32[]{:S(2)}, u32[]{:S(2)}) collective-permute-start(bf16[2,2,6,64,128]{4,3,2,1,0:T(8,128)(2,1)S(1)} %pad_maximum_fusion.refs_0_), channel_id=1, source_target_pairs={{0,2},{1,3},{2,4},{3,5},{4,6},{5,7},{8,10},{9,11},{10,12},{11,13},... | collective-permute-start | bytes 1179656 | tf_op jit(solution)/shard_map/ppermute | solution.py:37
  101.9 19.9 %collective-permute-start.7 = (bf16[2,2,6,64,128]{4,3,2,1,0:T(8,128)(2,1)S(1)}, bf16[2,2,6,64,128]{4,3,2,1,0:T(8,128)(2,1)S(1)}, u32[]{:S(2)}, u32[]{:S(2)}) collective-permute-start(bf16[2,2,6,64,128]{4,3,2,1,0:T(8,128)(2,1)S(1)} %pad_maximum_fusion.refs_0_), channel_id=1, source_target_pairs={{2,0},{3,1},{4,2},{5,3},{6,4},{7,5},{10,8},{11,9},{12,10},{13,11},... | collective-permute-start | bytes 1179656 | tf_op jit(solution)/shard_map/ppermute | solution.py:37
  108.8 29.9 %copy-start.2 = (bf16[2,2,6,64,128]{4,3,2,1,0:T(8,128)(2,1)}, bf16[2,2,6,64,128]{4,3,2,1,0:T(8,128)(2,1)S(1)}, u32[]{:S(2)}) copy-start(bf16[2,2,6,64,128]{4,3,2,1,0:T(8,128)(2,1)S(1)} %collective-permute-done.10.refs_5_) | copy-start | bytes 1179652
  108.8 15.6 %collective-permute-start.8 = (bf16[2,2,6,64,128]{4,3,2,1,0:T(8,128)(2,1)S(1)}, bf16[2,2,6,64,128]{4,3,2,1,0:T(8,128)(2,1)S(1)}, u32[]{:S(2)}, u32[]{:S(2)}) collective-permute-start(bf16[2,2,6,64,128]{4,3,2,1,0:T(8,128)(2,1)S(1)} %pad_maximum_fusion.refs_0_), channel_id=1, source_target_pairs={{0,4},{1,5},{2,6},{3,7},{8,12},{9,13},{10,14},{11,15},{16,20},{17,... | collective-permute-start | bytes 1179656 | tf_op jit(solution)/shard_map/ppermute | solution.py:37
  111.4 1.5 copy-start.1
  111.5 27.3 %collective-permute-start.9 = (bf16[2,2,6,64,128]{4,3,2,1,0:T(8,128)(2,1)S(1)}, bf16[2,2,6,64,128]{4,3,2,1,0:T(8,128)(2,1)S(1)}, u32[]{:S(2)}, u32[]{:S(2)}) collective-permute-start(bf16[2,2,6,64,128]{4,3,2,1,0:T(8,128)(2,1)S(1)} %pad_maximum_fusion.refs_0_), channel_id=1, source_target_pairs={{4,0},{5,1},{6,2},{7,3},{12,8},{13,9},{14,10},{15,11},{20,16},{21,... | collective-permute-start | bytes 1179656 | tf_op jit(solution)/shard_map/ppermute | solution.py:37
  117.5 21.3 %copy-start.3 = (bf16[2,2,6,64,128]{4,3,2,1,0:T(8,128)(2,1)}, bf16[2,2,6,64,128]{4,3,2,1,0:T(8,128)(2,1)S(1)}, u32[]{:S(2)}) copy-start(bf16[2,2,6,64,128]{4,3,2,1,0:T(8,128)(2,1)S(1)} %collective-permute-done.11.refs_6_) | copy-start | bytes 1179652
  117.5 21.2 %copy-start.4 = (bf16[2,2,6,64,128]{4,3,2,1,0:T(8,128)(2,1)}, bf16[2,2,6,64,128]{4,3,2,1,0:T(8,128)(2,1)S(1)}, u32[]{:S(2)}) copy-start(bf16[2,2,6,64,128]{4,3,2,1,0:T(8,128)(2,1)S(1)} %collective-permute-done.6.refs_1_) | copy-start | bytes 1179652
  121.8 16.9 %copy-start.5 = (bf16[2,2,6,64,128]{4,3,2,1,0:T(8,128)(2,1)}, bf16[2,2,6,64,128]{4,3,2,1,0:T(8,128)(2,1)S(1)}, u32[]{:S(2)}) copy-start(bf16[2,2,6,64,128]{4,3,2,1,0:T(8,128)(2,1)S(1)} %collective-permute-done.7.refs_2_) | copy-start | bytes 1179652
  124.4 14.3 %copy-start.6 = (bf16[2,2,6,64,128]{4,3,2,1,0:T(8,128)(2,1)}, bf16[2,2,6,64,128]{4,3,2,1,0:T(8,128)(2,1)S(1)}, u32[]{:S(2)}) copy-start(bf16[2,2,6,64,128]{4,3,2,1,0:T(8,128)(2,1)S(1)} %collective-permute-done.8.refs_3_) | copy-start | bytes 1179652
  138.8 0.7 copy-start.7
  145.0 1.3 collective-permute-start.16
  147.2 7.9 %copy-start.9 = (f32[4,12,12]{2,1,0:T(8,128)}, f32[4,12,12]{2,1,0:T(8,128)S(1)}, u32[]{:S(2)}) copy-start(f32[4,12,12]{2,1,0:T(8,128)S(1)} %get-tuple-element.25.refs_0_) | copy-start | bytes 6916
  147.2 4.0 %collective-permute-start.17 = (f32[4,12,12]{2,1,0:T(8,128)S(1)}, f32[4,12,12]{2,1,0:T(8,128)S(1)}, u32[]{:S(2)}, u32[]{:S(2)}) collective-permute-start(f32[4,12,12]{2,1,0:T(8,128)S(1)} %get-tuple-element.25.refs_0_), channel_id=1, source_target_pairs={{0,16},{8,24},{16,0},{24,8},{1,17},{9,25},{17,1},{25,9},{2,18},{10... | collective-permute-start | bytes 6920 | tf_op jit(solution)/shard_map/ppermute | solution.py:27
  148.7 4.2 %collective-permute-start.18 = (f32[4,12,12]{2,1,0:T(8,128)S(1)}, f32[4,12,12]{2,1,0:T(8,128)S(1)}, u32[]{:S(2)}, u32[]{:S(2)}) collective-permute-start(f32[4,12,12]{2,1,0:T(8,128)S(1)} %get-tuple-element.24), channel_id=1, source_target_pairs={{0,1},{1,0},{2,3},{3,2},{4,5},{5,4},{6,7},{7,6},{8,9},{9,8},{10,11... | collective-permute-start | bytes 6920 | tf_op jit(solution)/shard_map/ppermute | solution.py:27
  150.2 4.8 %collective-permute-start.19 = (f32[4,12,12]{2,1,0:T(8,128)S(1)}, f32[4,12,12]{2,1,0:T(8,128)S(1)}, u32[]{:S(2)}, u32[]{:S(2)}) collective-permute-start(f32[4,12,12]{2,1,0:T(8,128)S(1)} %get-tuple-element.24), channel_id=1, source_target_pairs={{0,17},{1,16},{2,19},{3,18},{4,21},{5,20},{6,23},{7,22},{8,25},{9,... | collective-permute-start | bytes 6920 | tf_op jit(solution)/shard_map/ppermute | solution.py:510
  151.1 3.9 %copy-start.10 = (f32[4,12,12]{2,1,0:T(8,128)}, f32[4,12,12]{2,1,0:T(8,128)S(1)}, u32[]{:S(2)}) copy-start(f32[4,12,12]{2,1,0:T(8,128)S(1)} %collective-permute-done.17.refs_1_) | copy-start | bytes 6916
  152.9 2.1 %copy-start.11 = (f32[4,12,12]{2,1,0:T(8,128)}, f32[4,12,12]{2,1,0:T(8,128)S(1)}, u32[]{:S(2)}) copy-start(f32[4,12,12]{2,1,0:T(8,128)S(1)} %collective-permute-done.18.refs_2_) | copy-start | bytes 6916
  155.1 0.6 copy-start.12

commit v2 on v1

--- a/solution.py
+++ b/solution.py
@@ -15,7 +15,7 @@
 F32 = jnp.float32
 BF16 = jnp.bfloat16
 CHUNK = 32
-VMEM_LIMIT = 58 * 1024 * 1024
+MEGA = 1024 * 1024
 
 ANY = pl.BlockSpec(memory_space=pl.ANY)
 SMEM = pl.BlockSpec(memory_space=pltpu.SMEM)
@@ -27,77 +27,102 @@
     return lax.ppermute(block, axis, [(i, i ^ mask) for i in range(count)])
 
 
-def along_line(block, distance, line):
-    route = [
-        (2 * z + x, 2 * (z + distance) + x)
-        for z in range(line)
-        for x in range(2)
-        if 0 <= z + distance < line
-    ]
+def along_line(block, moves):
+    route = [(2 * z + x, 2 * to + x) for z, to in moves.items() for x in range(2)]
     return lax.ppermute(block, "tm", route)
 
 
-def gather_by_swaps(block):
-    count = lax.axis_size("space")
+def share_line(keep, received, line):
+    piece = jnp.stack([keep, received])
+    if line != 4:
+        arrays, table = [keep, received], {0: (0, None), 1: (1, None)}
+        for distance in range(1, line):
+            moved = along_line(piece, {z: (z + distance) % line for z in range(line)})
+            for side in range(2):
+                table[2 * distance + side] = (len(arrays), side)
+            arrays.append(moved)
+        return arrays, table
+    between = along_line(piece, {1: 2, 2: 1})
+    far = along_line(piece, {0: 3, 3: 0})
+    skip = along_line(piece, {0: 2, 3: 1})
+    near = along_line(piece, {0: 1, 1: 0, 2: 3, 3: 2})
+    passed = along_line(between, {1: 0, 2: 3})
+    arrays = [keep, received, near, skip, between, passed, far]
+    table = {0: (0, None), 1: (1, None)}
+    for code in range(2, 12):
+        table[code] = (1 + code // 2, code % 2)
+    return arrays, table
+
+
+def line_code(here, there, side, line):
+    if line != 4:
+        return 2 * lax.rem(here - there + line, line) + side
+    apart = here ^ there
+    ends = (here == 0) | (here == line - 1)
+    return 2 * jnp.where(ends & (apart >= 2), apart + 2, apart) + side
+
+
+def swap_far(block):
     held = {0: block}
-    mask = count // 2
-    while mask:
+    mask = lax.axis_size("space") // 2
+    while mask >= 2:
         for key in sorted(held):
             held[key | mask] = swap_bit(held[key], "space", mask)
         mask //= 2
-    return [held[key] for key in range(count)]
-
-
-def params():
-    return pltpu.CompilerParams(vmem_limit_bytes=VMEM_LIMIT)
-
-
-def elemental_kernel(held, near, late, last, whole, first_colour, *refs):
+    return held
+
+
+def swap_near(held):
+    both = dict(held)
+    for key in sorted(held):
+        both[key | 1] = swap_bit(held[key], "space", 1)
+    return [both[key] for key in sorted(both)]
+
+
+def params(megabytes):
+    return pltpu.CompilerParams(vmem_limit_bytes=megabytes * MEGA)
+
+
+def elemental_kernel(held, near, late, *refs):
     move_ref, zphase_ref, phase_ref = refs[:3]
     slab_refs = refs[3 : 3 + held]
     rest = refs[3 + held :]
     if late:
-        prior_ref, rest = rest[0], rest[1:]
-    if last:
-        full_ref, keep_ref, send_ref = rest[:3]
-        rest = rest[3:]
+        prior_ref, acc_out, keep_ref, send_ref, slabs, turned, mixed, table, acc, before, sems = rest
     else:
-        out_ref, rest = rest[0], rest[1:]
-    slabs, turned, mixed, acc, sems = rest
-    operators = acc.shape[0]
-    vectors = acc.shape[2]
+        acc, slabs, turned, mixed, table, sems = rest
+    operators, _, vectors = acc.shape
     colours = turned.shape[0]
     count = lax.axis_size("space")
     me = lax.axis_index("space")
 
-    copies = []
-    for m in range(held):
-        source = slab_refs[m]
-        if m < whole:
-            source = source.at[:, pl.ds(first_colour, colours)]
-        copies.append(
-            pltpu.make_async_copy(source, slabs.at[m, :, :, pl.ds(0, PLANE), :], sems.at[2 * m])
-        )
-        copies.append(
+    def arriving(m):
+        return (
             pltpu.make_async_copy(
-                source.at[:, :, pl.ds(0, LX), :],
+                slab_refs[m], slabs.at[m, :, :, pl.ds(0, PLANE), :], sems.at[2 * m]
+            ),
+            pltpu.make_async_copy(
+                slab_refs[m].at[:, :, pl.ds(0, LX), :],
                 slabs.at[m, :, :, pl.ds(PLANE, LX), :],
                 sems.at[2 * m + 1],
-            )
+            ),
         )
-    for copy in copies:
-        copy.start()
+
+    for m in reversed(range(held)):
+        for copy in arriving(m):
+            copy.start()
     if late:
-        acc[...] = prior_ref[...]
-    else:
-        acc[...] = jnp.zeros_like(acc)
-    for copy in copies:
-        copy.wait()
-
-    row = lax.broadcasted_iota(jnp.int32, (PLANE, PLANE), 0)
-    column = lax.broadcasted_iota(jnp.int32, (PLANE, PLANE), 1)
-    wanted = jnp.where(row % LX == LX - 1, row - (LX - 1), row + 1)
-    step_x = (column == wanted).astype(F32).astype(BF16)
+        prior = pltpu.make_async_copy(prior_ref, before, sems.at[2 * held])
+        prior.start()
+    acc[...] = jnp.zeros_like(acc)
+    upright = phase_ref[...].T
+    for o in range(operators):
+        for part in range(2):
+            at = 2 * o + part
+            table[o, part] = jnp.broadcast_to(upright[:, at : at + 1], (PLANE, LANES))
+    for m in range(held):
+        for copy in arriving(m):
+            copy.wait()
 
     def one_slab(m, carry):
         here = me ^ m
@@ -113,8 +138,12 @@
                     same = flat if part == 0 else -flat
                     turned[colour, pl.ds(0, vectors), pl.ds(part * PLANE, PLANE)] = flat
                     turned[colour, pl.ds(vectors, vectors), pl.ds((1 - part) * PLANE, PLANE)] = same
-                    moved = jnp.dot(step_x, block, preferred_element_type=F32)
-                    slabs[held, part, colour, pl.ds(0, PLANE), :] = moved.astype(BF16)
+                    for begin in range(0, PLANE, CHUNK):
+                        rows = slabs[m, part, colour, pl.ds(begin, CHUNK), :].astype(F32)
+                        rows = pltpu.roll(rows.reshape(CHUNK // LX, LX, vectors), LX - 1, 1)
+                        slabs[held, part, colour, pl.ds(begin, CHUNK), :] = rows.reshape(
+                            CHUNK, vectors
+                        ).astype(BF16)
 
             def one_operator(o, inner):
                 move = move_ref[o]
@@ -126,8 +155,8 @@
                     off = pl.multiple_of(jnp.where(move == 2, LX, 0), LX)
                     cos_z, sin_z = zphase_ref[0, here, o], zphase_ref[1, here, o]
                     for begin in range(0, PLANE, CHUNK):
-                        cos_p = phase_ref[o, 0, pl.ds(begin, CHUNK), :]
-                        sin_p = phase_ref[o, 1, pl.ds(begin, CHUNK), :]
+                        cos_p = table[o, 0, pl.ds(begin, CHUNK), :]
+                        sin_p = table[o, 1, pl.ds(begin, CHUNK), :]
                         cosine = cos_p * cos_z - sin_p * sin_z
                         sine = sin_p * cos_z + cos_p * sin_z
                         cosine = jnp.concatenate([cosine] * (vectors // LANES), axis=1)
@@ -155,48 +184,48 @@
 
     lax.fori_loop(0, held, one_slab, 0)
 
-    if last:
+    if late:
         block_rows = keep_ref.shape[2]
         first = pl.multiple_of(me * block_rows, block_rows)
         half = lax.rem(lax.axis_index("tm"), 2)
+        prior.wait()
         for o in range(operators):
-            full_ref[o] = acc[o].astype(BF16)
-        for o in range(operators):
+            acc_out[o] = (acc[o] + before[o]).astype(BF16)
             for part in range(2):
-                own = full_ref[o, pl.ds(part * vectors + first, block_rows), :]
+                rows = pl.ds(part * vectors + first, block_rows)
+                own = (acc[o, rows, :] + before[o, rows, :]).astype(BF16)
                 low, high = own[:, :LANES], own[:, LANES:]
                 keep_ref[part, o] = jnp.where(half == 0, low, high)
                 send_ref[part, o] = jnp.where(half == 0, high, low)
-    else:
-        out_ref[...] = acc[...]
-
-
-def elementals(tables, slab_list, near, prior, last, colours, whole, first_colour, block_rows):
-    _, _, plane, vectors = slab_list[0].shape
+
+
+def elementals(tables, slab_list, near, prior, block_rows):
+    _, colours, plane, vectors = slab_list[0].shape
     held = len(slab_list)
     operators = tables[0].shape[0]
     late = prior is not None
     wide = jax.ShapeDtypeStruct((operators, 2 * vectors, vectors), F32)
-    if last:
+    scratch = [
+        pltpu.VMEM((held + 1, 2, colours, plane + LX, vectors), BF16),
+        pltpu.VMEM((colours, 2 * vectors, 2 * plane), BF16),
+        pltpu.VMEM((colours, 2 * plane, vectors), BF16),
+        pltpu.VMEM((operators, 2, plane, LANES), F32),
+    ]
+    if late:
         piece = jax.ShapeDtypeStruct((2, operators, block_rows, LANES), BF16)
         outs = (jax.ShapeDtypeStruct(wide.shape, BF16), piece, piece)
         out_specs = (VMEM, VMEM, VMEM)
+        scratch += [pltpu.VMEM(wide.shape, F32)] * 2
     else:
         outs, out_specs = wide, VMEM
     priors = [prior] if late else []
     return pl.pallas_call(
-        functools.partial(elemental_kernel, held, near, late, last, whole, first_colour),
+        functools.partial(elemental_kernel, held, near, late),
         out_shape=outs,
-        in_specs=[SMEM, SMEM, VMEM] + [ANY] * held + [VMEM] * len(priors),
+        in_specs=[SMEM, SMEM, VMEM] + [ANY] * (held + len(priors)),
         out_specs=out_specs,
-        scratch_shapes=[
-            pltpu.VMEM((held + 1, 2, colours, plane + LX, vectors), BF16),
-            pltpu.VMEM((colours, 2 * vectors, 2 * plane), BF16),
-            pltpu.VMEM((colours, 2 * plane, vectors), BF16),
-            pltpu.VMEM(wide.shape, F32),
-            pltpu.SemaphoreType.DMA((2 * held,)),
-        ],
-        compiler_params=params(),
+        scratch_shapes=scratch + [pltpu.SemaphoreType.DMA((2 * held + 1,))],
+        compiler_params=params(20 + held),
         cost_estimate=pl.CostEstimate(
             flops=8 * held * operators * colours * plane * vectors * vectors,
             bytes_accessed=held * 2 * colours * plane * vectors * 2,
@@ -288,12 +317,8 @@
             pltpu.VMEM((2, sources, operators * block_rows, 2 * vectors), BF16),
             pltpu.SemaphoreType.DMA((blocks,)),
         ],
-        compiler_params=params(),
-        cost_estimate=pl.CostEstimate(
-            flops=2 * 3 * sources * operators * 4 * block_rows * vectors * vectors,
-            bytes_accessed=8 * sources * vectors * vectors,
-            transcendentals=0,
-        ),
+        compiler_params=params(16),
+        cost_estimate=pl.CostEstimate(flops=0, bytes_accessed=0, transcendentals=0),
         name="both_sides",
     )(elements, *perams)
 
@@ -325,34 +350,31 @@
         in_specs=[VMEM, VMEM],
         out_specs=VMEM,
         scratch_shapes=[pltpu.VMEM((2 * rows * block_rows, lanes), F32)],
-        compiler_params=params(),
-        cost_estimate=pl.CostEstimate(
-            flops=own.size, bytes_accessed=8 * own.size, transcendentals=0
-        ),
+        compiler_params=params(12),
+        cost_estimate=pl.CostEstimate(flops=0, bytes_accessed=0, transcendentals=0),
         name="lay_out",
     )(own, pair)
 
 
-def trace_kernel(offsets, times_ref, *refs):
-    count = len(offsets)
+def trace_kernel(count, table, line, times_ref, *refs):
     pools = refs[:count]
-    laid_ref, mine_ref, pair_ref, picked, wide, sems = refs[count:]
+    laid_ref, out_ref, picked, wide, sems = refs[count:]
     sources = laid_ref.shape[0]
-    _, _, operators, block_rows, lanes = pools[0].shape
+    _, operators, block_rows, lanes = pools[0].shape
     rows = 2 * operators
     time = lax.axis_index("tm")
     for s in range(sources):
         source = times_ref[s]
-        away = source // 2 - time // 2
-        side = lax.rem(source + time, 2)
-        for at, distance in enumerate(offsets):
-
-            @pl.when(away == distance)
-            def _(at=at, s=s, side=side):
-                pltpu.make_async_copy(pools[at].at[side], picked.at[s], sems.at[s]).start()
+        code = line_code(time // 2, source // 2, lax.rem(source + time, 2), line)
+        for index, (at, inside) in table.items():
+
+            @pl.when(code == index)
+            def _(at=at, inside=inside, s=s):
+                block = pools[at] if inside is None else pools[at].at[inside]
+                pltpu.make_async_copy(block, picked.at[s], sems.at[s]).start()
 
     for s in range(sources):
-        pltpu.make_async_copy(pools[0].at[0], picked.at[s], sems.at[s]).wait()
+        pltpu.make_async_copy(pools[0], picked.at[s], sems.at[s]).wait()
         wide[...] = picked[s].astype(F32).reshape(rows * block_rows, lanes)
         product = lax.dot_general(
             laid_ref[s],
@@ -360,26 +382,25 @@
             (((1,), (1,)), ((), ())),
             preferred_element_type=F32,
         )
-        mine_ref[s] = product[:rows]
-        pair_ref[s] = product[rows:]
-
-
-def traces(source_times, offsets, pools, laid):
+        out_ref[0, s] = product[:rows]
+        out_ref[1, s] = product[rows:]
+
+
+def traces(source_times, pools, table, line, laid):
     sources = laid.shape[0]
-    _, _, operators, block_rows, lanes = pools[0].shape
+    _, operators, block_rows, lanes = pools[0].shape
     rows = 2 * operators
-    result = jax.ShapeDtypeStruct((sources, rows, rows), F32)
     return pl.pallas_call(
-        functools.partial(trace_kernel, offsets),
-        out_shape=(result, result),
-        in_specs=[SMEM] + [ANY] * len(offsets) + [VMEM],
-        out_specs=(VMEM, VMEM),
+        functools.partial(trace_kernel, len(pools), table, line),
+        out_shape=jax.ShapeDtypeStruct((2, sources, rows, rows), F32),
+        in_specs=[SMEM] + [ANY] * len(pools) + [VMEM],
+        out_specs=VMEM,
         scratch_shapes=[
-            pltpu.VMEM((sources,) + pools[0].shape[1:], BF16),
+            pltpu.VMEM((sources,) + pools[0].shape, BF16),
             pltpu.VMEM((rows * block_rows, lanes), F32),
             pltpu.SemaphoreType.DMA((sources,)),
         ],
-        compiler_params=params(),
+        compiler_params=params(12),
         cost_estimate=pl.CostEstimate(
             flops=4 * sources * rows * rows * block_rows * lanes,
             bytes_accessed=2 * laid.size,
@@ -392,38 +413,39 @@
 def finish_kernel(count, *refs):
     parts = refs[:count]
     correlator_ref, pairs_ref = refs[count:]
-    sources, rows, _ = parts[0].shape
+    sources, rows, _ = parts[1].shape
     n = rows // 2
     eye = lax.broadcasted_iota(jnp.int32, (n, n), 0) == lax.broadcasted_iota(jnp.int32, (n, n), 1)
     for s in range(sources):
-        terms = [ref[s] for ref in parts]
+        terms = [parts[0][0, s]] + [ref[s] for ref in parts[1:]]
         while len(terms) > 1:
             terms = [one + two for one, two in zip(terms[::2], terms[1::2])]
         total = terms[0]
         real = total[:n, :n] - total[n:, n:]
         imaginary = total[:n, n:] + total[n:, :n]
-        correlator_ref[0, s, 0] = real
-        correlator_ref[0, s, 1] = imaginary
+        correlator_ref[0, s, :, 0, :] = real
+        correlator_ref[0, s, :, 1, :] = imaginary
         down_real, down_imaginary, over_real, over_imaginary = (
             jnp.sum(jnp.where(eye, block, 0.0), axis=axis, keepdims=True)
             for axis in (1, 0)
             for block in (real, imaginary)
         )
-        pairs_ref[0, s, 0] = down_real * over_real - down_imaginary * over_imaginary
-        pairs_ref[0, s, 1] = down_real * over_imaginary + down_imaginary * over_real
+        pairs_ref[0, s, :, 0, :] = down_real * over_real - down_imaginary * over_imaginary
+        pairs_ref[0, s, :, 1, :] = down_real * over_imaginary + down_imaginary * over_real
 
 
 def finish(parts):
-    sources, rows, _ = parts[0].shape
-    result = jax.ShapeDtypeStruct((1, sources, 2, rows // 2, rows // 2), F32)
-    return pl.pallas_call(
+    sources, rows, _ = parts[1].shape
+    result = jax.ShapeDtypeStruct((1, sources, rows // 2, 2, rows // 2), F32)
+    correlator, pairs = pl.pallas_call(
         functools.partial(finish_kernel, len(parts)),
         out_shape=(result, result),
         in_specs=[VMEM] * len(parts),
         out_specs=(VMEM, VMEM),
-        compiler_params=params(),
+        compiler_params=params(4),
         name="finish",
     )(*parts)
+    return jnp.swapaxes(correlator, 2, 3), jnp.swapaxes(pairs, 2, 3)
 
 
 def phase_tables(momenta, z_coords, z_extent):
@@ -431,8 +453,7 @@
     along_x = (momenta[:, 0:1] * (plane % LX)[None] % LX).astype(F32) * (2.0 * math.pi / LX)
     along_y = (momenta[:, 1:2] * (plane // LX)[None] % LY).astype(F32) * (2.0 * math.pi / LY)
     angle = along_x + along_y
-    table = jnp.stack([jnp.cos(angle), jnp.sin(angle)], axis=1)
-    table = jnp.broadcast_to(table[..., None], table.shape + (LANES,))
+    table = jnp.stack([jnp.cos(angle), jnp.sin(angle)], axis=1).reshape(-1, PLANE)
     along_z = (momenta[:, 2][None, :] * z_coords[:, None] % z_extent).astype(F32) * (
         2.0 * math.pi / z_extent
     )
@@ -447,59 +468,34 @@
     near = 2
 
     own = eigenvectors.reshape(parts, colours, plane, vectors)
-    cut = colours - 1
-    groups = [(0, cut), (cut, colours - cut)]
-    far = [own[:, begin : begin + size] for begin, size in groups]
-    held = [{0: block} for block in far]
     beside = swap_bit(own, "space", 1)
-    mask = slabs // 2
-    while mask >= near:
-        for keys in held:
-            for key in sorted(keys):
-                keys[key | mask] = swap_bit(keys[key], "space", mask)
-        mask //= 2
+    keys = swap_far(own)
 
     plane_phase, z_phase = phase_tables(momenta, jnp.arange(slabs, dtype=jnp.int32), slabs)
     tables = (displacement, z_phase, plane_phase)
-    total = elementals(tables, [own, beside], near, None, False, colours, near, 0, block_rows)
-
-    for at, (begin, size) in enumerate(groups):
-        last = at == len(groups) - 1
-        keys = held[at]
-        arrived = sorted(key for key in keys if key >= near)
-        if at == 0:
-            tied = lax.optimization_barrier(tuple(keys[key] for key in arrived) + (total,))
-            keys.update(zip(arrived, tied))
-            total = tied[-1]
-        for key in arrived:
-            keys[key | 1] = swap_bit(keys[key], "space", 1)
-        slab_list = [own, beside] + [keys[key] for key in range(near, slabs)]
-        total = elementals(tables, slab_list, near, total, last, size, near, begin, block_rows)
-    full, keep, send = total
-
-    peram, _ = lax.optimization_barrier((perambulators[0], held[-1][slabs // 2]))
-    perams = gather_by_swaps(peram)
+    total = elementals(tables, [own, beside], near, None, block_rows)
+
+    keys, total = lax.optimization_barrier((keys, total))
+    slab_list = swap_near(keys)
+    slab_list[1] = beside
+    peram, _ = lax.optimization_barrier((perambulators[0], keys[slabs // 2]))
+    perams = swap_far(peram)
+    full, keep, send = elementals(tables, slab_list, near, total, block_rows)
+
+    perams = swap_near(lax.optimization_barrier((perams, full))[0])
 
     received = swap_bit(send, "tm", 1)
-    piece = jnp.stack([keep, received])
-    offsets, pools = [0], [piece]
-    for distance in range(1, line):
-        for sign in (1, -1):
-            offsets.append(-sign * distance)
-            pools.append(along_line(piece, sign * distance, line))
-
     g_keep, g_send = both_sides(full, perams)
+    g_send, received = lax.optimization_barrier((g_send, received))
+    arrays, table = share_line(keep, received, line)
     laid = lay_out(g_keep, swap_bit(g_send, "tm", 1))
-    mine, pair = traces(source_times, offsets, pools, laid)
-
-    both = jnp.stack([mine, pair])
+    both = traces(source_times, arrays, table, line, laid)
     both = both + swap_bit(both, "space", 1)
     mine, pair = both[0], both[1]
-    sums = [mine]
-    sums += [swap_bit(mine, "space", mask) for mask in range(2, slabs, 2)]
-    sums += [swap_bit(pair, "tm", 1)]
-    sums += [across(pair, mask) for mask in range(2, slabs, 2)]
-    return finish(sums)
+    near_sums = [swap_bit(mine, "space", mask) for mask in range(2, slabs, 2)]
+    pair_sums = [swap_bit(pair, "tm", 1)]
+    pair_sums += [across(pair, mask) for mask in range(2, slabs, 2)]
+    return finish([both] + near_sums + pair_sums)
 
 
 def across(block, mask):

time: 161 us -> 91.3 us (0.57)
  waiting for transfers between devices: 61.1 us -> 32.3 us
  Pallas kernels: 59.9 us -> 32.4 us
  local copies, waits for them, and re-layouts: 10.1 us -> 2.66 us
  starting transfers between devices: 25.3 us -> 22.8 us
  other arithmetic: 2.58 us -> 0.42 us
    pallas_call x4 -> x3, Pallas kernels: 46.9 us -> 26.4 us  [the longest x2 22.8 us: elementals(): pl.pallas_call(functools.partial(elemental_kernel, held, near, late), out...]
    ppermute x6 -> x5, waiting for transfers between devices: 26.8 us -> 12.5 us  [along_line(): return lax.ppermute(block, 'tm', route)]
    ppermute x13 -> x11, waiting for transfers between devices: 32.2 us -> 18.4 us  [swap_bit(): return lax.ppermute(block, axis, [(i, i ^ mask) for i in range(count)])]
    pallas_call x1, Pallas kernels: 6.77 us -> 3.09 us  [both_sides(): pl.pallas_call(functools.partial(both_kernel, blocks), out_shape=(piece,...]
    ppermute x6 -> x5, starting transfers between devices: 13.7 us -> 10.2 us  [along_line(): return lax.ppermute(block, 'tm', route)]
    pallas_call x2 -> x0, local copies, waits for them, and re-layouts: 2.75 us -> none  [finish(): pl.pallas_call(functools.partial(finish_kernel, len(parts)), out_shape=(r...]
    pallas_call x1, Pallas kernels: 4.54 us -> 1.99 us  [lay_out(): pl.pallas_call(lay_kernel, out_shape=jax.ShapeDtypeStruct((sources, 2 * r...]
    slice x2 -> x0, local copies, waits for them, and re-layouts: 2.04 us -> none  [body(): far = [own[:, begin:begin + size] for begin, size in groups]]
  transfers between devices with their start and end apart: 20 -> 17, of which waited for: 10 -> 11; matrix products, arithmetic and copies ran while one was open for 3% -> 1% of each run, Pallas kernels for 29% -> 30%
where the time goes in v2:
time: 91.3 us; the launch traced here: 91.4 us
  Pallas kernels  32.4 us (35%)
  waiting for transfers between devices  32.3 us (35%)
  starting transfers between devices  22.8 us (25%)
  local copies, waits for them, and re-layouts  2.66 us (3%)
    pallas_call x2, Pallas kernels, elementals(): pl.pallas_call(functools.partial(elemental_kernel, held, near, late), out...  22.8 us
    ppermute x11, waiting for transfers between devices, swap_bit(): return lax.ppermute(block, axis, [(i, i ^ mask) for i in range(count)])  18.4 us
    ppermute x5, waiting for transfers between devices, along_line(): return lax.ppermute(block, 'tm', route)  12.5 us
    ppermute x11, starting transfers between devices, swap_bit(): return lax.ppermute(block, axis, [(i, i ^ mask) for i in range(count)])  11.1 us
    ppermute x5, starting transfers between devices, along_line(): return lax.ppermute(block, 'tm', route)  10.2 us
    pallas_call x1, Pallas kernels, traces(): pl.pallas_call(functools.partial(trace_kernel, len(pools), table, line),...  3.64 us
    pallas_call x1, Pallas kernels, both_sides(): pl.pallas_call(functools.partial(both_kernel, blocks), out_shape=(piece,...  3.09 us
    pallas_call x1, Pallas kernels, lay_out(): pl.pallas_call(lay_kernel, out_shape=jax.ShapeDtypeStruct((sources, 2 * r...  1.99 us
  transfers between devices with their start and end apart: 17, of which 11 were waited for; matrix products, arithmetic and copies ran while one was open for 1% of the time, Pallas kernels for 30%

profile of v2, /device:TPU:0, one launch (start us, length us, event | category | flops | bytes accessed | tf_op | source)
XLA Modules:
  0.0 91.4 jit_solution(6723610751758509232)
XLA Ops:
  0.6 0.5 collective-permute-start.1
  1.1 2.6 %collective-permute-start = (bf16[2,3,256,256]{3,2,1,0:T(8,128)(2,1)}, bf16[2,3,256,256]{3,2,1,0:T(8,128)(2,1)S(1)}, u32[]{:S(2)}, u32[]{:S(2)}) collective-permute-start(bf16[2,3,256,256]{3,2,1,0:T(8,128)(2,1)} %bitcast.22), channel_id=1, source_target_pairs={{0,16},{8,24},{16,0},{24,8},{1,17},{9,25},{17,1},{25,9},{2,18},{10... | collective-permute-start | bytes 2359304 | tf_op jit(solution)/shard_map/ppermute | solution.py:27
  3.7 0.8 slice_bitcast_fusion.3
  4.5 0.3 fusion.13
  4.9 0.1 fusion.11
  5.0 0.0 copy-start
  5.0 0.0 collective-permute-done.1.refs_4_
  5.0 0.0 copy-start.2
  5.0 1.2 %copy-done.2 = bf16[1,2,3,1,256,256]{5,4,3,2,1,0:T(8,128)(2,1)S(1)} copy-done((bf16[1,2,3,1,256,256]{5,4,3,2,1,0:T(8,128)(2,1)S(1)}, bf16[1,2,3,1,256,256]{5,4,3,2,1,0:T(8,128)(2,1)}, u32[]{:S(2)}) %copy-start.2) | copy-done | bytes 786456
  6.2 0.7 copy-done.4
  6.8 9.4 %elementals_early.1.refs_7_ = f32[6,512,256]{2,1,0:T(8,128)S(1)} custom-call(s32[6]{0:T(128)S(1)} %copy-done.4, f32[2,4,6]{2,1,0:T(4,128)S(1)} %pad_maximum_fusion.2.refs_1_, f32[12,256]{1,0:T(8,128)S(1)} %reshape.399.refs_2_, bf16[2,3,256,256]{3,2,1,0:T(8,128)(2,1)S(1)} %bitcast.23, bf16[2,3,256,256]{3,2,1,0:T(8,128)(2,1)S(1)} %collective-permute-done.1.refs_4_), custom_call_target="tpu_custom_call" | custom-call | flops 4831838208 | bytes 1572864 | tf_op jit(solution)/shard_map/elementals_early/pallas_call | solution.py:222
  16.2 5.9 %collective-permute-done.refs_5_ = bf16[2,3,256,256]{3,2,1,0:T(8,128)(2,1)S(1)} collective-permute-done((bf16[2,3,256,256]{3,2,1,0:T(8,128)(2,1)}, bf16[2,3,256,256]{3,2,1,0:T(8,128)(2,1)S(1)}, u32[]{:S(2)}, u32[]{:S(2)}) %collective-permute-start) | collective-permute-done | bytes 786464 | tf_op jit(solution)/shard_map/ppermute | solution.py:27
  22.1 0.0 collective-permute-start.2
  22.1 0.0 copy-done
  22.1 1.8 %collective-permute-start.3 = (bf16[4,2,64,256]{3,2,1,0:T(8,128)(2,1)S(1)}, bf16[4,2,64,256]{3,2,1,0:T(8,128)(2,1)S(1)}, u32[]{:S(2)}, u32[]{:S(2)}) collective-permute-start(bf16[4,2,64,256]{3,2,1,0:T(8,128)(2,1)S(1)} %bitcast.18), channel_id=1, source_target_pairs={{0,16},{8,24},{16,0},{24,8},{1,17},{9,25},{17,1},{25,9},{2,18},{10... | collective-permute-start | bytes 786440 | tf_op jit(solution)/shard_map/ppermute | solution.py:27
  23.9 0.5 collective-permute-done.2.refs_6_
  24.4 13.4 %elementals_late.1 = (bf16[6,512,256]{2,1,0:T(8,128)(2,1)S(1)}, bf16[2,6,64,128]{3,2,1,0:T(8,128)(2,1)S(1)}, bf16[2,6,64,128]{3,2,1,0:T(8,128)(2,1)S(1)}) custom-call(s32[6]{0:T(128)S(1)} %copy-done.5, f32[2,4,6]{2,1,0:T(4,128)S(1)} %pad_maximum_fusion.2.refs_1_, f32[12,256]{1,0:T(8,128)S(1)} %reshape.399.refs_2_, bf16[2,3,256,256]{3,2,1,0:T(8,128)(2,1)S(1)} %bitcast.24, ...), custom_call_target="tpu_custom_call" | custom-call | flops 9663676416 | bytes 3145728 | tf_op jit(solution)/shard_map/elementals_late/pallas_call | solution.py:222
  37.8 0.0 collective-permute-done.3.refs_2_
  37.8 0.2 collective-permute-start.4
  38.0 0.4 collective-permute-start.5
  38.4 1.7 %collective-permute-start.6 = (bf16[2,6,64,128]{3,2,1,0:T(8,128)(2,1)S(1)}, bf16[2,6,64,128]{3,2,1,0:T(8,128)(2,1)S(1)}, u32[]{:S(2)}, u32[]{:S(2)}) collective-permute-start(bf16[2,6,64,128]{3,2,1,0:T(8,128)(2,1)S(1)} %get-tuple-element.26), channel_id=1, source_target_pairs={{0,1},{1,0},{2,3},{3,2},{4,5},{5,4},{6,7},{7,6},{8,9},{9,8},{10,11... | collective-permute-start | bytes 589832 | tf_op jit(solution)/shard_map/ppermute | solution.py:27
  40.1 0.0 collective-permute-done.4.refs_1_
  40.1 0.0 collective-permute-done.5.refs_3_
  40.1 3.1 %both_sides.1 = (bf16[4,2,6,64,128]{4,3,2,1,0:T(8,128)(2,1)S(1)}, bf16[4,2,6,64,128]{4,3,2,1,0:T(8,128)(2,1)S(1)}) custom-call(bf16[6,512,256]{2,1,0:T(8,128)(2,1)S(1)} %get-tuple-element.21.e_ref, bf16[4,2,64,256]{3,2,1,0:T(8,128)(2,1)S(1)} %bitcast.20, bf16[4,2,64,256]{3,2,1,0:T(8,128)(2,1)S(1)} %collective-permute-done.4.refs_1_, ...), custom_call_target="tpu_custom_call" | custom-call | tf_op jit(solution)/shard_map/both_sides/pallas_call | solution.py:309
  43.2 2.1 %collective-permute-done.6.refs_1_ = bf16[2,6,64,128]{3,2,1,0:T(8,128)(2,1)S(1)} collective-permute-done((bf16[2,6,64,128]{3,2,1,0:T(8,128)(2,1)S(1)}, bf16[2,6,64,128]{3,2,1,0:T(8,128)(2,1)S(1)}, u32[]{:S(2)}, u32[]{:S(2)}) %collective-permute-start.6) | collective-permute-done | bytes 196640 | tf_op jit(solution)/shard_map/ppermute | solution.py:27
  45.3 1.7 %collective-permute-start.12 = (bf16[4,2,6,64,128]{4,3,2,1,0:T(8,128)(2,1)S(1)}, bf16[4,2,6,64,128]{4,3,2,1,0:T(8,128)(2,1)S(1)}, u32[]{:S(2)}, u32[]{:S(2)}) collective-permute-start(bf16[4,2,6,64,128]{4,3,2,1,0:T(8,128)(2,1)S(1)} %get-tuple-element.29), channel_id=1, source_target_pairs={{0,1},{1,0},{2,3},{3,2},{4,5},{5,4},{6,7},{7,6},{8,9},{9,8},{10,11... | collective-permute-start | bytes 2359304 | tf_op jit(solution)/shard_map/ppermute | solution.py:27
  47.1 0.7 collective-permute-start.9
  47.8 5.5 %collective-permute-start.11 = (bf16[2,2,6,64,128]{4,3,2,1,0:T(8,128)(2,1)S(1)}, bf16[2,2,6,64,128]{4,3,2,1,0:T(8,128)(2,1)S(1)}, u32[]{:S(2)}, u32[]{:S(2)}) collective-permute-start(bf16[2,2,6,64,128]{4,3,2,1,0:T(8,128)(2,1)S(1)} %pad_maximum_fusion), channel_id=1, source_target_pairs={{0,6},{1,7},{6,0},{7,1},{8,14},{9,15},{14,8},{15,9},{16,22},{17,23... | collective-permute-start | bytes 1179656 | tf_op jit(solution)/shard_map/ppermute | solution.py:32
  53.3 0.1 collective-permute-start.7
  53.4 2.7 %collective-permute-start.8 = (bf16[2,2,6,64,128]{4,3,2,1,0:T(8,128)(2,1)S(1)}, bf16[2,2,6,64,128]{4,3,2,1,0:T(8,128)(2,1)S(1)}, u32[]{:S(2)}, u32[]{:S(2)}) collective-permute-start(bf16[2,2,6,64,128]{4,3,2,1,0:T(8,128)(2,1)S(1)} %pad_maximum_fusion), channel_id=1, source_target_pairs={{0,4},{1,5},{6,2},{7,3},{8,12},{9,13},{14,10},{15,11},{16,20},{17,... | collective-permute-start | bytes 1179656 | tf_op jit(solution)/shard_map/ppermute | solution.py:32
  56.1 0.0 collective-permute-done.9.refs_4_
  56.1 1.3 %collective-permute-start.10 = (bf16[2,2,6,64,128]{4,3,2,1,0:T(8,128)(2,1)S(1)}, bf16[2,2,6,64,128]{4,3,2,1,0:T(8,128)(2,1)S(1)}, u32[]{:S(2)}, u32[]{:S(2)}) collective-permute-start(bf16[2,2,6,64,128]{4,3,2,1,0:T(8,128)(2,1)S(1)} %collective-permute-done.9.refs_4_), channel_id=1, source_target_pairs={{2,0},{3,1},{4,6},{5,7},{10,8},{11,9},{12,14},{13,15},{18,16},{19,... | collective-permute-start | bytes 1179656 | tf_op jit(solution)/shard_map/ppermute | solution.py:32
  57.4 6.7 %collective-permute-done.12.pair_ref = bf16[4,2,6,64,128]{4,3,2,1,0:T(8,128)(2,1)S(1)} collective-permute-done((bf16[4,2,6,64,128]{4,3,2,1,0:T(8,128)(2,1)S(1)}, bf16[4,2,6,64,128]{4,3,2,1,0:T(8,128)(2,1)S(1)}, u32[]{:S(2)}, u32[]{:S(2)}) %collective-permute-start.12) | collective-permute-done | bytes 786464 | tf_op jit(solution)/shard_map/ppermute | solution.py:27
  64.1 2.0 %lay_out.1.refs_7_ = bf16[4,24,8192]{2,1,0:T(8,128)(2,1)S(1)} custom-call(bf16[4,2,6,64,128]{4,3,2,1,0:T(8,128)(2,1)S(1)} %get-tuple-element.28.own_ref, bf16[4,2,6,64,128]{4,3,2,1,0:T(8,128)(2,1)S(1)} %collective-permute-done.12.pair_ref), custom_call_target="tpu_custom_call" | custom-call | tf_op jit(solution)/shard_map/lay_out/pallas_call | solution.py:347
  66.1 0.0 collective-permute-done.11.refs_6_
  66.1 5.2 %collective-permute-done.7.refs_2_ = bf16[2,2,6,64,128]{4,3,2,1,0:T(8,128)(2,1)S(1)} collective-permute-done((bf16[2,2,6,64,128]{4,3,2,1,0:T(8,128)(2,1)S(1)}, bf16[2,2,6,64,128]{4,3,2,1,0:T(8,128)(2,1)S(1)}, u32[]{:S(2)}, u32[]{:S(2)}) %collective-permute-start.7) | collective-permute-done | bytes 393248 | tf_op jit(solution)/shard_map/ppermute | solution.py:32
  71.3 6.5 %collective-permute-done.8.refs_3_ = bf16[2,2,6,64,128]{4,3,2,1,0:T(8,128)(2,1)S(1)} collective-permute-done((bf16[2,2,6,64,128]{4,3,2,1,0:T(8,128)(2,1)S(1)}, bf16[2,2,6,64,128]{4,3,2,1,0:T(8,128)(2,1)S(1)}, u32[]{:S(2)}, u32[]{:S(2)}) %collective-permute-start.8) | collective-permute-done | bytes 393248 | tf_op jit(solution)/shard_map/ppermute | solution.py:32
  77.8 0.8 collective-permute-done.10.refs_5_
  78.6 3.6 %traces.1 = f32[2,4,12,12]{3,2,1,0:T(8,128)S(1)} custom-call(s32[4]{0:T(128)S(1)} %copy-done.1, bf16[2,6,64,128]{3,2,1,0:T(8,128)(2,1)S(1)} %get-tuple-element.20.refs_0_, bf16[2,6,64,128]{3,2,1,0:T(8,128)(2,1)S(1)} %collective-permute-done.6.refs_1_, bf16[2,2,6,64,128]{4,3,2,1,0:T(8,128)(2,1)S(1)} %collective-permute-done.7.refs_2_, ...), custom_call_target="tpu_custom_call" | custom-call | flops 18874368 | bytes 1572864 | tf_op jit(solution)/shard_map/traces/pallas_call | solution.py:393
  82.2 0.1 collective-permute-start.13
  82.3 1.2 %collective-permute-done.13 = f32[2,4,12,12]{3,2,1,0:T(8,128)S(1)} collective-permute-done((f32[2,4,12,12]{3,2,1,0:T(8,128)S(1)}, f32[2,4,12,12]{3,2,1,0:T(8,128)S(1)}, u32[]{:S(2)}, u32[]{:S(2)}) %collective-permute-start.13) | collective-permute-done | bytes 4640 | tf_op jit(solution)/shard_map/ppermute | solution.py:27
  83.6 1.6 %collective-permute-start.14 = (f32[4,12,12]{2,1,0:T(8,128)S(1)}, f32[4,12,12]{2,1,0:T(8,128)S(1)}, u32[]{:S(2)}, u32[]{:S(2)}) collective-permute-start(f32[4,12,12]{2,1,0:T(8,128)S(1)} %get-tuple-element.33), channel_id=1, source_target_pairs={{0,16},{8,24},{16,0},{24,8},{1,17},{9,25},{17,1},{25,9},{2,18},{10... | collective-permute-start | bytes 6920 | tf_op jit(solution)/shard_map/ppermute | solution.py:27
  85.1 0.5 collective-permute-start.15
  85.7 1.5 %collective-permute-start.16 = (f32[4,12,12]{2,1,0:T(8,128)S(1)}, f32[4,12,12]{2,1,0:T(8,128)S(1)}, u32[]{:S(2)}, u32[]{:S(2)}) collective-permute-start(f32[4,12,12]{2,1,0:T(8,128)S(1)} %get-tuple-element.32), channel_id=1, source_target_pairs={{0,17},{1,16},{2,19},{3,18},{4,21},{5,20},{6,23},{7,22},{8,25},{9,... | collective-permute-start | bytes 6920 | tf_op jit(solution)/shard_map/ppermute | solution.py:506
  87.1 0.4 collective-permute-done.14.refs_1_
  87.6 1.5 %collective-permute-done.15.refs_2_ = f32[4,12,12]{2,1,0:T(8,128)S(1)} collective-permute-done((f32[4,12,12]{2,1,0:T(8,128)S(1)}, f32[4,12,12]{2,1,0:T(8,128)S(1)}, u32[]{:S(2)}, u32[]{:S(2)}) %collective-permute-start.15) | collective-permute-done | bytes 2336 | tf_op jit(solution)/shard_map/ppermute | solution.py:27
  89.1 1.4 %collective-permute-done.16.refs_3_ = f32[4,12,12]{2,1,0:T(8,128)S(1)} collective-permute-done((f32[4,12,12]{2,1,0:T(8,128)S(1)}, f32[4,12,12]{2,1,0:T(8,128)S(1)}, u32[]{:S(2)}, u32[]{:S(2)}) %collective-permute-start.16) | collective-permute-done | bytes 2336 | tf_op jit(solution)/shard_map/ppermute | solution.py:506
  90.5 0.9 finish.1
  (14 shorter events, 0.1 us)
Async XLA Ops:
  0.6 4.3 %collective-permute-start.1 = (bf16[2,3,256,256]{3,2,1,0:T(8,128)(2,1)}, bf16[2,3,256,256]{3,2,1,0:T(8,128)(2,1)S(1)}, u32[]{:S(2)}, u32[]{:S(2)}) collective-permute-start(bf16[2,3,256,256]{3,2,1,0:T(8,128)(2,1)} %bitcast.21), channel_id=1, source_target_pairs={{0,8},{8,0},{16,24},{24,16},{1,9},{9,1},{17,25},{25,17},{2,10},{10... | collective-permute-start | bytes 2359304 | tf_op jit(solution)/shard_map/ppermute | solution.py:27
  1.1 20.9 %collective-permute-start = (bf16[2,3,256,256]{3,2,1,0:T(8,128)(2,1)}, bf16[2,3,256,256]{3,2,1,0:T(8,128)(2,1)S(1)}, u32[]{:S(2)}, u32[]{:S(2)}) collective-permute-start(bf16[2,3,256,256]{3,2,1,0:T(8,128)(2,1)} %bitcast.22), channel_id=1, source_target_pairs={{0,16},{8,24},{16,0},{24,8},{1,17},{9,25},{17,1},{25,9},{2,18},{10... | collective-permute-start | bytes 2359304 | tf_op jit(solution)/shard_map/ppermute | solution.py:27
  5.0 17.1 %copy-start = (bf16[1,4,2,64,256]{4,3,2,1,0:T(8,128)(2,1)S(1)}, bf16[1,4,2,64,256]{4,3,2,1,0:T(8,128)(2,1)}, u32[]{:S(2)}) copy-start(bf16[1,4,2,64,256]{4,3,2,1,0:T(8,128)(2,1)} %param.9) | copy-start | bytes 786436
  5.0 1.2 %copy-start.2 = (bf16[1,2,3,1,256,256]{5,4,3,2,1,0:T(8,128)(2,1)S(1)}, bf16[1,2,3,1,256,256]{5,4,3,2,1,0:T(8,128)(2,1)}, u32[]{:S(2)}) copy-start(bf16[1,2,3,1,256,256]{5,4,3,2,1,0:T(8,128)(2,1)} %param.5) | copy-start | bytes 2359300
  6.2 0.7 copy-start.4
  6.8 17.6 %copy-start.3 = (bf16[1,2,3,1,256,256]{5,4,3,2,1,0:T(8,128)(2,1)S(1)}, bf16[1,2,3,1,256,256]{5,4,3,2,1,0:T(8,128)(2,1)}, u32[]{:S(2)}) copy-start(bf16[1,2,3,1,256,256]{5,4,3,2,1,0:T(8,128)(2,1)} %param.5) | copy-start | bytes 2359300
  6.8 17.6 %copy-start.5 = (s32[6]{0:T(128)S(1)}, s32[6]{0:T(128)}, u32[]{:S(2)}) copy-start(s32[6]{0:T(128)} %refs_0_.3) | copy-start | bytes 76
  22.1 2.3 %collective-permute-start.2 = (bf16[2,3,256,256]{3,2,1,0:T(8,128)(2,1)S(1)}, bf16[2,3,256,256]{3,2,1,0:T(8,128)(2,1)S(1)}, u32[]{:S(2)}, u32[]{:S(2)}) collective-permute-start(bf16[2,3,256,256]{3,2,1,0:T(8,128)(2,1)S(1)} %collective-permute-done.refs_5_), channel_id=1, source_target_pairs={{0,8},{8,0},{16,24},{24,16},{1,9},{9,1},{17,25},{25,17},{2,10},{10... | collective-permute-start | bytes 2359304 | tf_op jit(solution)/shard_map/ppermute | solution.py:27
  22.1 15.7 %collective-permute-start.3 = (bf16[4,2,64,256]{3,2,1,0:T(8,128)(2,1)S(1)}, bf16[4,2,64,256]{3,2,1,0:T(8,128)(2,1)S(1)}, u32[]{:S(2)}, u32[]{:S(2)}) collective-permute-start(bf16[4,2,64,256]{3,2,1,0:T(8,128)(2,1)S(1)} %bitcast.18), channel_id=1, source_target_pairs={{0,16},{8,24},{16,0},{24,8},{1,17},{9,25},{17,1},{25,9},{2,18},{10... | collective-permute-start | bytes 786440 | tf_op jit(solution)/shard_map/ppermute | solution.py:27
  37.8 2.3 %collective-permute-start.4 = (bf16[4,2,64,256]{3,2,1,0:T(8,128)(2,1)S(1)}, bf16[4,2,64,256]{3,2,1,0:T(8,128)(2,1)S(1)}, u32[]{:S(2)}, u32[]{:S(2)}) collective-permute-start(bf16[4,2,64,256]{3,2,1,0:T(8,128)(2,1)S(1)} %bitcast.19), channel_id=1, source_target_pairs={{0,8},{8,0},{16,24},{24,16},{1,9},{9,1},{17,25},{25,17},{2,10},{10... | collective-permute-start | bytes 786440 | tf_op jit(solution)/shard_map/ppermute | solution.py:27
  38.0 2.1 %collective-permute-start.5 = (bf16[4,2,64,256]{3,2,1,0:T(8,128)(2,1)S(1)}, bf16[4,2,64,256]{3,2,1,0:T(8,128)(2,1)S(1)}, u32[]{:S(2)}, u32[]{:S(2)}) collective-permute-start(bf16[4,2,64,256]{3,2,1,0:T(8,128)(2,1)S(1)} %collective-permute-done.3.refs_2_), channel_id=1, source_target_pairs={{0,8},{8,0},{16,24},{24,16},{1,9},{9,1},{17,25},{25,17},{2,10},{10... | collective-permute-start | bytes 786440 | tf_op jit(solution)/shard_map/ppermute | solution.py:27
  38.4 6.9 %collective-permute-start.6 = (bf16[2,6,64,128]{3,2,1,0:T(8,128)(2,1)S(1)}, bf16[2,6,64,128]{3,2,1,0:T(8,128)(2,1)S(1)}, u32[]{:S(2)}, u32[]{:S(2)}) collective-permute-start(bf16[2,6,64,128]{3,2,1,0:T(8,128)(2,1)S(1)} %get-tuple-element.26), channel_id=1, source_target_pairs={{0,1},{1,0},{2,3},{3,2},{4,5},{5,4},{6,7},{7,6},{8,9},{9,8},{10,11... | collective-permute-start | bytes 589832 | tf_op jit(solution)/shard_map/ppermute | solution.py:27
  45.3 18.8 %collective-permute-start.12 = (bf16[4,2,6,64,128]{4,3,2,1,0:T(8,128)(2,1)S(1)}, bf16[4,2,6,64,128]{4,3,2,1,0:T(8,128)(2,1)S(1)}, u32[]{:S(2)}, u32[]{:S(2)}) collective-permute-start(bf16[4,2,6,64,128]{4,3,2,1,0:T(8,128)(2,1)S(1)} %get-tuple-element.29), channel_id=1, source_target_pairs={{0,1},{1,0},{2,3},{3,2},{4,5},{5,4},{6,7},{7,6},{8,9},{9,8},{10,11... | collective-permute-start | bytes 2359304 | tf_op jit(solution)/shard_map/ppermute | solution.py:27
  47.1 9.0 %collective-permute-start.9 = (bf16[2,2,6,64,128]{4,3,2,1,0:T(8,128)(2,1)S(1)}, bf16[2,2,6,64,128]{4,3,2,1,0:T(8,128)(2,1)S(1)}, u32[]{:S(2)}, u32[]{:S(2)}) collective-permute-start(bf16[2,2,6,64,128]{4,3,2,1,0:T(8,128)(2,1)S(1)} %pad_maximum_fusion), channel_id=1, source_target_pairs={{2,4},{3,5},{4,2},{5,3},{10,12},{11,13},{12,10},{13,11},{18,20},{1... | collective-permute-start | bytes 1179656 | tf_op jit(solution)/shard_map/ppermute | solution.py:32
  47.8 18.3 %collective-permute-start.11 = (bf16[2,2,6,64,128]{4,3,2,1,0:T(8,128)(2,1)S(1)}, bf16[2,2,6,64,128]{4,3,2,1,0:T(8,128)(2,1)S(1)}, u32[]{:S(2)}, u32[]{:S(2)}) collective-permute-start(bf16[2,2,6,64,128]{4,3,2,1,0:T(8,128)(2,1)S(1)} %pad_maximum_fusion), channel_id=1, source_target_pairs={{0,6},{1,7},{6,0},{7,1},{8,14},{9,15},{14,8},{15,9},{16,22},{17,23... | collective-permute-start | bytes 1179656 | tf_op jit(solution)/shard_map/ppermute | solution.py:32
  53.3 18.0 %collective-permute-start.7 = (bf16[2,2,6,64,128]{4,3,2,1,0:T(8,128)(2,1)S(1)}, bf16[2,2,6,64,128]{4,3,2,1,0:T(8,128)(2,1)S(1)}, u32[]{:S(2)}, u32[]{:S(2)}) collective-permute-start(bf16[2,2,6,64,128]{4,3,2,1,0:T(8,128)(2,1)S(1)} %pad_maximum_fusion), channel_id=1, source_target_pairs={{0,2},{1,3},{2,0},{3,1},{4,6},{5,7},{6,4},{7,5},{8,10},{9,11},{10,... | collective-permute-start | bytes 1179656 | tf_op jit(solution)/shard_map/ppermute | solution.py:32
  53.4 24.4 %collective-permute-start.8 = (bf16[2,2,6,64,128]{4,3,2,1,0:T(8,128)(2,1)S(1)}, bf16[2,2,6,64,128]{4,3,2,1,0:T(8,128)(2,1)S(1)}, u32[]{:S(2)}, u32[]{:S(2)}) collective-permute-start(bf16[2,2,6,64,128]{4,3,2,1,0:T(8,128)(2,1)S(1)} %pad_maximum_fusion), channel_id=1, source_target_pairs={{0,4},{1,5},{6,2},{7,3},{8,12},{9,13},{14,10},{15,11},{16,20},{17,... | collective-permute-start | bytes 1179656 | tf_op jit(solution)/shard_map/ppermute | solution.py:32
  56.1 22.5 %collective-permute-start.10 = (bf16[2,2,6,64,128]{4,3,2,1,0:T(8,128)(2,1)S(1)}, bf16[2,2,6,64,128]{4,3,2,1,0:T(8,128)(2,1)S(1)}, u32[]{:S(2)}, u32[]{:S(2)}) collective-permute-start(bf16[2,2,6,64,128]{4,3,2,1,0:T(8,128)(2,1)S(1)} %collective-permute-done.9.refs_4_), channel_id=1, source_target_pairs={{2,0},{3,1},{4,6},{5,7},{10,8},{11,9},{12,14},{13,15},{18,16},{19,... | collective-permute-start | bytes 1179656 | tf_op jit(solution)/shard_map/ppermute | solution.py:32
  64.1 14.5 %copy-start.1 = (s32[4]{0:T(128)S(1)}, s32[4]{0:T(128)}, u32[]{:S(2)}) copy-start(s32[4]{0:T(128)} %times_ref.1) | copy-start | bytes 52
  82.2 1.3 %collective-permute-start.13 = (f32[2,4,12,12]{3,2,1,0:T(8,128)S(1)}, f32[2,4,12,12]{3,2,1,0:T(8,128)S(1)}, u32[]{:S(2)}, u32[]{:S(2)}) collective-permute-start(f32[2,4,12,12]{3,2,1,0:T(8,128)S(1)} %traces.1), channel_id=1, source_target_pairs={{0,8},{8,0},{16,24},{24,16},{1,9},{9,1},{17,25},{25,17},{2,10},{10... | collective-permute-start | bytes 13832 | tf_op jit(solution)/shard_map/ppermute | solution.py:27
  83.6 4.0 %collective-permute-start.14 = (f32[4,12,12]{2,1,0:T(8,128)S(1)}, f32[4,12,12]{2,1,0:T(8,128)S(1)}, u32[]{:S(2)}, u32[]{:S(2)}) collective-permute-start(f32[4,12,12]{2,1,0:T(8,128)S(1)} %get-tuple-element.33), channel_id=1, source_target_pairs={{0,16},{8,24},{16,0},{24,8},{1,17},{9,25},{17,1},{25,9},{2,18},{10... | collective-permute-start | bytes 6920 | tf_op jit(solution)/shard_map/ppermute | solution.py:27
  85.1 3.9 %collective-permute-start.15 = (f32[4,12,12]{2,1,0:T(8,128)S(1)}, f32[4,12,12]{2,1,0:T(8,128)S(1)}, u32[]{:S(2)}, u32[]{:S(2)}) collective-permute-start(f32[4,12,12]{2,1,0:T(8,128)S(1)} %get-tuple-element.32), channel_id=1, source_target_pairs={{0,1},{1,0},{2,3},{3,2},{4,5},{5,4},{6,7},{7,6},{8,9},{9,8},{10,11... | collective-permute-start | bytes 6920 | tf_op jit(solution)/shard_map/ppermute | solution.py:27
  85.7 4.8 %collective-permute-start.16 = (f32[4,12,12]{2,1,0:T(8,128)S(1)}, f32[4,12,12]{2,1,0:T(8,128)S(1)}, u32[]{:S(2)}, u32[]{:S(2)}) collective-permute-start(f32[4,12,12]{2,1,0:T(8,128)S(1)} %get-tuple-element.32), channel_id=1, source_target_pairs={{0,17},{1,16},{2,19},{3,18},{4,21},{5,20},{6,23},{7,22},{8,25},{9,... | collective-permute-start | bytes 6920 | tf_op jit(solution)/shard_map/ppermute | solution.py:506

commit v3 on v2

--- a/solution.py
+++ b/solution.py
@@ -15,6 +15,7 @@
 F32 = jnp.float32
 BF16 = jnp.bfloat16
 CHUNK = 32
+FOLD = 8
 MEGA = 1024 * 1024
 
 ANY = pl.BlockSpec(memory_space=pl.ANY)
@@ -32,7 +33,7 @@
     return lax.ppermute(block, "tm", route)
 
 
-def share_line(keep, received, line):
+def share_line(keep, received, g_send, line):
     piece = jnp.stack([keep, received])
     if line != 4:
         arrays, table = [keep, received], {0: (0, None), 1: (1, None)}
@@ -41,17 +42,19 @@
             for side in range(2):
                 table[2 * distance + side] = (len(arrays), side)
             arrays.append(moved)
-        return arrays, table
-    between = along_line(piece, {1: 2, 2: 1})
-    far = along_line(piece, {0: 3, 3: 0})
+        return arrays, table, g_send
+    outward = {1: 0, 2: 3}
+    received, g_send = lax.optimization_barrier((received, g_send))
+    piece = jnp.stack([keep, received])
+    opposite = along_line(piece, {1: 2, 2: 1, 0: 3, 3: 0})
     skip = along_line(piece, {0: 2, 3: 1})
     near = along_line(piece, {0: 1, 1: 0, 2: 3, 3: 2})
-    passed = along_line(between, {1: 0, 2: 3})
-    arrays = [keep, received, near, skip, between, passed, far]
+    passed = along_line(opposite, outward)
+    arrays = [keep, received, near, skip, opposite, passed]
     table = {0: (0, None), 1: (1, None)}
-    for code in range(2, 12):
+    for code in range(2, 10):
         table[code] = (1 + code // 2, code % 2)
-    return arrays, table
+    return arrays, table, g_send
 
 
 def line_code(here, there, side, line):
@@ -59,7 +62,7 @@
         return 2 * lax.rem(here - there + line, line) + side
     apart = here ^ there
     ends = (here == 0) | (here == line - 1)
-    return 2 * jnp.where(ends & (apart >= 2), apart + 2, apart) + side
+    return 2 * jnp.where(ends & (apart == 2), 4, apart) + side
 
 
 def swap_far(block):
@@ -83,7 +86,7 @@
     return pltpu.CompilerParams(vmem_limit_bytes=megabytes * MEGA)
 
 
-def elemental_kernel(held, near, late, *refs):
+def elemental_kernel(held, near, late, block_rows, *refs):
     move_ref, zphase_ref, phase_ref = refs[:3]
     slab_refs = refs[3 : 3 + held]
     rest = refs[3 + held :]
@@ -91,10 +94,12 @@
         prior_ref, acc_out, keep_ref, send_ref, slabs, turned, mixed, table, acc, before, sems = rest
     else:
         acc, slabs, turned, mixed, table, sems = rest
-    operators, _, vectors = acc.shape
+    operators, half_rows, vectors = acc.shape
+    half_rows //= 2
     colours = turned.shape[0]
     count = lax.axis_size("space")
     me = lax.axis_index("space")
+    core = lax.rem(me, 2)
 
     def arriving(m):
         return (
@@ -108,7 +113,8 @@
             ),
         )
 
-    for m in reversed(range(held)):
+    order = list(range(near, held)) + list(range(min(near, held)))
+    for m in order:
         for copy in arriving(m):
             copy.start()
     if late:
@@ -120,40 +126,32 @@
         for part in range(2):
             at = 2 * o + part
             table[o, part] = jnp.broadcast_to(upright[:, at : at + 1], (PLANE, LANES))
-    for m in range(held):
-        for copy in arriving(m):
-            copy.wait()
-
-    def one_slab(m, carry):
+    first_slab = order[0]
+    for copy in arriving(first_slab):
+        copy.wait()
+
+    def one_slab(step, carry):
+        m = lax.rem(step + first_slab, held)
         here = me ^ m
         above = lax.rem(here + 1, count) ^ me
         far = above >= near
 
-        @pl.when((m >= near) | far if late else m >= 0)
-        def _():
-            for colour in range(colours):
-                for part in range(2):
-                    block = slabs[m, part, colour, pl.ds(0, PLANE), :]
-                    flat = block.T
-                    same = flat if part == 0 else -flat
-                    turned[colour, pl.ds(0, vectors), pl.ds(part * PLANE, PLANE)] = flat
-                    turned[colour, pl.ds(vectors, vectors), pl.ds((1 - part) * PLANE, PLANE)] = same
-                    for begin in range(0, PLANE, CHUNK):
-                        rows = slabs[m, part, colour, pl.ds(begin, CHUNK), :].astype(F32)
-                        rows = pltpu.roll(rows.reshape(CHUNK // LX, LX, vectors), LX - 1, 1)
-                        slabs[held, part, colour, pl.ds(begin, CHUNK), :] = rows.reshape(
-                            CHUNK, vectors
-                        ).astype(BF16)
-
-            def one_operator(o, inner):
-                move = move_ref[o]
-                waits = (m >= near) | ((move == 3) & far)
-
-                @pl.when(waits if late else jnp.logical_not(waits))
-                def _():
-                    src = jnp.where(move == 3, above, jnp.where(move == 1, held, m))
-                    off = pl.multiple_of(jnp.where(move == 2, LX, 0), LX)
-                    cos_z, sin_z = zphase_ref[0, here, o], zphase_ref[1, here, o]
+        def wait_others():
+            for other in order[1:]:
+                for copy in arriving(other):
+                    copy.wait()
+
+        def one_operator(o, inner):
+            move = move_ref[o]
+            waits = (m >= near) | ((move == 3) & far)
+
+            @pl.when((waits if late else jnp.logical_not(waits)) & ((move == 3) == inner))
+            def _():
+                src = jnp.where(move == 3, above, jnp.where(move == 1, held, m))
+                off = pl.multiple_of(jnp.where(move == 2, LX, 0), LX)
+                cos_z, sin_z = zphase_ref[0, here, o], zphase_ref[1, here, o]
+                total = None
+                for colour in range(colours):
                     for begin in range(0, PLANE, CHUNK):
                         cos_p = table[o, 0, pl.ds(begin, CHUNK), :]
                         sin_p = table[o, 1, pl.ds(begin, CHUNK), :]
@@ -161,38 +159,59 @@
                         sine = sin_p * cos_z + cos_p * sin_z
                         cosine = jnp.concatenate([cosine] * (vectors // LANES), axis=1)
                         sine = jnp.concatenate([sine] * (vectors // LANES), axis=1)
-                        for colour in range(colours):
-                            real = slabs[src, 0, colour, pl.ds(off + begin, CHUNK), :].astype(F32)
-                            imag = slabs[src, 1, colour, pl.ds(off + begin, CHUNK), :].astype(F32)
-                            mixed[colour, pl.ds(begin, CHUNK), :] = (
-                                cosine * real + sine * imag
-                            ).astype(BF16)
-                            mixed[colour, pl.ds(PLANE + begin, CHUNK), :] = (
-                                cosine * imag - sine * real
-                            ).astype(BF16)
-                    total = None
-                    for colour in range(colours):
-                        term = jnp.dot(turned[colour], mixed[colour], preferred_element_type=F32)
-                        total = term if total is None else total + term
-                    acc[o] += total
-
-                return inner
-
-            lax.fori_loop(0, operators, one_operator, 0)
+                        real = slabs[src, 0, colour, pl.ds(off + begin, CHUNK), :].astype(F32)
+                        imag = slabs[src, 1, colour, pl.ds(off + begin, CHUNK), :].astype(F32)
+                        mixed[colour, pl.ds(begin, CHUNK), :] = (
+                            cosine * real + sine * imag
+                        ).astype(BF16)
+                        mixed[colour, pl.ds(PLANE + begin, CHUNK), :] = (
+                            cosine * imag - sine * real
+                        ).astype(BF16)
+                    term = jnp.dot(turned[colour], mixed[colour], preferred_element_type=F32)
+                    total = term if total is None else total + term
+                acc[o] += total
+
+            return inner
+
+        @pl.when((m >= near) | far if late else m >= 0)
+        def _():
+            for colour in range(colours):
+                for part in range(2):
+                    block = slabs[m, part, colour, pl.ds(0, PLANE), :]
+                    flat = block.T.reshape(half_rows // block_rows, 2, block_rows, PLANE)
+                    flat = jnp.where(core == 0, flat[:, 0], flat[:, 1]).reshape(half_rows, PLANE)
+                    same = flat if part == 0 else -flat
+                    lower = pl.ds(half_rows, half_rows)
+                    turned[colour, pl.ds(0, half_rows), pl.ds(part * PLANE, PLANE)] = flat
+                    turned[colour, lower, pl.ds((1 - part) * PLANE, PLANE)] = same
+                    for begin in range(0, PLANE, CHUNK):
+                        rows = slabs[m, part, colour, pl.ds(begin, CHUNK), :].astype(F32)
+                        rows = pltpu.roll(rows.reshape(CHUNK // LX, LX, vectors), LX - 1, 1)
+                        slabs[held, part, colour, pl.ds(begin, CHUNK), :] = rows.reshape(
+                            CHUNK, vectors
+                        ).astype(BF16)
+            lax.fori_loop(0, operators, one_operator, False)
+
+        @pl.when(step == 0)
+        def _():
+            wait_others()
+
+        @pl.when((m >= near) | far if late else m >= 0)
+        def _():
+            lax.fori_loop(0, operators, one_operator, True)
 
         return carry
 
     lax.fori_loop(0, held, one_slab, 0)
 
     if late:
-        block_rows = keep_ref.shape[2]
-        first = pl.multiple_of(me * block_rows, block_rows)
+        first = pl.multiple_of(me // 2 * block_rows, block_rows)
         half = lax.rem(lax.axis_index("tm"), 2)
         prior.wait()
         for o in range(operators):
             acc_out[o] = (acc[o] + before[o]).astype(BF16)
             for part in range(2):
-                rows = pl.ds(part * vectors + first, block_rows)
+                rows = pl.ds(part * half_rows + first, block_rows)
                 own = (acc[o, rows, :] + before[o, rows, :]).astype(BF16)
                 low, high = own[:, :LANES], own[:, LANES:]
                 keep_ref[part, o] = jnp.where(half == 0, low, high)
@@ -204,10 +223,10 @@
     held = len(slab_list)
     operators = tables[0].shape[0]
     late = prior is not None
-    wide = jax.ShapeDtypeStruct((operators, 2 * vectors, vectors), F32)
+    wide = jax.ShapeDtypeStruct((operators, vectors, vectors), F32)
     scratch = [
         pltpu.VMEM((held + 1, 2, colours, plane + LX, vectors), BF16),
-        pltpu.VMEM((colours, 2 * vectors, 2 * plane), BF16),
+        pltpu.VMEM((colours, vectors, 2 * plane), BF16),
         pltpu.VMEM((colours, 2 * plane, vectors), BF16),
         pltpu.VMEM((operators, 2, plane, LANES), F32),
     ]
@@ -220,7 +239,7 @@
         outs, out_specs = wide, VMEM
     priors = [prior] if late else []
     return pl.pallas_call(
-        functools.partial(elemental_kernel, held, near, late),
+        functools.partial(elemental_kernel, held, near, late, block_rows),
         out_shape=outs,
         in_specs=[SMEM, SMEM, VMEM] + [ANY] * (held + len(priors)),
         out_specs=out_specs,
@@ -235,9 +254,9 @@
     )(*tables, *slab_list, *priors)
 
 
-def both_kernel(blocks, e_ref, *refs):
+def both_kernel(blocks, e_ref, other_ref, *refs):
     peram_refs = refs[:blocks]
-    keep_ref, send_ref, whole, left, middle, sems = refs[blocks:]
+    keep_ref, send_ref, whole, sorted_rows, left, middle, sems = refs[blocks:]
     sources, _, vectors, _ = whole.shape
     operators = e_ref.shape[0]
     block_rows = keep_ref.shape[3]
@@ -248,7 +267,14 @@
         begin = pl.multiple_of((me ^ m) * block_rows, block_rows)
         copies.append(
             pltpu.make_async_copy(
-                peram_refs[m], whole.at[:, :, pl.ds(begin, block_rows), :], sems.at[m]
+                peram_refs[m], whole.at[:, :, pl.ds(begin, block_rows), :], sems.at[2 * m]
+            )
+        )
+        begin = (m % 2) * (vectors // 2) + (me ^ m) // 2 * block_rows
+        begin = pl.multiple_of(begin, block_rows)
+        copies.append(
+            pltpu.make_async_copy(
+                peram_refs[m], sorted_rows.at[:, :, pl.ds(begin, block_rows), :], sems.at[2 * m + 1]
             )
         )
     for copy in copies:
@@ -265,12 +291,22 @@
             )
             left[pl.ds((part * sources + s) * block_rows, block_rows), :] = flat.astype(BF16)
     group = sources * block_rows
+    cut = vectors // 2
     for a in range(operators):
-        product = lax.dot_general(
-            left[...], e_ref[a], (((1,), (1,)), ((), ())), preferred_element_type=F32
-        )
-        real = product[:group, :vectors] - product[group:, vectors:]
-        imaginary = product[:group, vectors:] + product[group:, :vectors]
+        sides = []
+        for ref in (e_ref, other_ref):
+            product = lax.dot_general(
+                left[...], ref[a], (((1,), (1,)), ((), ())), preferred_element_type=F32
+            )
+            sides.append(
+                (
+                    product[:group, :cut] - product[group:, cut:],
+                    product[:group, cut:] + product[group:, :cut],
+                )
+            )
+        real, imaginary = (
+            jnp.concatenate([one, two], axis=1) for one, two in zip(*sides)
+        )
         for part, block in enumerate((real, imaginary)):
             high = block.astype(BF16)
             low = (block - high.astype(F32)).astype(BF16)
@@ -281,7 +317,7 @@
                 middle[0, s, rows, columns] = high[base : base + block_rows]
                 middle[1, s, rows, columns] = low[base : base + block_rows]
     for s in range(sources):
-        real, imaginary = whole[s, 0], whole[s, 1]
+        real, imaginary = sorted_rows[s, 0], sorted_rows[s, 1]
         right = jnp.concatenate(
             [
                 jnp.concatenate([real, -imaginary], axis=1),
@@ -301,7 +337,7 @@
                 send_ref[s, part, a] = jnp.where(half == 0, high, low)
 
 
-def both_sides(elements, perams):
+def both_sides(elements, others, perams):
     blocks = len(perams)
     sources, _, block_rows, vectors = perams[0].shape
     operators = elements.shape[0]
@@ -309,23 +345,25 @@
     return pl.pallas_call(
         functools.partial(both_kernel, blocks),
         out_shape=(piece, piece),
-        in_specs=[VMEM] + [ANY] * blocks,
+        in_specs=[VMEM, VMEM] + [ANY] * blocks,
         out_specs=(VMEM, VMEM),
         scratch_shapes=[
             pltpu.VMEM((sources, 2, vectors, vectors), BF16),
+            pltpu.VMEM((sources, 2, vectors, vectors), BF16),
             pltpu.VMEM((2 * sources * block_rows, vectors), BF16),
             pltpu.VMEM((2, sources, operators * block_rows, 2 * vectors), BF16),
-            pltpu.SemaphoreType.DMA((blocks,)),
+            pltpu.SemaphoreType.DMA((2 * blocks,)),
         ],
         compiler_params=params(16),
         cost_estimate=pl.CostEstimate(flops=0, bytes_accessed=0, transcendentals=0),
         name="both_sides",
-    )(elements, *perams)
+    )(elements, others, *perams)
 
 
 def spread(wide, count_rows, block_rows):
     pieces = [
-        wide[pl.ds(k, count_rows, stride=block_rows), :].astype(BF16) for k in range(block_rows)
+        wide[pl.ds(k, count_rows * block_rows // FOLD, stride=FOLD), :].astype(BF16)
+        for k in range(FOLD)
     ]
     return jnp.concatenate(pieces, axis=1)
 
@@ -346,7 +384,9 @@
     rows = 2 * operators
     return pl.pallas_call(
         lay_kernel,
-        out_shape=jax.ShapeDtypeStruct((sources, 2 * rows, block_rows * lanes), BF16),
+        out_shape=jax.ShapeDtypeStruct(
+            (sources, 2 * rows * block_rows // FOLD, FOLD * lanes), BF16
+        ),
         in_specs=[VMEM, VMEM],
         out_specs=VMEM,
         scratch_shapes=[pltpu.VMEM((2 * rows * block_rows, lanes), F32)],
@@ -373,17 +413,37 @@
                 block = pools[at] if inside is None else pools[at].at[inside]
                 pltpu.make_async_copy(block, picked.at[s], sems.at[s]).start()
 
+    groups = block_rows // FOLD
+    shape = (2 * rows * groups, rows * groups)
+    down = lax.broadcasted_iota(jnp.int32, shape, 0)
+    over = lax.broadcasted_iota(jnp.int32, shape, 1)
+    same = down % groups == over % groups
+    shape = (rows * groups, rows)
+    down = lax.broadcasted_iota(jnp.int32, shape, 0)
+    over = lax.broadcasted_iota(jnp.int32, shape, 1)
+    gather = (down // groups == over).astype(F32)
     for s in range(sources):
         pltpu.make_async_copy(pools[0], picked.at[s], sems.at[s]).wait()
-        wide[...] = picked[s].astype(F32).reshape(rows * block_rows, lanes)
+        wide[s] = picked[s].astype(F32).reshape(rows * block_rows, lanes)
+    sums = []
+    for s in range(sources):
         product = lax.dot_general(
             laid_ref[s],
-            spread(wide, rows, block_rows),
+            spread(wide.at[s], rows, block_rows),
             (((1,), (1,)), ((), ())),
             preferred_element_type=F32,
         )
-        out_ref[0, s] = product[:rows]
-        out_ref[1, s] = product[rows:]
+        product = jnp.where(same, product, 0.0).reshape(2 * rows, groups, rows * groups)
+        sums.append(jnp.sum(product, axis=1))
+    folded = jnp.dot(
+        jnp.concatenate(sums, axis=0),
+        gather,
+        precision=lax.Precision.HIGHEST,
+        preferred_element_type=F32,
+    )
+    for s in range(sources):
+        out_ref[0, s] = folded[2 * rows * s : 2 * rows * s + rows]
+        out_ref[1, s] = folded[2 * rows * s + rows : 2 * rows * (s + 1)]
 
 
 def traces(source_times, pools, table, line, laid):
@@ -397,7 +457,7 @@
         out_specs=VMEM,
         scratch_shapes=[
             pltpu.VMEM((sources,) + pools[0].shape, BF16),
-            pltpu.VMEM((rows * block_rows, lanes), F32),
+            pltpu.VMEM((sources, rows * block_rows, lanes), F32),
             pltpu.SemaphoreType.DMA((sources,)),
         ],
         compiler_params=params(12),
@@ -482,12 +542,12 @@
     perams = swap_far(peram)
     full, keep, send = elementals(tables, slab_list, near, total, block_rows)
 
-    perams = swap_near(lax.optimization_barrier((perams, full))[0])
+    perams, full, send = lax.optimization_barrier((perams, full, send))
+    perams = swap_near(perams)
 
     received = swap_bit(send, "tm", 1)
-    g_keep, g_send = both_sides(full, perams)
-    g_send, received = lax.optimization_barrier((g_send, received))
-    arrays, table = share_line(keep, received, line)
+    g_keep, g_send = both_sides(full, swap_bit(full, "space", 1), perams)
+    arrays, table, g_send = share_line(keep, received, g_send, line)
     laid = lay_out(g_keep, swap_bit(g_send, "tm", 1))
     both = traces(source_times, arrays, table, line, laid)
     both = both + swap_bit(both, "space", 1)

time: 91.3 us -> 87.9 us (0.963)
  Pallas kernels: 32.4 us -> 27.3 us
  waiting for transfers between devices: 32.3 us -> 36.7 us
  starting transfers between devices: 22.8 us -> 20.3 us
    ppermute x5 -> x4, waiting for transfers between devices: 12.5 us -> 19.7 us  [along_line(): return lax.ppermute(block, 'tm', route)]
    pallas_call x2, Pallas kernels: 22.8 us -> 19.8 us  [elementals(): pl.pallas_call(functools.partial(elemental_kernel, held, near, late, bloc...]
    ppermute x11 -> x12, waiting for transfers between devices: 18.4 us -> 15.6 us  [swap_bit(): return lax.ppermute(block, axis, [(i, i ^ mask) for i in range(count)])]
    ppermute x5 -> x4, starting transfers between devices: 10.2 us -> 7.65 us  [along_line(): return lax.ppermute(block, 'tm', route)]
    pallas_call x1, Pallas kernels: 1.99 us -> 0.67 us  [lay_out(): pl.pallas_call(lay_kernel, out_shape=jax.ShapeDtypeStruct((sources, 2 * r...]
    ppermute x11 -> x12, starting transfers between devices: 11.1 us -> 11.2 us  [swap_bit(): return lax.ppermute(block, axis, [(i, i ^ mask) for i in range(count)])]
  transfers between devices with their start and end apart: 17 -> 17, of which waited for: 11 -> 14; matrix products, arithmetic and copies ran while one was open for 1% -> 1% of each run, Pallas kernels for 30% -> 27%
where the time goes in v3:
time: 87.9 us; the launch traced here: 88.2 us
  waiting for transfers between devices  36.7 us (42%)
  Pallas kernels  27.3 us (31%)
  starting transfers between devices  20.3 us (23%)
  local copies, waits for them, and re-layouts  2.66 us (3%)
    pallas_call x2, Pallas kernels, elementals(): pl.pallas_call(functools.partial(elemental_kernel, held, near, late, bloc...  19.8 us
    ppermute x4, waiting for transfers between devices, along_line(): return lax.ppermute(block, 'tm', route)  19.7 us
    ppermute x12, waiting for transfers between devices, swap_bit(): return lax.ppermute(block, axis, [(i, i ^ mask) for i in range(count)])  15.6 us
    ppermute x12, starting transfers between devices, swap_bit(): return lax.ppermute(block, axis, [(i, i ^ mask) for i in range(count)])  11.2 us
    ppermute x4, starting transfers between devices, along_line(): return lax.ppermute(block, 'tm', route)  7.65 us
    pallas_call x1, Pallas kernels, both_sides(): pl.pallas_call(functools.partial(both_kernel, blocks), out_shape=(piece,...  3.2 us
    pallas_call x1, Pallas kernels, traces(): pl.pallas_call(functools.partial(trace_kernel, len(pools), table, line),...  2.8 us
    unnamed x12, local copies, waits for them, and re-layouts  1.84 us
  transfers between devices with their start and end apart: 17, of which 14 were waited for; matrix products, arithmetic and copies ran while one was open for 1% of the time, Pallas kernels for 27%

profile of v3, /device:TPU:0, one launch (start us, length us, event | category | flops | bytes accessed | tf_op | source)
XLA Modules:
  0.0 88.2 jit_solution(6174605784777649497)
XLA Ops:
  0.6 0.5 collective-permute-start.1
  1.1 2.6 %collective-permute-start = (bf16[2,3,256,256]{3,2,1,0:T(8,128)(2,1)}, bf16[2,3,256,256]{3,2,1,0:T(8,128)(2,1)S(1)}, u32[]{:S(2)}, u32[]{:S(2)}) collective-permute-start(bf16[2,3,256,256]{3,2,1,0:T(8,128)(2,1)} %bitcast.22), channel_id=1, source_target_pairs={{0,16},{8,24},{16,0},{24,8},{1,17},{9,25},{17,1},{25,9},{2,18},{10... | collective-permute-start | bytes 2359304 | tf_op jit(solution)/shard_map/ppermute | solution.py:28
  3.7 0.8 slice_bitcast_fusion.3
  4.5 0.3 fusion.13
  4.9 0.1 fusion.11
  5.0 0.0 copy-start
  5.0 0.0 collective-permute-done.1.refs_4_
  5.0 0.0 copy-start.2
  5.0 1.2 %copy-done.2 = bf16[1,2,3,1,256,256]{5,4,3,2,1,0:T(8,128)(2,1)S(1)} copy-done((bf16[1,2,3,1,256,256]{5,4,3,2,1,0:T(8,128)(2,1)S(1)}, bf16[1,2,3,1,256,256]{5,4,3,2,1,0:T(8,128)(2,1)}, u32[]{:S(2)}) %copy-start.2) | copy-done | bytes 786456
  6.2 0.7 copy-done.4
  6.8 7.6 %elementals_early.1.refs_7_ = f32[6,256,256]{2,1,0:T(8,128)S(1)} custom-call(s32[6]{0:T(128)S(1)} %copy-done.4, f32[2,4,6]{2,1,0:T(4,128)S(1)} %pad_maximum_fusion.2.refs_1_, f32[12,256]{1,0:T(8,128)S(1)} %reshape.399.refs_2_, bf16[2,3,256,256]{3,2,1,0:T(8,128)(2,1)S(1)} %bitcast.23, bf16[2,3,256,256]{3,2,1,0:T(8,128)(2,1)S(1)} %collective-permute-done.1.refs_4_), custom_call_target="tpu_custom_call" | custom-call | flops 4831838208 | bytes 1572864 | tf_op jit(solution)/shard_map/elementals_early/pallas_call | solution.py:241
  14.4 7.7 %collective-permute-done.refs_5_ = bf16[2,3,256,256]{3,2,1,0:T(8,128)(2,1)S(1)} collective-permute-done((bf16[2,3,256,256]{3,2,1,0:T(8,128)(2,1)}, bf16[2,3,256,256]{3,2,1,0:T(8,128)(2,1)S(1)}, u32[]{:S(2)}, u32[]{:S(2)}) %collective-permute-start) | collective-permute-done | bytes 786464 | tf_op jit(solution)/shard_map/ppermute | solution.py:28
  22.1 0.0 collective-permute-start.2
  22.1 1.8 %collective-permute-start.3 = (bf16[4,2,64,256]{3,2,1,0:T(8,128)(2,1)S(1)}, bf16[4,2,64,256]{3,2,1,0:T(8,128)(2,1)S(1)}, u32[]{:S(2)}, u32[]{:S(2)}) collective-permute-start(bf16[4,2,64,256]{3,2,1,0:T(8,128)(2,1)S(1)} %bitcast.18), channel_id=1, source_target_pairs={{0,16},{8,24},{16,0},{24,8},{1,17},{9,25},{17,1},{25,9},{2,18},{10... | collective-permute-start | bytes 786440 | tf_op jit(solution)/shard_map/ppermute | solution.py:28
  23.9 0.5 collective-permute-done.2.refs_6_
  24.4 0.0 copy-done.5
  24.4 12.2 %elementals_late.1 = (bf16[6,256,256]{2,1,0:T(8,128)(2,1)S(1)}, bf16[2,6,64,128]{3,2,1,0:T(8,128)(2,1)S(1)}, bf16[2,6,64,128]{3,2,1,0:T(8,128)(2,1)S(1)}) custom-call(s32[6]{0:T(128)S(1)} %copy-done.5, f32[2,4,6]{2,1,0:T(4,128)S(1)} %pad_maximum_fusion.2.refs_1_, f32[12,256]{1,0:T(8,128)S(1)} %reshape.399.refs_2_, bf16[2,3,256,256]{3,2,1,0:T(8,128)(2,1)S(1)} %bitcast.24, ...), custom_call_target="tpu_custom_call" | custom-call | flops 9663676416 | bytes 3145728 | tf_op jit(solution)/shard_map/elementals_late/pallas_call | solution.py:241
  36.6 0.0 collective-permute-done.3.refs_2_
  36.6 0.2 collective-permute-start.5
  36.8 0.4 collective-permute-start.6
  37.1 0.1 collective-permute-start.7
  37.3 1.7 %collective-permute-start.4 = (bf16[2,6,64,128]{3,2,1,0:T(8,128)(2,1)S(1)}, bf16[2,6,64,128]{3,2,1,0:T(8,128)(2,1)S(1)}, u32[]{:S(2)}, u32[]{:S(2)}) collective-permute-start(bf16[2,6,64,128]{3,2,1,0:T(8,128)(2,1)S(1)} %get-tuple-element.26), channel_id=1, source_target_pairs={{0,1},{1,0},{2,3},{3,2},{4,5},{5,4},{6,7},{7,6},{8,9},{9,8},{10,11... | collective-permute-start | bytes 589832 | tf_op jit(solution)/shard_map/ppermute | solution.py:28
  39.0 0.3 collective-permute-done.6.refs_1_
  39.3 0.4 collective-permute-done.7.refs_3_
  39.7 0.0 collective-permute-done.5.other_ref
  39.7 3.2 %both_sides.1 = (bf16[4,2,6,64,128]{4,3,2,1,0:T(8,128)(2,1)S(1)}, bf16[4,2,6,64,128]{4,3,2,1,0:T(8,128)(2,1)S(1)}) custom-call(bf16[6,256,256]{2,1,0:T(8,128)(2,1)S(1)} %get-tuple-element.27.e_ref, bf16[6,256,256]{2,1,0:T(8,128)(2,1)S(1)} %collective-permute-done.5.other_ref, bf16[4,2,64,256]{3,2,1,0:T(8,128)(2,1)S(1)} %bitcast.20, ...), custom_call_target="tpu_custom_call" | custom-call | tf_op jit(solution)/shard_map/both_sides/pallas_call | solution.py:345
  42.9 1.6 %collective-permute-done.4.refs_1_ = bf16[2,6,64,128]{3,2,1,0:T(8,128)(2,1)S(1)} collective-permute-done((bf16[2,6,64,128]{3,2,1,0:T(8,128)(2,1)S(1)}, bf16[2,6,64,128]{3,2,1,0:T(8,128)(2,1)S(1)}, u32[]{:S(2)}, u32[]{:S(2)}) %collective-permute-start.4) | collective-permute-done | bytes 196640 | tf_op jit(solution)/shard_map/ppermute | solution.py:28
  44.5 1.7 %collective-permute-start.12 = (bf16[4,2,6,64,128]{4,3,2,1,0:T(8,128)(2,1)S(1)}, bf16[4,2,6,64,128]{4,3,2,1,0:T(8,128)(2,1)S(1)}, u32[]{:S(2)}, u32[]{:S(2)}) collective-permute-start(bf16[4,2,6,64,128]{4,3,2,1,0:T(8,128)(2,1)S(1)} %get-tuple-element.33), channel_id=1, source_target_pairs={{0,1},{1,0},{2,3},{3,2},{4,5},{5,4},{6,7},{7,6},{8,9},{9,8},{10,11... | collective-permute-start | bytes 2359304 | tf_op jit(solution)/shard_map/ppermute | solution.py:28
  46.2 3.7 %collective-permute-start.10 = (bf16[2,2,6,64,128]{4,3,2,1,0:T(8,128)(2,1)S(1)}, bf16[2,2,6,64,128]{4,3,2,1,0:T(8,128)(2,1)S(1)}, u32[]{:S(2)}, u32[]{:S(2)}) collective-permute-start(bf16[2,2,6,64,128]{4,3,2,1,0:T(8,128)(2,1)S(1)} %pad_maximum_fusion), channel_id=1, source_target_pairs={{2,4},{3,5},{4,2},{5,3},{0,6},{1,7},{6,0},{7,1},{10,12},{11,13},{1... | collective-permute-start | bytes 1179656 | tf_op jit(solution)/shard_map/ppermute | solution.py:33
  49.9 0.0 collective-permute-start.8
  49.9 2.7 %collective-permute-start.9 = (bf16[2,2,6,64,128]{4,3,2,1,0:T(8,128)(2,1)S(1)}, bf16[2,2,6,64,128]{4,3,2,1,0:T(8,128)(2,1)S(1)}, u32[]{:S(2)}, u32[]{:S(2)}) collective-permute-start(bf16[2,2,6,64,128]{4,3,2,1,0:T(8,128)(2,1)S(1)} %pad_maximum_fusion), channel_id=1, source_target_pairs={{0,4},{1,5},{6,2},{7,3},{8,12},{9,13},{14,10},{15,11},{16,20},{17,... | collective-permute-start | bytes 1179656 | tf_op jit(solution)/shard_map/ppermute | solution.py:33
  52.6 7.6 %collective-permute-done.10.refs_4_ = bf16[2,2,6,64,128]{4,3,2,1,0:T(8,128)(2,1)S(1)} collective-permute-done((bf16[2,2,6,64,128]{4,3,2,1,0:T(8,128)(2,1)S(1)}, bf16[2,2,6,64,128]{4,3,2,1,0:T(8,128)(2,1)S(1)}, u32[]{:S(2)}, u32[]{:S(2)}) %collective-permute-start.10) | collective-permute-done | bytes 393248 | tf_op jit(solution)/shard_map/ppermute | solution.py:33
  60.2 1.3 %collective-permute-start.11 = (bf16[2,2,6,64,128]{4,3,2,1,0:T(8,128)(2,1)S(1)}, bf16[2,2,6,64,128]{4,3,2,1,0:T(8,128)(2,1)S(1)}, u32[]{:S(2)}, u32[]{:S(2)}) collective-permute-start(bf16[2,2,6,64,128]{4,3,2,1,0:T(8,128)(2,1)S(1)} %collective-permute-done.10.refs_4_), channel_id=1, source_target_pairs={{2,0},{3,1},{4,6},{5,7},{10,8},{11,9},{12,14},{13,15},{18,16},{19,... | collective-permute-start | bytes 1179656 | tf_op jit(solution)/shard_map/ppermute | solution.py:33
  61.5 2.0 %collective-permute-done.12.pair_ref = bf16[4,2,6,64,128]{4,3,2,1,0:T(8,128)(2,1)S(1)} collective-permute-done((bf16[4,2,6,64,128]{4,3,2,1,0:T(8,128)(2,1)S(1)}, bf16[4,2,6,64,128]{4,3,2,1,0:T(8,128)(2,1)S(1)}, u32[]{:S(2)}, u32[]{:S(2)}) %collective-permute-start.12) | collective-permute-done | bytes 786464 | tf_op jit(solution)/shard_map/ppermute | solution.py:28
  63.5 0.7 lay_out.1.refs_6_
  64.1 3.7 %collective-permute-done.8.refs_2_ = bf16[2,2,6,64,128]{4,3,2,1,0:T(8,128)(2,1)S(1)} collective-permute-done((bf16[2,2,6,64,128]{4,3,2,1,0:T(8,128)(2,1)S(1)}, bf16[2,2,6,64,128]{4,3,2,1,0:T(8,128)(2,1)S(1)}, u32[]{:S(2)}, u32[]{:S(2)}) %collective-permute-start.8) | collective-permute-done | bytes 393248 | tf_op jit(solution)/shard_map/ppermute | solution.py:33
  67.9 6.7 %collective-permute-done.9.refs_3_ = bf16[2,2,6,64,128]{4,3,2,1,0:T(8,128)(2,1)S(1)} collective-permute-done((bf16[2,2,6,64,128]{4,3,2,1,0:T(8,128)(2,1)S(1)}, bf16[2,2,6,64,128]{4,3,2,1,0:T(8,128)(2,1)S(1)}, u32[]{:S(2)}, u32[]{:S(2)}) %collective-permute-start.9) | collective-permute-done | bytes 393248 | tf_op jit(solution)/shard_map/ppermute | solution.py:33
  74.6 1.6 %collective-permute-done.11.refs_5_ = bf16[2,2,6,64,128]{4,3,2,1,0:T(8,128)(2,1)S(1)} collective-permute-done((bf16[2,2,6,64,128]{4,3,2,1,0:T(8,128)(2,1)S(1)}, bf16[2,2,6,64,128]{4,3,2,1,0:T(8,128)(2,1)S(1)}, u32[]{:S(2)}, u32[]{:S(2)}) %collective-permute-start.11) | collective-permute-done | bytes 393248 | tf_op jit(solution)/shard_map/ppermute | solution.py:33
  76.2 2.8 %traces.1 = f32[2,4,12,12]{3,2,1,0:T(8,128)S(1)} custom-call(s32[4]{0:T(128)S(1)} %copy-done.1, bf16[2,6,64,128]{3,2,1,0:T(8,128)(2,1)S(1)} %get-tuple-element.22.refs_0_, bf16[2,6,64,128]{3,2,1,0:T(8,128)(2,1)S(1)} %collective-permute-done.4.refs_1_, bf16[2,2,6,64,128]{4,3,2,1,0:T(8,128)(2,1)S(1)} %collective-permute-done.8.refs_2_, ...), custom_call_target="tpu_custom_call" | custom-call | flops 18874368 | bytes 1572864 | tf_op jit(solution)/shard_map/traces/pallas_call | solution.py:453
  79.0 0.1 collective-permute-start.13
  79.1 1.2 %collective-permute-done.13 = f32[2,4,12,12]{3,2,1,0:T(8,128)S(1)} collective-permute-done((f32[2,4,12,12]{3,2,1,0:T(8,128)S(1)}, f32[2,4,12,12]{3,2,1,0:T(8,128)S(1)}, u32[]{:S(2)}, u32[]{:S(2)}) %collective-permute-start.13) | collective-permute-done | bytes 4640 | tf_op jit(solution)/shard_map/ppermute | solution.py:28
  80.4 1.6 %collective-permute-start.14 = (f32[4,12,12]{2,1,0:T(8,128)S(1)}, f32[4,12,12]{2,1,0:T(8,128)S(1)}, u32[]{:S(2)}, u32[]{:S(2)}) collective-permute-start(f32[4,12,12]{2,1,0:T(8,128)S(1)} %get-tuple-element.37), channel_id=1, source_target_pairs={{0,16},{8,24},{16,0},{24,8},{1,17},{9,25},{17,1},{25,9},{2,18},{10... | collective-permute-start | bytes 6920 | tf_op jit(solution)/shard_map/ppermute | solution.py:28
  82.0 0.5 collective-permute-start.15
  82.5 1.4 %collective-permute-start.16 = (f32[4,12,12]{2,1,0:T(8,128)S(1)}, f32[4,12,12]{2,1,0:T(8,128)S(1)}, u32[]{:S(2)}, u32[]{:S(2)}) collective-permute-start(f32[4,12,12]{2,1,0:T(8,128)S(1)} %get-tuple-element.36), channel_id=1, source_target_pairs={{0,17},{1,16},{2,19},{3,18},{4,21},{5,20},{6,23},{7,22},{8,25},{9,... | collective-permute-start | bytes 6920 | tf_op jit(solution)/shard_map/ppermute | solution.py:566
  83.9 0.4 collective-permute-done.14.refs_1_
  84.4 1.5 %collective-permute-done.15.refs_2_ = f32[4,12,12]{2,1,0:T(8,128)S(1)} collective-permute-done((f32[4,12,12]{2,1,0:T(8,128)S(1)}, f32[4,12,12]{2,1,0:T(8,128)S(1)}, u32[]{:S(2)}, u32[]{:S(2)}) %collective-permute-start.15) | collective-permute-done | bytes 2336 | tf_op jit(solution)/shard_map/ppermute | solution.py:28
  85.9 1.4 %collective-permute-done.16.refs_3_ = f32[4,12,12]{2,1,0:T(8,128)S(1)} collective-permute-done((f32[4,12,12]{2,1,0:T(8,128)S(1)}, f32[4,12,12]{2,1,0:T(8,128)S(1)}, u32[]{:S(2)}, u32[]{:S(2)}) %collective-permute-start.16) | collective-permute-done | bytes 2336 | tf_op jit(solution)/shard_map/ppermute | solution.py:566
  87.3 0.9 finish.1
  (14 shorter events, 0.1 us)
Async XLA Ops:
  0.6 4.3 %collective-permute-start.1 = (bf16[2,3,256,256]{3,2,1,0:T(8,128)(2,1)}, bf16[2,3,256,256]{3,2,1,0:T(8,128)(2,1)S(1)}, u32[]{:S(2)}, u32[]{:S(2)}) collective-permute-start(bf16[2,3,256,256]{3,2,1,0:T(8,128)(2,1)} %bitcast.21), channel_id=1, source_target_pairs={{0,8},{8,0},{16,24},{24,16},{1,9},{9,1},{17,25},{25,17},{2,10},{10... | collective-permute-start | bytes 2359304 | tf_op jit(solution)/shard_map/ppermute | solution.py:28
  1.1 20.9 %collective-permute-start = (bf16[2,3,256,256]{3,2,1,0:T(8,128)(2,1)}, bf16[2,3,256,256]{3,2,1,0:T(8,128)(2,1)S(1)}, u32[]{:S(2)}, u32[]{:S(2)}) collective-permute-start(bf16[2,3,256,256]{3,2,1,0:T(8,128)(2,1)} %bitcast.22), channel_id=1, source_target_pairs={{0,16},{8,24},{16,0},{24,8},{1,17},{9,25},{17,1},{25,9},{2,18},{10... | collective-permute-start | bytes 2359304 | tf_op jit(solution)/shard_map/ppermute | solution.py:28
  5.0 17.1 %copy-start = (bf16[1,4,2,64,256]{4,3,2,1,0:T(8,128)(2,1)S(1)}, bf16[1,4,2,64,256]{4,3,2,1,0:T(8,128)(2,1)}, u32[]{:S(2)}) copy-start(bf16[1,4,2,64,256]{4,3,2,1,0:T(8,128)(2,1)} %param.9) | copy-start | bytes 786436
  5.0 1.2 %copy-start.2 = (bf16[1,2,3,1,256,256]{5,4,3,2,1,0:T(8,128)(2,1)S(1)}, bf16[1,2,3,1,256,256]{5,4,3,2,1,0:T(8,128)(2,1)}, u32[]{:S(2)}) copy-start(bf16[1,2,3,1,256,256]{5,4,3,2,1,0:T(8,128)(2,1)} %param.5) | copy-start | bytes 2359300
  6.2 0.7 copy-start.4
  6.8 17.6 %copy-start.3 = (bf16[1,2,3,1,256,256]{5,4,3,2,1,0:T(8,128)(2,1)S(1)}, bf16[1,2,3,1,256,256]{5,4,3,2,1,0:T(8,128)(2,1)}, u32[]{:S(2)}) copy-start(bf16[1,2,3,1,256,256]{5,4,3,2,1,0:T(8,128)(2,1)} %param.5) | copy-start | bytes 2359300
  6.8 17.6 %copy-start.5 = (s32[6]{0:T(128)S(1)}, s32[6]{0:T(128)}, u32[]{:S(2)}) copy-start(s32[6]{0:T(128)} %refs_0_.3) | copy-start | bytes 76
  22.1 2.3 %collective-permute-start.2 = (bf16[2,3,256,256]{3,2,1,0:T(8,128)(2,1)S(1)}, bf16[2,3,256,256]{3,2,1,0:T(8,128)(2,1)S(1)}, u32[]{:S(2)}, u32[]{:S(2)}) collective-permute-start(bf16[2,3,256,256]{3,2,1,0:T(8,128)(2,1)S(1)} %collective-permute-done.refs_5_), channel_id=1, source_target_pairs={{0,8},{8,0},{16,24},{24,16},{1,9},{9,1},{17,25},{25,17},{2,10},{10... | collective-permute-start | bytes 2359304 | tf_op jit(solution)/shard_map/ppermute | solution.py:28
  22.1 14.5 %collective-permute-start.3 = (bf16[4,2,64,256]{3,2,1,0:T(8,128)(2,1)S(1)}, bf16[4,2,64,256]{3,2,1,0:T(8,128)(2,1)S(1)}, u32[]{:S(2)}, u32[]{:S(2)}) collective-permute-start(bf16[4,2,64,256]{3,2,1,0:T(8,128)(2,1)S(1)} %bitcast.18), channel_id=1, source_target_pairs={{0,16},{8,24},{16,0},{24,8},{1,17},{9,25},{17,1},{25,9},{2,18},{10... | collective-permute-start | bytes 786440 | tf_op jit(solution)/shard_map/ppermute | solution.py:28
  36.6 3.1 %collective-permute-start.5 = (bf16[6,256,256]{2,1,0:T(8,128)(2,1)S(1)}, bf16[6,256,256]{2,1,0:T(8,128)(2,1)S(1)}, u32[]{:S(2)}, u32[]{:S(2)}) collective-permute-start(bf16[6,256,256]{2,1,0:T(8,128)(2,1)S(1)} %get-tuple-element.27.e_ref), channel_id=1, source_target_pairs={{0,8},{8,0},{16,24},{24,16},{1,9},{9,1},{17,25},{25,17},{2,10},{10... | collective-permute-start | bytes 2359304 | tf_op jit(solution)/shard_map/ppermute | solution.py:28
  36.8 2.5 %collective-permute-start.6 = (bf16[4,2,64,256]{3,2,1,0:T(8,128)(2,1)S(1)}, bf16[4,2,64,256]{3,2,1,0:T(8,128)(2,1)S(1)}, u32[]{:S(2)}, u32[]{:S(2)}) collective-permute-start(bf16[4,2,64,256]{3,2,1,0:T(8,128)(2,1)S(1)} %bitcast.19), channel_id=1, source_target_pairs={{0,8},{8,0},{16,24},{24,16},{1,9},{9,1},{17,25},{25,17},{2,10},{10... | collective-permute-start | bytes 786440 | tf_op jit(solution)/shard_map/ppermute | solution.py:28
  37.1 2.5 %collective-permute-start.7 = (bf16[4,2,64,256]{3,2,1,0:T(8,128)(2,1)S(1)}, bf16[4,2,64,256]{3,2,1,0:T(8,128)(2,1)S(1)}, u32[]{:S(2)}, u32[]{:S(2)}) collective-permute-start(bf16[4,2,64,256]{3,2,1,0:T(8,128)(2,1)S(1)} %collective-permute-done.3.refs_2_), channel_id=1, source_target_pairs={{0,8},{8,0},{16,24},{24,16},{1,9},{9,1},{17,25},{25,17},{2,10},{10... | collective-permute-start | bytes 786440 | tf_op jit(solution)/shard_map/ppermute | solution.py:28
  37.3 7.2 %collective-permute-start.4 = (bf16[2,6,64,128]{3,2,1,0:T(8,128)(2,1)S(1)}, bf16[2,6,64,128]{3,2,1,0:T(8,128)(2,1)S(1)}, u32[]{:S(2)}, u32[]{:S(2)}) collective-permute-start(bf16[2,6,64,128]{3,2,1,0:T(8,128)(2,1)S(1)} %get-tuple-element.26), channel_id=1, source_target_pairs={{0,1},{1,0},{2,3},{3,2},{4,5},{5,4},{6,7},{7,6},{8,9},{9,8},{10,11... | collective-permute-start | bytes 589832 | tf_op jit(solution)/shard_map/ppermute | solution.py:28
  44.5 19.0 %collective-permute-start.12 = (bf16[4,2,6,64,128]{4,3,2,1,0:T(8,128)(2,1)S(1)}, bf16[4,2,6,64,128]{4,3,2,1,0:T(8,128)(2,1)S(1)}, u32[]{:S(2)}, u32[]{:S(2)}) collective-permute-start(bf16[4,2,6,64,128]{4,3,2,1,0:T(8,128)(2,1)S(1)} %get-tuple-element.33), channel_id=1, source_target_pairs={{0,1},{1,0},{2,3},{3,2},{4,5},{5,4},{6,7},{7,6},{8,9},{9,8},{10,11... | collective-permute-start | bytes 2359304 | tf_op jit(solution)/shard_map/ppermute | solution.py:28
  46.2 14.0 %collective-permute-start.10 = (bf16[2,2,6,64,128]{4,3,2,1,0:T(8,128)(2,1)S(1)}, bf16[2,2,6,64,128]{4,3,2,1,0:T(8,128)(2,1)S(1)}, u32[]{:S(2)}, u32[]{:S(2)}) collective-permute-start(bf16[2,2,6,64,128]{4,3,2,1,0:T(8,128)(2,1)S(1)} %pad_maximum_fusion), channel_id=1, source_target_pairs={{2,4},{3,5},{4,2},{5,3},{0,6},{1,7},{6,0},{7,1},{10,12},{11,13},{1... | collective-permute-start | bytes 1179656 | tf_op jit(solution)/shard_map/ppermute | solution.py:33
  49.9 18.0 %collective-permute-start.8 = (bf16[2,2,6,64,128]{4,3,2,1,0:T(8,128)(2,1)S(1)}, bf16[2,2,6,64,128]{4,3,2,1,0:T(8,128)(2,1)S(1)}, u32[]{:S(2)}, u32[]{:S(2)}) collective-permute-start(bf16[2,2,6,64,128]{4,3,2,1,0:T(8,128)(2,1)S(1)} %pad_maximum_fusion), channel_id=1, source_target_pairs={{0,2},{1,3},{2,0},{3,1},{4,6},{5,7},{6,4},{7,5},{8,10},{9,11},{10,... | collective-permute-start | bytes 1179656 | tf_op jit(solution)/shard_map/ppermute | solution.py:33
  49.9 24.7 %collective-permute-start.9 = (bf16[2,2,6,64,128]{4,3,2,1,0:T(8,128)(2,1)S(1)}, bf16[2,2,6,64,128]{4,3,2,1,0:T(8,128)(2,1)S(1)}, u32[]{:S(2)}, u32[]{:S(2)}) collective-permute-start(bf16[2,2,6,64,128]{4,3,2,1,0:T(8,128)(2,1)S(1)} %pad_maximum_fusion), channel_id=1, source_target_pairs={{0,4},{1,5},{6,2},{7,3},{8,12},{9,13},{14,10},{15,11},{16,20},{17,... | collective-permute-start | bytes 1179656 | tf_op jit(solution)/shard_map/ppermute | solution.py:33
  60.2 16.0 %collective-permute-start.11 = (bf16[2,2,6,64,128]{4,3,2,1,0:T(8,128)(2,1)S(1)}, bf16[2,2,6,64,128]{4,3,2,1,0:T(8,128)(2,1)S(1)}, u32[]{:S(2)}, u32[]{:S(2)}) collective-permute-start(bf16[2,2,6,64,128]{4,3,2,1,0:T(8,128)(2,1)S(1)} %collective-permute-done.10.refs_4_), channel_id=1, source_target_pairs={{2,0},{3,1},{4,6},{5,7},{10,8},{11,9},{12,14},{13,15},{18,16},{19,... | collective-permute-start | bytes 1179656 | tf_op jit(solution)/shard_map/ppermute | solution.py:33
  63.5 12.8 %copy-start.1 = (s32[4]{0:T(128)S(1)}, s32[4]{0:T(128)}, u32[]{:S(2)}) copy-start(s32[4]{0:T(128)} %times_ref.1) | copy-start | bytes 52
  79.0 1.3 %collective-permute-start.13 = (f32[2,4,12,12]{3,2,1,0:T(8,128)S(1)}, f32[2,4,12,12]{3,2,1,0:T(8,128)S(1)}, u32[]{:S(2)}, u32[]{:S(2)}) collective-permute-start(f32[2,4,12,12]{3,2,1,0:T(8,128)S(1)} %traces.1), channel_id=1, source_target_pairs={{0,8},{8,0},{16,24},{24,16},{1,9},{9,1},{17,25},{25,17},{2,10},{10... | collective-permute-start | bytes 13832 | tf_op jit(solution)/shard_map/ppermute | solution.py:28
  80.4 4.0 %collective-permute-start.14 = (f32[4,12,12]{2,1,0:T(8,128)S(1)}, f32[4,12,12]{2,1,0:T(8,128)S(1)}, u32[]{:S(2)}, u32[]{:S(2)}) collective-permute-start(f32[4,12,12]{2,1,0:T(8,128)S(1)} %get-tuple-element.37), channel_id=1, source_target_pairs={{0,16},{8,24},{16,0},{24,8},{1,17},{9,25},{17,1},{25,9},{2,18},{10... | collective-permute-start | bytes 6920 | tf_op jit(solution)/shard_map/ppermute | solution.py:28
  82.0 3.9 %collective-permute-start.15 = (f32[4,12,12]{2,1,0:T(8,128)S(1)}, f32[4,12,12]{2,1,0:T(8,128)S(1)}, u32[]{:S(2)}, u32[]{:S(2)}) collective-permute-start(f32[4,12,12]{2,1,0:T(8,128)S(1)} %get-tuple-element.36), channel_id=1, source_target_pairs={{0,1},{1,0},{2,3},{3,2},{4,5},{5,4},{6,7},{7,6},{8,9},{9,8},{10,11... | collective-permute-start | bytes 6920 | tf_op jit(solution)/shard_map/ppermute | solution.py:28
  82.5 4.8 %collective-permute-start.16 = (f32[4,12,12]{2,1,0:T(8,128)S(1)}, f32[4,12,12]{2,1,0:T(8,128)S(1)}, u32[]{:S(2)}, u32[]{:S(2)}) collective-permute-start(f32[4,12,12]{2,1,0:T(8,128)S(1)} %get-tuple-element.36), channel_id=1, source_target_pairs={{0,17},{1,16},{2,19},{3,18},{4,21},{5,20},{6,23},{7,22},{8,25},{9,... | collective-permute-start | bytes 6920 | tf_op jit(solution)/shard_map/ppermute | solution.py:566

commit v4 on v3

--- a/solution.py
+++ b/solution.py
@@ -15,10 +15,9 @@
 F32 = jnp.float32
 BF16 = jnp.bfloat16
 CHUNK = 32
-FOLD = 8
+GROUPS = 8
 MEGA = 1024 * 1024
 
-ANY = pl.BlockSpec(memory_space=pl.ANY)
 SMEM = pl.BlockSpec(memory_space=pltpu.SMEM)
 VMEM = pl.BlockSpec(memory_space=pltpu.VMEM)
 
@@ -87,13 +86,16 @@
 
 
 def elemental_kernel(held, near, late, block_rows, *refs):
-    move_ref, zphase_ref, phase_ref = refs[:3]
-    slab_refs = refs[3 : 3 + held]
-    rest = refs[3 + held :]
+    move_ref, zphase_ref = refs[:2]
+    slab_refs = refs[2 : 2 + held]
+    rest = refs[2 + held :]
+    if not late:
+        phase_ref, rest = rest[0], rest[1:]
     if late:
-        prior_ref, acc_out, keep_ref, send_ref, slabs, turned, mixed, table, acc, before, sems = rest
+        table, prior_ref, acc_out, keep_ref, send_ref = rest[:5]
+        slabs, turned, mixed_a, mixed_b, todo, acc, wide = rest[5:]
     else:
-        acc, slabs, turned, mixed, table, sems = rest
+        acc, table, slabs, turned, mixed_a, mixed_b, todo = rest
     operators, half_rows, vectors = acc.shape
     half_rows //= 2
     colours = turned.shape[0]
@@ -101,79 +103,62 @@
     me = lax.axis_index("space")
     core = lax.rem(me, 2)
 
-    def arriving(m):
-        return (
-            pltpu.make_async_copy(
-                slab_refs[m], slabs.at[m, :, :, pl.ds(0, PLANE), :], sems.at[2 * m]
-            ),
-            pltpu.make_async_copy(
-                slab_refs[m].at[:, :, pl.ds(0, LX), :],
-                slabs.at[m, :, :, pl.ds(PLANE, LX), :],
-                sems.at[2 * m + 1],
-            ),
-        )
-
-    order = list(range(near, held)) + list(range(min(near, held)))
-    for m in order:
-        for copy in arriving(m):
-            copy.start()
-    if late:
-        prior = pltpu.make_async_copy(prior_ref, before, sems.at[2 * held])
-        prior.start()
+    for m in range(held):
+        slabs[m, :, :, pl.ds(0, PLANE), :] = slab_refs[m][...]
+        slabs[m, :, :, pl.ds(PLANE, LX), :] = slab_refs[m][:, :, pl.ds(0, LX), :]
     acc[...] = jnp.zeros_like(acc)
-    upright = phase_ref[...].T
-    for o in range(operators):
-        for part in range(2):
-            at = 2 * o + part
-            table[o, part] = jnp.broadcast_to(upright[:, at : at + 1], (PLANE, LANES))
-    first_slab = order[0]
-    for copy in arriving(first_slab):
-        copy.wait()
-
-    def one_slab(step, carry):
-        m = lax.rem(step + first_slab, held)
+    if not late:
+        upright = phase_ref[...].T
+        for o in range(operators):
+            for part in range(2):
+                at = 2 * o + part
+                table[o, part] = jnp.broadcast_to(upright[:, at : at + 1], (PLANE, LANES))
+    def one_slab(m, carry):
         here = me ^ m
         above = lax.rem(here + 1, count) ^ me
         far = above >= near
 
-        def wait_others():
-            for other in order[1:]:
-                for copy in arriving(other):
-                    copy.wait()
-
-        def one_operator(o, inner):
+        def collect(o, found):
+            waits = (m >= near) | ((move_ref[o] == 3) & far)
+            chosen = waits if late else jnp.logical_not(waits)
+
+            @pl.when(chosen)
+            def _():
+                todo[found] = o
+
+            return found + chosen.astype(jnp.int32)
+
+        def turn_phases(o, mixed, colour):
             move = move_ref[o]
-            waits = (m >= near) | ((move == 3) & far)
-
-            @pl.when((waits if late else jnp.logical_not(waits)) & ((move == 3) == inner))
-            def _():
-                src = jnp.where(move == 3, above, jnp.where(move == 1, held, m))
-                off = pl.multiple_of(jnp.where(move == 2, LX, 0), LX)
-                cos_z, sin_z = zphase_ref[0, here, o], zphase_ref[1, here, o]
-                total = None
-                for colour in range(colours):
-                    for begin in range(0, PLANE, CHUNK):
-                        cos_p = table[o, 0, pl.ds(begin, CHUNK), :]
-                        sin_p = table[o, 1, pl.ds(begin, CHUNK), :]
-                        cosine = cos_p * cos_z - sin_p * sin_z
-                        sine = sin_p * cos_z + cos_p * sin_z
-                        cosine = jnp.concatenate([cosine] * (vectors // LANES), axis=1)
-                        sine = jnp.concatenate([sine] * (vectors // LANES), axis=1)
-                        real = slabs[src, 0, colour, pl.ds(off + begin, CHUNK), :].astype(F32)
-                        imag = slabs[src, 1, colour, pl.ds(off + begin, CHUNK), :].astype(F32)
-                        mixed[colour, pl.ds(begin, CHUNK), :] = (
-                            cosine * real + sine * imag
-                        ).astype(BF16)
-                        mixed[colour, pl.ds(PLANE + begin, CHUNK), :] = (
-                            cosine * imag - sine * real
-                        ).astype(BF16)
-                    term = jnp.dot(turned[colour], mixed[colour], preferred_element_type=F32)
-                    total = term if total is None else total + term
-                acc[o] += total
-
-            return inner
-
-        @pl.when((m >= near) | far if late else m >= 0)
+            src = jnp.where(move == 3, above, jnp.where(move == 1, held, m))
+            off = pl.multiple_of(jnp.where(move == 2, LX, 0), LX)
+            cos_z, sin_z = zphase_ref[0, here, o], zphase_ref[1, here, o]
+            for begin in range(0, PLANE, CHUNK):
+                cos_p = table[o, 0, pl.ds(begin, CHUNK), :]
+                sin_p = table[o, 1, pl.ds(begin, CHUNK), :]
+                cosine = cos_p * cos_z - sin_p * sin_z
+                sine = sin_p * cos_z + cos_p * sin_z
+                cosine = jnp.concatenate([cosine] * (vectors // LANES), axis=1)
+                sine = jnp.concatenate([sine] * (vectors // LANES), axis=1)
+                real = slabs[src, 0, colour, pl.ds(off + begin, CHUNK), :].astype(F32)
+                imag = slabs[src, 1, colour, pl.ds(off + begin, CHUNK), :].astype(F32)
+                mixed[colour, pl.ds(begin, CHUNK), :] = (cosine * real + sine * imag).astype(BF16)
+                mixed[colour, pl.ds(PLANE + begin, CHUNK), :] = (
+                    cosine * imag - sine * real
+                ).astype(BF16)
+
+        def step(o, mixed, later, following):
+            total = None
+            for colour in range(colours):
+                turn_phases(later, following, colour)
+            for colour in range(colours):
+                term = jnp.dot(turned[colour], mixed[colour], preferred_element_type=F32)
+                total = term if total is None else total + term
+            acc[o] += total
+
+        found = lax.fori_loop(0, operators, collect, jnp.int32(0))
+
+        @pl.when(found > 0)
         def _():
             for colour in range(colours):
                 for part in range(2):
@@ -184,21 +169,34 @@
                     lower = pl.ds(half_rows, half_rows)
                     turned[colour, pl.ds(0, half_rows), pl.ds(part * PLANE, PLANE)] = flat
                     turned[colour, lower, pl.ds((1 - part) * PLANE, PLANE)] = same
+
+        @pl.when((found > 0) & (m >= near if late else m >= 0))
+        def _():
+            for colour in range(colours):
+                for part in range(2):
                     for begin in range(0, PLANE, CHUNK):
                         rows = slabs[m, part, colour, pl.ds(begin, CHUNK), :].astype(F32)
                         rows = pltpu.roll(rows.reshape(CHUNK // LX, LX, vectors), LX - 1, 1)
                         slabs[held, part, colour, pl.ds(begin, CHUNK), :] = rows.reshape(
                             CHUNK, vectors
                         ).astype(BF16)
-            lax.fori_loop(0, operators, one_operator, False)
-
-        @pl.when(step == 0)
+
+        @pl.when(found > 0)
         def _():
-            wait_others()
-
-        @pl.when((m >= near) | far if late else m >= 0)
-        def _():
-            lax.fori_loop(0, operators, one_operator, True)
+            for colour in range(colours):
+                turn_phases(todo[0], mixed_a, colour)
+
+            def two(i, inner):
+                step(todo[2 * i], mixed_a, todo[jnp.minimum(2 * i + 1, found - 1)], mixed_b)
+
+                @pl.when(2 * i + 1 < found)
+                def _():
+                    after = todo[jnp.minimum(2 * i + 2, found - 1)]
+                    step(todo[2 * i + 1], mixed_b, after, mixed_a)
+
+                return inner
+
+            lax.fori_loop(0, (found + 1) // 2, two, 0)
 
         return carry
 
@@ -207,15 +205,17 @@
     if late:
         first = pl.multiple_of(me // 2 * block_rows, block_rows)
         half = lax.rem(lax.axis_index("tm"), 2)
-        prior.wait()
         for o in range(operators):
-            acc_out[o] = (acc[o] + before[o]).astype(BF16)
-            for part in range(2):
+            acc_out[o] = (acc[o] + prior_ref[o]).astype(BF16)
+        for part in range(2):
+            for o in range(operators):
                 rows = pl.ds(part * half_rows + first, block_rows)
-                own = (acc[o, rows, :] + before[o, rows, :]).astype(BF16)
-                low, high = own[:, :LANES], own[:, LANES:]
-                keep_ref[part, o] = jnp.where(half == 0, low, high)
-                send_ref[part, o] = jnp.where(half == 0, high, low)
+                own = acc[o, rows, :] + prior_ref[o, rows, :]
+                at = pl.ds((part * operators + o) * block_rows, block_rows)
+                wide[0, at, :] = own[:, :LANES]
+                wide[1, at, :] = own[:, LANES:]
+        keep_ref[...] = spread(wide.at[half], 2 * operators, block_rows)
+        send_ref[...] = spread(wide.at[1 - half], 2 * operators, block_rows)
 
 
 def elementals(tables, slab_list, near, prior, block_rows):
@@ -228,22 +228,28 @@
         pltpu.VMEM((held + 1, 2, colours, plane + LX, vectors), BF16),
         pltpu.VMEM((colours, vectors, 2 * plane), BF16),
         pltpu.VMEM((colours, 2 * plane, vectors), BF16),
-        pltpu.VMEM((operators, 2, plane, LANES), F32),
+        pltpu.VMEM((colours, 2 * plane, vectors), BF16),
+        pltpu.SMEM((operators,), jnp.int32),
     ]
     if late:
-        piece = jax.ShapeDtypeStruct((2, operators, block_rows, LANES), BF16)
+        piece = jax.ShapeDtypeStruct(
+            (2 * operators * GROUPS, block_rows // GROUPS * LANES), BF16
+        )
         outs = (jax.ShapeDtypeStruct(wide.shape, BF16), piece, piece)
         out_specs = (VMEM, VMEM, VMEM)
-        scratch += [pltpu.VMEM(wide.shape, F32)] * 2
+        scratch.append(pltpu.VMEM(wide.shape, F32))
+        scratch.append(pltpu.VMEM((2, 2 * operators * block_rows, LANES), F32))
     else:
-        outs, out_specs = wide, VMEM
-    priors = [prior] if late else []
+        outs = (wide, jax.ShapeDtypeStruct((operators, 2, plane, LANES), F32))
+        out_specs = (VMEM, VMEM)
+    move, z_phase, phases = tables
+    priors = [phases, prior] if late else [phases]
     return pl.pallas_call(
         functools.partial(elemental_kernel, held, near, late, block_rows),
         out_shape=outs,
-        in_specs=[SMEM, SMEM, VMEM] + [ANY] * (held + len(priors)),
+        in_specs=[SMEM, SMEM] + [VMEM] * (held + len(priors)),
         out_specs=out_specs,
-        scratch_shapes=scratch + [pltpu.SemaphoreType.DMA((2 * held + 1,))],
+        scratch_shapes=scratch,
         compiler_params=params(20 + held),
         cost_estimate=pl.CostEstimate(
             flops=8 * held * operators * colours * plane * vectors * vectors,
@@ -251,36 +257,26 @@
             transcendentals=0,
         ),
         name="elementals_late" if late else "elementals_early",
-    )(*tables, *slab_list, *priors)
+    )(move, z_phase, *slab_list, *priors)
 
 
 def both_kernel(blocks, e_ref, other_ref, *refs):
     peram_refs = refs[:blocks]
-    keep_ref, send_ref, whole, sorted_rows, left, middle, sems = refs[blocks:]
+    keep_ref, rest = refs[blocks], refs[blocks + 1 :]
+    whole, sorted_rows, left, middle = rest[-4:]
+    send_refs = rest[:-4]
+    each = keep_ref.shape[0] // len(send_refs)
     sources, _, vectors, _ = whole.shape
     operators = e_ref.shape[0]
     block_rows = keep_ref.shape[3]
     me = lax.axis_index("space")
     half = lax.rem(lax.axis_index("tm"), 2)
-    copies = []
     for m in range(blocks):
         begin = pl.multiple_of((me ^ m) * block_rows, block_rows)
-        copies.append(
-            pltpu.make_async_copy(
-                peram_refs[m], whole.at[:, :, pl.ds(begin, block_rows), :], sems.at[2 * m]
-            )
-        )
+        whole[:, :, pl.ds(begin, block_rows), :] = peram_refs[m][...]
         begin = (m % 2) * (vectors // 2) + (me ^ m) // 2 * block_rows
         begin = pl.multiple_of(begin, block_rows)
-        copies.append(
-            pltpu.make_async_copy(
-                peram_refs[m], sorted_rows.at[:, :, pl.ds(begin, block_rows), :], sems.at[2 * m + 1]
-            )
-        )
-    for copy in copies:
-        copy.start()
-    for copy in copies:
-        copy.wait()
+        sorted_rows[:, :, pl.ds(begin, block_rows), :] = peram_refs[m][...]
     row = lax.broadcasted_iota(jnp.int32, (block_rows, vectors), 0)
     column = lax.broadcasted_iota(jnp.int32, (block_rows, vectors), 1)
     chosen = (column == row + me * block_rows).astype(F32).astype(BF16)
@@ -334,7 +330,7 @@
                 low = rows[:, part * vectors : part * vectors + LANES]
                 high = rows[:, part * vectors + LANES : (part + 1) * vectors]
                 keep_ref[s, part, a] = jnp.where(half == 0, low, high)
-                send_ref[s, part, a] = jnp.where(half == 0, high, low)
+                send_refs[s // each][s % each, part, a] = jnp.where(half == 0, high, low)
 
 
 def both_sides(elements, others, perams):
@@ -342,17 +338,18 @@
     sources, _, block_rows, vectors = perams[0].shape
     operators = elements.shape[0]
     piece = jax.ShapeDtypeStruct((sources, 2, operators, block_rows, LANES), BF16)
+    sends = 2 - sources % 2
+    part = jax.ShapeDtypeStruct((sources // sends,) + piece.shape[1:], BF16)
     return pl.pallas_call(
         functools.partial(both_kernel, blocks),
-        out_shape=(piece, piece),
-        in_specs=[VMEM, VMEM] + [ANY] * blocks,
-        out_specs=(VMEM, VMEM),
+        out_shape=(piece,) + (part,) * sends,
+        in_specs=[VMEM] * (2 + blocks),
+        out_specs=(VMEM,) * (1 + sends),
         scratch_shapes=[
             pltpu.VMEM((sources, 2, vectors, vectors), BF16),
             pltpu.VMEM((sources, 2, vectors, vectors), BF16),
             pltpu.VMEM((2 * sources * block_rows, vectors), BF16),
             pltpu.VMEM((2, sources, operators * block_rows, 2 * vectors), BF16),
-            pltpu.SemaphoreType.DMA((2 * blocks,)),
         ],
         compiler_params=params(16),
         cost_estimate=pl.CostEstimate(flops=0, bytes_accessed=0, transcendentals=0),
@@ -361,20 +358,22 @@
 
 
 def spread(wide, count_rows, block_rows):
+    fold = block_rows // GROUPS
     pieces = [
-        wide[pl.ds(k, count_rows * block_rows // FOLD, stride=FOLD), :].astype(BF16)
-        for k in range(FOLD)
+        wide[pl.ds(k, count_rows * GROUPS, stride=fold), :].astype(BF16) for k in range(fold)
     ]
     return jnp.concatenate(pieces, axis=1)
 
 
-def lay_kernel(own_ref, pair_ref, out_ref, wide):
+def lay_kernel(own_ref, *refs):
+    pair_refs, out_ref, wide = refs[:-2], refs[-2], refs[-1]
+    each = own_ref.shape[0] // len(pair_refs)
     sources, _, operators, block_rows, lanes = own_ref.shape
     rows = 2 * operators
     for s in range(sources):
-        for at, ref in enumerate((own_ref, pair_ref)):
+        for at, ref in enumerate((own_ref.at[s], pair_refs[s // each].at[s % each])):
             wide[pl.ds(at * rows * block_rows, rows * block_rows), :] = (
-                ref[s].astype(F32).reshape(rows * block_rows, lanes)
+                ref[...].astype(F32).reshape(rows * block_rows, lanes)
             )
         out_ref[s] = spread(wide, 2 * rows, block_rows)
 
@@ -385,23 +384,23 @@
     return pl.pallas_call(
         lay_kernel,
         out_shape=jax.ShapeDtypeStruct(
-            (sources, 2 * rows * block_rows // FOLD, FOLD * lanes), BF16
+            (sources, 2 * rows * GROUPS, block_rows // GROUPS * lanes), BF16
         ),
-        in_specs=[VMEM, VMEM],
+        in_specs=[VMEM] * (1 + len(pair)),
         out_specs=VMEM,
         scratch_shapes=[pltpu.VMEM((2 * rows * block_rows, lanes), F32)],
         compiler_params=params(12),
         cost_estimate=pl.CostEstimate(flops=0, bytes_accessed=0, transcendentals=0),
         name="lay_out",
-    )(own, pair)
+    )(own, *pair)
 
 
 def trace_kernel(count, table, line, times_ref, *refs):
     pools = refs[:count]
-    laid_ref, out_ref, picked, wide, sems = refs[count:]
+    laid_ref, out_ref, picked = refs[count:]
     sources = laid_ref.shape[0]
-    _, operators, block_rows, lanes = pools[0].shape
-    rows = 2 * operators
+    groups = GROUPS
+    rows = pools[0].shape[0] // groups
     time = lax.axis_index("tm")
     for s in range(sources):
         source = times_ref[s]
@@ -411,9 +410,8 @@
             @pl.when(code == index)
             def _(at=at, inside=inside, s=s):
                 block = pools[at] if inside is None else pools[at].at[inside]
-                pltpu.make_async_copy(block, picked.at[s], sems.at[s]).start()
-
-    groups = block_rows // FOLD
+                picked[s] = block[...]
+
     shape = (2 * rows * groups, rows * groups)
     down = lax.broadcasted_iota(jnp.int32, shape, 0)
     over = lax.broadcasted_iota(jnp.int32, shape, 1)
@@ -422,14 +420,11 @@
     down = lax.broadcasted_iota(jnp.int32, shape, 0)
     over = lax.broadcasted_iota(jnp.int32, shape, 1)
     gather = (down // groups == over).astype(F32)
-    for s in range(sources):
-        pltpu.make_async_copy(pools[0], picked.at[s], sems.at[s]).wait()
-        wide[s] = picked[s].astype(F32).reshape(rows * block_rows, lanes)
     sums = []
     for s in range(sources):
         product = lax.dot_general(
             laid_ref[s],
-            spread(wide.at[s], rows, block_rows),
+            picked[s],
             (((1,), (1,)), ((), ())),
             preferred_element_type=F32,
         )
@@ -448,21 +443,18 @@
 
 def traces(source_times, pools, table, line, laid):
     sources = laid.shape[0]
-    _, operators, block_rows, lanes = pools[0].shape
-    rows = 2 * operators
+    rows = pools[0].shape[0] // GROUPS
     return pl.pallas_call(
         functools.partial(trace_kernel, len(pools), table, line),
         out_shape=jax.ShapeDtypeStruct((2, sources, rows, rows), F32),
-        in_specs=[SMEM] + [ANY] * len(pools) + [VMEM],
+        in_specs=[SMEM] + [VMEM] * (len(pools) + 1),
         out_specs=VMEM,
         scratch_shapes=[
             pltpu.VMEM((sources,) + pools[0].shape, BF16),
-            pltpu.VMEM((sources, rows * block_rows, lanes), F32),
-            pltpu.SemaphoreType.DMA((sources,)),
         ],
         compiler_params=params(12),
         cost_estimate=pl.CostEstimate(
-            flops=4 * sources * rows * rows * block_rows * lanes,
+            flops=4 * laid.size * rows,
             bytes_accessed=2 * laid.size,
             transcendentals=0,
         ),
@@ -533,22 +525,23 @@
 
     plane_phase, z_phase = phase_tables(momenta, jnp.arange(slabs, dtype=jnp.int32), slabs)
     tables = (displacement, z_phase, plane_phase)
-    total = elementals(tables, [own, beside], near, None, block_rows)
+    total, wide_phase = elementals(tables, [own, beside], near, None, block_rows)
 
     keys, total = lax.optimization_barrier((keys, total))
     slab_list = swap_near(keys)
     slab_list[1] = beside
     peram, _ = lax.optimization_barrier((perambulators[0], keys[slabs // 2]))
     perams = swap_far(peram)
+    tables = (displacement, z_phase, wide_phase)
     full, keep, send = elementals(tables, slab_list, near, total, block_rows)
 
     perams, full, send = lax.optimization_barrier((perams, full, send))
     perams = swap_near(perams)
 
     received = swap_bit(send, "tm", 1)
-    g_keep, g_send = both_sides(full, swap_bit(full, "space", 1), perams)
+    g_keep, *g_send = both_sides(full, swap_bit(full, "space", 1), perams)
     arrays, table, g_send = share_line(keep, received, g_send, line)
-    laid = lay_out(g_keep, swap_bit(g_send, "tm", 1))
+    laid = lay_out(g_keep, [swap_bit(block, "tm", 1) for block in g_send])
     both = traces(source_times, arrays, table, line, laid)
     both = both + swap_bit(both, "space", 1)
     mine, pair = both[0], both[1]

time: 87.9 us -> 85.7 us (0.975)
  Pallas kernels: 27.3 us -> 25.4 us
    ppermute x4, waiting for transfers between devices: 19.7 us -> 12.6 us  [along_line(): return lax.ppermute(block, 'tm', route)]
    ppermute x12 -> x13, waiting for transfers between devices: 15.6 us -> 21.3 us  [swap_bit(): return lax.ppermute(block, axis, [(i, i ^ mask) for i in range(count)])]
    ppermute x12 -> x13, starting transfers between devices: 11.2 us -> 12.5 us  [swap_bit(): return lax.ppermute(block, axis, [(i, i ^ mask) for i in range(count)])]
    pallas_call x1, Pallas kernels: 2.8 us -> 1.63 us  [traces(): pl.pallas_call(functools.partial(trace_kernel, len(pools), table, line),...]
    ppermute x1, starting transfers between devices: 1.43 us -> 0.46 us  [across(): return lax.ppermute(block, ('space', 'tm'), route)]
  transfers between devices with their start and end apart: 17 -> 18, of which waited for: 14 -> 14; matrix products, arithmetic and copies ran while one was open for 1% -> 1% of each run, Pallas kernels for 27% -> 27%
where the time goes in v4:
time: 85.7 us; the launch traced here: 86 us
  waiting for transfers between devices  36 us (42%)
  Pallas kernels  25.4 us (30%)
  starting transfers between devices  20.7 us (24%)
  local copies, waits for them, and re-layouts  2.66 us (3%)
    ppermute x13, waiting for transfers between devices, swap_bit(): return lax.ppermute(block, axis, [(i, i ^ mask) for i in range(count)])  21.3 us
    pallas_call x2, Pallas kernels, elementals(): pl.pallas_call(functools.partial(elemental_kernel, held, near, late, bloc...  19.1 us
    ppermute x4, waiting for transfers between devices, along_line(): return lax.ppermute(block, 'tm', route)  12.6 us
    ppermute x13, starting transfers between devices, swap_bit(): return lax.ppermute(block, axis, [(i, i ^ mask) for i in range(count)])  12.5 us
    ppermute x4, starting transfers between devices, along_line(): return lax.ppermute(block, 'tm', route)  7.74 us
    pallas_call x1, Pallas kernels, both_sides(): pl.pallas_call(functools.partial(both_kernel, blocks), out_shape=(piece,)...  3.11 us
    ppermute x1, waiting for transfers between devices, across(): return lax.ppermute(block, ('space', 'tm'), route)  2.1 us
    unnamed x12, local copies, waits for them, and re-layouts  1.84 us
  transfers between devices with their start and end apart: 18, of which 14 were waited for; matrix products, arithmetic and copies ran while one was open for 1% of the time, Pallas kernels for 27%

profile of v4, /device:TPU:0, one launch (start us, length us, event | category | flops | bytes accessed | tf_op | source)
XLA Modules:
  0.0 86.0 jit_solution(2235859823567554114)
XLA Ops:
  0.6 0.5 collective-permute-start.1
  1.1 2.6 %collective-permute-start = (bf16[2,3,256,256]{3,2,1,0:T(8,128)(2,1)}, bf16[2,3,256,256]{3,2,1,0:T(8,128)(2,1)S(1)}, u32[]{:S(2)}, u32[]{:S(2)}) collective-permute-start(bf16[2,3,256,256]{3,2,1,0:T(8,128)(2,1)} %bitcast.22), channel_id=1, source_target_pairs={{0,16},{8,24},{16,0},{24,8},{1,17},{9,25},{17,1},{25,9},{2,18},{10... | collective-permute-start | bytes 2359304 | tf_op jit(solution)/shard_map/ppermute | solution.py:27
  3.7 0.8 slice_bitcast_fusion.3
  4.5 0.3 fusion.13
  4.9 0.1 fusion.11
  5.0 0.0 copy-start
  5.0 0.0 collective-permute-done.1.refs_3_
  5.0 0.0 copy-start.2
  5.0 1.2 %copy-done.2 = bf16[1,2,3,1,256,256]{5,4,3,2,1,0:T(8,128)(2,1)S(1)} copy-done((bf16[1,2,3,1,256,256]{5,4,3,2,1,0:T(8,128)(2,1)S(1)}, bf16[1,2,3,1,256,256]{5,4,3,2,1,0:T(8,128)(2,1)}, u32[]{:S(2)}) %copy-start.2) | copy-done | bytes 786456
  6.2 0.7 copy-done.4
  6.8 7.7 %elementals_early.1 = (f32[6,256,256]{2,1,0:T(8,128)S(1)}, f32[6,2,256,128]{3,2,1,0:T(8,128)S(1)}) custom-call(s32[6]{0:T(128)S(1)} %copy-done.4, f32[2,4,6]{2,1,0:T(4,128)S(1)} %pad_maximum_fusion.2.refs_1_, bf16[2,3,256,256]{3,2,1,0:T(8,128)(2,1)S(1)} %bitcast.23, bf16[2,3,256,256]{3,2,1,0:T(8,128)(2,1)S(1)} %collective-permute-done.1.refs_3_, ...), custom_call_target="tpu_custom_call" | custom-call | flops 4831838208 | bytes 1572864 | tf_op jit(solution)/shard_map/elementals_early/pallas_call | solution.py:247
  14.6 7.5 %collective-permute-done.refs_4_ = bf16[2,3,256,256]{3,2,1,0:T(8,128)(2,1)S(1)} collective-permute-done((bf16[2,3,256,256]{3,2,1,0:T(8,128)(2,1)}, bf16[2,3,256,256]{3,2,1,0:T(8,128)(2,1)S(1)}, u32[]{:S(2)}, u32[]{:S(2)}) %collective-permute-start) | collective-permute-done | bytes 786464 | tf_op jit(solution)/shard_map/ppermute | solution.py:27
  22.1 0.0 collective-permute-start.2
  22.1 1.8 %collective-permute-start.3 = (bf16[4,2,64,256]{3,2,1,0:T(8,128)(2,1)S(1)}, bf16[4,2,64,256]{3,2,1,0:T(8,128)(2,1)S(1)}, u32[]{:S(2)}, u32[]{:S(2)}) collective-permute-start(bf16[4,2,64,256]{3,2,1,0:T(8,128)(2,1)S(1)} %bitcast.18), channel_id=1, source_target_pairs={{0,16},{8,24},{16,0},{24,8},{1,17},{9,25},{17,1},{25,9},{2,18},{10... | collective-permute-start | bytes 786440 | tf_op jit(solution)/shard_map/ppermute | solution.py:27
  23.9 0.5 collective-permute-done.2.refs_5_
  24.4 11.4 %elementals_late.1 = (bf16[6,256,256]{2,1,0:T(8,128)(2,1)S(1)}, bf16[96,1024]{1,0:T(8,128)(2,1)S(1)}, bf16[96,1024]{1,0:T(8,128)(2,1)S(1)}) custom-call(s32[6]{0:T(128)S(1)} %copy-done.5, f32[2,4,6]{2,1,0:T(4,128)S(1)} %pad_maximum_fusion.2.refs_1_, bf16[2,3,256,256]{3,2,1,0:T(8,128)(2,1)S(1)} %bitcast.24, ...), custom_call_target="tpu_custom_call" | custom-call | flops 9663676416 | bytes 3145728 | tf_op jit(solution)/shard_map/elementals_late/pallas_call | solution.py:247
  35.8 0.0 collective-permute-done.3.refs_2_
  35.8 0.2 collective-permute-start.5
  36.0 0.4 collective-permute-start.6
  36.3 0.1 collective-permute-start.7
  36.5 1.7 %collective-permute-start.4 = (bf16[96,1024]{1,0:T(8,128)(2,1)S(1)}, bf16[96,1024]{1,0:T(8,128)(2,1)S(1)}, u32[]{:S(2)}, u32[]{:S(2)}) collective-permute-start(bf16[96,1024]{1,0:T(8,128)(2,1)S(1)} %get-tuple-element.32), channel_id=1, source_target_pairs={{0,1},{1,0},{2,3},{3,2},{4,5},{5,4},{6,7},{7,6},{8,9},{9,8},{10,11... | collective-permute-start | bytes 589832 | tf_op jit(solution)/shard_map/ppermute | solution.py:27
  38.2 0.3 collective-permute-done.6.refs_1_
  38.5 0.4 collective-permute-done.7.refs_3_
  38.9 0.0 collective-permute-done.5.other_ref
  38.9 3.1 %both_sides.1 = (bf16[4,2,6,64,128]{4,3,2,1,0:T(8,128)(2,1)S(1)}, bf16[2,2,6,64,128]{4,3,2,1,0:T(8,128)(2,1)S(1)}, bf16[2,2,6,64,128]{4,3,2,1,0:T(8,128)(2,1)S(1)}) custom-call(bf16[6,256,256]{2,1,0:T(8,128)(2,1)S(1)} %get-tuple-element.33.e_ref, bf16[6,256,256]{2,1,0:T(8,128)(2,1)S(1)} %collective-permute-done.5.other_ref, ...), custom_call_target="tpu_custom_call" | custom-call | tf_op jit(solution)/shard_map/both_sides/pallas_call | solution.py:343
  42.0 1.7 %collective-permute-done.4.refs_1_ = bf16[96,1024]{1,0:T(8,128)(2,1)S(1)} collective-permute-done((bf16[96,1024]{1,0:T(8,128)(2,1)S(1)}, bf16[96,1024]{1,0:T(8,128)(2,1)S(1)}, u32[]{:S(2)}, u32[]{:S(2)}) %collective-permute-start.4) | collective-permute-done | bytes 196640 | tf_op jit(solution)/shard_map/ppermute | solution.py:27
  43.7 3.9 %collective-permute-start.10 = (bf16[2,96,1024]{2,1,0:T(8,128)(2,1)S(1)}, bf16[2,96,1024]{2,1,0:T(8,128)(2,1)S(1)}, u32[]{:S(2)}, u32[]{:S(2)}) collective-permute-start(bf16[2,96,1024]{2,1,0:T(8,128)(2,1)S(1)} %pad_maximum_fusion), channel_id=1, source_target_pairs={{2,4},{3,5},{4,2},{5,3},{0,6},{1,7},{6,0},{7,1},{10,12},{11,13},{1... | collective-permute-start | bytes 1179656 | tf_op jit(solution)/shard_map/ppermute | solution.py:32
  47.6 1.5 %collective-permute-start.12 = (bf16[2,2,6,64,128]{4,3,2,1,0:T(8,128)(2,1)S(1)}, bf16[2,2,6,64,128]{4,3,2,1,0:T(8,128)(2,1)S(1)}, u32[]{:S(2)}, u32[]{:S(2)}) collective-permute-start(bf16[2,2,6,64,128]{4,3,2,1,0:T(8,128)(2,1)S(1)} %get-tuple-element.40), channel_id=1, source_target_pairs={{0,1},{1,0},{2,3},{3,2},{4,5},{5,4},{6,7},{7,6},{8,9},{9,8},{10,11... | collective-permute-start | bytes 1179656 | tf_op jit(solution)/shard_map/ppermute | solution.py:27
  49.1 0.5 collective-permute-start.13
  49.6 0.0 collective-permute-start.8
  49.6 2.6 %collective-permute-start.9 = (bf16[2,96,1024]{2,1,0:T(8,128)(2,1)S(1)}, bf16[2,96,1024]{2,1,0:T(8,128)(2,1)S(1)}, u32[]{:S(2)}, u32[]{:S(2)}) collective-permute-start(bf16[2,96,1024]{2,1,0:T(8,128)(2,1)S(1)} %pad_maximum_fusion), channel_id=1, source_target_pairs={{0,4},{1,5},{6,2},{7,3},{8,12},{9,13},{14,10},{15,11},{16,20},{17,... | collective-permute-start | bytes 1179656 | tf_op jit(solution)/shard_map/ppermute | solution.py:32
  52.2 5.4 %collective-permute-done.10.refs_4_ = bf16[2,96,1024]{2,1,0:T(8,128)(2,1)S(1)} collective-permute-done((bf16[2,96,1024]{2,1,0:T(8,128)(2,1)S(1)}, bf16[2,96,1024]{2,1,0:T(8,128)(2,1)S(1)}, u32[]{:S(2)}, u32[]{:S(2)}) %collective-permute-start.10) | collective-permute-done | bytes 393248 | tf_op jit(solution)/shard_map/ppermute | solution.py:32
  57.6 1.3 %collective-permute-start.11 = (bf16[2,96,1024]{2,1,0:T(8,128)(2,1)S(1)}, bf16[2,96,1024]{2,1,0:T(8,128)(2,1)S(1)}, u32[]{:S(2)}, u32[]{:S(2)}) collective-permute-start(bf16[2,96,1024]{2,1,0:T(8,128)(2,1)S(1)} %collective-permute-done.10.refs_4_), channel_id=1, source_target_pairs={{2,0},{3,1},{4,6},{5,7},{10,8},{11,9},{12,14},{13,15},{18,16},{19,... | collective-permute-start | bytes 1179656 | tf_op jit(solution)/shard_map/ppermute | solution.py:32
  58.9 0.7 collective-permute-done.12.refs_0_
  59.7 6.7 %collective-permute-done.13.refs_1_ = bf16[2,2,6,64,128]{4,3,2,1,0:T(8,128)(2,1)S(1)} collective-permute-done((bf16[2,2,6,64,128]{4,3,2,1,0:T(8,128)(2,1)S(1)}, bf16[2,2,6,64,128]{4,3,2,1,0:T(8,128)(2,1)S(1)}, u32[]{:S(2)}, u32[]{:S(2)}) %collective-permute-start.13) | collective-permute-done | bytes 393248 | tf_op jit(solution)/shard_map/ppermute | solution.py:27
  66.3 0.7 lay_out.1.refs_6_
  67.0 5.6 %collective-permute-done.9.refs_3_ = bf16[2,96,1024]{2,1,0:T(8,128)(2,1)S(1)} collective-permute-done((bf16[2,96,1024]{2,1,0:T(8,128)(2,1)S(1)}, bf16[2,96,1024]{2,1,0:T(8,128)(2,1)S(1)}, u32[]{:S(2)}, u32[]{:S(2)}) %collective-permute-start.9) | collective-permute-done | bytes 393248 | tf_op jit(solution)/shard_map/ppermute | solution.py:32
  72.6 1.6 %collective-permute-done.11.refs_5_ = bf16[2,96,1024]{2,1,0:T(8,128)(2,1)S(1)} collective-permute-done((bf16[2,96,1024]{2,1,0:T(8,128)(2,1)S(1)}, bf16[2,96,1024]{2,1,0:T(8,128)(2,1)S(1)}, u32[]{:S(2)}, u32[]{:S(2)}) %collective-permute-start.11) | collective-permute-done | bytes 393248 | tf_op jit(solution)/shard_map/ppermute | solution.py:32
  74.2 1.6 %traces.1 = f32[2,4,12,12]{3,2,1,0:T(8,128)S(1)} custom-call(s32[4]{0:T(128)S(1)} %copy-done.1, bf16[96,1024]{1,0:T(8,128)(2,1)S(1)} %get-tuple-element.28.refs_0_, bf16[96,1024]{1,0:T(8,128)(2,1)S(1)} %collective-permute-done.4.refs_1_, bf16[2,96,1024]{2,1,0:T(8,128)(2,1)S(1)} %collective-permute-done.8.refs_2_, ...), custom_call_target="tpu_custom_call" | custom-call | flops 37748736 | bytes 1572864 | tf_op jit(solution)/shard_map/traces/pallas_call | solution.py:447
  75.9 0.1 collective-permute-start.14
  75.9 1.2 %collective-permute-done.14 = f32[2,4,12,12]{3,2,1,0:T(8,128)S(1)} collective-permute-done((f32[2,4,12,12]{3,2,1,0:T(8,128)S(1)}, f32[2,4,12,12]{3,2,1,0:T(8,128)S(1)}, u32[]{:S(2)}, u32[]{:S(2)}) %collective-permute-start.14) | collective-permute-done | bytes 4640 | tf_op jit(solution)/shard_map/ppermute | solution.py:27
  77.2 1.6 %collective-permute-start.15 = (f32[4,12,12]{2,1,0:T(8,128)S(1)}, f32[4,12,12]{2,1,0:T(8,128)S(1)}, u32[]{:S(2)}, u32[]{:S(2)}) collective-permute-start(f32[4,12,12]{2,1,0:T(8,128)S(1)} %get-tuple-element.45), channel_id=1, source_target_pairs={{0,16},{8,24},{16,0},{24,8},{1,17},{9,25},{17,1},{25,9},{2,18},{10... | collective-permute-start | bytes 6920 | tf_op jit(solution)/shard_map/ppermute | solution.py:27
  78.8 1.5 %collective-permute-start.16 = (f32[4,12,12]{2,1,0:T(8,128)S(1)}, f32[4,12,12]{2,1,0:T(8,128)S(1)}, u32[]{:S(2)}, u32[]{:S(2)}) collective-permute-start(f32[4,12,12]{2,1,0:T(8,128)S(1)} %get-tuple-element.44), channel_id=1, source_target_pairs={{0,1},{1,0},{2,3},{3,2},{4,5},{5,4},{6,7},{7,6},{8,9},{9,8},{10,11... | collective-permute-start | bytes 6920 | tf_op jit(solution)/shard_map/ppermute | solution.py:27
  80.3 0.5 collective-permute-start.17
  80.8 0.4 collective-permute-done.15.refs_1_
  81.2 1.8 %collective-permute-done.16.refs_2_ = f32[4,12,12]{2,1,0:T(8,128)S(1)} collective-permute-done((f32[4,12,12]{2,1,0:T(8,128)S(1)}, f32[4,12,12]{2,1,0:T(8,128)S(1)}, u32[]{:S(2)}, u32[]{:S(2)}) %collective-permute-start.16) | collective-permute-done | bytes 2336 | tf_op jit(solution)/shard_map/ppermute | solution.py:27
  83.0 2.1 %collective-permute-done.17.refs_3_ = f32[4,12,12]{2,1,0:T(8,128)S(1)} collective-permute-done((f32[4,12,12]{2,1,0:T(8,128)S(1)}, f32[4,12,12]{2,1,0:T(8,128)S(1)}, u32[]{:S(2)}, u32[]{:S(2)}) %collective-permute-start.17) | collective-permute-done | bytes 2336 | tf_op jit(solution)/shard_map/ppermute | solution.py:559
  85.1 0.9 %finish.1 = (f32[1,4,6,2,6]{4,3,2,1,0:T(2,128)}, f32[1,4,6,2,6]{4,3,2,1,0:T(2,128)}) custom-call(f32[2,4,12,12]{3,2,1,0:T(8,128)S(1)} %add.86.refs_0_, f32[4,12,12]{2,1,0:T(8,128)S(1)} %collective-permute-done.15.refs_1_, f32[4,12,12]{2,1,0:T(8,128)S(1)} %collective-permute-done.16.refs_2_, f32[4,12,12]{2,1,0:T(8,128)S(1)} %collective-permute-done.17.refs_3_), custom_call_target="tpu_custom_call" | custom-call | tf_op jit(solution)/shard_map/finish/pallas_call | solution.py:492
  (16 shorter events, 0.1 us)
Async XLA Ops:
  0.6 4.3 %collective-permute-start.1 = (bf16[2,3,256,256]{3,2,1,0:T(8,128)(2,1)}, bf16[2,3,256,256]{3,2,1,0:T(8,128)(2,1)S(1)}, u32[]{:S(2)}, u32[]{:S(2)}) collective-permute-start(bf16[2,3,256,256]{3,2,1,0:T(8,128)(2,1)} %bitcast.21), channel_id=1, source_target_pairs={{0,8},{8,0},{16,24},{24,16},{1,9},{9,1},{17,25},{25,17},{2,10},{10... | collective-permute-start | bytes 2359304 | tf_op jit(solution)/shard_map/ppermute | solution.py:27
  1.1 20.9 %collective-permute-start = (bf16[2,3,256,256]{3,2,1,0:T(8,128)(2,1)}, bf16[2,3,256,256]{3,2,1,0:T(8,128)(2,1)S(1)}, u32[]{:S(2)}, u32[]{:S(2)}) collective-permute-start(bf16[2,3,256,256]{3,2,1,0:T(8,128)(2,1)} %bitcast.22), channel_id=1, source_target_pairs={{0,16},{8,24},{16,0},{24,8},{1,17},{9,25},{17,1},{25,9},{2,18},{10... | collective-permute-start | bytes 2359304 | tf_op jit(solution)/shard_map/ppermute | solution.py:27
  5.0 17.1 %copy-start = (bf16[1,4,2,64,256]{4,3,2,1,0:T(8,128)(2,1)S(1)}, bf16[1,4,2,64,256]{4,3,2,1,0:T(8,128)(2,1)}, u32[]{:S(2)}) copy-start(bf16[1,4,2,64,256]{4,3,2,1,0:T(8,128)(2,1)} %param.9) | copy-start | bytes 786436
  5.0 1.2 %copy-start.2 = (bf16[1,2,3,1,256,256]{5,4,3,2,1,0:T(8,128)(2,1)S(1)}, bf16[1,2,3,1,256,256]{5,4,3,2,1,0:T(8,128)(2,1)}, u32[]{:S(2)}) copy-start(bf16[1,2,3,1,256,256]{5,4,3,2,1,0:T(8,128)(2,1)} %param.5) | copy-start | bytes 2359300
  6.2 0.7 copy-start.4
  6.8 17.6 %copy-start.3 = (bf16[1,2,3,1,256,256]{5,4,3,2,1,0:T(8,128)(2,1)S(1)}, bf16[1,2,3,1,256,256]{5,4,3,2,1,0:T(8,128)(2,1)}, u32[]{:S(2)}) copy-start(bf16[1,2,3,1,256,256]{5,4,3,2,1,0:T(8,128)(2,1)} %param.5) | copy-start | bytes 2359300
  6.8 17.6 %copy-start.5 = (s32[6]{0:T(128)S(1)}, s32[6]{0:T(128)}, u32[]{:S(2)}) copy-start(s32[6]{0:T(128)} %refs_0_.3) | copy-start | bytes 76
  22.1 2.3 %collective-permute-start.2 = (bf16[2,3,256,256]{3,2,1,0:T(8,128)(2,1)S(1)}, bf16[2,3,256,256]{3,2,1,0:T(8,128)(2,1)S(1)}, u32[]{:S(2)}, u32[]{:S(2)}) collective-permute-start(bf16[2,3,256,256]{3,2,1,0:T(8,128)(2,1)S(1)} %collective-permute-done.refs_4_), channel_id=1, source_target_pairs={{0,8},{8,0},{16,24},{24,16},{1,9},{9,1},{17,25},{25,17},{2,10},{10... | collective-permute-start | bytes 2359304 | tf_op jit(solution)/shard_map/ppermute | solution.py:27
  22.1 13.7 %collective-permute-start.3 = (bf16[4,2,64,256]{3,2,1,0:T(8,128)(2,1)S(1)}, bf16[4,2,64,256]{3,2,1,0:T(8,128)(2,1)S(1)}, u32[]{:S(2)}, u32[]{:S(2)}) collective-permute-start(bf16[4,2,64,256]{3,2,1,0:T(8,128)(2,1)S(1)} %bitcast.18), channel_id=1, source_target_pairs={{0,16},{8,24},{16,0},{24,8},{1,17},{9,25},{17,1},{25,9},{2,18},{10... | collective-permute-start | bytes 786440 | tf_op jit(solution)/shard_map/ppermute | solution.py:27
  35.8 3.1 %collective-permute-start.5 = (bf16[6,256,256]{2,1,0:T(8,128)(2,1)S(1)}, bf16[6,256,256]{2,1,0:T(8,128)(2,1)S(1)}, u32[]{:S(2)}, u32[]{:S(2)}) collective-permute-start(bf16[6,256,256]{2,1,0:T(8,128)(2,1)S(1)} %get-tuple-element.33.e_ref), channel_id=1, source_target_pairs={{0,8},{8,0},{16,24},{24,16},{1,9},{9,1},{17,25},{25,17},{2,10},{10... | collective-permute-start | bytes 2359304 | tf_op jit(solution)/shard_map/ppermute | solution.py:27
  36.0 2.5 %collective-permute-start.6 = (bf16[4,2,64,256]{3,2,1,0:T(8,128)(2,1)S(1)}, bf16[4,2,64,256]{3,2,1,0:T(8,128)(2,1)S(1)}, u32[]{:S(2)}, u32[]{:S(2)}) collective-permute-start(bf16[4,2,64,256]{3,2,1,0:T(8,128)(2,1)S(1)} %bitcast.19), channel_id=1, source_target_pairs={{0,8},{8,0},{16,24},{24,16},{1,9},{9,1},{17,25},{25,17},{2,10},{10... | collective-permute-start | bytes 786440 | tf_op jit(solution)/shard_map/ppermute | solution.py:27
  36.3 2.5 %collective-permute-start.7 = (bf16[4,2,64,256]{3,2,1,0:T(8,128)(2,1)S(1)}, bf16[4,2,64,256]{3,2,1,0:T(8,128)(2,1)S(1)}, u32[]{:S(2)}, u32[]{:S(2)}) collective-permute-start(bf16[4,2,64,256]{3,2,1,0:T(8,128)(2,1)S(1)} %collective-permute-done.3.refs_2_), channel_id=1, source_target_pairs={{0,8},{8,0},{16,24},{24,16},{1,9},{9,1},{17,25},{25,17},{2,10},{10... | collective-permute-start | bytes 786440 | tf_op jit(solution)/shard_map/ppermute | solution.py:27
  36.5 7.2 %collective-permute-start.4 = (bf16[96,1024]{1,0:T(8,128)(2,1)S(1)}, bf16[96,1024]{1,0:T(8,128)(2,1)S(1)}, u32[]{:S(2)}, u32[]{:S(2)}) collective-permute-start(bf16[96,1024]{1,0:T(8,128)(2,1)S(1)} %get-tuple-element.32), channel_id=1, source_target_pairs={{0,1},{1,0},{2,3},{3,2},{4,5},{5,4},{6,7},{7,6},{8,9},{9,8},{10,11... | collective-permute-start | bytes 589832 | tf_op jit(solution)/shard_map/ppermute | solution.py:27
  43.7 13.9 %collective-permute-start.10 = (bf16[2,96,1024]{2,1,0:T(8,128)(2,1)S(1)}, bf16[2,96,1024]{2,1,0:T(8,128)(2,1)S(1)}, u32[]{:S(2)}, u32[]{:S(2)}) collective-permute-start(bf16[2,96,1024]{2,1,0:T(8,128)(2,1)S(1)} %pad_maximum_fusion), channel_id=1, source_target_pairs={{2,4},{3,5},{4,2},{5,3},{0,6},{1,7},{6,0},{7,1},{10,12},{11,13},{1... | collective-permute-start | bytes 1179656 | tf_op jit(solution)/shard_map/ppermute | solution.py:32
  47.6 12.1 %collective-permute-start.12 = (bf16[2,2,6,64,128]{4,3,2,1,0:T(8,128)(2,1)S(1)}, bf16[2,2,6,64,128]{4,3,2,1,0:T(8,128)(2,1)S(1)}, u32[]{:S(2)}, u32[]{:S(2)}) collective-permute-start(bf16[2,2,6,64,128]{4,3,2,1,0:T(8,128)(2,1)S(1)} %get-tuple-element.40), channel_id=1, source_target_pairs={{0,1},{1,0},{2,3},{3,2},{4,5},{5,4},{6,7},{7,6},{8,9},{9,8},{10,11... | collective-permute-start | bytes 1179656 | tf_op jit(solution)/shard_map/ppermute | solution.py:27
  49.1 17.2 %collective-permute-start.13 = (bf16[2,2,6,64,128]{4,3,2,1,0:T(8,128)(2,1)S(1)}, bf16[2,2,6,64,128]{4,3,2,1,0:T(8,128)(2,1)S(1)}, u32[]{:S(2)}, u32[]{:S(2)}) collective-permute-start(bf16[2,2,6,64,128]{4,3,2,1,0:T(8,128)(2,1)S(1)} %get-tuple-element.41), channel_id=1, source_target_pairs={{0,1},{1,0},{2,3},{3,2},{4,5},{5,4},{6,7},{7,6},{8,9},{9,8},{10,11... | collective-permute-start | bytes 1179656 | tf_op jit(solution)/shard_map/ppermute | solution.py:27
  49.6 17.4 %collective-permute-start.8 = (bf16[2,96,1024]{2,1,0:T(8,128)(2,1)S(1)}, bf16[2,96,1024]{2,1,0:T(8,128)(2,1)S(1)}, u32[]{:S(2)}, u32[]{:S(2)}) collective-permute-start(bf16[2,96,1024]{2,1,0:T(8,128)(2,1)S(1)} %pad_maximum_fusion), channel_id=1, source_target_pairs={{0,2},{1,3},{2,0},{3,1},{4,6},{5,7},{6,4},{7,5},{8,10},{9,11},{10,... | collective-permute-start | bytes 1179656 | tf_op jit(solution)/shard_map/ppermute | solution.py:32
  49.6 23.0 %collective-permute-start.9 = (bf16[2,96,1024]{2,1,0:T(8,128)(2,1)S(1)}, bf16[2,96,1024]{2,1,0:T(8,128)(2,1)S(1)}, u32[]{:S(2)}, u32[]{:S(2)}) collective-permute-start(bf16[2,96,1024]{2,1,0:T(8,128)(2,1)S(1)} %pad_maximum_fusion), channel_id=1, source_target_pairs={{0,4},{1,5},{6,2},{7,3},{8,12},{9,13},{14,10},{15,11},{16,20},{17,... | collective-permute-start | bytes 1179656 | tf_op jit(solution)/shard_map/ppermute | solution.py:32
  57.6 16.6 %collective-permute-start.11 = (bf16[2,96,1024]{2,1,0:T(8,128)(2,1)S(1)}, bf16[2,96,1024]{2,1,0:T(8,128)(2,1)S(1)}, u32[]{:S(2)}, u32[]{:S(2)}) collective-permute-start(bf16[2,96,1024]{2,1,0:T(8,128)(2,1)S(1)} %collective-permute-done.10.refs_4_), channel_id=1, source_target_pairs={{2,0},{3,1},{4,6},{5,7},{10,8},{11,9},{12,14},{13,15},{18,16},{19,... | collective-permute-start | bytes 1179656 | tf_op jit(solution)/shard_map/ppermute | solution.py:32
  66.3 7.9 %copy-start.1 = (s32[4]{0:T(128)S(1)}, s32[4]{0:T(128)}, u32[]{:S(2)}) copy-start(s32[4]{0:T(128)} %times_ref.1) | copy-start | bytes 52
  75.9 1.3 %collective-permute-start.14 = (f32[2,4,12,12]{3,2,1,0:T(8,128)S(1)}, f32[2,4,12,12]{3,2,1,0:T(8,128)S(1)}, u32[]{:S(2)}, u32[]{:S(2)}) collective-permute-start(f32[2,4,12,12]{3,2,1,0:T(8,128)S(1)} %traces.1), channel_id=1, source_target_pairs={{0,8},{8,0},{16,24},{24,16},{1,9},{9,1},{17,25},{25,17},{2,10},{10... | collective-permute-start | bytes 13832 | tf_op jit(solution)/shard_map/ppermute | solution.py:27
  77.2 4.0 %collective-permute-start.15 = (f32[4,12,12]{2,1,0:T(8,128)S(1)}, f32[4,12,12]{2,1,0:T(8,128)S(1)}, u32[]{:S(2)}, u32[]{:S(2)}) collective-permute-start(f32[4,12,12]{2,1,0:T(8,128)S(1)} %get-tuple-element.45), channel_id=1, source_target_pairs={{0,16},{8,24},{16,0},{24,8},{1,17},{9,25},{17,1},{25,9},{2,18},{10... | collective-permute-start | bytes 6920 | tf_op jit(solution)/shard_map/ppermute | solution.py:27
  78.8 4.2 %collective-permute-start.16 = (f32[4,12,12]{2,1,0:T(8,128)S(1)}, f32[4,12,12]{2,1,0:T(8,128)S(1)}, u32[]{:S(2)}, u32[]{:S(2)}) collective-permute-start(f32[4,12,12]{2,1,0:T(8,128)S(1)} %get-tuple-element.44), channel_id=1, source_target_pairs={{0,1},{1,0},{2,3},{3,2},{4,5},{5,4},{6,7},{7,6},{8,9},{9,8},{10,11... | collective-permute-start | bytes 6920 | tf_op jit(solution)/shard_map/ppermute | solution.py:27
  80.3 4.8 %collective-permute-start.17 = (f32[4,12,12]{2,1,0:T(8,128)S(1)}, f32[4,12,12]{2,1,0:T(8,128)S(1)}, u32[]{:S(2)}, u32[]{:S(2)}) collective-permute-start(f32[4,12,12]{2,1,0:T(8,128)S(1)} %get-tuple-element.44), channel_id=1, source_target_pairs={{0,17},{1,16},{2,19},{3,18},{4,21},{5,20},{6,23},{7,22},{8,25},{9,... | collective-permute-start | bytes 6920 | tf_op jit(solution)/shard_map/ppermute | solution.py:559

commit v5 on v4

--- a/solution.py
+++ b/solution.py
@@ -106,7 +106,7 @@
     for m in range(held):
         slabs[m, :, :, pl.ds(0, PLANE), :] = slab_refs[m][...]
         slabs[m, :, :, pl.ds(PLANE, LX), :] = slab_refs[m][:, :, pl.ds(0, LX), :]
-    acc[...] = jnp.zeros_like(acc)
+    acc[...] = prior_ref[...] if late else jnp.zeros_like(acc)
     if not late:
         upright = phase_ref[...].T
         for o in range(operators):
@@ -158,6 +158,17 @@
 
         found = lax.fori_loop(0, operators, collect, jnp.int32(0))
 
+        @pl.when((found > 0) & (m >= near if late else m >= 0))
+        def _():
+            for colour in range(colours):
+                for part in range(2):
+                    for begin in range(0, PLANE, CHUNK):
+                        rows = slabs[m, part, colour, pl.ds(begin, CHUNK), :].astype(F32)
+                        rows = pltpu.roll(rows.reshape(CHUNK // LX, LX, vectors), LX - 1, 1)
+                        slabs[held, part, colour, pl.ds(begin, CHUNK), :] = rows.reshape(
+                            CHUNK, vectors
+                        ).astype(BF16)
+
         @pl.when(found > 0)
         def _():
             for colour in range(colours):
@@ -169,20 +180,6 @@
                     lower = pl.ds(half_rows, half_rows)
                     turned[colour, pl.ds(0, half_rows), pl.ds(part * PLANE, PLANE)] = flat
                     turned[colour, lower, pl.ds((1 - part) * PLANE, PLANE)] = same
-
-        @pl.when((found > 0) & (m >= near if late else m >= 0))
-        def _():
-            for colour in range(colours):
-                for part in range(2):
-                    for begin in range(0, PLANE, CHUNK):
-                        rows = slabs[m, part, colour, pl.ds(begin, CHUNK), :].astype(F32)
-                        rows = pltpu.roll(rows.reshape(CHUNK // LX, LX, vectors), LX - 1, 1)
-                        slabs[held, part, colour, pl.ds(begin, CHUNK), :] = rows.reshape(
-                            CHUNK, vectors
-                        ).astype(BF16)
-
-        @pl.when(found > 0)
-        def _():
             for colour in range(colours):
                 turn_phases(todo[0], mixed_a, colour)
 
@@ -206,11 +203,11 @@
         first = pl.multiple_of(me // 2 * block_rows, block_rows)
         half = lax.rem(lax.axis_index("tm"), 2)
         for o in range(operators):
-            acc_out[o] = (acc[o] + prior_ref[o]).astype(BF16)
+            acc_out[o] = acc[o].astype(BF16)
         for part in range(2):
             for o in range(operators):
                 rows = pl.ds(part * half_rows + first, block_rows)
-                own = acc[o, rows, :] + prior_ref[o, rows, :]
+                own = acc[o, rows, :]
                 at = pl.ds((part * operators + o) * block_rows, block_rows)
                 wide[0, at, :] = own[:, :LANES]
                 wide[1, at, :] = own[:, LANES:]

time: 85.7 us -> 85.1 us (level)
  waiting for transfers between devices: 36 us -> 35.1 us
    ppermute x13, waiting for transfers between devices: 21.3 us -> 20.3 us  [swap_bit(): return lax.ppermute(block, axis, [(i, i ^ mask) for i in range(count)])]
where the time goes in v5:
time: 85.1 us; the launch traced here: 84.8 us
  waiting for transfers between devices  35.1 us (41%)
  Pallas kernels  25.1 us (29%)
  starting transfers between devices  20.7 us (24%)
  local copies, waits for them, and re-layouts  2.66 us (3%)
    ppermute x13, waiting for transfers between devices, swap_bit(): return lax.ppermute(block, axis, [(i, i ^ mask) for i in range(count)])  20.3 us
    pallas_call x2, Pallas kernels, elementals(): pl.pallas_call(functools.partial(elemental_kernel, held, near, late, bloc...  18.8 us
    ppermute x4, waiting for transfers between devices, along_line(): return lax.ppermute(block, 'tm', route)  12.7 us
    ppermute x13, starting transfers between devices, swap_bit(): return lax.ppermute(block, axis, [(i, i ^ mask) for i in range(count)])  12.5 us
    ppermute x4, starting transfers between devices, along_line(): return lax.ppermute(block, 'tm', route)  7.74 us
    pallas_call x1, Pallas kernels, both_sides(): pl.pallas_call(functools.partial(both_kernel, blocks), out_shape=(piece,)...  3.11 us
    ppermute x1, waiting for transfers between devices, across(): return lax.ppermute(block, ('space', 'tm'), route)  2.09 us
    unnamed x12, local copies, waits for them, and re-layouts  1.84 us
  transfers between devices with their start and end apart: 18, of which 14 were waited for; matrix products, arithmetic and copies ran while one was open for 1% of the time, Pallas kernels for 27%

profile of v5, /device:TPU:0, one launch (start us, length us, event | category | flops | bytes accessed | tf_op | source)
XLA Modules:
  0.0 84.8 jit_solution(14494779716917082565)
XLA Ops:
  0.6 0.5 collective-permute-start.1
  1.1 2.6 %collective-permute-start = (bf16[2,3,256,256]{3,2,1,0:T(8,128)(2,1)}, bf16[2,3,256,256]{3,2,1,0:T(8,128)(2,1)S(1)}, u32[]{:S(2)}, u32[]{:S(2)}) collective-permute-start(bf16[2,3,256,256]{3,2,1,0:T(8,128)(2,1)} %bitcast.22), channel_id=1, source_target_pairs={{0,16},{8,24},{16,0},{24,8},{1,17},{9,25},{17,1},{25,9},{2,18},{10... | collective-permute-start | bytes 2359304 | tf_op jit(solution)/shard_map/ppermute | solution.py:27
  3.7 0.8 slice_bitcast_fusion.3
  4.5 0.3 fusion.13
  4.9 0.1 fusion.11
  5.0 0.0 copy-start
  5.0 0.0 copy-start.2
  5.0 1.2 %copy-done.2 = bf16[1,2,3,1,256,256]{5,4,3,2,1,0:T(8,128)(2,1)S(1)} copy-done((bf16[1,2,3,1,256,256]{5,4,3,2,1,0:T(8,128)(2,1)S(1)}, bf16[1,2,3,1,256,256]{5,4,3,2,1,0:T(8,128)(2,1)}, u32[]{:S(2)}) %copy-start.2) | copy-done | bytes 786456
  6.2 0.7 copy-done.4
  6.8 8.6 %elementals_early.1 = (f32[6,256,256]{2,1,0:T(8,128)S(1)}, f32[6,2,256,128]{3,2,1,0:T(8,128)S(1)}) custom-call(s32[6]{0:T(128)S(1)} %copy-done.4, f32[2,4,6]{2,1,0:T(4,128)S(1)} %pad_maximum_fusion.2.refs_1_, bf16[2,3,256,256]{3,2,1,0:T(8,128)(2,1)S(1)} %bitcast.23, bf16[2,3,256,256]{3,2,1,0:T(8,128)(2,1)S(1)} %collective-permute-done.1.refs_3_, ...), custom_call_target="tpu_custom_call" | custom-call | flops 4831838208 | bytes 1572864 | tf_op jit(solution)/shard_map/elementals_early/pallas_call | solution.py:244
  15.4 6.6 %collective-permute-done.refs_4_ = bf16[2,3,256,256]{3,2,1,0:T(8,128)(2,1)S(1)} collective-permute-done((bf16[2,3,256,256]{3,2,1,0:T(8,128)(2,1)}, bf16[2,3,256,256]{3,2,1,0:T(8,128)(2,1)S(1)}, u32[]{:S(2)}, u32[]{:S(2)}) %collective-permute-start) | collective-permute-done | bytes 786464 | tf_op jit(solution)/shard_map/ppermute | solution.py:27
  22.1 0.0 collective-permute-start.2
  22.1 1.8 %collective-permute-start.3 = (bf16[4,2,64,256]{3,2,1,0:T(8,128)(2,1)S(1)}, bf16[4,2,64,256]{3,2,1,0:T(8,128)(2,1)S(1)}, u32[]{:S(2)}, u32[]{:S(2)}) collective-permute-start(bf16[4,2,64,256]{3,2,1,0:T(8,128)(2,1)S(1)} %bitcast.18), channel_id=1, source_target_pairs={{0,16},{8,24},{16,0},{24,8},{1,17},{9,25},{17,1},{25,9},{2,18},{10... | collective-permute-start | bytes 786440 | tf_op jit(solution)/shard_map/ppermute | solution.py:27
  23.9 0.5 collective-permute-done.2.refs_5_
  24.4 10.2 %elementals_late.1 = (bf16[6,256,256]{2,1,0:T(8,128)(2,1)S(1)}, bf16[96,1024]{1,0:T(8,128)(2,1)S(1)}, bf16[96,1024]{1,0:T(8,128)(2,1)S(1)}) custom-call(s32[6]{0:T(128)S(1)} %copy-done.5, f32[2,4,6]{2,1,0:T(4,128)S(1)} %pad_maximum_fusion.2.refs_1_, bf16[2,3,256,256]{3,2,1,0:T(8,128)(2,1)S(1)} %bitcast.24, ...), custom_call_target="tpu_custom_call" | custom-call | flops 9663676416 | bytes 3145728 | tf_op jit(solution)/shard_map/elementals_late/pallas_call | solution.py:244
  34.5 0.0 collective-permute-done.3.refs_2_
  34.5 0.2 collective-permute-start.5
  34.8 0.4 collective-permute-start.6
  35.1 0.1 collective-permute-start.7
  35.3 1.7 %collective-permute-start.4 = (bf16[96,1024]{1,0:T(8,128)(2,1)S(1)}, bf16[96,1024]{1,0:T(8,128)(2,1)S(1)}, u32[]{:S(2)}, u32[]{:S(2)}) collective-permute-start(bf16[96,1024]{1,0:T(8,128)(2,1)S(1)} %get-tuple-element.32), channel_id=1, source_target_pairs={{0,1},{1,0},{2,3},{3,2},{4,5},{5,4},{6,7},{7,6},{8,9},{9,8},{10,11... | collective-permute-start | bytes 589832 | tf_op jit(solution)/shard_map/ppermute | solution.py:27
  37.0 0.3 collective-permute-done.6.refs_1_
  37.3 0.4 collective-permute-done.7.refs_3_
  37.6 0.0 collective-permute-done.5.other_ref
  37.7 3.1 %both_sides.1 = (bf16[4,2,6,64,128]{4,3,2,1,0:T(8,128)(2,1)S(1)}, bf16[2,2,6,64,128]{4,3,2,1,0:T(8,128)(2,1)S(1)}, bf16[2,2,6,64,128]{4,3,2,1,0:T(8,128)(2,1)S(1)}) custom-call(bf16[6,256,256]{2,1,0:T(8,128)(2,1)S(1)} %get-tuple-element.33.e_ref, bf16[6,256,256]{2,1,0:T(8,128)(2,1)S(1)} %collective-permute-done.5.other_ref, ...), custom_call_target="tpu_custom_call" | custom-call | tf_op jit(solution)/shard_map/both_sides/pallas_call | solution.py:340
  40.8 1.7 %collective-permute-done.4.refs_1_ = bf16[96,1024]{1,0:T(8,128)(2,1)S(1)} collective-permute-done((bf16[96,1024]{1,0:T(8,128)(2,1)S(1)}, bf16[96,1024]{1,0:T(8,128)(2,1)S(1)}, u32[]{:S(2)}, u32[]{:S(2)}) %collective-permute-start.4) | collective-permute-done | bytes 196640 | tf_op jit(solution)/shard_map/ppermute | solution.py:27
  42.5 3.9 %collective-permute-start.10 = (bf16[2,96,1024]{2,1,0:T(8,128)(2,1)S(1)}, bf16[2,96,1024]{2,1,0:T(8,128)(2,1)S(1)}, u32[]{:S(2)}, u32[]{:S(2)}) collective-permute-start(bf16[2,96,1024]{2,1,0:T(8,128)(2,1)S(1)} %pad_maximum_fusion), channel_id=1, source_target_pairs={{2,4},{3,5},{4,2},{5,3},{0,6},{1,7},{6,0},{7,1},{10,12},{11,13},{1... | collective-permute-start | bytes 1179656 | tf_op jit(solution)/shard_map/ppermute | solution.py:32
  46.4 1.5 %collective-permute-start.12 = (bf16[2,2,6,64,128]{4,3,2,1,0:T(8,128)(2,1)S(1)}, bf16[2,2,6,64,128]{4,3,2,1,0:T(8,128)(2,1)S(1)}, u32[]{:S(2)}, u32[]{:S(2)}) collective-permute-start(bf16[2,2,6,64,128]{4,3,2,1,0:T(8,128)(2,1)S(1)} %get-tuple-element.40), channel_id=1, source_target_pairs={{0,1},{1,0},{2,3},{3,2},{4,5},{5,4},{6,7},{7,6},{8,9},{9,8},{10,11... | collective-permute-start | bytes 1179656 | tf_op jit(solution)/shard_map/ppermute | solution.py:27
  47.9 0.5 collective-permute-start.13
  48.4 0.0 collective-permute-start.8
  48.4 2.6 %collective-permute-start.9 = (bf16[2,96,1024]{2,1,0:T(8,128)(2,1)S(1)}, bf16[2,96,1024]{2,1,0:T(8,128)(2,1)S(1)}, u32[]{:S(2)}, u32[]{:S(2)}) collective-permute-start(bf16[2,96,1024]{2,1,0:T(8,128)(2,1)S(1)} %pad_maximum_fusion), channel_id=1, source_target_pairs={{0,4},{1,5},{6,2},{7,3},{8,12},{9,13},{14,10},{15,11},{16,20},{17,... | collective-permute-start | bytes 1179656 | tf_op jit(solution)/shard_map/ppermute | solution.py:32
  51.0 5.4 %collective-permute-done.10.refs_4_ = bf16[2,96,1024]{2,1,0:T(8,128)(2,1)S(1)} collective-permute-done((bf16[2,96,1024]{2,1,0:T(8,128)(2,1)S(1)}, bf16[2,96,1024]{2,1,0:T(8,128)(2,1)S(1)}, u32[]{:S(2)}, u32[]{:S(2)}) %collective-permute-start.10) | collective-permute-done | bytes 393248 | tf_op jit(solution)/shard_map/ppermute | solution.py:32
  56.4 1.3 %collective-permute-start.11 = (bf16[2,96,1024]{2,1,0:T(8,128)(2,1)S(1)}, bf16[2,96,1024]{2,1,0:T(8,128)(2,1)S(1)}, u32[]{:S(2)}, u32[]{:S(2)}) collective-permute-start(bf16[2,96,1024]{2,1,0:T(8,128)(2,1)S(1)} %collective-permute-done.10.refs_4_), channel_id=1, source_target_pairs={{2,0},{3,1},{4,6},{5,7},{10,8},{11,9},{12,14},{13,15},{18,16},{19,... | collective-permute-start | bytes 1179656 | tf_op jit(solution)/shard_map/ppermute | solution.py:32
  57.7 0.7 collective-permute-done.12.refs_0_
  58.4 6.7 %collective-permute-done.13.refs_1_ = bf16[2,2,6,64,128]{4,3,2,1,0:T(8,128)(2,1)S(1)} collective-permute-done((bf16[2,2,6,64,128]{4,3,2,1,0:T(8,128)(2,1)S(1)}, bf16[2,2,6,64,128]{4,3,2,1,0:T(8,128)(2,1)S(1)}, u32[]{:S(2)}, u32[]{:S(2)}) %collective-permute-start.13) | collective-permute-done | bytes 393248 | tf_op jit(solution)/shard_map/ppermute | solution.py:27
  65.1 0.7 lay_out.1.refs_6_
  65.8 0.0 collective-permute-done.8.refs_2_
  65.8 5.6 %collective-permute-done.9.refs_3_ = bf16[2,96,1024]{2,1,0:T(8,128)(2,1)S(1)} collective-permute-done((bf16[2,96,1024]{2,1,0:T(8,128)(2,1)S(1)}, bf16[2,96,1024]{2,1,0:T(8,128)(2,1)S(1)}, u32[]{:S(2)}, u32[]{:S(2)}) %collective-permute-start.9) | collective-permute-done | bytes 393248 | tf_op jit(solution)/shard_map/ppermute | solution.py:32
  71.4 1.7 %collective-permute-done.11.refs_5_ = bf16[2,96,1024]{2,1,0:T(8,128)(2,1)S(1)} collective-permute-done((bf16[2,96,1024]{2,1,0:T(8,128)(2,1)S(1)}, bf16[2,96,1024]{2,1,0:T(8,128)(2,1)S(1)}, u32[]{:S(2)}, u32[]{:S(2)}) %collective-permute-start.11) | collective-permute-done | bytes 393248 | tf_op jit(solution)/shard_map/ppermute | solution.py:32
  73.0 1.6 %traces.1 = f32[2,4,12,12]{3,2,1,0:T(8,128)S(1)} custom-call(s32[4]{0:T(128)S(1)} %copy-done.1, bf16[96,1024]{1,0:T(8,128)(2,1)S(1)} %get-tuple-element.28.refs_0_, bf16[96,1024]{1,0:T(8,128)(2,1)S(1)} %collective-permute-done.4.refs_1_, bf16[2,96,1024]{2,1,0:T(8,128)(2,1)S(1)} %collective-permute-done.8.refs_2_, ...), custom_call_target="tpu_custom_call" | custom-call | flops 37748736 | bytes 1572864 | tf_op jit(solution)/shard_map/traces/pallas_call | solution.py:444
  74.7 0.1 collective-permute-start.14
  74.8 1.2 %collective-permute-done.14 = f32[2,4,12,12]{3,2,1,0:T(8,128)S(1)} collective-permute-done((f32[2,4,12,12]{3,2,1,0:T(8,128)S(1)}, f32[2,4,12,12]{3,2,1,0:T(8,128)S(1)}, u32[]{:S(2)}, u32[]{:S(2)}) %collective-permute-start.14) | collective-permute-done | bytes 4640 | tf_op jit(solution)/shard_map/ppermute | solution.py:27
  76.0 1.6 %collective-permute-start.15 = (f32[4,12,12]{2,1,0:T(8,128)S(1)}, f32[4,12,12]{2,1,0:T(8,128)S(1)}, u32[]{:S(2)}, u32[]{:S(2)}) collective-permute-start(f32[4,12,12]{2,1,0:T(8,128)S(1)} %get-tuple-element.45), channel_id=1, source_target_pairs={{0,16},{8,24},{16,0},{24,8},{1,17},{9,25},{17,1},{25,9},{2,18},{10... | collective-permute-start | bytes 6920 | tf_op jit(solution)/shard_map/ppermute | solution.py:27
  77.6 1.5 %collective-permute-start.16 = (f32[4,12,12]{2,1,0:T(8,128)S(1)}, f32[4,12,12]{2,1,0:T(8,128)S(1)}, u32[]{:S(2)}, u32[]{:S(2)}) collective-permute-start(f32[4,12,12]{2,1,0:T(8,128)S(1)} %get-tuple-element.44), channel_id=1, source_target_pairs={{0,1},{1,0},{2,3},{3,2},{4,5},{5,4},{6,7},{7,6},{8,9},{9,8},{10,11... | collective-permute-start | bytes 6920 | tf_op jit(solution)/shard_map/ppermute | solution.py:27
  79.1 0.5 collective-permute-start.17
  79.6 0.4 collective-permute-done.15.refs_1_
  80.0 1.8 %collective-permute-done.16.refs_2_ = f32[4,12,12]{2,1,0:T(8,128)S(1)} collective-permute-done((f32[4,12,12]{2,1,0:T(8,128)S(1)}, f32[4,12,12]{2,1,0:T(8,128)S(1)}, u32[]{:S(2)}, u32[]{:S(2)}) %collective-permute-start.16) | collective-permute-done | bytes 2336 | tf_op jit(solution)/shard_map/ppermute | solution.py:27
  81.8 2.1 %collective-permute-done.17.refs_3_ = f32[4,12,12]{2,1,0:T(8,128)S(1)} collective-permute-done((f32[4,12,12]{2,1,0:T(8,128)S(1)}, f32[4,12,12]{2,1,0:T(8,128)S(1)}, u32[]{:S(2)}, u32[]{:S(2)}) %collective-permute-start.17) | collective-permute-done | bytes 2336 | tf_op jit(solution)/shard_map/ppermute | solution.py:556
  83.9 0.9 %finish.1 = (f32[1,4,6,2,6]{4,3,2,1,0:T(2,128)}, f32[1,4,6,2,6]{4,3,2,1,0:T(2,128)}) custom-call(f32[2,4,12,12]{3,2,1,0:T(8,128)S(1)} %add.86.refs_0_, f32[4,12,12]{2,1,0:T(8,128)S(1)} %collective-permute-done.15.refs_1_, f32[4,12,12]{2,1,0:T(8,128)S(1)} %collective-permute-done.16.refs_2_, f32[4,12,12]{2,1,0:T(8,128)S(1)} %collective-permute-done.17.refs_3_), custom_call_target="tpu_custom_call" | custom-call | tf_op jit(solution)/shard_map/finish/pallas_call | solution.py:489
  (16 shorter events, 0.1 us)
Async XLA Ops:
  0.6 4.3 %collective-permute-start.1 = (bf16[2,3,256,256]{3,2,1,0:T(8,128)(2,1)}, bf16[2,3,256,256]{3,2,1,0:T(8,128)(2,1)S(1)}, u32[]{:S(2)}, u32[]{:S(2)}) collective-permute-start(bf16[2,3,256,256]{3,2,1,0:T(8,128)(2,1)} %bitcast.21), channel_id=1, source_target_pairs={{0,8},{8,0},{16,24},{24,16},{1,9},{9,1},{17,25},{25,17},{2,10},{10... | collective-permute-start | bytes 2359304 | tf_op jit(solution)/shard_map/ppermute | solution.py:27
  1.1 20.9 %collective-permute-start = (bf16[2,3,256,256]{3,2,1,0:T(8,128)(2,1)}, bf16[2,3,256,256]{3,2,1,0:T(8,128)(2,1)S(1)}, u32[]{:S(2)}, u32[]{:S(2)}) collective-permute-start(bf16[2,3,256,256]{3,2,1,0:T(8,128)(2,1)} %bitcast.22), channel_id=1, source_target_pairs={{0,16},{8,24},{16,0},{24,8},{1,17},{9,25},{17,1},{25,9},{2,18},{10... | collective-permute-start | bytes 2359304 | tf_op jit(solution)/shard_map/ppermute | solution.py:27
  5.0 17.1 %copy-start = (bf16[1,4,2,64,256]{4,3,2,1,0:T(8,128)(2,1)S(1)}, bf16[1,4,2,64,256]{4,3,2,1,0:T(8,128)(2,1)}, u32[]{:S(2)}) copy-start(bf16[1,4,2,64,256]{4,3,2,1,0:T(8,128)(2,1)} %param.9) | copy-start | bytes 786436
  5.0 1.2 %copy-start.2 = (bf16[1,2,3,1,256,256]{5,4,3,2,1,0:T(8,128)(2,1)S(1)}, bf16[1,2,3,1,256,256]{5,4,3,2,1,0:T(8,128)(2,1)}, u32[]{:S(2)}) copy-start(bf16[1,2,3,1,256,256]{5,4,3,2,1,0:T(8,128)(2,1)} %param.5) | copy-start | bytes 2359300
  6.2 0.7 copy-start.4
  6.8 17.6 %copy-start.3 = (bf16[1,2,3,1,256,256]{5,4,3,2,1,0:T(8,128)(2,1)S(1)}, bf16[1,2,3,1,256,256]{5,4,3,2,1,0:T(8,128)(2,1)}, u32[]{:S(2)}) copy-start(bf16[1,2,3,1,256,256]{5,4,3,2,1,0:T(8,128)(2,1)} %param.5) | copy-start | bytes 2359300
  6.8 17.6 %copy-start.5 = (s32[6]{0:T(128)S(1)}, s32[6]{0:T(128)}, u32[]{:S(2)}) copy-start(s32[6]{0:T(128)} %refs_0_.3) | copy-start | bytes 76
  22.1 2.3 %collective-permute-start.2 = (bf16[2,3,256,256]{3,2,1,0:T(8,128)(2,1)S(1)}, bf16[2,3,256,256]{3,2,1,0:T(8,128)(2,1)S(1)}, u32[]{:S(2)}, u32[]{:S(2)}) collective-permute-start(bf16[2,3,256,256]{3,2,1,0:T(8,128)(2,1)S(1)} %collective-permute-done.refs_4_), channel_id=1, source_target_pairs={{0,8},{8,0},{16,24},{24,16},{1,9},{9,1},{17,25},{25,17},{2,10},{10... | collective-permute-start | bytes 2359304 | tf_op jit(solution)/shard_map/ppermute | solution.py:27
  22.1 12.4 %collective-permute-start.3 = (bf16[4,2,64,256]{3,2,1,0:T(8,128)(2,1)S(1)}, bf16[4,2,64,256]{3,2,1,0:T(8,128)(2,1)S(1)}, u32[]{:S(2)}, u32[]{:S(2)}) collective-permute-start(bf16[4,2,64,256]{3,2,1,0:T(8,128)(2,1)S(1)} %bitcast.18), channel_id=1, source_target_pairs={{0,16},{8,24},{16,0},{24,8},{1,17},{9,25},{17,1},{25,9},{2,18},{10... | collective-permute-start | bytes 786440 | tf_op jit(solution)/shard_map/ppermute | solution.py:27
  34.5 3.1 %collective-permute-start.5 = (bf16[6,256,256]{2,1,0:T(8,128)(2,1)S(1)}, bf16[6,256,256]{2,1,0:T(8,128)(2,1)S(1)}, u32[]{:S(2)}, u32[]{:S(2)}) collective-permute-start(bf16[6,256,256]{2,1,0:T(8,128)(2,1)S(1)} %get-tuple-element.33.e_ref), channel_id=1, source_target_pairs={{0,8},{8,0},{16,24},{24,16},{1,9},{9,1},{17,25},{25,17},{2,10},{10... | collective-permute-start | bytes 2359304 | tf_op jit(solution)/shard_map/ppermute | solution.py:27
  34.8 2.5 %collective-permute-start.6 = (bf16[4,2,64,256]{3,2,1,0:T(8,128)(2,1)S(1)}, bf16[4,2,64,256]{3,2,1,0:T(8,128)(2,1)S(1)}, u32[]{:S(2)}, u32[]{:S(2)}) collective-permute-start(bf16[4,2,64,256]{3,2,1,0:T(8,128)(2,1)S(1)} %bitcast.19), channel_id=1, source_target_pairs={{0,8},{8,0},{16,24},{24,16},{1,9},{9,1},{17,25},{25,17},{2,10},{10... | collective-permute-start | bytes 786440 | tf_op jit(solution)/shard_map/ppermute | solution.py:27
  35.1 2.5 %collective-permute-start.7 = (bf16[4,2,64,256]{3,2,1,0:T(8,128)(2,1)S(1)}, bf16[4,2,64,256]{3,2,1,0:T(8,128)(2,1)S(1)}, u32[]{:S(2)}, u32[]{:S(2)}) collective-permute-start(bf16[4,2,64,256]{3,2,1,0:T(8,128)(2,1)S(1)} %collective-permute-done.3.refs_2_), channel_id=1, source_target_pairs={{0,8},{8,0},{16,24},{24,16},{1,9},{9,1},{17,25},{25,17},{2,10},{10... | collective-permute-start | bytes 786440 | tf_op jit(solution)/shard_map/ppermute | solution.py:27
  35.3 7.2 %collective-permute-start.4 = (bf16[96,1024]{1,0:T(8,128)(2,1)S(1)}, bf16[96,1024]{1,0:T(8,128)(2,1)S(1)}, u32[]{:S(2)}, u32[]{:S(2)}) collective-permute-start(bf16[96,1024]{1,0:T(8,128)(2,1)S(1)} %get-tuple-element.32), channel_id=1, source_target_pairs={{0,1},{1,0},{2,3},{3,2},{4,5},{5,4},{6,7},{7,6},{8,9},{9,8},{10,11... | collective-permute-start | bytes 589832 | tf_op jit(solution)/shard_map/ppermute | solution.py:27
  42.5 13.9 %collective-permute-start.10 = (bf16[2,96,1024]{2,1,0:T(8,128)(2,1)S(1)}, bf16[2,96,1024]{2,1,0:T(8,128)(2,1)S(1)}, u32[]{:S(2)}, u32[]{:S(2)}) collective-permute-start(bf16[2,96,1024]{2,1,0:T(8,128)(2,1)S(1)} %pad_maximum_fusion), channel_id=1, source_target_pairs={{2,4},{3,5},{4,2},{5,3},{0,6},{1,7},{6,0},{7,1},{10,12},{11,13},{1... | collective-permute-start | bytes 1179656 | tf_op jit(solution)/shard_map/ppermute | solution.py:32
  46.4 12.1 %collective-permute-start.12 = (bf16[2,2,6,64,128]{4,3,2,1,0:T(8,128)(2,1)S(1)}, bf16[2,2,6,64,128]{4,3,2,1,0:T(8,128)(2,1)S(1)}, u32[]{:S(2)}, u32[]{:S(2)}) collective-permute-start(bf16[2,2,6,64,128]{4,3,2,1,0:T(8,128)(2,1)S(1)} %get-tuple-element.40), channel_id=1, source_target_pairs={{0,1},{1,0},{2,3},{3,2},{4,5},{5,4},{6,7},{7,6},{8,9},{9,8},{10,11... | collective-permute-start | bytes 1179656 | tf_op jit(solution)/shard_map/ppermute | solution.py:27
  47.9 17.2 %collective-permute-start.13 = (bf16[2,2,6,64,128]{4,3,2,1,0:T(8,128)(2,1)S(1)}, bf16[2,2,6,64,128]{4,3,2,1,0:T(8,128)(2,1)S(1)}, u32[]{:S(2)}, u32[]{:S(2)}) collective-permute-start(bf16[2,2,6,64,128]{4,3,2,1,0:T(8,128)(2,1)S(1)} %get-tuple-element.41), channel_id=1, source_target_pairs={{0,1},{1,0},{2,3},{3,2},{4,5},{5,4},{6,7},{7,6},{8,9},{9,8},{10,11... | collective-permute-start | bytes 1179656 | tf_op jit(solution)/shard_map/ppermute | solution.py:27
  48.4 17.4 %collective-permute-start.8 = (bf16[2,96,1024]{2,1,0:T(8,128)(2,1)S(1)}, bf16[2,96,1024]{2,1,0:T(8,128)(2,1)S(1)}, u32[]{:S(2)}, u32[]{:S(2)}) collective-permute-start(bf16[2,96,1024]{2,1,0:T(8,128)(2,1)S(1)} %pad_maximum_fusion), channel_id=1, source_target_pairs={{0,2},{1,3},{2,0},{3,1},{4,6},{5,7},{6,4},{7,5},{8,10},{9,11},{10,... | collective-permute-start | bytes 1179656 | tf_op jit(solution)/shard_map/ppermute | solution.py:32
  48.4 23.0 %collective-permute-start.9 = (bf16[2,96,1024]{2,1,0:T(8,128)(2,1)S(1)}, bf16[2,96,1024]{2,1,0:T(8,128)(2,1)S(1)}, u32[]{:S(2)}, u32[]{:S(2)}) collective-permute-start(bf16[2,96,1024]{2,1,0:T(8,128)(2,1)S(1)} %pad_maximum_fusion), channel_id=1, source_target_pairs={{0,4},{1,5},{6,2},{7,3},{8,12},{9,13},{14,10},{15,11},{16,20},{17,... | collective-permute-start | bytes 1179656 | tf_op jit(solution)/shard_map/ppermute | solution.py:32
  56.4 16.6 %collective-permute-start.11 = (bf16[2,96,1024]{2,1,0:T(8,128)(2,1)S(1)}, bf16[2,96,1024]{2,1,0:T(8,128)(2,1)S(1)}, u32[]{:S(2)}, u32[]{:S(2)}) collective-permute-start(bf16[2,96,1024]{2,1,0:T(8,128)(2,1)S(1)} %collective-permute-done.10.refs_4_), channel_id=1, source_target_pairs={{2,0},{3,1},{4,6},{5,7},{10,8},{11,9},{12,14},{13,15},{18,16},{19,... | collective-permute-start | bytes 1179656 | tf_op jit(solution)/shard_map/ppermute | solution.py:32
  65.1 8.0 %copy-start.1 = (s32[4]{0:T(128)S(1)}, s32[4]{0:T(128)}, u32[]{:S(2)}) copy-start(s32[4]{0:T(128)} %times_ref.1) | copy-start | bytes 52
  74.7 1.3 %collective-permute-start.14 = (f32[2,4,12,12]{3,2,1,0:T(8,128)S(1)}, f32[2,4,12,12]{3,2,1,0:T(8,128)S(1)}, u32[]{:S(2)}, u32[]{:S(2)}) collective-permute-start(f32[2,4,12,12]{3,2,1,0:T(8,128)S(1)} %traces.1), channel_id=1, source_target_pairs={{0,8},{8,0},{16,24},{24,16},{1,9},{9,1},{17,25},{25,17},{2,10},{10... | collective-permute-start | bytes 13832 | tf_op jit(solution)/shard_map/ppermute | solution.py:27
  76.0 4.0 %collective-permute-start.15 = (f32[4,12,12]{2,1,0:T(8,128)S(1)}, f32[4,12,12]{2,1,0:T(8,128)S(1)}, u32[]{:S(2)}, u32[]{:S(2)}) collective-permute-start(f32[4,12,12]{2,1,0:T(8,128)S(1)} %get-tuple-element.45), channel_id=1, source_target_pairs={{0,16},{8,24},{16,0},{24,8},{1,17},{9,25},{17,1},{25,9},{2,18},{10... | collective-permute-start | bytes 6920 | tf_op jit(solution)/shard_map/ppermute | solution.py:27
  77.6 4.2 %collective-permute-start.16 = (f32[4,12,12]{2,1,0:T(8,128)S(1)}, f32[4,12,12]{2,1,0:T(8,128)S(1)}, u32[]{:S(2)}, u32[]{:S(2)}) collective-permute-start(f32[4,12,12]{2,1,0:T(8,128)S(1)} %get-tuple-element.44), channel_id=1, source_target_pairs={{0,1},{1,0},{2,3},{3,2},{4,5},{5,4},{6,7},{7,6},{8,9},{9,8},{10,11... | collective-permute-start | bytes 6920 | tf_op jit(solution)/shard_map/ppermute | solution.py:27
  79.1 4.8 %collective-permute-start.17 = (f32[4,12,12]{2,1,0:T(8,128)S(1)}, f32[4,12,12]{2,1,0:T(8,128)S(1)}, u32[]{:S(2)}, u32[]{:S(2)}) collective-permute-start(f32[4,12,12]{2,1,0:T(8,128)S(1)} %get-tuple-element.44), channel_id=1, source_target_pairs={{0,17},{1,16},{2,19},{3,18},{4,21},{5,20},{6,23},{7,22},{8,25},{9,... | collective-permute-start | bytes 6920 | tf_op jit(solution)/shard_map/ppermute | solution.py:556

commit v6 on v5

--- a/solution.py
+++ b/solution.py
@@ -43,7 +43,6 @@
             arrays.append(moved)
         return arrays, table, g_send
     outward = {1: 0, 2: 3}
-    received, g_send = lax.optimization_barrier((received, g_send))
     piece = jnp.stack([keep, received])
     opposite = along_line(piece, {1: 2, 2: 1, 0: 3, 3: 0})
     skip = along_line(piece, {0: 2, 3: 1})

time: 85.1 us -> 85.2 us (level)
    ppermute x13, waiting for transfers between devices: 20.3 us -> 32.1 us  [swap_bit(): return lax.ppermute(block, axis, [(i, i ^ mask) for i in range(count)])]
    ppermute x4, waiting for transfers between devices: 12.7 us -> 1.25 us  [along_line(): return lax.ppermute(block, 'tm', route)]
  transfers between devices with their start and end apart: 18 -> 18, of which waited for: 14 -> 12; matrix products, arithmetic and copies ran while one was open for 1% -> 1% of each run, Pallas kernels for 27% -> 26%
where the time goes in v6:
time: 85.2 us
  waiting for transfers between devices  35.5 us (42%)
  Pallas kernels  25.1 us (29%)
  starting transfers between devices  20.8 us (24%)
  local copies, waits for them, and re-layouts  2.66 us (3%)
    ppermute x13, waiting for transfers between devices, swap_bit(): return lax.ppermute(block, axis, [(i, i ^ mask) for i in range(count)])  32.1 us
    pallas_call x2, Pallas kernels, elementals(): pl.pallas_call(functools.partial(elemental_kernel, held, near, late, bloc...  18.8 us
    ppermute x13, starting transfers between devices, swap_bit(): return lax.ppermute(block, axis, [(i, i ^ mask) for i in range(count)])  12.6 us
    ppermute x4, starting transfers between devices, along_line(): return lax.ppermute(block, 'tm', route)  7.76 us
    pallas_call x1, Pallas kernels, both_sides(): pl.pallas_call(functools.partial(both_kernel, blocks), out_shape=(piece,)...  3.11 us
    ppermute x1, waiting for transfers between devices, across(): return lax.ppermute(block, ('space', 'tm'), route)  2.1 us
    unnamed x12, local copies, waits for them, and re-layouts  1.84 us
  transfers between devices with their start and end apart: 18, of which 12 were waited for; matrix products, arithmetic and copies ran while one was open for 1% of the time, Pallas kernels for 26%

profile of v6, /device:TPU:0, one launch (start us, length us, event | category | flops | bytes accessed | tf_op | source)
XLA Modules:
  0.0 85.2 jit_solution(3815010906967823056)
XLA Ops:
  0.6 0.5 collective-permute-start.1
  1.1 2.6 %collective-permute-start = (bf16[2,3,256,256]{3,2,1,0:T(8,128)(2,1)}, bf16[2,3,256,256]{3,2,1,0:T(8,128)(2,1)S(1)}, u32[]{:S(2)}, u32[]{:S(2)}) collective-permute-start(bf16[2,3,256,256]{3,2,1,0:T(8,128)(2,1)} %bitcast.22), channel_id=1, source_target_pairs={{0,16},{8,24},{16,0},{24,8},{1,17},{9,25},{17,1},{25,9},{2,18},{10... | collective-permute-start | bytes 2359304 | tf_op jit(solution)/shard_map/ppermute | solution.py:27
  3.7 0.8 slice_bitcast_fusion.3
  4.5 0.3 fusion.13
  4.9 0.1 fusion.11
  5.0 0.0 copy-start
  5.0 0.0 collective-permute-done.1.refs_3_
  5.0 0.0 copy-start.2
  5.0 1.2 %copy-done.2 = bf16[1,2,3,1,256,256]{5,4,3,2,1,0:T(8,128)(2,1)S(1)} copy-done((bf16[1,2,3,1,256,256]{5,4,3,2,1,0:T(8,128)(2,1)S(1)}, bf16[1,2,3,1,256,256]{5,4,3,2,1,0:T(8,128)(2,1)}, u32[]{:S(2)}) %copy-start.2) | copy-done | bytes 786456
  6.2 0.7 copy-done.4
  6.8 7.6 %elementals_early.1 = (f32[6,256,256]{2,1,0:T(8,128)S(1)}, f32[6,2,256,128]{3,2,1,0:T(8,128)S(1)}) custom-call(s32[6]{0:T(128)S(1)} %copy-done.4, f32[2,4,6]{2,1,0:T(4,128)S(1)} %pad_maximum_fusion.2.refs_1_, bf16[2,3,256,256]{3,2,1,0:T(8,128)(2,1)S(1)} %bitcast.23, bf16[2,3,256,256]{3,2,1,0:T(8,128)(2,1)S(1)} %collective-permute-done.1.refs_3_, ...), custom_call_target="tpu_custom_call" | custom-call | flops 4831838208 | bytes 1572864 | tf_op jit(solution)/shard_map/elementals_early/pallas_call | solution.py:243
  14.5 7.6 %collective-permute-done.refs_4_ = bf16[2,3,256,256]{3,2,1,0:T(8,128)(2,1)S(1)} collective-permute-done((bf16[2,3,256,256]{3,2,1,0:T(8,128)(2,1)}, bf16[2,3,256,256]{3,2,1,0:T(8,128)(2,1)S(1)}, u32[]{:S(2)}, u32[]{:S(2)}) %collective-permute-start) | collective-permute-done | bytes 786464 | tf_op jit(solution)/shard_map/ppermute | solution.py:27
  22.1 0.0 collective-permute-start.2
  22.1 1.8 %collective-permute-start.3 = (bf16[4,2,64,256]{3,2,1,0:T(8,128)(2,1)S(1)}, bf16[4,2,64,256]{3,2,1,0:T(8,128)(2,1)S(1)}, u32[]{:S(2)}, u32[]{:S(2)}) collective-permute-start(bf16[4,2,64,256]{3,2,1,0:T(8,128)(2,1)S(1)} %bitcast.18), channel_id=1, source_target_pairs={{0,16},{8,24},{16,0},{24,8},{1,17},{9,25},{17,1},{25,9},{2,18},{10... | collective-permute-start | bytes 786440 | tf_op jit(solution)/shard_map/ppermute | solution.py:27
  23.9 0.5 collective-permute-done.2.refs_5_
  24.4 11.2 %elementals_late.1 = (bf16[6,256,256]{2,1,0:T(8,128)(2,1)S(1)}, bf16[96,1024]{1,0:T(8,128)(2,1)S(1)}, bf16[96,1024]{1,0:T(8,128)(2,1)S(1)}) custom-call(s32[6]{0:T(128)S(1)} %copy-done.5, f32[2,4,6]{2,1,0:T(4,128)S(1)} %pad_maximum_fusion.2.refs_1_, bf16[2,3,256,256]{3,2,1,0:T(8,128)(2,1)S(1)} %bitcast.24, ...), custom_call_target="tpu_custom_call" | custom-call | flops 9663676416 | bytes 3145728 | tf_op jit(solution)/shard_map/elementals_late/pallas_call | solution.py:243
  35.5 0.0 collective-permute-done.3.refs_2_
  35.5 0.2 collective-permute-start.9
  35.7 1.7 %collective-permute-start.4 = (bf16[96,1024]{1,0:T(8,128)(2,1)S(1)}, bf16[96,1024]{1,0:T(8,128)(2,1)S(1)}, u32[]{:S(2)}, u32[]{:S(2)}) collective-permute-start(bf16[96,1024]{1,0:T(8,128)(2,1)S(1)} %get-tuple-element.29), channel_id=1, source_target_pairs={{0,1},{1,0},{2,3},{3,2},{4,5},{5,4},{6,7},{7,6},{8,9},{9,8},{10,11... | collective-permute-start | bytes 589832 | tf_op jit(solution)/shard_map/ppermute | solution.py:27
  37.5 5.4 %collective-permute-done.4.refs_1_ = bf16[96,1024]{1,0:T(8,128)(2,1)S(1)} collective-permute-done((bf16[96,1024]{1,0:T(8,128)(2,1)S(1)}, bf16[96,1024]{1,0:T(8,128)(2,1)S(1)}, u32[]{:S(2)}, u32[]{:S(2)}) %collective-permute-start.4) | collective-permute-done | bytes 196640 | tf_op jit(solution)/shard_map/ppermute | solution.py:27
  43.0 3.9 %collective-permute-start.7 = (bf16[2,96,1024]{2,1,0:T(8,128)(2,1)S(1)}, bf16[2,96,1024]{2,1,0:T(8,128)(2,1)S(1)}, u32[]{:S(2)}, u32[]{:S(2)}) collective-permute-start(bf16[2,96,1024]{2,1,0:T(8,128)(2,1)S(1)} %pad_maximum_fusion), channel_id=1, source_target_pairs={{2,4},{3,5},{4,2},{5,3},{0,6},{1,7},{6,0},{7,1},{10,12},{11,13},{1... | collective-permute-start | bytes 1179656 | tf_op jit(solution)/shard_map/ppermute | solution.py:32
  46.9 0.0 collective-permute-start.10
  46.9 0.5 collective-permute-start.11
  47.4 1.0 %collective-permute-done.10.refs_1_ = bf16[4,2,64,256]{3,2,1,0:T(8,128)(2,1)S(1)} collective-permute-done((bf16[4,2,64,256]{3,2,1,0:T(8,128)(2,1)S(1)}, bf16[4,2,64,256]{3,2,1,0:T(8,128)(2,1)S(1)}, u32[]{:S(2)}, u32[]{:S(2)}) %collective-permute-start.10) | collective-permute-done | bytes 262176 | tf_op jit(solution)/shard_map/ppermute | solution.py:27
  48.4 0.4 collective-permute-done.11.refs_3_
  48.8 0.0 collective-permute-done.9.other_ref
  48.8 3.1 %both_sides.1 = (bf16[4,2,6,64,128]{4,3,2,1,0:T(8,128)(2,1)S(1)}, bf16[2,2,6,64,128]{4,3,2,1,0:T(8,128)(2,1)S(1)}, bf16[2,2,6,64,128]{4,3,2,1,0:T(8,128)(2,1)S(1)}) custom-call(bf16[6,256,256]{2,1,0:T(8,128)(2,1)S(1)} %get-tuple-element.30.e_ref, bf16[6,256,256]{2,1,0:T(8,128)(2,1)S(1)} %collective-permute-done.9.other_ref, ...), custom_call_target="tpu_custom_call" | custom-call | tf_op jit(solution)/shard_map/both_sides/pallas_call | solution.py:339
  51.9 1.6 %collective-permute-start.12 = (bf16[2,2,6,64,128]{4,3,2,1,0:T(8,128)(2,1)S(1)}, bf16[2,2,6,64,128]{4,3,2,1,0:T(8,128)(2,1)S(1)}, u32[]{:S(2)}, u32[]{:S(2)}) collective-permute-start(bf16[2,2,6,64,128]{4,3,2,1,0:T(8,128)(2,1)S(1)} %get-tuple-element.34), channel_id=1, source_target_pairs={{0,1},{1,0},{2,3},{3,2},{4,5},{5,4},{6,7},{7,6},{8,9},{9,8},{10,11... | collective-permute-start | bytes 1179656 | tf_op jit(solution)/shard_map/ppermute | solution.py:27
  53.5 0.5 collective-permute-start.13
  54.0 0.0 collective-permute-start.5
  54.0 2.6 %collective-permute-start.6 = (bf16[2,96,1024]{2,1,0:T(8,128)(2,1)S(1)}, bf16[2,96,1024]{2,1,0:T(8,128)(2,1)S(1)}, u32[]{:S(2)}, u32[]{:S(2)}) collective-permute-start(bf16[2,96,1024]{2,1,0:T(8,128)(2,1)S(1)} %pad_maximum_fusion), channel_id=1, source_target_pairs={{0,4},{1,5},{6,2},{7,3},{8,12},{9,13},{14,10},{15,11},{16,20},{17,... | collective-permute-start | bytes 1179656 | tf_op jit(solution)/shard_map/ppermute | solution.py:32
  56.6 0.0 collective-permute-done.7.refs_4_
  56.6 1.3 %collective-permute-start.8 = (bf16[2,96,1024]{2,1,0:T(8,128)(2,1)S(1)}, bf16[2,96,1024]{2,1,0:T(8,128)(2,1)S(1)}, u32[]{:S(2)}, u32[]{:S(2)}) collective-permute-start(bf16[2,96,1024]{2,1,0:T(8,128)(2,1)S(1)} %collective-permute-done.7.refs_4_), channel_id=1, source_target_pairs={{2,0},{3,1},{4,6},{5,7},{10,8},{11,9},{12,14},{13,15},{18,16},{19,... | collective-permute-start | bytes 1179656 | tf_op jit(solution)/shard_map/ppermute | solution.py:32
  57.9 6.1 %collective-permute-done.12.refs_0_ = bf16[2,2,6,64,128]{4,3,2,1,0:T(8,128)(2,1)S(1)} collective-permute-done((bf16[2,2,6,64,128]{4,3,2,1,0:T(8,128)(2,1)S(1)}, bf16[2,2,6,64,128]{4,3,2,1,0:T(8,128)(2,1)S(1)}, u32[]{:S(2)}, u32[]{:S(2)}) %collective-permute-start.12) | collective-permute-done | bytes 393248 | tf_op jit(solution)/shard_map/ppermute | solution.py:27
  63.9 7.6 %collective-permute-done.13.refs_1_ = bf16[2,2,6,64,128]{4,3,2,1,0:T(8,128)(2,1)S(1)} collective-permute-done((bf16[2,2,6,64,128]{4,3,2,1,0:T(8,128)(2,1)S(1)}, bf16[2,2,6,64,128]{4,3,2,1,0:T(8,128)(2,1)S(1)}, u32[]{:S(2)}, u32[]{:S(2)}) %collective-permute-start.13) | collective-permute-done | bytes 393248 | tf_op jit(solution)/shard_map/ppermute | solution.py:27
  71.6 0.7 lay_out.1.refs_6_
  72.2 0.0 collective-permute-done.5.refs_2_
  72.3 1.2 %collective-permute-done.8.refs_5_ = bf16[2,96,1024]{2,1,0:T(8,128)(2,1)S(1)} collective-permute-done((bf16[2,96,1024]{2,1,0:T(8,128)(2,1)S(1)}, bf16[2,96,1024]{2,1,0:T(8,128)(2,1)S(1)}, u32[]{:S(2)}, u32[]{:S(2)}) %collective-permute-start.8) | collective-permute-done | bytes 393248 | tf_op jit(solution)/shard_map/ppermute | solution.py:32
  73.5 1.6 %traces.1 = f32[2,4,12,12]{3,2,1,0:T(8,128)S(1)} custom-call(s32[4]{0:T(128)S(1)} %copy-done.1, bf16[96,1024]{1,0:T(8,128)(2,1)S(1)} %get-tuple-element.25.refs_0_, bf16[96,1024]{1,0:T(8,128)(2,1)S(1)} %collective-permute-done.4.refs_1_, bf16[2,96,1024]{2,1,0:T(8,128)(2,1)S(1)} %collective-permute-done.5.refs_2_, ...), custom_call_target="tpu_custom_call" | custom-call | flops 37748736 | bytes 1572864 | tf_op jit(solution)/shard_map/traces/pallas_call | solution.py:443
  75.1 0.1 collective-permute-start.14
  75.2 1.2 %collective-permute-done.14 = f32[2,4,12,12]{3,2,1,0:T(8,128)S(1)} collective-permute-done((f32[2,4,12,12]{3,2,1,0:T(8,128)S(1)}, f32[2,4,12,12]{3,2,1,0:T(8,128)S(1)}, u32[]{:S(2)}, u32[]{:S(2)}) %collective-permute-start.14) | collective-permute-done | bytes 4640 | tf_op jit(solution)/shard_map/ppermute | solution.py:27
  76.5 1.6 %collective-permute-start.15 = (f32[4,12,12]{2,1,0:T(8,128)S(1)}, f32[4,12,12]{2,1,0:T(8,128)S(1)}, u32[]{:S(2)}, u32[]{:S(2)}) collective-permute-start(f32[4,12,12]{2,1,0:T(8,128)S(1)} %get-tuple-element.39), channel_id=1, source_target_pairs={{0,16},{8,24},{16,0},{24,8},{1,17},{9,25},{17,1},{25,9},{2,18},{10... | collective-permute-start | bytes 6920 | tf_op jit(solution)/shard_map/ppermute | solution.py:27
  78.1 1.5 %collective-permute-start.16 = (f32[4,12,12]{2,1,0:T(8,128)S(1)}, f32[4,12,12]{2,1,0:T(8,128)S(1)}, u32[]{:S(2)}, u32[]{:S(2)}) collective-permute-start(f32[4,12,12]{2,1,0:T(8,128)S(1)} %get-tuple-element.38), channel_id=1, source_target_pairs={{0,1},{1,0},{2,3},{3,2},{4,5},{5,4},{6,7},{7,6},{8,9},{9,8},{10,11... | collective-permute-start | bytes 6920 | tf_op jit(solution)/shard_map/ppermute | solution.py:27
  79.6 0.5 collective-permute-start.17
  80.0 0.4 collective-permute-done.15.refs_1_
  80.5 1.8 %collective-permute-done.16.refs_2_ = f32[4,12,12]{2,1,0:T(8,128)S(1)} collective-permute-done((f32[4,12,12]{2,1,0:T(8,128)S(1)}, f32[4,12,12]{2,1,0:T(8,128)S(1)}, u32[]{:S(2)}, u32[]{:S(2)}) %collective-permute-start.16) | collective-permute-done | bytes 2336 | tf_op jit(solution)/shard_map/ppermute | solution.py:27
  82.3 2.1 %collective-permute-done.17.refs_3_ = f32[4,12,12]{2,1,0:T(8,128)S(1)} collective-permute-done((f32[4,12,12]{2,1,0:T(8,128)S(1)}, f32[4,12,12]{2,1,0:T(8,128)S(1)}, u32[]{:S(2)}, u32[]{:S(2)}) %collective-permute-start.17) | collective-permute-done | bytes 2336 | tf_op jit(solution)/shard_map/ppermute | solution.py:555
  84.4 0.9 %finish.1 = (f32[1,4,6,2,6]{4,3,2,1,0:T(2,128)}, f32[1,4,6,2,6]{4,3,2,1,0:T(2,128)}) custom-call(f32[2,4,12,12]{3,2,1,0:T(8,128)S(1)} %add.86.refs_0_, f32[4,12,12]{2,1,0:T(8,128)S(1)} %collective-permute-done.15.refs_1_, f32[4,12,12]{2,1,0:T(8,128)S(1)} %collective-permute-done.16.refs_2_, f32[4,12,12]{2,1,0:T(8,128)S(1)} %collective-permute-done.17.refs_3_), custom_call_target="tpu_custom_call" | custom-call | tf_op jit(solution)/shard_map/finish/pallas_call | solution.py:488
  (16 shorter events, 0.1 us)
Async XLA Ops:
  0.6 4.3 %collective-permute-start.1 = (bf16[2,3,256,256]{3,2,1,0:T(8,128)(2,1)}, bf16[2,3,256,256]{3,2,1,0:T(8,128)(2,1)S(1)}, u32[]{:S(2)}, u32[]{:S(2)}) collective-permute-start(bf16[2,3,256,256]{3,2,1,0:T(8,128)(2,1)} %bitcast.21), channel_id=1, source_target_pairs={{0,8},{8,0},{16,24},{24,16},{1,9},{9,1},{17,25},{25,17},{2,10},{10... | collective-permute-start | bytes 2359304 | tf_op jit(solution)/shard_map/ppermute | solution.py:27
  1.1 20.9 %collective-permute-start = (bf16[2,3,256,256]{3,2,1,0:T(8,128)(2,1)}, bf16[2,3,256,256]{3,2,1,0:T(8,128)(2,1)S(1)}, u32[]{:S(2)}, u32[]{:S(2)}) collective-permute-start(bf16[2,3,256,256]{3,2,1,0:T(8,128)(2,1)} %bitcast.22), channel_id=1, source_target_pairs={{0,16},{8,24},{16,0},{24,8},{1,17},{9,25},{17,1},{25,9},{2,18},{10... | collective-permute-start | bytes 2359304 | tf_op jit(solution)/shard_map/ppermute | solution.py:27
  5.0 17.1 %copy-start = (bf16[1,4,2,64,256]{4,3,2,1,0:T(8,128)(2,1)S(1)}, bf16[1,4,2,64,256]{4,3,2,1,0:T(8,128)(2,1)}, u32[]{:S(2)}) copy-start(bf16[1,4,2,64,256]{4,3,2,1,0:T(8,128)(2,1)} %param.9) | copy-start | bytes 786436
  5.0 1.2 %copy-start.2 = (bf16[1,2,3,1,256,256]{5,4,3,2,1,0:T(8,128)(2,1)S(1)}, bf16[1,2,3,1,256,256]{5,4,3,2,1,0:T(8,128)(2,1)}, u32[]{:S(2)}) copy-start(bf16[1,2,3,1,256,256]{5,4,3,2,1,0:T(8,128)(2,1)} %param.5) | copy-start | bytes 2359300
  6.2 0.7 copy-start.4
  6.8 17.6 %copy-start.3 = (bf16[1,2,3,1,256,256]{5,4,3,2,1,0:T(8,128)(2,1)S(1)}, bf16[1,2,3,1,256,256]{5,4,3,2,1,0:T(8,128)(2,1)}, u32[]{:S(2)}) copy-start(bf16[1,2,3,1,256,256]{5,4,3,2,1,0:T(8,128)(2,1)} %param.5) | copy-start | bytes 2359300
  6.8 17.6 %copy-start.5 = (s32[6]{0:T(128)S(1)}, s32[6]{0:T(128)}, u32[]{:S(2)}) copy-start(s32[6]{0:T(128)} %refs_0_.3) | copy-start | bytes 76
  22.1 2.3 %collective-permute-start.2 = (bf16[2,3,256,256]{3,2,1,0:T(8,128)(2,1)S(1)}, bf16[2,3,256,256]{3,2,1,0:T(8,128)(2,1)S(1)}, u32[]{:S(2)}, u32[]{:S(2)}) collective-permute-start(bf16[2,3,256,256]{3,2,1,0:T(8,128)(2,1)S(1)} %collective-permute-done.refs_4_), channel_id=1, source_target_pairs={{0,8},{8,0},{16,24},{24,16},{1,9},{9,1},{17,25},{25,17},{2,10},{10... | collective-permute-start | bytes 2359304 | tf_op jit(solution)/shard_map/ppermute | solution.py:27
  22.1 13.4 %collective-permute-start.3 = (bf16[4,2,64,256]{3,2,1,0:T(8,128)(2,1)S(1)}, bf16[4,2,64,256]{3,2,1,0:T(8,128)(2,1)S(1)}, u32[]{:S(2)}, u32[]{:S(2)}) collective-permute-start(bf16[4,2,64,256]{3,2,1,0:T(8,128)(2,1)S(1)} %bitcast.18), channel_id=1, source_target_pairs={{0,16},{8,24},{16,0},{24,8},{1,17},{9,25},{17,1},{25,9},{2,18},{10... | collective-permute-start | bytes 786440 | tf_op jit(solution)/shard_map/ppermute | solution.py:27
  35.5 13.2 %collective-permute-start.9 = (bf16[6,256,256]{2,1,0:T(8,128)(2,1)S(1)}, bf16[6,256,256]{2,1,0:T(8,128)(2,1)S(1)}, u32[]{:S(2)}, u32[]{:S(2)}) collective-permute-start(bf16[6,256,256]{2,1,0:T(8,128)(2,1)S(1)} %get-tuple-element.30.e_ref), channel_id=1, source_target_pairs={{0,8},{8,0},{16,24},{24,16},{1,9},{9,1},{17,25},{25,17},{2,10},{10... | collective-permute-start | bytes 2359304 | tf_op jit(solution)/shard_map/ppermute | solution.py:27
  35.7 7.2 %collective-permute-start.4 = (bf16[96,1024]{1,0:T(8,128)(2,1)S(1)}, bf16[96,1024]{1,0:T(8,128)(2,1)S(1)}, u32[]{:S(2)}, u32[]{:S(2)}) collective-permute-start(bf16[96,1024]{1,0:T(8,128)(2,1)S(1)} %get-tuple-element.29), channel_id=1, source_target_pairs={{0,1},{1,0},{2,3},{3,2},{4,5},{5,4},{6,7},{7,6},{8,9},{9,8},{10,11... | collective-permute-start | bytes 589832 | tf_op jit(solution)/shard_map/ppermute | solution.py:27
  43.0 13.6 %collective-permute-start.7 = (bf16[2,96,1024]{2,1,0:T(8,128)(2,1)S(1)}, bf16[2,96,1024]{2,1,0:T(8,128)(2,1)S(1)}, u32[]{:S(2)}, u32[]{:S(2)}) collective-permute-start(bf16[2,96,1024]{2,1,0:T(8,128)(2,1)S(1)} %pad_maximum_fusion), channel_id=1, source_target_pairs={{2,4},{3,5},{4,2},{5,3},{0,6},{1,7},{6,0},{7,1},{10,12},{11,13},{1... | collective-permute-start | bytes 1179656 | tf_op jit(solution)/shard_map/ppermute | solution.py:32
  46.9 1.5 %collective-permute-start.10 = (bf16[4,2,64,256]{3,2,1,0:T(8,128)(2,1)S(1)}, bf16[4,2,64,256]{3,2,1,0:T(8,128)(2,1)S(1)}, u32[]{:S(2)}, u32[]{:S(2)}) collective-permute-start(bf16[4,2,64,256]{3,2,1,0:T(8,128)(2,1)S(1)} %bitcast.19), channel_id=1, source_target_pairs={{0,8},{8,0},{16,24},{24,16},{1,9},{9,1},{17,25},{25,17},{2,10},{10... | collective-permute-start | bytes 786440 | tf_op jit(solution)/shard_map/ppermute | solution.py:27
  46.9 1.9 %collective-permute-start.11 = (bf16[4,2,64,256]{3,2,1,0:T(8,128)(2,1)S(1)}, bf16[4,2,64,256]{3,2,1,0:T(8,128)(2,1)S(1)}, u32[]{:S(2)}, u32[]{:S(2)}) collective-permute-start(bf16[4,2,64,256]{3,2,1,0:T(8,128)(2,1)S(1)} %collective-permute-done.3.refs_2_), channel_id=1, source_target_pairs={{0,8},{8,0},{16,24},{24,16},{1,9},{9,1},{17,25},{25,17},{2,10},{10... | collective-permute-start | bytes 786440 | tf_op jit(solution)/shard_map/ppermute | solution.py:27
  51.9 12.0 %collective-permute-start.12 = (bf16[2,2,6,64,128]{4,3,2,1,0:T(8,128)(2,1)S(1)}, bf16[2,2,6,64,128]{4,3,2,1,0:T(8,128)(2,1)S(1)}, u32[]{:S(2)}, u32[]{:S(2)}) collective-permute-start(bf16[2,2,6,64,128]{4,3,2,1,0:T(8,128)(2,1)S(1)} %get-tuple-element.34), channel_id=1, source_target_pairs={{0,1},{1,0},{2,3},{3,2},{4,5},{5,4},{6,7},{7,6},{8,9},{9,8},{10,11... | collective-permute-start | bytes 1179656 | tf_op jit(solution)/shard_map/ppermute | solution.py:27
  53.5 18.1 %collective-permute-start.13 = (bf16[2,2,6,64,128]{4,3,2,1,0:T(8,128)(2,1)S(1)}, bf16[2,2,6,64,128]{4,3,2,1,0:T(8,128)(2,1)S(1)}, u32[]{:S(2)}, u32[]{:S(2)}) collective-permute-start(bf16[2,2,6,64,128]{4,3,2,1,0:T(8,128)(2,1)S(1)} %get-tuple-element.35), channel_id=1, source_target_pairs={{0,1},{1,0},{2,3},{3,2},{4,5},{5,4},{6,7},{7,6},{8,9},{9,8},{10,11... | collective-permute-start | bytes 1179656 | tf_op jit(solution)/shard_map/ppermute | solution.py:27
  54.0 18.2 %collective-permute-start.5 = (bf16[2,96,1024]{2,1,0:T(8,128)(2,1)S(1)}, bf16[2,96,1024]{2,1,0:T(8,128)(2,1)S(1)}, u32[]{:S(2)}, u32[]{:S(2)}) collective-permute-start(bf16[2,96,1024]{2,1,0:T(8,128)(2,1)S(1)} %pad_maximum_fusion), channel_id=1, source_target_pairs={{0,2},{1,3},{2,0},{3,1},{4,6},{5,7},{6,4},{7,5},{8,10},{9,11},{10,... | collective-permute-start | bytes 1179656 | tf_op jit(solution)/shard_map/ppermute | solution.py:32
  54.0 18.2 %collective-permute-start.6 = (bf16[2,96,1024]{2,1,0:T(8,128)(2,1)S(1)}, bf16[2,96,1024]{2,1,0:T(8,128)(2,1)S(1)}, u32[]{:S(2)}, u32[]{:S(2)}) collective-permute-start(bf16[2,96,1024]{2,1,0:T(8,128)(2,1)S(1)} %pad_maximum_fusion), channel_id=1, source_target_pairs={{0,4},{1,5},{6,2},{7,3},{8,12},{9,13},{14,10},{15,11},{16,20},{17,... | collective-permute-start | bytes 1179656 | tf_op jit(solution)/shard_map/ppermute | solution.py:32
  56.6 16.9 %collective-permute-start.8 = (bf16[2,96,1024]{2,1,0:T(8,128)(2,1)S(1)}, bf16[2,96,1024]{2,1,0:T(8,128)(2,1)S(1)}, u32[]{:S(2)}, u32[]{:S(2)}) collective-permute-start(bf16[2,96,1024]{2,1,0:T(8,128)(2,1)S(1)} %collective-permute-done.7.refs_4_), channel_id=1, source_target_pairs={{2,0},{3,1},{4,6},{5,7},{10,8},{11,9},{12,14},{13,15},{18,16},{19,... | collective-permute-start | bytes 1179656 | tf_op jit(solution)/shard_map/ppermute | solution.py:32
  71.6 1.9 %copy-start.1 = (s32[4]{0:T(128)S(1)}, s32[4]{0:T(128)}, u32[]{:S(2)}) copy-start(s32[4]{0:T(128)} %times_ref.1) | copy-start | bytes 52
  75.1 1.3 %collective-permute-start.14 = (f32[2,4,12,12]{3,2,1,0:T(8,128)S(1)}, f32[2,4,12,12]{3,2,1,0:T(8,128)S(1)}, u32[]{:S(2)}, u32[]{:S(2)}) collective-permute-start(f32[2,4,12,12]{3,2,1,0:T(8,128)S(1)} %traces.1), channel_id=1, source_target_pairs={{0,8},{8,0},{16,24},{24,16},{1,9},{9,1},{17,25},{25,17},{2,10},{10... | collective-permute-start | bytes 13832 | tf_op jit(solution)/shard_map/ppermute | solution.py:27
  76.5 4.0 %collective-permute-start.15 = (f32[4,12,12]{2,1,0:T(8,128)S(1)}, f32[4,12,12]{2,1,0:T(8,128)S(1)}, u32[]{:S(2)}, u32[]{:S(2)}) collective-permute-start(f32[4,12,12]{2,1,0:T(8,128)S(1)} %get-tuple-element.39), channel_id=1, source_target_pairs={{0,16},{8,24},{16,0},{24,8},{1,17},{9,25},{17,1},{25,9},{2,18},{10... | collective-permute-start | bytes 6920 | tf_op jit(solution)/shard_map/ppermute | solution.py:27
  78.1 4.2 %collective-permute-start.16 = (f32[4,12,12]{2,1,0:T(8,128)S(1)}, f32[4,12,12]{2,1,0:T(8,128)S(1)}, u32[]{:S(2)}, u32[]{:S(2)}) collective-permute-start(f32[4,12,12]{2,1,0:T(8,128)S(1)} %get-tuple-element.38), channel_id=1, source_target_pairs={{0,1},{1,0},{2,3},{3,2},{4,5},{5,4},{6,7},{7,6},{8,9},{9,8},{10,11... | collective-permute-start | bytes 6920 | tf_op jit(solution)/shard_map/ppermute | solution.py:27
  79.6 4.8 %collective-permute-start.17 = (f32[4,12,12]{2,1,0:T(8,128)S(1)}, f32[4,12,12]{2,1,0:T(8,128)S(1)}, u32[]{:S(2)}, u32[]{:S(2)}) collective-permute-start(f32[4,12,12]{2,1,0:T(8,128)S(1)} %get-tuple-element.38), channel_id=1, source_target_pairs={{0,17},{1,16},{2,19},{3,18},{4,21},{5,20},{6,23},{7,22},{8,25},{9,... | collective-permute-start | bytes 6920 | tf_op jit(solution)/shard_map/ppermute | solution.py:555

commit v7 on v6

--- a/solution.py
+++ b/solution.py
@@ -300,14 +300,12 @@
             jnp.concatenate([one, two], axis=1) for one, two in zip(*sides)
         )
         for part, block in enumerate((real, imaginary)):
-            high = block.astype(BF16)
-            low = (block - high.astype(F32)).astype(BF16)
+            block = block.astype(BF16)
             for s in range(sources):
                 base = s * block_rows
                 rows = pl.ds(a * block_rows, block_rows)
                 columns = pl.ds(part * vectors, vectors)
-                middle[0, s, rows, columns] = high[base : base + block_rows]
-                middle[1, s, rows, columns] = low[base : base + block_rows]
+                middle[s, rows, columns] = block[base : base + block_rows]
     for s in range(sources):
         real, imaginary = sorted_rows[s, 0], sorted_rows[s, 1]
         right = jnp.concatenate(
@@ -317,8 +315,7 @@
             ],
             axis=0,
         )
-        image = jnp.dot(middle[0, s], right, preferred_element_type=F32)
-        image = image + jnp.dot(middle[1, s], right, preferred_element_type=F32)
+        image = jnp.dot(middle[s], right, preferred_element_type=F32)
         image = image.astype(BF16)
         for a in range(operators):
             for part in range(2):
@@ -345,7 +342,7 @@
             pltpu.VMEM((sources, 2, vectors, vectors), BF16),
             pltpu.VMEM((sources, 2, vectors, vectors), BF16),
             pltpu.VMEM((2 * sources * block_rows, vectors), BF16),
-            pltpu.VMEM((2, sources, operators * block_rows, 2 * vectors), BF16),
+            pltpu.VMEM((sources, operators * block_rows, 2 * vectors), BF16),
         ],
         compiler_params=params(16),
         cost_estimate=pl.CostEstimate(flops=0, bytes_accessed=0, transcendentals=0),

time: 85.2 us -> 84.5 us (level)
    ppermute x13, waiting for transfers between devices: 32.1 us -> 30 us  [swap_bit(): return lax.ppermute(block, axis, [(i, i ^ mask) for i in range(count)])]
    ppermute x4, waiting for transfers between devices: 1.25 us -> 3.21 us  [along_line(): return lax.ppermute(block, 'tm', route)]
  transfers between devices with their start and end apart: 18 -> 18, of which waited for: 12 -> 14; matrix products, arithmetic and copies ran while one was open for 1% -> 1% of each run, Pallas kernels for 26% -> 26%
where the time goes in v7:
time: 84.5 us; the launch traced here: 84.3 us
  waiting for transfers between devices  35.3 us (42%)
  Pallas kernels  24.3 us (29%)
  starting transfers between devices  20.8 us (25%)
  local copies, waits for them, and re-layouts  2.66 us (3%)
    ppermute x13, waiting for transfers between devices, swap_bit(): return lax.ppermute(block, axis, [(i, i ^ mask) for i in range(count)])  30 us
    pallas_call x2, Pallas kernels, elementals(): pl.pallas_call(functools.partial(elemental_kernel, held, near, late, bloc...  18.9 us
    ppermute x13, starting transfers between devices, swap_bit(): return lax.ppermute(block, axis, [(i, i ^ mask) for i in range(count)])  12.6 us
    ppermute x4, starting transfers between devices, along_line(): return lax.ppermute(block, 'tm', route)  7.73 us
    ppermute x4, waiting for transfers between devices, along_line(): return lax.ppermute(block, 'tm', route)  3.21 us
    pallas_call x1, Pallas kernels, both_sides(): pl.pallas_call(functools.partial(both_kernel, blocks), out_shape=(piece,)...  2.29 us
    ppermute x1, waiting for transfers between devices, across(): return lax.ppermute(block, ('space', 'tm'), route)  2.14 us
    unnamed x12, local copies, waits for them, and re-layouts  1.84 us
  transfers between devices with their start and end apart: 18, of which 14 were waited for; matrix products, arithmetic and copies ran while one was open for 1% of the time, Pallas kernels for 26%

profile of v7, /device:TPU:0, one launch (start us, length us, event | category | flops | bytes accessed | tf_op | source)
XLA Modules:
  0.0 84.3 jit_solution(8478941593653485533)
XLA Ops:
  0.6 0.5 collective-permute-start.1
  1.1 2.6 %collective-permute-start = (bf16[2,3,256,256]{3,2,1,0:T(8,128)(2,1)}, bf16[2,3,256,256]{3,2,1,0:T(8,128)(2,1)S(1)}, u32[]{:S(2)}, u32[]{:S(2)}) collective-permute-start(bf16[2,3,256,256]{3,2,1,0:T(8,128)(2,1)} %bitcast.22), channel_id=1, source_target_pairs={{0,16},{8,24},{16,0},{24,8},{1,17},{9,25},{17,1},{25,9},{2,18},{10... | collective-permute-start | bytes 2359304 | tf_op jit(solution)/shard_map/ppermute | solution.py:27
  3.7 0.8 slice_bitcast_fusion.3
  4.5 0.3 fusion.13
  4.9 0.1 fusion.11
  5.0 0.0 copy-start
  5.0 0.0 collective-permute-done.1.refs_3_
  5.0 0.0 copy-start.2
  5.0 1.2 %copy-done.2 = bf16[1,2,3,1,256,256]{5,4,3,2,1,0:T(8,128)(2,1)S(1)} copy-done((bf16[1,2,3,1,256,256]{5,4,3,2,1,0:T(8,128)(2,1)S(1)}, bf16[1,2,3,1,256,256]{5,4,3,2,1,0:T(8,128)(2,1)}, u32[]{:S(2)}) %copy-start.2) | copy-done | bytes 786456
  6.2 0.7 copy-done.4
  6.8 8.7 %elementals_early.1 = (f32[6,256,256]{2,1,0:T(8,128)S(1)}, f32[6,2,256,128]{3,2,1,0:T(8,128)S(1)}) custom-call(s32[6]{0:T(128)S(1)} %copy-done.4, f32[2,4,6]{2,1,0:T(4,128)S(1)} %pad_maximum_fusion.2.refs_1_, bf16[2,3,256,256]{3,2,1,0:T(8,128)(2,1)S(1)} %bitcast.23, bf16[2,3,256,256]{3,2,1,0:T(8,128)(2,1)S(1)} %collective-permute-done.1.refs_3_, ...), custom_call_target="tpu_custom_call" | custom-call | flops 4831838208 | bytes 1572864 | tf_op jit(solution)/shard_map/elementals_early/pallas_call | solution.py:243
  15.5 6.6 %collective-permute-done.refs_4_ = bf16[2,3,256,256]{3,2,1,0:T(8,128)(2,1)S(1)} collective-permute-done((bf16[2,3,256,256]{3,2,1,0:T(8,128)(2,1)}, bf16[2,3,256,256]{3,2,1,0:T(8,128)(2,1)S(1)}, u32[]{:S(2)}, u32[]{:S(2)}) %collective-permute-start) | collective-permute-done | bytes 786464 | tf_op jit(solution)/shard_map/ppermute | solution.py:27
  22.1 1.8 %collective-permute-start.3 = (bf16[4,2,64,256]{3,2,1,0:T(8,128)(2,1)S(1)}, bf16[4,2,64,256]{3,2,1,0:T(8,128)(2,1)S(1)}, u32[]{:S(2)}, u32[]{:S(2)}) collective-permute-start(bf16[4,2,64,256]{3,2,1,0:T(8,128)(2,1)S(1)} %bitcast.18), channel_id=1, source_target_pairs={{0,16},{8,24},{16,0},{24,8},{1,17},{9,25},{17,1},{25,9},{2,18},{10... | collective-permute-start | bytes 786440 | tf_op jit(solution)/shard_map/ppermute | solution.py:27
  23.9 0.5 collective-permute-done.2.refs_5_
  24.4 10.2 %elementals_late.1 = (bf16[6,256,256]{2,1,0:T(8,128)(2,1)S(1)}, bf16[96,1024]{1,0:T(8,128)(2,1)S(1)}, bf16[96,1024]{1,0:T(8,128)(2,1)S(1)}) custom-call(s32[6]{0:T(128)S(1)} %copy-done.5, f32[2,4,6]{2,1,0:T(4,128)S(1)} %pad_maximum_fusion.2.refs_1_, bf16[2,3,256,256]{3,2,1,0:T(8,128)(2,1)S(1)} %bitcast.24, ...), custom_call_target="tpu_custom_call" | custom-call | flops 9663676416 | bytes 3145728 | tf_op jit(solution)/shard_map/elementals_late/pallas_call | solution.py:243
  34.6 0.0 collective-permute-done.3.refs_2_
  34.6 0.2 collective-permute-start.9
  34.8 1.7 %collective-permute-start.4 = (bf16[96,1024]{1,0:T(8,128)(2,1)S(1)}, bf16[96,1024]{1,0:T(8,128)(2,1)S(1)}, u32[]{:S(2)}, u32[]{:S(2)}) collective-permute-start(bf16[96,1024]{1,0:T(8,128)(2,1)S(1)} %get-tuple-element.29), channel_id=1, source_target_pairs={{0,1},{1,0},{2,3},{3,2},{4,5},{5,4},{6,7},{7,6},{8,9},{9,8},{10,11... | collective-permute-start | bytes 589832 | tf_op jit(solution)/shard_map/ppermute | solution.py:27
  36.5 5.4 %collective-permute-done.4.refs_1_ = bf16[96,1024]{1,0:T(8,128)(2,1)S(1)} collective-permute-done((bf16[96,1024]{1,0:T(8,128)(2,1)S(1)}, bf16[96,1024]{1,0:T(8,128)(2,1)S(1)}, u32[]{:S(2)}, u32[]{:S(2)}) %collective-permute-start.4) | collective-permute-done | bytes 196640 | tf_op jit(solution)/shard_map/ppermute | solution.py:27
  42.0 3.9 %collective-permute-start.7 = (bf16[2,96,1024]{2,1,0:T(8,128)(2,1)S(1)}, bf16[2,96,1024]{2,1,0:T(8,128)(2,1)S(1)}, u32[]{:S(2)}, u32[]{:S(2)}) collective-permute-start(bf16[2,96,1024]{2,1,0:T(8,128)(2,1)S(1)} %pad_maximum_fusion), channel_id=1, source_target_pairs={{2,4},{3,5},{4,2},{5,3},{0,6},{1,7},{6,0},{7,1},{10,12},{11,13},{1... | collective-permute-start | bytes 1179656 | tf_op jit(solution)/shard_map/ppermute | solution.py:32
  45.9 0.0 collective-permute-start.10
  45.9 0.5 collective-permute-start.11
  46.4 1.0 %collective-permute-done.10.refs_1_ = bf16[4,2,64,256]{3,2,1,0:T(8,128)(2,1)S(1)} collective-permute-done((bf16[4,2,64,256]{3,2,1,0:T(8,128)(2,1)S(1)}, bf16[4,2,64,256]{3,2,1,0:T(8,128)(2,1)S(1)}, u32[]{:S(2)}, u32[]{:S(2)}) %collective-permute-start.10) | collective-permute-done | bytes 262176 | tf_op jit(solution)/shard_map/ppermute | solution.py:27
  47.5 0.4 collective-permute-done.11.refs_3_
  47.8 0.0 collective-permute-done.9.other_ref
  47.8 2.3 %both_sides.1 = (bf16[4,2,6,64,128]{4,3,2,1,0:T(8,128)(2,1)S(1)}, bf16[2,2,6,64,128]{4,3,2,1,0:T(8,128)(2,1)S(1)}, bf16[2,2,6,64,128]{4,3,2,1,0:T(8,128)(2,1)S(1)}) custom-call(bf16[6,256,256]{2,1,0:T(8,128)(2,1)S(1)} %get-tuple-element.30.e_ref, bf16[6,256,256]{2,1,0:T(8,128)(2,1)S(1)} %collective-permute-done.9.other_ref, ...), custom_call_target="tpu_custom_call" | custom-call | tf_op jit(solution)/shard_map/both_sides/pallas_call | solution.py:336
  50.1 1.6 %collective-permute-start.12 = (bf16[2,2,6,64,128]{4,3,2,1,0:T(8,128)(2,1)S(1)}, bf16[2,2,6,64,128]{4,3,2,1,0:T(8,128)(2,1)S(1)}, u32[]{:S(2)}, u32[]{:S(2)}) collective-permute-start(bf16[2,2,6,64,128]{4,3,2,1,0:T(8,128)(2,1)S(1)} %get-tuple-element.34), channel_id=1, source_target_pairs={{0,1},{1,0},{2,3},{3,2},{4,5},{5,4},{6,7},{7,6},{8,9},{9,8},{10,11... | collective-permute-start | bytes 1179656 | tf_op jit(solution)/shard_map/ppermute | solution.py:27
  51.7 0.5 collective-permute-start.13
  52.2 0.0 collective-permute-start.5
  52.2 2.6 %collective-permute-start.6 = (bf16[2,96,1024]{2,1,0:T(8,128)(2,1)S(1)}, bf16[2,96,1024]{2,1,0:T(8,128)(2,1)S(1)}, u32[]{:S(2)}, u32[]{:S(2)}) collective-permute-start(bf16[2,96,1024]{2,1,0:T(8,128)(2,1)S(1)} %pad_maximum_fusion), channel_id=1, source_target_pairs={{0,4},{1,5},{6,2},{7,3},{8,12},{9,13},{14,10},{15,11},{16,20},{17,... | collective-permute-start | bytes 1179656 | tf_op jit(solution)/shard_map/ppermute | solution.py:32
  54.8 1.1 %collective-permute-done.7.refs_4_ = bf16[2,96,1024]{2,1,0:T(8,128)(2,1)S(1)} collective-permute-done((bf16[2,96,1024]{2,1,0:T(8,128)(2,1)S(1)}, bf16[2,96,1024]{2,1,0:T(8,128)(2,1)S(1)}, u32[]{:S(2)}, u32[]{:S(2)}) %collective-permute-start.7) | collective-permute-done | bytes 393248 | tf_op jit(solution)/shard_map/ppermute | solution.py:32
  55.9 1.3 %collective-permute-start.8 = (bf16[2,96,1024]{2,1,0:T(8,128)(2,1)S(1)}, bf16[2,96,1024]{2,1,0:T(8,128)(2,1)S(1)}, u32[]{:S(2)}, u32[]{:S(2)}) collective-permute-start(bf16[2,96,1024]{2,1,0:T(8,128)(2,1)S(1)} %collective-permute-done.7.refs_4_), channel_id=1, source_target_pairs={{2,0},{3,1},{4,6},{5,7},{10,8},{11,9},{12,14},{13,15},{18,16},{19,... | collective-permute-start | bytes 1179656 | tf_op jit(solution)/shard_map/ppermute | solution.py:32
  57.2 5.0 %collective-permute-done.12.refs_0_ = bf16[2,2,6,64,128]{4,3,2,1,0:T(8,128)(2,1)S(1)} collective-permute-done((bf16[2,2,6,64,128]{4,3,2,1,0:T(8,128)(2,1)S(1)}, bf16[2,2,6,64,128]{4,3,2,1,0:T(8,128)(2,1)S(1)}, u32[]{:S(2)}, u32[]{:S(2)}) %collective-permute-start.12) | collective-permute-done | bytes 393248 | tf_op jit(solution)/shard_map/ppermute | solution.py:27
  62.2 7.6 %collective-permute-done.13.refs_1_ = bf16[2,2,6,64,128]{4,3,2,1,0:T(8,128)(2,1)S(1)} collective-permute-done((bf16[2,2,6,64,128]{4,3,2,1,0:T(8,128)(2,1)S(1)}, bf16[2,2,6,64,128]{4,3,2,1,0:T(8,128)(2,1)S(1)}, u32[]{:S(2)}, u32[]{:S(2)}) %collective-permute-start.13) | collective-permute-done | bytes 393248 | tf_op jit(solution)/shard_map/ppermute | solution.py:27
  69.8 0.7 lay_out.1.refs_6_
  70.5 0.0 collective-permute-done.5.refs_2_
  70.5 0.4 collective-permute-done.6.refs_3_
  70.9 1.7 %collective-permute-done.8.refs_5_ = bf16[2,96,1024]{2,1,0:T(8,128)(2,1)S(1)} collective-permute-done((bf16[2,96,1024]{2,1,0:T(8,128)(2,1)S(1)}, bf16[2,96,1024]{2,1,0:T(8,128)(2,1)S(1)}, u32[]{:S(2)}, u32[]{:S(2)}) %collective-permute-start.8) | collective-permute-done | bytes 393248 | tf_op jit(solution)/shard_map/ppermute | solution.py:32
  72.6 1.6 %traces.1 = f32[2,4,12,12]{3,2,1,0:T(8,128)S(1)} custom-call(s32[4]{0:T(128)S(1)} %copy-done.1, bf16[96,1024]{1,0:T(8,128)(2,1)S(1)} %get-tuple-element.25.refs_0_, bf16[96,1024]{1,0:T(8,128)(2,1)S(1)} %collective-permute-done.4.refs_1_, bf16[2,96,1024]{2,1,0:T(8,128)(2,1)S(1)} %collective-permute-done.5.refs_2_, ...), custom_call_target="tpu_custom_call" | custom-call | flops 37748736 | bytes 1572864 | tf_op jit(solution)/shard_map/traces/pallas_call | solution.py:440
  74.2 0.1 collective-permute-start.14
  74.3 1.2 %collective-permute-done.14 = f32[2,4,12,12]{3,2,1,0:T(8,128)S(1)} collective-permute-done((f32[2,4,12,12]{3,2,1,0:T(8,128)S(1)}, f32[2,4,12,12]{3,2,1,0:T(8,128)S(1)}, u32[]{:S(2)}, u32[]{:S(2)}) %collective-permute-start.14) | collective-permute-done | bytes 4640 | tf_op jit(solution)/shard_map/ppermute | solution.py:27
  75.6 1.5 %collective-permute-start.15 = (f32[4,12,12]{2,1,0:T(8,128)S(1)}, f32[4,12,12]{2,1,0:T(8,128)S(1)}, u32[]{:S(2)}, u32[]{:S(2)}) collective-permute-start(f32[4,12,12]{2,1,0:T(8,128)S(1)} %get-tuple-element.39), channel_id=1, source_target_pairs={{0,16},{8,24},{16,0},{24,8},{1,17},{9,25},{17,1},{25,9},{2,18},{10... | collective-permute-start | bytes 6920 | tf_op jit(solution)/shard_map/ppermute | solution.py:27
  77.1 1.5 %collective-permute-start.16 = (f32[4,12,12]{2,1,0:T(8,128)S(1)}, f32[4,12,12]{2,1,0:T(8,128)S(1)}, u32[]{:S(2)}, u32[]{:S(2)}) collective-permute-start(f32[4,12,12]{2,1,0:T(8,128)S(1)} %get-tuple-element.38), channel_id=1, source_target_pairs={{0,1},{1,0},{2,3},{3,2},{4,5},{5,4},{6,7},{7,6},{8,9},{9,8},{10,11... | collective-permute-start | bytes 6920 | tf_op jit(solution)/shard_map/ppermute | solution.py:27
  78.6 0.5 collective-permute-start.17
  79.1 0.4 collective-permute-done.15.refs_1_
  79.5 1.8 %collective-permute-done.16.refs_2_ = f32[4,12,12]{2,1,0:T(8,128)S(1)} collective-permute-done((f32[4,12,12]{2,1,0:T(8,128)S(1)}, f32[4,12,12]{2,1,0:T(8,128)S(1)}, u32[]{:S(2)}, u32[]{:S(2)}) %collective-permute-start.16) | collective-permute-done | bytes 2336 | tf_op jit(solution)/shard_map/ppermute | solution.py:27
  81.3 2.1 %collective-permute-done.17.refs_3_ = f32[4,12,12]{2,1,0:T(8,128)S(1)} collective-permute-done((f32[4,12,12]{2,1,0:T(8,128)S(1)}, f32[4,12,12]{2,1,0:T(8,128)S(1)}, u32[]{:S(2)}, u32[]{:S(2)}) %collective-permute-start.17) | collective-permute-done | bytes 2336 | tf_op jit(solution)/shard_map/ppermute | solution.py:552
  83.4 0.9 %finish.1 = (f32[1,4,6,2,6]{4,3,2,1,0:T(2,128)}, f32[1,4,6,2,6]{4,3,2,1,0:T(2,128)}) custom-call(f32[2,4,12,12]{3,2,1,0:T(8,128)S(1)} %add.86.refs_0_, f32[4,12,12]{2,1,0:T(8,128)S(1)} %collective-permute-done.15.refs_1_, f32[4,12,12]{2,1,0:T(8,128)S(1)} %collective-permute-done.16.refs_2_, f32[4,12,12]{2,1,0:T(8,128)S(1)} %collective-permute-done.17.refs_3_), custom_call_target="tpu_custom_call" | custom-call | tf_op jit(solution)/shard_map/finish/pallas_call | solution.py:485
  (16 shorter events, 0.1 us)
Async XLA Ops:
  0.6 4.3 %collective-permute-start.1 = (bf16[2,3,256,256]{3,2,1,0:T(8,128)(2,1)}, bf16[2,3,256,256]{3,2,1,0:T(8,128)(2,1)S(1)}, u32[]{:S(2)}, u32[]{:S(2)}) collective-permute-start(bf16[2,3,256,256]{3,2,1,0:T(8,128)(2,1)} %bitcast.21), channel_id=1, source_target_pairs={{0,8},{8,0},{16,24},{24,16},{1,9},{9,1},{17,25},{25,17},{2,10},{10... | collective-permute-start | bytes 2359304 | tf_op jit(solution)/shard_map/ppermute | solution.py:27
  1.1 20.9 %collective-permute-start = (bf16[2,3,256,256]{3,2,1,0:T(8,128)(2,1)}, bf16[2,3,256,256]{3,2,1,0:T(8,128)(2,1)S(1)}, u32[]{:S(2)}, u32[]{:S(2)}) collective-permute-start(bf16[2,3,256,256]{3,2,1,0:T(8,128)(2,1)} %bitcast.22), channel_id=1, source_target_pairs={{0,16},{8,24},{16,0},{24,8},{1,17},{9,25},{17,1},{25,9},{2,18},{10... | collective-permute-start | bytes 2359304 | tf_op jit(solution)/shard_map/ppermute | solution.py:27
  5.0 17.1 %copy-start = (bf16[1,4,2,64,256]{4,3,2,1,0:T(8,128)(2,1)S(1)}, bf16[1,4,2,64,256]{4,3,2,1,0:T(8,128)(2,1)}, u32[]{:S(2)}) copy-start(bf16[1,4,2,64,256]{4,3,2,1,0:T(8,128)(2,1)} %param.9) | copy-start | bytes 786436
  5.0 1.2 %copy-start.2 = (bf16[1,2,3,1,256,256]{5,4,3,2,1,0:T(8,128)(2,1)S(1)}, bf16[1,2,3,1,256,256]{5,4,3,2,1,0:T(8,128)(2,1)}, u32[]{:S(2)}) copy-start(bf16[1,2,3,1,256,256]{5,4,3,2,1,0:T(8,128)(2,1)} %param.5) | copy-start | bytes 2359300
  6.2 0.7 copy-start.4
  6.8 17.6 %copy-start.3 = (bf16[1,2,3,1,256,256]{5,4,3,2,1,0:T(8,128)(2,1)S(1)}, bf16[1,2,3,1,256,256]{5,4,3,2,1,0:T(8,128)(2,1)}, u32[]{:S(2)}) copy-start(bf16[1,2,3,1,256,256]{5,4,3,2,1,0:T(8,128)(2,1)} %param.5) | copy-start | bytes 2359300
  6.8 17.6 %copy-start.5 = (s32[6]{0:T(128)S(1)}, s32[6]{0:T(128)}, u32[]{:S(2)}) copy-start(s32[6]{0:T(128)} %refs_0_.3) | copy-start | bytes 76
  22.1 2.3 %collective-permute-start.2 = (bf16[2,3,256,256]{3,2,1,0:T(8,128)(2,1)S(1)}, bf16[2,3,256,256]{3,2,1,0:T(8,128)(2,1)S(1)}, u32[]{:S(2)}, u32[]{:S(2)}) collective-permute-start(bf16[2,3,256,256]{3,2,1,0:T(8,128)(2,1)S(1)} %collective-permute-done.refs_4_), channel_id=1, source_target_pairs={{0,8},{8,0},{16,24},{24,16},{1,9},{9,1},{17,25},{25,17},{2,10},{10... | collective-permute-start | bytes 2359304 | tf_op jit(solution)/shard_map/ppermute | solution.py:27
  22.1 12.5 %collective-permute-start.3 = (bf16[4,2,64,256]{3,2,1,0:T(8,128)(2,1)S(1)}, bf16[4,2,64,256]{3,2,1,0:T(8,128)(2,1)S(1)}, u32[]{:S(2)}, u32[]{:S(2)}) collective-permute-start(bf16[4,2,64,256]{3,2,1,0:T(8,128)(2,1)S(1)} %bitcast.18), channel_id=1, source_target_pairs={{0,16},{8,24},{16,0},{24,8},{1,17},{9,25},{17,1},{25,9},{2,18},{10... | collective-permute-start | bytes 786440 | tf_op jit(solution)/shard_map/ppermute | solution.py:27
  34.6 13.2 %collective-permute-start.9 = (bf16[6,256,256]{2,1,0:T(8,128)(2,1)S(1)}, bf16[6,256,256]{2,1,0:T(8,128)(2,1)S(1)}, u32[]{:S(2)}, u32[]{:S(2)}) collective-permute-start(bf16[6,256,256]{2,1,0:T(8,128)(2,1)S(1)} %get-tuple-element.30.e_ref), channel_id=1, source_target_pairs={{0,8},{8,0},{16,24},{24,16},{1,9},{9,1},{17,25},{25,17},{2,10},{10... | collective-permute-start | bytes 2359304 | tf_op jit(solution)/shard_map/ppermute | solution.py:27
  34.8 7.2 %collective-permute-start.4 = (bf16[96,1024]{1,0:T(8,128)(2,1)S(1)}, bf16[96,1024]{1,0:T(8,128)(2,1)S(1)}, u32[]{:S(2)}, u32[]{:S(2)}) collective-permute-start(bf16[96,1024]{1,0:T(8,128)(2,1)S(1)} %get-tuple-element.29), channel_id=1, source_target_pairs={{0,1},{1,0},{2,3},{3,2},{4,5},{5,4},{6,7},{7,6},{8,9},{9,8},{10,11... | collective-permute-start | bytes 589832 | tf_op jit(solution)/shard_map/ppermute | solution.py:27
  42.0 13.9 %collective-permute-start.7 = (bf16[2,96,1024]{2,1,0:T(8,128)(2,1)S(1)}, bf16[2,96,1024]{2,1,0:T(8,128)(2,1)S(1)}, u32[]{:S(2)}, u32[]{:S(2)}) collective-permute-start(bf16[2,96,1024]{2,1,0:T(8,128)(2,1)S(1)} %pad_maximum_fusion), channel_id=1, source_target_pairs={{2,4},{3,5},{4,2},{5,3},{0,6},{1,7},{6,0},{7,1},{10,12},{11,13},{1... | collective-permute-start | bytes 1179656 | tf_op jit(solution)/shard_map/ppermute | solution.py:32
  45.9 1.5 %collective-permute-start.10 = (bf16[4,2,64,256]{3,2,1,0:T(8,128)(2,1)S(1)}, bf16[4,2,64,256]{3,2,1,0:T(8,128)(2,1)S(1)}, u32[]{:S(2)}, u32[]{:S(2)}) collective-permute-start(bf16[4,2,64,256]{3,2,1,0:T(8,128)(2,1)S(1)} %bitcast.19), channel_id=1, source_target_pairs={{0,8},{8,0},{16,24},{24,16},{1,9},{9,1},{17,25},{25,17},{2,10},{10... | collective-permute-start | bytes 786440 | tf_op jit(solution)/shard_map/ppermute | solution.py:27
  45.9 1.9 %collective-permute-start.11 = (bf16[4,2,64,256]{3,2,1,0:T(8,128)(2,1)S(1)}, bf16[4,2,64,256]{3,2,1,0:T(8,128)(2,1)S(1)}, u32[]{:S(2)}, u32[]{:S(2)}) collective-permute-start(bf16[4,2,64,256]{3,2,1,0:T(8,128)(2,1)S(1)} %collective-permute-done.3.refs_2_), channel_id=1, source_target_pairs={{0,8},{8,0},{16,24},{24,16},{1,9},{9,1},{17,25},{25,17},{2,10},{10... | collective-permute-start | bytes 786440 | tf_op jit(solution)/shard_map/ppermute | solution.py:27
  50.1 12.0 %collective-permute-start.12 = (bf16[2,2,6,64,128]{4,3,2,1,0:T(8,128)(2,1)S(1)}, bf16[2,2,6,64,128]{4,3,2,1,0:T(8,128)(2,1)S(1)}, u32[]{:S(2)}, u32[]{:S(2)}) collective-permute-start(bf16[2,2,6,64,128]{4,3,2,1,0:T(8,128)(2,1)S(1)} %get-tuple-element.34), channel_id=1, source_target_pairs={{0,1},{1,0},{2,3},{3,2},{4,5},{5,4},{6,7},{7,6},{8,9},{9,8},{10,11... | collective-permute-start | bytes 1179656 | tf_op jit(solution)/shard_map/ppermute | solution.py:27
  51.7 18.1 %collective-permute-start.13 = (bf16[2,2,6,64,128]{4,3,2,1,0:T(8,128)(2,1)S(1)}, bf16[2,2,6,64,128]{4,3,2,1,0:T(8,128)(2,1)S(1)}, u32[]{:S(2)}, u32[]{:S(2)}) collective-permute-start(bf16[2,2,6,64,128]{4,3,2,1,0:T(8,128)(2,1)S(1)} %get-tuple-element.35), channel_id=1, source_target_pairs={{0,1},{1,0},{2,3},{3,2},{4,5},{5,4},{6,7},{7,6},{8,9},{9,8},{10,11... | collective-permute-start | bytes 1179656 | tf_op jit(solution)/shard_map/ppermute | solution.py:27
  52.2 18.2 %collective-permute-start.5 = (bf16[2,96,1024]{2,1,0:T(8,128)(2,1)S(1)}, bf16[2,96,1024]{2,1,0:T(8,128)(2,1)S(1)}, u32[]{:S(2)}, u32[]{:S(2)}) collective-permute-start(bf16[2,96,1024]{2,1,0:T(8,128)(2,1)S(1)} %pad_maximum_fusion), channel_id=1, source_target_pairs={{0,2},{1,3},{2,0},{3,1},{4,6},{5,7},{6,4},{7,5},{8,10},{9,11},{10,... | collective-permute-start | bytes 1179656 | tf_op jit(solution)/shard_map/ppermute | solution.py:32
  52.2 18.7 %collective-permute-start.6 = (bf16[2,96,1024]{2,1,0:T(8,128)(2,1)S(1)}, bf16[2,96,1024]{2,1,0:T(8,128)(2,1)S(1)}, u32[]{:S(2)}, u32[]{:S(2)}) collective-permute-start(bf16[2,96,1024]{2,1,0:T(8,128)(2,1)S(1)} %pad_maximum_fusion), channel_id=1, source_target_pairs={{0,4},{1,5},{6,2},{7,3},{8,12},{9,13},{14,10},{15,11},{16,20},{17,... | collective-permute-start | bytes 1179656 | tf_op jit(solution)/shard_map/ppermute | solution.py:32
  55.9 16.7 %collective-permute-start.8 = (bf16[2,96,1024]{2,1,0:T(8,128)(2,1)S(1)}, bf16[2,96,1024]{2,1,0:T(8,128)(2,1)S(1)}, u32[]{:S(2)}, u32[]{:S(2)}) collective-permute-start(bf16[2,96,1024]{2,1,0:T(8,128)(2,1)S(1)} %collective-permute-done.7.refs_4_), channel_id=1, source_target_pairs={{2,0},{3,1},{4,6},{5,7},{10,8},{11,9},{12,14},{13,15},{18,16},{19,... | collective-permute-start | bytes 1179656 | tf_op jit(solution)/shard_map/ppermute | solution.py:32
  69.8 2.8 %copy-start.1 = (s32[4]{0:T(128)S(1)}, s32[4]{0:T(128)}, u32[]{:S(2)}) copy-start(s32[4]{0:T(128)} %times_ref.1) | copy-start | bytes 52
  74.2 1.3 %collective-permute-start.14 = (f32[2,4,12,12]{3,2,1,0:T(8,128)S(1)}, f32[2,4,12,12]{3,2,1,0:T(8,128)S(1)}, u32[]{:S(2)}, u32[]{:S(2)}) collective-permute-start(f32[2,4,12,12]{3,2,1,0:T(8,128)S(1)} %traces.1), channel_id=1, source_target_pairs={{0,8},{8,0},{16,24},{24,16},{1,9},{9,1},{17,25},{25,17},{2,10},{10... | collective-permute-start | bytes 13832 | tf_op jit(solution)/shard_map/ppermute | solution.py:27
  75.6 4.0 %collective-permute-start.15 = (f32[4,12,12]{2,1,0:T(8,128)S(1)}, f32[4,12,12]{2,1,0:T(8,128)S(1)}, u32[]{:S(2)}, u32[]{:S(2)}) collective-permute-start(f32[4,12,12]{2,1,0:T(8,128)S(1)} %get-tuple-element.39), channel_id=1, source_target_pairs={{0,16},{8,24},{16,0},{24,8},{1,17},{9,25},{17,1},{25,9},{2,18},{10... | collective-permute-start | bytes 6920 | tf_op jit(solution)/shard_map/ppermute | solution.py:27
  77.1 4.2 %collective-permute-start.16 = (f32[4,12,12]{2,1,0:T(8,128)S(1)}, f32[4,12,12]{2,1,0:T(8,128)S(1)}, u32[]{:S(2)}, u32[]{:S(2)}) collective-permute-start(f32[4,12,12]{2,1,0:T(8,128)S(1)} %get-tuple-element.38), channel_id=1, source_target_pairs={{0,1},{1,0},{2,3},{3,2},{4,5},{5,4},{6,7},{7,6},{8,9},{9,8},{10,11... | collective-permute-start | bytes 6920 | tf_op jit(solution)/shard_map/ppermute | solution.py:27
  78.6 4.8 %collective-permute-start.17 = (f32[4,12,12]{2,1,0:T(8,128)S(1)}, f32[4,12,12]{2,1,0:T(8,128)S(1)}, u32[]{:S(2)}, u32[]{:S(2)}) collective-permute-start(f32[4,12,12]{2,1,0:T(8,128)S(1)} %get-tuple-element.38), channel_id=1, source_target_pairs={{0,17},{1,16},{2,19},{3,18},{4,21},{5,20},{6,23},{7,22},{8,25},{9,... | collective-permute-start | bytes 6920 | tf_op jit(solution)/shard_map/ppermute | solution.py:552

commit v8 on v6

--- a/solution.py
+++ b/solution.py
@@ -45,8 +45,8 @@
     outward = {1: 0, 2: 3}
     piece = jnp.stack([keep, received])
     opposite = along_line(piece, {1: 2, 2: 1, 0: 3, 3: 0})
+    near = along_line(piece, {0: 1, 1: 0, 2: 3, 3: 2})
     skip = along_line(piece, {0: 2, 3: 1})
-    near = along_line(piece, {0: 1, 1: 0, 2: 3, 3: 2})
     passed = along_line(opposite, outward)
     arrays = [keep, received, near, skip, opposite, passed]
     table = {0: (0, None), 1: (1, None)}

time: 85.2 us -> 84.7 us (level)
  waiting for transfers between devices: 35.5 us -> 34.5 us
    ppermute x13, waiting for transfers between devices: 32.1 us -> 31.1 us  [swap_bit(): return lax.ppermute(block, axis, [(i, i ^ mask) for i in range(count)])]
  transfers between devices with their start and end apart: 18 -> 18, of which waited for: 12 -> 12; matrix products, arithmetic and copies ran while one was open for 1% -> 1% of each run, Pallas kernels for 26% -> 27%
where the time goes in v8:
time: 84.7 us; the launch traced here: 84.3 us
  waiting for transfers between devices  34.5 us (41%)
  Pallas kernels  25.2 us (30%)
  starting transfers between devices  20.8 us (25%)
  local copies, waits for them, and re-layouts  2.66 us (3%)
    ppermute x13, waiting for transfers between devices, swap_bit(): return lax.ppermute(block, axis, [(i, i ^ mask) for i in range(count)])  31.1 us
    pallas_call x2, Pallas kernels, elementals(): pl.pallas_call(functools.partial(elemental_kernel, held, near, late, bloc...  18.9 us
    ppermute x13, starting transfers between devices, swap_bit(): return lax.ppermute(block, axis, [(i, i ^ mask) for i in range(count)])  12.6 us
    ppermute x4, starting transfers between devices, along_line(): return lax.ppermute(block, 'tm', route)  7.75 us
    pallas_call x1, Pallas kernels, both_sides(): pl.pallas_call(functools.partial(both_kernel, blocks), out_shape=(piece,)...  3.11 us
    ppermute x1, waiting for transfers between devices, across(): return lax.ppermute(block, ('space', 'tm'), route)  2.1 us
    unnamed x12, local copies, waits for them, and re-layouts  1.84 us
  transfers between devices with their start and end apart: 18, of which 12 were waited for; matrix products, arithmetic and copies ran while one was open for 1% of the time, Pallas kernels for 27%

profile of v8, /device:TPU:0, one launch (start us, length us, event | category | flops | bytes accessed | tf_op | source)
XLA Modules:
  0.0 84.3 jit_solution(3815010906967823056)
XLA Ops:
  0.6 0.5 collective-permute-start.1
  1.1 2.6 %collective-permute-start = (bf16[2,3,256,256]{3,2,1,0:T(8,128)(2,1)}, bf16[2,3,256,256]{3,2,1,0:T(8,128)(2,1)S(1)}, u32[]{:S(2)}, u32[]{:S(2)}) collective-permute-start(bf16[2,3,256,256]{3,2,1,0:T(8,128)(2,1)} %bitcast.22), channel_id=1, source_target_pairs={{0,16},{8,24},{16,0},{24,8},{1,17},{9,25},{17,1},{25,9},{2,18},{10... | collective-permute-start | bytes 2359304 | tf_op jit(solution)/shard_map/ppermute | solution.py:27
  3.7 0.8 slice_bitcast_fusion.3
  4.5 0.3 fusion.13
  4.9 0.1 fusion.11
  5.0 0.0 copy-start
  5.0 0.0 collective-permute-done.1.refs_3_
  5.0 0.0 copy-start.2
  5.0 1.2 %copy-done.2 = bf16[1,2,3,1,256,256]{5,4,3,2,1,0:T(8,128)(2,1)S(1)} copy-done((bf16[1,2,3,1,256,256]{5,4,3,2,1,0:T(8,128)(2,1)S(1)}, bf16[1,2,3,1,256,256]{5,4,3,2,1,0:T(8,128)(2,1)}, u32[]{:S(2)}) %copy-start.2) | copy-done | bytes 786456
  6.2 0.7 copy-done.4
  6.8 8.7 %elementals_early.1 = (f32[6,256,256]{2,1,0:T(8,128)S(1)}, f32[6,2,256,128]{3,2,1,0:T(8,128)S(1)}) custom-call(s32[6]{0:T(128)S(1)} %copy-done.4, f32[2,4,6]{2,1,0:T(4,128)S(1)} %pad_maximum_fusion.2.refs_1_, bf16[2,3,256,256]{3,2,1,0:T(8,128)(2,1)S(1)} %bitcast.23, bf16[2,3,256,256]{3,2,1,0:T(8,128)(2,1)S(1)} %collective-permute-done.1.refs_3_, ...), custom_call_target="tpu_custom_call" | custom-call | flops 4831838208 | bytes 1572864 | tf_op jit(solution)/shard_map/elementals_early/pallas_call | solution.py:243
  15.5 6.6 %collective-permute-done.refs_4_ = bf16[2,3,256,256]{3,2,1,0:T(8,128)(2,1)S(1)} collective-permute-done((bf16[2,3,256,256]{3,2,1,0:T(8,128)(2,1)}, bf16[2,3,256,256]{3,2,1,0:T(8,128)(2,1)S(1)}, u32[]{:S(2)}, u32[]{:S(2)}) %collective-permute-start) | collective-permute-done | bytes 786464 | tf_op jit(solution)/shard_map/ppermute | solution.py:27
  22.1 0.0 collective-permute-start.2
  22.1 1.8 %collective-permute-start.3 = (bf16[4,2,64,256]{3,2,1,0:T(8,128)(2,1)S(1)}, bf16[4,2,64,256]{3,2,1,0:T(8,128)(2,1)S(1)}, u32[]{:S(2)}, u32[]{:S(2)}) collective-permute-start(bf16[4,2,64,256]{3,2,1,0:T(8,128)(2,1)S(1)} %bitcast.18), channel_id=1, source_target_pairs={{0,16},{8,24},{16,0},{24,8},{1,17},{9,25},{17,1},{25,9},{2,18},{10... | collective-permute-start | bytes 786440 | tf_op jit(solution)/shard_map/ppermute | solution.py:27
  23.9 0.5 collective-permute-done.2.refs_5_
  24.4 10.2 %elementals_late.1 = (bf16[6,256,256]{2,1,0:T(8,128)(2,1)S(1)}, bf16[96,1024]{1,0:T(8,128)(2,1)S(1)}, bf16[96,1024]{1,0:T(8,128)(2,1)S(1)}) custom-call(s32[6]{0:T(128)S(1)} %copy-done.5, f32[2,4,6]{2,1,0:T(4,128)S(1)} %pad_maximum_fusion.2.refs_1_, bf16[2,3,256,256]{3,2,1,0:T(8,128)(2,1)S(1)} %bitcast.24, ...), custom_call_target="tpu_custom_call" | custom-call | flops 9663676416 | bytes 3145728 | tf_op jit(solution)/shard_map/elementals_late/pallas_call | solution.py:243
  34.6 0.0 collective-permute-done.3.refs_2_
  34.6 0.2 collective-permute-start.9
  34.8 1.7 %collective-permute-start.4 = (bf16[96,1024]{1,0:T(8,128)(2,1)S(1)}, bf16[96,1024]{1,0:T(8,128)(2,1)S(1)}, u32[]{:S(2)}, u32[]{:S(2)}) collective-permute-start(bf16[96,1024]{1,0:T(8,128)(2,1)S(1)} %get-tuple-element.29), channel_id=1, source_target_pairs={{0,1},{1,0},{2,3},{3,2},{4,5},{5,4},{6,7},{7,6},{8,9},{9,8},{10,11... | collective-permute-start | bytes 589832 | tf_op jit(solution)/shard_map/ppermute | solution.py:27
  36.5 5.4 %collective-permute-done.4.refs_1_ = bf16[96,1024]{1,0:T(8,128)(2,1)S(1)} collective-permute-done((bf16[96,1024]{1,0:T(8,128)(2,1)S(1)}, bf16[96,1024]{1,0:T(8,128)(2,1)S(1)}, u32[]{:S(2)}, u32[]{:S(2)}) %collective-permute-start.4) | collective-permute-done | bytes 196640 | tf_op jit(solution)/shard_map/ppermute | solution.py:27
  42.0 3.9 %collective-permute-start.7 = (bf16[2,96,1024]{2,1,0:T(8,128)(2,1)S(1)}, bf16[2,96,1024]{2,1,0:T(8,128)(2,1)S(1)}, u32[]{:S(2)}, u32[]{:S(2)}) collective-permute-start(bf16[2,96,1024]{2,1,0:T(8,128)(2,1)S(1)} %pad_maximum_fusion), channel_id=1, source_target_pairs={{2,4},{3,5},{4,2},{5,3},{0,6},{1,7},{6,0},{7,1},{10,12},{11,13},{1... | collective-permute-start | bytes 1179656 | tf_op jit(solution)/shard_map/ppermute | solution.py:32
  45.9 0.0 collective-permute-start.10
  45.9 0.5 collective-permute-start.11
  46.4 1.0 %collective-permute-done.10.refs_1_ = bf16[4,2,64,256]{3,2,1,0:T(8,128)(2,1)S(1)} collective-permute-done((bf16[4,2,64,256]{3,2,1,0:T(8,128)(2,1)S(1)}, bf16[4,2,64,256]{3,2,1,0:T(8,128)(2,1)S(1)}, u32[]{:S(2)}, u32[]{:S(2)}) %collective-permute-start.10) | collective-permute-done | bytes 262176 | tf_op jit(solution)/shard_map/ppermute | solution.py:27
  47.5 0.4 collective-permute-done.11.refs_3_
  47.8 0.0 collective-permute-done.9.other_ref
  47.8 3.1 %both_sides.1 = (bf16[4,2,6,64,128]{4,3,2,1,0:T(8,128)(2,1)S(1)}, bf16[2,2,6,64,128]{4,3,2,1,0:T(8,128)(2,1)S(1)}, bf16[2,2,6,64,128]{4,3,2,1,0:T(8,128)(2,1)S(1)}) custom-call(bf16[6,256,256]{2,1,0:T(8,128)(2,1)S(1)} %get-tuple-element.30.e_ref, bf16[6,256,256]{2,1,0:T(8,128)(2,1)S(1)} %collective-permute-done.9.other_ref, ...), custom_call_target="tpu_custom_call" | custom-call | tf_op jit(solution)/shard_map/both_sides/pallas_call | solution.py:339
  51.0 1.6 %collective-permute-start.12 = (bf16[2,2,6,64,128]{4,3,2,1,0:T(8,128)(2,1)S(1)}, bf16[2,2,6,64,128]{4,3,2,1,0:T(8,128)(2,1)S(1)}, u32[]{:S(2)}, u32[]{:S(2)}) collective-permute-start(bf16[2,2,6,64,128]{4,3,2,1,0:T(8,128)(2,1)S(1)} %get-tuple-element.34), channel_id=1, source_target_pairs={{0,1},{1,0},{2,3},{3,2},{4,5},{5,4},{6,7},{7,6},{8,9},{9,8},{10,11... | collective-permute-start | bytes 1179656 | tf_op jit(solution)/shard_map/ppermute | solution.py:27
  52.5 0.5 collective-permute-start.13
  53.1 0.0 collective-permute-start.5
  53.1 2.6 %collective-permute-start.6 = (bf16[2,96,1024]{2,1,0:T(8,128)(2,1)S(1)}, bf16[2,96,1024]{2,1,0:T(8,128)(2,1)S(1)}, u32[]{:S(2)}, u32[]{:S(2)}) collective-permute-start(bf16[2,96,1024]{2,1,0:T(8,128)(2,1)S(1)} %pad_maximum_fusion), channel_id=1, source_target_pairs={{0,4},{1,5},{6,2},{7,3},{8,12},{9,13},{14,10},{15,11},{16,20},{17,... | collective-permute-start | bytes 1179656 | tf_op jit(solution)/shard_map/ppermute | solution.py:32
  55.6 1.3 %collective-permute-start.8 = (bf16[2,96,1024]{2,1,0:T(8,128)(2,1)S(1)}, bf16[2,96,1024]{2,1,0:T(8,128)(2,1)S(1)}, u32[]{:S(2)}, u32[]{:S(2)}) collective-permute-start(bf16[2,96,1024]{2,1,0:T(8,128)(2,1)S(1)} %collective-permute-done.7.refs_4_), channel_id=1, source_target_pairs={{2,0},{3,1},{4,6},{5,7},{10,8},{11,9},{12,14},{13,15},{18,16},{19,... | collective-permute-start | bytes 1179656 | tf_op jit(solution)/shard_map/ppermute | solution.py:32
  56.9 6.1 %collective-permute-done.12.refs_0_ = bf16[2,2,6,64,128]{4,3,2,1,0:T(8,128)(2,1)S(1)} collective-permute-done((bf16[2,2,6,64,128]{4,3,2,1,0:T(8,128)(2,1)S(1)}, bf16[2,2,6,64,128]{4,3,2,1,0:T(8,128)(2,1)S(1)}, u32[]{:S(2)}, u32[]{:S(2)}) %collective-permute-start.12) | collective-permute-done | bytes 393248 | tf_op jit(solution)/shard_map/ppermute | solution.py:27
  63.0 7.6 %collective-permute-done.13.refs_1_ = bf16[2,2,6,64,128]{4,3,2,1,0:T(8,128)(2,1)S(1)} collective-permute-done((bf16[2,2,6,64,128]{4,3,2,1,0:T(8,128)(2,1)S(1)}, bf16[2,2,6,64,128]{4,3,2,1,0:T(8,128)(2,1)S(1)}, u32[]{:S(2)}, u32[]{:S(2)}) %collective-permute-start.13) | collective-permute-done | bytes 393248 | tf_op jit(solution)/shard_map/ppermute | solution.py:27
  70.6 0.7 lay_out.1.refs_6_
  71.3 0.0 collective-permute-done.5.refs_2_
  71.3 0.0 collective-permute-done.6.refs_3_
  71.3 1.2 %collective-permute-done.8.refs_5_ = bf16[2,96,1024]{2,1,0:T(8,128)(2,1)S(1)} collective-permute-done((bf16[2,96,1024]{2,1,0:T(8,128)(2,1)S(1)}, bf16[2,96,1024]{2,1,0:T(8,128)(2,1)S(1)}, u32[]{:S(2)}, u32[]{:S(2)}) %collective-permute-start.8) | collective-permute-done | bytes 393248 | tf_op jit(solution)/shard_map/ppermute | solution.py:32
  72.6 1.6 %traces.1 = f32[2,4,12,12]{3,2,1,0:T(8,128)S(1)} custom-call(s32[4]{0:T(128)S(1)} %copy-done.1, bf16[96,1024]{1,0:T(8,128)(2,1)S(1)} %get-tuple-element.25.refs_0_, bf16[96,1024]{1,0:T(8,128)(2,1)S(1)} %collective-permute-done.4.refs_1_, bf16[2,96,1024]{2,1,0:T(8,128)(2,1)S(1)} %collective-permute-done.5.refs_2_, ...), custom_call_target="tpu_custom_call" | custom-call | flops 37748736 | bytes 1572864 | tf_op jit(solution)/shard_map/traces/pallas_call | solution.py:443
  74.2 0.1 collective-permute-start.14
  74.3 1.2 %collective-permute-done.14 = f32[2,4,12,12]{3,2,1,0:T(8,128)S(1)} collective-permute-done((f32[2,4,12,12]{3,2,1,0:T(8,128)S(1)}, f32[2,4,12,12]{3,2,1,0:T(8,128)S(1)}, u32[]{:S(2)}, u32[]{:S(2)}) %collective-permute-start.14) | collective-permute-done | bytes 4640 | tf_op jit(solution)/shard_map/ppermute | solution.py:27
  75.5 1.6 %collective-permute-start.15 = (f32[4,12,12]{2,1,0:T(8,128)S(1)}, f32[4,12,12]{2,1,0:T(8,128)S(1)}, u32[]{:S(2)}, u32[]{:S(2)}) collective-permute-start(f32[4,12,12]{2,1,0:T(8,128)S(1)} %get-tuple-element.39), channel_id=1, source_target_pairs={{0,16},{8,24},{16,0},{24,8},{1,17},{9,25},{17,1},{25,9},{2,18},{10... | collective-permute-start | bytes 6920 | tf_op jit(solution)/shard_map/ppermute | solution.py:27
  77.1 1.5 %collective-permute-start.16 = (f32[4,12,12]{2,1,0:T(8,128)S(1)}, f32[4,12,12]{2,1,0:T(8,128)S(1)}, u32[]{:S(2)}, u32[]{:S(2)}) collective-permute-start(f32[4,12,12]{2,1,0:T(8,128)S(1)} %get-tuple-element.38), channel_id=1, source_target_pairs={{0,1},{1,0},{2,3},{3,2},{4,5},{5,4},{6,7},{7,6},{8,9},{9,8},{10,11... | collective-permute-start | bytes 6920 | tf_op jit(solution)/shard_map/ppermute | solution.py:27
  78.6 0.5 collective-permute-start.17
  79.1 0.4 collective-permute-done.15.refs_1_
  79.5 1.8 %collective-permute-done.16.refs_2_ = f32[4,12,12]{2,1,0:T(8,128)S(1)} collective-permute-done((f32[4,12,12]{2,1,0:T(8,128)S(1)}, f32[4,12,12]{2,1,0:T(8,128)S(1)}, u32[]{:S(2)}, u32[]{:S(2)}) %collective-permute-start.16) | collective-permute-done | bytes 2336 | tf_op jit(solution)/shard_map/ppermute | solution.py:27
  81.3 2.1 %collective-permute-done.17.refs_3_ = f32[4,12,12]{2,1,0:T(8,128)S(1)} collective-permute-done((f32[4,12,12]{2,1,0:T(8,128)S(1)}, f32[4,12,12]{2,1,0:T(8,128)S(1)}, u32[]{:S(2)}, u32[]{:S(2)}) %collective-permute-start.17) | collective-permute-done | bytes 2336 | tf_op jit(solution)/shard_map/ppermute | solution.py:555
  83.4 0.9 %finish.1 = (f32[1,4,6,2,6]{4,3,2,1,0:T(2,128)}, f32[1,4,6,2,6]{4,3,2,1,0:T(2,128)}) custom-call(f32[2,4,12,12]{3,2,1,0:T(8,128)S(1)} %add.86.refs_0_, f32[4,12,12]{2,1,0:T(8,128)S(1)} %collective-permute-done.15.refs_1_, f32[4,12,12]{2,1,0:T(8,128)S(1)} %collective-permute-done.16.refs_2_, f32[4,12,12]{2,1,0:T(8,128)S(1)} %collective-permute-done.17.refs_3_), custom_call_target="tpu_custom_call" | custom-call | tf_op jit(solution)/shard_map/finish/pallas_call | solution.py:488
  (16 shorter events, 0.1 us)
Async XLA Ops:
  0.6 4.3 %collective-permute-start.1 = (bf16[2,3,256,256]{3,2,1,0:T(8,128)(2,1)}, bf16[2,3,256,256]{3,2,1,0:T(8,128)(2,1)S(1)}, u32[]{:S(2)}, u32[]{:S(2)}) collective-permute-start(bf16[2,3,256,256]{3,2,1,0:T(8,128)(2,1)} %bitcast.21), channel_id=1, source_target_pairs={{0,8},{8,0},{16,24},{24,16},{1,9},{9,1},{17,25},{25,17},{2,10},{10... | collective-permute-start | bytes 2359304 | tf_op jit(solution)/shard_map/ppermute | solution.py:27
  1.1 20.9 %collective-permute-start = (bf16[2,3,256,256]{3,2,1,0:T(8,128)(2,1)}, bf16[2,3,256,256]{3,2,1,0:T(8,128)(2,1)S(1)}, u32[]{:S(2)}, u32[]{:S(2)}) collective-permute-start(bf16[2,3,256,256]{3,2,1,0:T(8,128)(2,1)} %bitcast.22), channel_id=1, source_target_pairs={{0,16},{8,24},{16,0},{24,8},{1,17},{9,25},{17,1},{25,9},{2,18},{10... | collective-permute-start | bytes 2359304 | tf_op jit(solution)/shard_map/ppermute | solution.py:27
  5.0 17.1 %copy-start = (bf16[1,4,2,64,256]{4,3,2,1,0:T(8,128)(2,1)S(1)}, bf16[1,4,2,64,256]{4,3,2,1,0:T(8,128)(2,1)}, u32[]{:S(2)}) copy-start(bf16[1,4,2,64,256]{4,3,2,1,0:T(8,128)(2,1)} %param.9) | copy-start | bytes 786436
  5.0 1.2 %copy-start.2 = (bf16[1,2,3,1,256,256]{5,4,3,2,1,0:T(8,128)(2,1)S(1)}, bf16[1,2,3,1,256,256]{5,4,3,2,1,0:T(8,128)(2,1)}, u32[]{:S(2)}) copy-start(bf16[1,2,3,1,256,256]{5,4,3,2,1,0:T(8,128)(2,1)} %param.5) | copy-start | bytes 2359300
  6.2 0.7 copy-start.4
  6.8 17.6 %copy-start.3 = (bf16[1,2,3,1,256,256]{5,4,3,2,1,0:T(8,128)(2,1)S(1)}, bf16[1,2,3,1,256,256]{5,4,3,2,1,0:T(8,128)(2,1)}, u32[]{:S(2)}) copy-start(bf16[1,2,3,1,256,256]{5,4,3,2,1,0:T(8,128)(2,1)} %param.5) | copy-start | bytes 2359300
  6.8 17.6 %copy-start.5 = (s32[6]{0:T(128)S(1)}, s32[6]{0:T(128)}, u32[]{:S(2)}) copy-start(s32[6]{0:T(128)} %refs_0_.3) | copy-start | bytes 76
  22.1 2.3 %collective-permute-start.2 = (bf16[2,3,256,256]{3,2,1,0:T(8,128)(2,1)S(1)}, bf16[2,3,256,256]{3,2,1,0:T(8,128)(2,1)S(1)}, u32[]{:S(2)}, u32[]{:S(2)}) collective-permute-start(bf16[2,3,256,256]{3,2,1,0:T(8,128)(2,1)S(1)} %collective-permute-done.refs_4_), channel_id=1, source_target_pairs={{0,8},{8,0},{16,24},{24,16},{1,9},{9,1},{17,25},{25,17},{2,10},{10... | collective-permute-start | bytes 2359304 | tf_op jit(solution)/shard_map/ppermute | solution.py:27
  22.1 12.5 %collective-permute-start.3 = (bf16[4,2,64,256]{3,2,1,0:T(8,128)(2,1)S(1)}, bf16[4,2,64,256]{3,2,1,0:T(8,128)(2,1)S(1)}, u32[]{:S(2)}, u32[]{:S(2)}) collective-permute-start(bf16[4,2,64,256]{3,2,1,0:T(8,128)(2,1)S(1)} %bitcast.18), channel_id=1, source_target_pairs={{0,16},{8,24},{16,0},{24,8},{1,17},{9,25},{17,1},{25,9},{2,18},{10... | collective-permute-start | bytes 786440 | tf_op jit(solution)/shard_map/ppermute | solution.py:27
  34.6 13.2 %collective-permute-start.9 = (bf16[6,256,256]{2,1,0:T(8,128)(2,1)S(1)}, bf16[6,256,256]{2,1,0:T(8,128)(2,1)S(1)}, u32[]{:S(2)}, u32[]{:S(2)}) collective-permute-start(bf16[6,256,256]{2,1,0:T(8,128)(2,1)S(1)} %get-tuple-element.30.e_ref), channel_id=1, source_target_pairs={{0,8},{8,0},{16,24},{24,16},{1,9},{9,1},{17,25},{25,17},{2,10},{10... | collective-permute-start | bytes 2359304 | tf_op jit(solution)/shard_map/ppermute | solution.py:27
  34.8 7.2 %collective-permute-start.4 = (bf16[96,1024]{1,0:T(8,128)(2,1)S(1)}, bf16[96,1024]{1,0:T(8,128)(2,1)S(1)}, u32[]{:S(2)}, u32[]{:S(2)}) collective-permute-start(bf16[96,1024]{1,0:T(8,128)(2,1)S(1)} %get-tuple-element.29), channel_id=1, source_target_pairs={{0,1},{1,0},{2,3},{3,2},{4,5},{5,4},{6,7},{7,6},{8,9},{9,8},{10,11... | collective-permute-start | bytes 589832 | tf_op jit(solution)/shard_map/ppermute | solution.py:27
  42.0 13.6 %collective-permute-start.7 = (bf16[2,96,1024]{2,1,0:T(8,128)(2,1)S(1)}, bf16[2,96,1024]{2,1,0:T(8,128)(2,1)S(1)}, u32[]{:S(2)}, u32[]{:S(2)}) collective-permute-start(bf16[2,96,1024]{2,1,0:T(8,128)(2,1)S(1)} %pad_maximum_fusion), channel_id=1, source_target_pairs={{2,4},{3,5},{4,2},{5,3},{0,6},{1,7},{6,0},{7,1},{10,12},{11,13},{1... | collective-permute-start | bytes 1179656 | tf_op jit(solution)/shard_map/ppermute | solution.py:32
  45.9 1.5 %collective-permute-start.10 = (bf16[4,2,64,256]{3,2,1,0:T(8,128)(2,1)S(1)}, bf16[4,2,64,256]{3,2,1,0:T(8,128)(2,1)S(1)}, u32[]{:S(2)}, u32[]{:S(2)}) collective-permute-start(bf16[4,2,64,256]{3,2,1,0:T(8,128)(2,1)S(1)} %bitcast.19), channel_id=1, source_target_pairs={{0,8},{8,0},{16,24},{24,16},{1,9},{9,1},{17,25},{25,17},{2,10},{10... | collective-permute-start | bytes 786440 | tf_op jit(solution)/shard_map/ppermute | solution.py:27
  45.9 1.9 %collective-permute-start.11 = (bf16[4,2,64,256]{3,2,1,0:T(8,128)(2,1)S(1)}, bf16[4,2,64,256]{3,2,1,0:T(8,128)(2,1)S(1)}, u32[]{:S(2)}, u32[]{:S(2)}) collective-permute-start(bf16[4,2,64,256]{3,2,1,0:T(8,128)(2,1)S(1)} %collective-permute-done.3.refs_2_), channel_id=1, source_target_pairs={{0,8},{8,0},{16,24},{24,16},{1,9},{9,1},{17,25},{25,17},{2,10},{10... | collective-permute-start | bytes 786440 | tf_op jit(solution)/shard_map/ppermute | solution.py:27
  51.0 12.0 %collective-permute-start.12 = (bf16[2,2,6,64,128]{4,3,2,1,0:T(8,128)(2,1)S(1)}, bf16[2,2,6,64,128]{4,3,2,1,0:T(8,128)(2,1)S(1)}, u32[]{:S(2)}, u32[]{:S(2)}) collective-permute-start(bf16[2,2,6,64,128]{4,3,2,1,0:T(8,128)(2,1)S(1)} %get-tuple-element.34), channel_id=1, source_target_pairs={{0,1},{1,0},{2,3},{3,2},{4,5},{5,4},{6,7},{7,6},{8,9},{9,8},{10,11... | collective-permute-start | bytes 1179656 | tf_op jit(solution)/shard_map/ppermute | solution.py:27
  52.5 18.1 %collective-permute-start.13 = (bf16[2,2,6,64,128]{4,3,2,1,0:T(8,128)(2,1)S(1)}, bf16[2,2,6,64,128]{4,3,2,1,0:T(8,128)(2,1)S(1)}, u32[]{:S(2)}, u32[]{:S(2)}) collective-permute-start(bf16[2,2,6,64,128]{4,3,2,1,0:T(8,128)(2,1)S(1)} %get-tuple-element.35), channel_id=1, source_target_pairs={{0,1},{1,0},{2,3},{3,2},{4,5},{5,4},{6,7},{7,6},{8,9},{9,8},{10,11... | collective-permute-start | bytes 1179656 | tf_op jit(solution)/shard_map/ppermute | solution.py:27
  53.1 18.2 %collective-permute-start.5 = (bf16[2,96,1024]{2,1,0:T(8,128)(2,1)S(1)}, bf16[2,96,1024]{2,1,0:T(8,128)(2,1)S(1)}, u32[]{:S(2)}, u32[]{:S(2)}) collective-permute-start(bf16[2,96,1024]{2,1,0:T(8,128)(2,1)S(1)} %pad_maximum_fusion), channel_id=1, source_target_pairs={{0,2},{1,3},{2,0},{3,1},{4,6},{5,7},{6,4},{7,5},{8,10},{9,11},{10,... | collective-permute-start | bytes 1179656 | tf_op jit(solution)/shard_map/ppermute | solution.py:32
  53.1 18.2 %collective-permute-start.6 = (bf16[2,96,1024]{2,1,0:T(8,128)(2,1)S(1)}, bf16[2,96,1024]{2,1,0:T(8,128)(2,1)S(1)}, u32[]{:S(2)}, u32[]{:S(2)}) collective-permute-start(bf16[2,96,1024]{2,1,0:T(8,128)(2,1)S(1)} %pad_maximum_fusion), channel_id=1, source_target_pairs={{0,4},{1,5},{6,2},{7,3},{8,12},{9,13},{14,10},{15,11},{16,20},{17,... | collective-permute-start | bytes 1179656 | tf_op jit(solution)/shard_map/ppermute | solution.py:32
  55.6 16.9 %collective-permute-start.8 = (bf16[2,96,1024]{2,1,0:T(8,128)(2,1)S(1)}, bf16[2,96,1024]{2,1,0:T(8,128)(2,1)S(1)}, u32[]{:S(2)}, u32[]{:S(2)}) collective-permute-start(bf16[2,96,1024]{2,1,0:T(8,128)(2,1)S(1)} %collective-permute-done.7.refs_4_), channel_id=1, source_target_pairs={{2,0},{3,1},{4,6},{5,7},{10,8},{11,9},{12,14},{13,15},{18,16},{19,... | collective-permute-start | bytes 1179656 | tf_op jit(solution)/shard_map/ppermute | solution.py:32
  70.6 1.9 %copy-start.1 = (s32[4]{0:T(128)S(1)}, s32[4]{0:T(128)}, u32[]{:S(2)}) copy-start(s32[4]{0:T(128)} %times_ref.1) | copy-start | bytes 52
  74.2 1.3 %collective-permute-start.14 = (f32[2,4,12,12]{3,2,1,0:T(8,128)S(1)}, f32[2,4,12,12]{3,2,1,0:T(8,128)S(1)}, u32[]{:S(2)}, u32[]{:S(2)}) collective-permute-start(f32[2,4,12,12]{3,2,1,0:T(8,128)S(1)} %traces.1), channel_id=1, source_target_pairs={{0,8},{8,0},{16,24},{24,16},{1,9},{9,1},{17,25},{25,17},{2,10},{10... | collective-permute-start | bytes 13832 | tf_op jit(solution)/shard_map/ppermute | solution.py:27
  75.5 4.0 %collective-permute-start.15 = (f32[4,12,12]{2,1,0:T(8,128)S(1)}, f32[4,12,12]{2,1,0:T(8,128)S(1)}, u32[]{:S(2)}, u32[]{:S(2)}) collective-permute-start(f32[4,12,12]{2,1,0:T(8,128)S(1)} %get-tuple-element.39), channel_id=1, source_target_pairs={{0,16},{8,24},{16,0},{24,8},{1,17},{9,25},{17,1},{25,9},{2,18},{10... | collective-permute-start | bytes 6920 | tf_op jit(solution)/shard_map/ppermute | solution.py:27
  77.1 4.2 %collective-permute-start.16 = (f32[4,12,12]{2,1,0:T(8,128)S(1)}, f32[4,12,12]{2,1,0:T(8,128)S(1)}, u32[]{:S(2)}, u32[]{:S(2)}) collective-permute-start(f32[4,12,12]{2,1,0:T(8,128)S(1)} %get-tuple-element.38), channel_id=1, source_target_pairs={{0,1},{1,0},{2,3},{3,2},{4,5},{5,4},{6,7},{7,6},{8,9},{9,8},{10,11... | collective-permute-start | bytes 6920 | tf_op jit(solution)/shard_map/ppermute | solution.py:27
  78.6 4.8 %collective-permute-start.17 = (f32[4,12,12]{2,1,0:T(8,128)S(1)}, f32[4,12,12]{2,1,0:T(8,128)S(1)}, u32[]{:S(2)}, u32[]{:S(2)}) collective-permute-start(f32[4,12,12]{2,1,0:T(8,128)S(1)} %get-tuple-element.38), channel_id=1, source_target_pairs={{0,17},{1,16},{2,19},{3,18},{4,21},{5,20},{6,23},{7,22},{8,25},{9,... | collective-permute-start | bytes 6920 | tf_op jit(solution)/shard_map/ppermute | solution.py:555
